TPU v7x, 32 devices: a whole 2x2x4 slice. The times are simulated.
32 devices in a mesh: seq: 8 (over z, y), head: 4 (over x, core).
Axes of the slice: x: 2, y: 2, z: 4, core: 2. Of those that a mesh axis runs over, the one named last changes fastest.
Arguments:
- tokens: float32 [4, 2048, 1536], P(None, 'seq'), may hold values from -6 to 6
- teacher: float32 [4, 2048, 1536], P(None, 'seq', 'head'), may hold values from -6 to 6
- document_start: int32 [4, 2048], P(None, 'seq'), may hold values from 0 to 2047, as said below
- valid_mask: int32 [4, 2048], replicated, may hold values from 0 to 1, as said below
- input_gain: float32 [1536], replicated, may hold values from 0.5 to 1.5
- gate_weight: bfloat16 [1536, 3072], P(None, 'head'), may hold values from -0.15625 to 0.15625
- value_weight: bfloat16 [1536, 3072], P(None, 'head'), may hold values from -0.15625 to 0.15625
- keyquery_weight: bfloat16 [1536, 256], replicated, may hold values from -0.15625 to 0.15625
- step_weight: bfloat16 [1536, 48], P(None, 'head'), may hold values from -0.15625 to 0.15625
- value_conv_weight: float32 [4, 3072], P(None, 'head'), may hold values from -3 to 3
- value_conv_bias: float32 [3072], P('head'), may hold values from -3 to 3
- keyquery_conv_weight: float32 [4, 256], replicated, may hold values from -3 to 3
- keyquery_conv_bias: float32 [256], replicated, may hold values from -3 to 3
- step_bias: float32 [48], P('head'), may hold values from -9 to -5
- rate_log: float32 [48], P('head'), may hold values from -1 to 1.5
- skip_gain: float32 [48], P('head'), may hold values from 0.5 to 1.5
- norm_gain: float32 [3072], P('head'), may hold values from 0.5 to 1.5
- out_weight: bfloat16 [3072, 1536], P('head'), may hold values from -0.109375 to 0.109375
Outputs:
- output: float32 [4, 2048, 1536], P(None, 'seq', 'head')
- loss_value: float32 [], replicated
- tokens_grad: float32 [4, 2048, 1536], P(None, 'seq', 'head')
- input_gain_grad: float32 [1536], P('head')
- gate_weight_grad: float32 [1536, 3072], P('seq', 'head')
- value_weight_grad: float32 [1536, 3072], P('seq', 'head')
- keyquery_weight_grad: float32 [1536, 256], P('seq')
- step_weight_grad: float32 [1536, 48], P('seq', 'head')
- value_conv_weight_grad: float32 [4, 3072], P(None, 'head')
- value_conv_bias_grad: float32 [3072], P('head')
- keyquery_conv_weight_grad: float32 [4, 256], replicated
- keyquery_conv_bias_grad: float32 [256], replicated
- step_bias_grad: float32 [48], P('head')
- rate_log_grad: float32 [48], P('head')
- skip_gain_grad: float32 [48], P('head')
- norm_gain_grad: float32 [3072], P('head')
- out_weight_grad: float32 [3072, 1536], P('head', 'seq')
Inputs may be any that keep to these rules, and one draw needn't show every extreme that they name: document_start[b, t] is the first position of the document that holds position t of sequence b: document_start[b, 0] = 0, it never falls along t and document_start[b, t] <= t. In every draw one sequence is a single document of all 2048 positions, and in every other sequence the last position begins a document of its own. `valid_mask`: the last position of every sequence is valid.
All inputs are finite; a program needn't handle non-finite values.
Results may differ from a plain program's by a relative error of at most 0.0081.
Values may be sent and summed in bfloat16 or wider, within the bound.
A program may use at most 192 MiB of HBM per device.

v0:
```python
import jax
import jax.numpy as jnp
from jax import lax
from jax.sharding import PartitionSpec as P

D = 1536
NHEADS = 48
HEADDIM = 64
STATE = 128


norm_eps = 1e-05
highest = lax.Precision.HIGHEST


def passed_along(x, axis, by):
    count = lax.axis_size(axis)
    pairs = [(i, i + by) for i in range(count) if 0 <= i + by < count]
    return lax.ppermute(x, axis, pairs)


def carried_in(part, axis, combine, identity, reverse):
    count = lax.axis_size(axis)
    place = lax.axis_index(axis)
    ahead = count - 1 - place if reverse else place
    gathered = jax.tree.map(lambda a: lax.all_gather(a, axis), part)
    state = jax.tree.map(lambda a, e: jnp.zeros_like(a) + jnp.asarray(e, a.dtype), part, identity)

    def one(hop, state):
        source = count - 1 - hop if reverse else hop
        return combine(
            state, jax.tree.map(lambda a: lax.dynamic_index_in_dim(a, source, 0, False), gathered)
        )

    return lax.fori_loop(0, ahead, one, state)


def combine_states(earlier, later):
    return (earlier[0] * later[0], later[0][:, :, None, None] * earlier[1] + later[1])


def silu_slope(linear):
    sigmoid_value = jax.nn.sigmoid(linear)
    return sigmoid_value * (1.0 + linear * (1.0 - sigmoid_value))


def body(
    tokens,
    teacher,
    document_start,
    valid_mask,
    input_gain,
    gate_weight,
    value_weight,
    keyquery_weight,
    step_weight,
    value_conv_weight,
    value_conv_bias,
    keyquery_conv_weight,
    keyquery_conv_bias,
    step_bias,
    rate_log,
    skip_gain,
    norm_gain,
    out_weight,
):
    head_index = lax.axis_index("head")
    sequence_index = lax.axis_index("seq")
    sequence_count = tokens.shape[0]
    shard_length = tokens.shape[1]
    local_heads = skip_gain.shape[0]
    local_inner = local_heads * HEADDIM
    inner_total = NHEADS * HEADDIM
    column_count = D // lax.axis_size("head")
    column_start = head_index * column_count
    shard_begin = sequence_index * shard_length
    positions = shard_begin + jnp.arange(shard_length, dtype=jnp.int32)
    valid_count = jnp.sum(valid_mask.astype(jnp.float32))
    local_mask = lax.dynamic_slice_in_dim(valid_mask, shard_begin, shard_length, 1).astype(
        jnp.float32
    )
    inverse_root = lax.rsqrt(jnp.mean(tokens * tokens, axis=-1, keepdims=True) + norm_eps)
    normed = (tokens * inverse_root * input_gain).astype(jnp.bfloat16)
    gate_linear = jnp.dot(normed, gate_weight, preferred_element_type=jnp.float32)
    values_linear = jnp.dot(normed, value_weight, preferred_element_type=jnp.float32).astype(
        jnp.bfloat16
    )
    keyquery_linear = jnp.dot(normed, keyquery_weight, preferred_element_type=jnp.float32).astype(
        jnp.bfloat16
    )
    steps_linear = jnp.dot(normed, step_weight, preferred_element_type=jnp.float32)
    conv_input = jnp.concatenate([values_linear, keyquery_linear], axis=-1)
    conv_lags = value_conv_weight.shape[0]
    previous = passed_along(conv_input[:, shard_length - (conv_lags - 1) :], "seq", 1)
    extended = jnp.concatenate([previous, conv_input], axis=1).astype(jnp.float32)
    conv_weight = jnp.concatenate([value_conv_weight, keyquery_conv_weight], axis=1)
    conv_offset = jnp.concatenate([value_conv_bias, keyquery_conv_bias], axis=0)
    usable = []
    windows = []
    conv_linear = conv_offset + jnp.zeros_like(extended[:, :shard_length])
    for lag_index in range(conv_lags):
        usable.append(
            (positions[None, :] - lag_index >= document_start).astype(jnp.float32)[:, :, None]
        )
        windows.append(
            extended[:, conv_lags - 1 - lag_index : conv_lags - 1 - lag_index + shard_length]
        )
        conv_linear = conv_linear + conv_weight[lag_index] * windows[lag_index] * usable[lag_index]
    conv_out = jax.nn.silu(conv_linear)
    keys_input = conv_out[..., local_inner : local_inner + STATE]
    queries = conv_out[..., local_inner + STATE :]
    heads_input = conv_out[..., :local_inner].reshape(
        sequence_count, shard_length, local_heads, HEADDIM
    )
    steps = jax.nn.softplus(steps_linear + step_bias)
    decay_rate = -jnp.exp(rate_log)
    rates = steps * decay_rate
    cumulative = jnp.transpose(jnp.cumsum(rates, axis=1), (0, 2, 1))
    steps_heads = jnp.transpose(steps, (0, 2, 1))
    linked = (positions[None, None, :] >= document_start[:, :, None]) & (
        positions[None, None, :] <= positions[None, :, None]
    )
    linked_heads = linked[:, None]
    decay_mat = jnp.where(
        linked_heads,
        jnp.exp(
            jnp.where(linked_heads, cumulative[:, :, :, None] - cumulative[:, :, None, :], 0.0)
        ),
        0.0,
    )
    scores = jnp.einsum("btn,bun->btu", queries, keys_input, precision=highest)
    mixing = decay_mat * scores[:, None] * steps_heads[:, :, None, :]
    local_out = jnp.einsum("bhtu,buhp->bthp", mixing, heads_input, precision=highest)
    kept_mask = (document_start < shard_begin).astype(jnp.float32)
    entering = jnp.exp(cumulative) * kept_mask[:, None, :]
    trailing = (positions[None, :] >= document_start[:, -1:]).astype(jnp.float32)
    end_decay = jnp.exp(cumulative[:, :, -1:] - cumulative) * trailing[:, None, :]
    weights_end = end_decay * steps_heads
    state_local = jnp.einsum(
        "bhu,buhp,bun->bhpn", weights_end, heads_input, keys_input, precision=highest
    )
    passed = jnp.exp(cumulative[:, :, -1]) * kept_mask[:, -1:]
    identity = (jnp.ones_like(passed), jnp.zeros_like(state_local))
    state_in = carried_in((passed, state_local), "seq", combine_states, identity, False)[1]
    projected = jnp.einsum("btn,bhpn->bthp", queries, state_in, precision=highest)
    entering_rows = jnp.transpose(entering, (0, 2, 1))
    mixed_heads = (
        local_out + entering_rows[..., None] * projected + skip_gain[:, None] * heads_input
    )
    mixed_flat = mixed_heads.reshape(sequence_count, shard_length, local_inner)
    gate_act = jax.nn.silu(gate_linear)
    gated_out = mixed_flat * gate_act
    square_sum = lax.psum(jnp.sum(gated_out * gated_out, axis=-1), "head")
    row_scale = lax.rsqrt(square_sum / inner_total + norm_eps)[..., None]
    normed_out = (gated_out * row_scale * norm_gain).astype(jnp.bfloat16)
    branch_terms = jnp.dot(normed_out, out_weight, preferred_element_type=jnp.float32)
    branch = lax.psum_scatter(branch_terms, "head", scatter_dimension=2, tiled=True)
    token_cols = lax.dynamic_slice_in_dim(tokens, column_start, column_count, 2)
    output = token_cols + branch
    difference = output - teacher
    loss_part = jnp.sum(local_mask[..., None] * difference * difference)
    out_grad = 2.0 * difference * local_mask[..., None] / (D * valid_count)
    piece_cols = lax.all_gather(out_grad.astype(jnp.bfloat16), "head", axis=2, tiled=True)
    grad_rows = jnp.einsum(
        "btd,cd->btc", piece_cols, out_weight, preferred_element_type=jnp.float32
    )
    column_grad = jnp.einsum(
        "btc,btd->cd", normed_out, piece_cols, preferred_element_type=jnp.float32
    )
    gain_out_grad = jnp.sum(grad_rows * gated_out * row_scale, axis=(0, 1))
    row_partial = jnp.sum(norm_gain * grad_rows * gated_out, axis=-1)
    row_total, loss_heads = lax.psum((row_partial, loss_part), "head")
    gated_grad = (
        row_scale * norm_gain * grad_rows
        - gated_out * row_scale**3 * (row_total / inner_total)[..., None]
    )
    mixed_grad = gated_grad * gate_act
    gate_grad = (gated_grad * mixed_flat * silu_slope(gate_linear)).astype(jnp.bfloat16)
    heads_grad = mixed_grad.reshape(sequence_count, shard_length, local_heads, HEADDIM)
    skip_gain_grad = jnp.einsum("bthp,bthp->h", heads_grad, heads_input, precision=highest)
    state_local_grad = jnp.einsum(
        "bht,bthp,btn->bhpn", entering, heads_grad, queries, precision=highest
    )
    end_grad = carried_in((passed, state_local_grad), "seq", combine_states, identity, True)[1]
    pairwise = jnp.einsum("bthp,buhp->bhtu", heads_grad, heads_input, precision=highest)
    heads_input_grad = skip_gain[:, None] * heads_grad
    heads_input_grad = heads_input_grad + jnp.einsum(
        "bhtu,bthp->buhp", mixing, heads_grad, precision=highest
    )
    heads_input_grad = heads_input_grad + jnp.einsum(
        "bhu,bhpn,bun->buhp", weights_end, end_grad, keys_input, precision=highest
    )
    weighted = pairwise * decay_mat
    scores_grad = jnp.einsum("bhtu,bhu->btu", weighted, steps_heads, precision=highest)
    steps_grad = jnp.einsum("bhtu,btu->bhu", weighted, scores, precision=highest)
    cum_terms = weighted * scores[:, None] * steps_heads[:, :, None, :]
    cum_grad = jnp.sum(cum_terms, axis=-1) - jnp.sum(cum_terms, axis=-2)
    queries_grad = jnp.einsum("btu,bun->btn", scores_grad, keys_input, precision=highest)
    queries_grad = queries_grad + jnp.einsum(
        "bht,bthp,bhpn->btn", entering, heads_grad, state_in, precision=highest
    )
    keys_grad = jnp.einsum("btu,btn->bun", scores_grad, queries, precision=highest)
    keys_grad = keys_grad + jnp.einsum(
        "bhu,bhpn,buhp->bun", weights_end, end_grad, heads_input, precision=highest
    )
    entering_grad = jnp.einsum("bthp,bthp->bht", heads_grad, projected, precision=highest)
    cum_grad = cum_grad + entering_grad * entering
    passed_grad = jnp.einsum("bhpn,bhpn->bh", end_grad, state_in, precision=highest)
    end_term = jnp.einsum(
        "bhpn,buhp,bun->bhu", end_grad, heads_input, keys_input, precision=highest
    )
    steps_grad = steps_grad + end_term * end_decay
    end_mix = end_term * weights_end
    cum_grad = cum_grad - end_mix
    last_term = passed_grad * passed + jnp.sum(end_mix, axis=-1)
    last_slot = (jnp.arange(shard_length, dtype=jnp.int32) == shard_length - 1).astype(jnp.float32)
    cum_grad = cum_grad + last_term[:, :, None] * last_slot
    rates_grad = jnp.flip(jnp.cumsum(jnp.flip(cum_grad, axis=-1), axis=-1), axis=-1)
    steps_grad = steps_grad + rates_grad * decay_rate[None, :, None]
    rate_log_grad = jnp.sum(rates_grad * steps_heads, axis=(0, 2)) * decay_rate
    steps_linear_grad = jnp.transpose(steps_grad, (0, 2, 1)) * jax.nn.sigmoid(
        steps_linear + step_bias
    )
    step_bias_grad = jnp.sum(steps_linear_grad, axis=(0, 1))
    keyquery_sums = lax.psum(jnp.concatenate([keys_grad, queries_grad], axis=-1), "head")
    conv_out_grad = jnp.concatenate(
        [heads_input_grad.reshape(sequence_count, shard_length, local_inner), keyquery_sums],
        axis=-1,
    )
    conv_linear_grad = conv_out_grad * silu_slope(conv_linear)
    conv_offset_grad = jnp.sum(conv_linear_grad, axis=(0, 1))
    conv_channels = conv_linear_grad.shape[2]
    weight_rows = []
    conv_input_grad = conv_weight[0] * conv_linear_grad * usable[0]
    edge_grad = jnp.zeros((sequence_count, conv_lags - 1, conv_channels), jnp.float32)
    for lag_index in range(conv_lags):
        masked = conv_linear_grad * usable[lag_index]
        weight_rows.append(jnp.sum(masked * windows[lag_index], axis=(0, 1)))
        if lag_index > 0:
            tail_zeros = jnp.zeros((sequence_count, lag_index, conv_channels), jnp.float32)
            conv_input_grad = conv_input_grad + conv_weight[lag_index] * jnp.concatenate(
                [masked[:, lag_index:], tail_zeros], axis=1
            )
            head_zeros = jnp.zeros(
                (sequence_count, conv_lags - 1 - lag_index, conv_channels), jnp.float32
            )
            edge_grad = edge_grad + jnp.concatenate(
                [head_zeros, conv_weight[lag_index] * masked[:, :lag_index]], axis=1
            )
    conv_weight_grad = jnp.stack(weight_rows, axis=0)
    incoming = passed_along(edge_grad, "seq", -1)
    lead_zeros = jnp.zeros(
        (sequence_count, shard_length - (conv_lags - 1), conv_channels), jnp.float32
    )
    conv_input_grad = conv_input_grad + jnp.concatenate([lead_zeros, incoming], axis=1)
    values_grad = conv_input_grad[..., :local_inner].astype(jnp.bfloat16)
    keyquery_grad = conv_input_grad[..., local_inner:].astype(jnp.bfloat16)
    steps_low = steps_linear_grad.astype(jnp.bfloat16)
    input_terms = jnp.einsum(
        "btc,dc->btd", gate_grad, gate_weight, preferred_element_type=jnp.float32
    )
    input_terms = input_terms + jnp.einsum(
        "btc,dc->btd", values_grad, value_weight, preferred_element_type=jnp.float32
    )
    input_terms = input_terms + jnp.einsum(
        "btc,dc->btd", steps_low, step_weight, preferred_element_type=jnp.float32
    )
    normed_grad = lax.psum_scatter(input_terms, "head", scatter_dimension=2, tiled=True)
    keyquery_rows = lax.dynamic_slice_in_dim(keyquery_weight, column_start, column_count, 0)
    normed_grad = normed_grad + jnp.einsum(
        "btc,dc->btd", keyquery_grad, keyquery_rows, preferred_element_type=jnp.float32
    )
    gain_cols = lax.dynamic_slice_in_dim(input_gain, column_start, column_count, 0)
    row_input = jnp.sum(gain_cols * normed_grad * token_cols, axis=-1)
    row_input_total = lax.psum(row_input, "head")
    tokens_grad = (
        out_grad
        + inverse_root * gain_cols * normed_grad
        - token_cols * inverse_root**3 * row_input_total[..., None] / D
    )
    input_gain_partial = jnp.sum(normed_grad * token_cols * inverse_root, axis=(0, 1))
    gate_weight_part = jnp.einsum(
        "btd,btc->dc", normed, gate_grad, preferred_element_type=jnp.float32
    )
    value_weight_part = jnp.einsum(
        "btd,btc->dc", normed, values_grad, preferred_element_type=jnp.float32
    )
    step_weight_part = jnp.einsum(
        "btd,btc->dc", normed, steps_low, preferred_element_type=jnp.float32
    )
    keyquery_weight_part = jnp.einsum(
        "btd,btc->dc", normed, keyquery_grad, preferred_element_type=jnp.float32
    )
    gate_weight_grad, value_weight_grad, step_weight_grad, keyquery_weight_grad, out_weight_grad = (
        lax.psum_scatter(gate_weight_part, "seq", scatter_dimension=0, tiled=True),
        lax.psum_scatter(value_weight_part, "seq", scatter_dimension=0, tiled=True),
        lax.psum_scatter(step_weight_part, "seq", scatter_dimension=0, tiled=True),
        lax.psum_scatter(keyquery_weight_part, "seq", scatter_dimension=0, tiled=True),
        lax.psum_scatter(column_grad, "seq", scatter_dimension=1, tiled=True),
    )
    small_sums = lax.psum(
        (
            conv_weight_grad,
            conv_offset_grad,
            step_bias_grad,
            rate_log_grad,
            skip_gain_grad,
            gain_out_grad,
            input_gain_partial,
            loss_heads,
        ),
        "seq",
    )
    (
        conv_weight_total,
        conv_offset_total,
        step_bias_total,
        rate_log_total,
        skip_gain_total,
        norm_gain_total,
        input_gain_total,
        loss_total,
    ) = small_sums
    loss_value = loss_total / (D * valid_count)
    return (
        output,
        loss_value,
        tokens_grad,
        input_gain_total,
        gate_weight_grad,
        value_weight_grad,
        keyquery_weight_grad,
        step_weight_grad,
        conv_weight_total[:, :local_inner],
        conv_offset_total[:local_inner],
        conv_weight_total[:, local_inner:],
        conv_offset_total[local_inner:],
        step_bias_total,
        rate_log_total,
        skip_gain_total,
        norm_gain_total,
        out_weight_grad,
    )


def solution(mesh):
    placed = (
        P(None, "seq", None),
        P(None, "seq", "head"),
        P(None, "seq"),
        P(),
        P(),
        P(None, "head"),
        P(None, "head"),
        P(),
        P(None, "head"),
        P(None, "head"),
        P("head"),
        P(),
        P(),
        P("head"),
        P("head"),
        P("head"),
        P("head"),
        P("head", None),
    )
    return jax.shard_map(
        body,
        mesh=mesh,
        in_specs=placed,
        out_specs=(
            P(None, "seq", "head"),
            P(),
            P(None, "seq", "head"),
            P("head"),
            P("seq", "head"),
            P("seq", "head"),
            P("seq", None),
            P("seq", "head"),
            P(None, "head"),
            P("head"),
            P(),
            P(),
            P("head"),
            P("head"),
            P("head"),
            P("head"),
            P("head", "seq"),
        ),
        check_vma=False,
    )
```

profile of v0, /device:TPU:0, one launch (start us, length us, event | category | flops | bytes accessed | tf_op | source)
XLA Modules:
  0.0 1227.9 jit_solution(11565499431297374519)
XLA Ops:
  53.8 26.8 %all_gather.21 = f32[8,4,12]{2,1,0:T(4,128)S(1)} all-gather(f32[1,4,12]{2,1,0:T(4,128)S(1)} %bitcast_multiply_fusion.1), channel_id=1, replica_groups=mesh['seq'=8,'head'=4] {'seq'}, dimensions={0}, use_global_device_ids=true | all-gather | bytes 1728 | tf_op jit(solution)/shard_map/all_gather | solution.py:26
  83.9 146.1 %all-gather.8.cloned.1.call-done = f32[32,12,64,128]{3,2,1,0:T(8,128)} async-done(((f32[4,12,64,128]{3,2,1,0:T(8,128)}), f32[32,12,64,128]{3,2,1,0:T(8,128)}) %all-gather.8.cloned.1.call-update) | async-done | bytes 12582928 | tf_op jit(solution)/shard_map/all_gather | solution.py:26
  236.4 16.1 %fusion.19 = f32[4,256,12,64]{1,3,2,0:T(8,128)} fusion(f32[4,256,12,64]{1,3,2,0:T(8,128)S(1)} %bitcast.217, f32[4,256,12,64]{1,3,2,0:T(8,128)S(1)} %fusion.60, f32[4,12,256]{2,1,0:T(8,128)S(1)} %copy-done.38, f32[4,256,256]{2,1,0:T(8,128)S(1)} %fusion.71, f32[4,12,256]{2,1,0:T(8,128)S(1)} %copy-done.41, pred[4,256,256]{2,1,0:T(8,128)(4,1)S(1)} %copy-done.31, ...), kind=kOutput, calls=%fused_computation.44 | convolution fusion | flops 2434793472 | bytes 10895408 | tf_op jit(solution)/shard_map/bhtu,buhp->bthp/dot_general | solution.py:133
  256.0 8.9 multiply_reduce_fusion.12
  264.9 6.8 psum.91
  273.6 7.9 fusion.31
  284.9 75.7 %reduce-scatter.10.cloned.1.call-done = f32[4,256,384]{2,1,0:T(8,128)} async-done(((f32[4,256,1536]{2,1,0:T(8,128)}), f32[4,256,384]{2,1,0:T(8,128)}) %reduce-scatter.10.cloned.1.call-update) | async-done | bytes 1572880 | tf_op jit(solution)/shard_map/reduce_scatter | solution.py:157
  365.0 28.4 %all-gather.6.cloned.1.call-done = bf16[4,256,1536]{2,1,0:T(8,128)(2,1)} async-done(((bf16[4,256,384]{2,1,0:T(8,128)(2,1)}), bf16[4,256,1536]{2,1,0:T(8,128)(2,1)}) %all-gather.6.cloned.1.call-update) | async-done | bytes 3145744 | tf_op jit(solution)/shard_map/all_gather | solution.py:163
  393.4 8.6 multiply_reduce_fusion.10
  402.0 6.6 psum.94
  409.2 7.1 multiply_convert_fusion.1
  426.5 8.6 fusion.53
  443.9 18.4 %fusion.3 = (f32[4,12,256]{2,1,0:T(8,128)}, f32[4,12,256]{2,1,0:T(8,128)}, f32[4,12,256,256]{3,2,1,0:T(8,128)}) fusion(f32[4,12,256]{2,1,0:T(8,128)S(1)} %copy-done.39, f32[4,256,256]{2,1,0:T(8,128)S(1)} %fusion.71, f32[4,12,256]{2,1,0:T(8,128)S(1)} %copy-done.42, pred[4,256,256]{2,1,0:T(8,128)(4,1)S(1)} %copy-done.32, ...), kind=kOutput, calls=%fused_computation.12 | convolution fusion | flops 2441060352 | bytes 20381696 | tf_op jit(solution)/shard_map/bthp,buhp->bhtu/dot_general | solution.py:185
  462.2 6.2 multiply_reduce_fusion
  468.4 135.2 %all-gather.10.cloned.1.call-done = f32[32,12,64,128]{3,2,1,0:T(8,128)} async-done(((f32[4,12,64,128]{3,2,1,0:T(8,128)}), f32[32,12,64,128]{3,2,1,0:T(8,128)}) %all-gather.10.cloned.1.call-update) | async-done | bytes 12582928 | tf_op jit(solution)/shard_map/all_gather | solution.py:26
  604.9 23.1 %while.27 = (s32[]{:T(128)}, f32[4,12,64,128]{3,2,1,0:T(8,128)}, s32[]{:T(128)}, f32[8,4,12]{2,1,0:T(4,128)S(1)}, f32[8,4,12,64,128]{4,3,2,1,0:T(8,128)}, /*index=5*/s32[]{:T(128)}, s32[]{:T(128)}, s32[]{:T(128)}, s32[]{:T(128)}) while((s32[]{:T(128)}, f32[4,12,64,128]{3,2,1,0:T(8,128)}, s32[]{:T(128)}, f32[8,4,12]{2,1,0:T(4,128)S(1)}, ...), condition=%wide.region_15.16_spmd, body=%wide.region_14.15_spmd.sunk | while | flops 786438 | bytes 4719323 | solution.py:35
  629.9 7.1 fusion.50
  641.4 13.0 %fusion.18 = f32[4,256,12,64]{1,3,2,0:T(8,128)} fusion(f32[4,256,12,64]{1,3,2,0:T(8,128)S(1)} %get-tuple-element.230, f32[4,256,12,64]{1,3,2,0:T(8,128)S(1)} %bitcast.226, f32[4,12,256]{2,1,0:T(8,128)S(1)} %copy-done.40, f32[4,256,256]{2,1,0:T(8,128)S(1)} %fusion.71, f32[4,12,256]{2,1,0:T(8,128)S(1)} %copy-done.43, pred[4,256,256]{2,1,0:T(8,128)(4,1)S(1)} %copy-done.33, ...), kind=kOutput, calls=%fused_computation.42 | convolution fusion | flops 2434793472 | bytes 10895408 | tf_op jit(solution)/shard_map/bhtu,bthp->buhp/dot_general | solution.py:187
  677.9 29.5 %all-reduce.10.cloned.1.call-done = f32[4,256,256]{2,1,0:T(8,128)} async-done(((f32[4,256,256]{2,1,0:T(8,128)}), f32[4,256,256]{2,1,0:T(8,128)}) %all-reduce.10.cloned.1.call-update) | async-done | bytes 1048592 | tf_op jit(solution)/shard_map/psum | solution.py:225
  707.4 15.4 %multiply_reduce_fusion.6 = (f32[1024]{0:T(1024)S(1)}, f32[1024]{0:T(1024)S(1)}, f32[1024]{0:T(1024)S(1)}, f32[1024]{0:T(1024)S(1)}, f32[1024]{0:T(1024)S(1)}, /...) fusion(f32[4,259,1024]{2,1,0:T(8,128)} %copy-done.2, ...), kind=kLoop, calls=%fused_computation.33 | loop fusion | flops 23063552 | bytes 41979904 | tf_op jit(solution)/shard_map/reduce_sum | solution.py:238
  739.2 7.4 add_add_fusion
  747.4 7.8 convolution_bitcast_fusion
  755.3 7.2 convolution_bitcast_fusion.2
  767.0 6.8 convolution_bitcast_fusion.1
  780.3 12.4 %reduce-scatter.22.cloned.1.call-done = f32[192,12]{1,0:T(8,128)} async-done(((f32[1536,12]{1,0:T(8,128)}), f32[192,12]{1,0:T(8,128)}) %reduce-scatter.22.cloned.1.call-update) | async-done | bytes 9232
  794.3 58.5 %reduce-scatter.12.cloned.1.call-done = f32[4,256,384]{2,1,0:T(8,128)} async-done(((f32[4,256,1536]{2,1,0:T(8,128)}), f32[4,256,384]{2,1,0:T(8,128)}) %reduce-scatter.12.cloned.1.call-update) | async-done | bytes 1572880 | tf_op jit(solution)/shard_map/reduce_scatter | solution.py:268
  856.6 6.5 all-reduce.7
  863.1 40.7 %all-reduce.6 = (f32[]{:T(128)}, f32[384]{0:T(512)}, f32[4,1024]{1,0:T(4,128)S(1)}, f32[1024]{0:T(1024)S(1)}, f32[12]{0:T(128)}, /*index=5*/f32[12]{0:T(128)}, f32[12]{0:T(128)}, f32[768]{0:T(1024)}) all-reduce(f32[]{:T(128)} %get-tuple-element.186, f32[384]{0:T(512)S(1)} %get-tuple-element.149, ...), channel_id=1, replica_groups=mesh['seq'=8,'head'=4] {'seq'}, use_global_device_ids=true, to_apply=%region_10.11 | all-reduce | flops 6309 | bytes 50472 | tf_op jit(solution)/shard_map/psum | solution.py:301
  910.9 42.1 %reduce-scatter.20.cloned.1.call-done = f32[768,192]{0,1:T(8,128)} async-done(((f32[768,1536]{0,1:T(8,128)}), f32[768,192]{0,1:T(8,128)}) %reduce-scatter.20.cloned.1.call-update) | async-done | bytes 589840 | tf_op jit(solution)/shard_map/reduce_scatter | solution.py:299
  953.0 99.3 %reduce-scatter.14.cloned.1.call-done = f32[192,768]{1,0:T(8,128)} async-done(((f32[1536,768]{1,0:T(8,128)}), f32[192,768]{1,0:T(8,128)}) %reduce-scatter.14.cloned.1.call-update) | async-done | bytes 589840 | tf_op jit(solution)/shard_map/reduce_scatter | solution.py:295
  1052.3 68.5 %reduce-scatter.18.cloned.1.call-done = f32[192,256]{1,0:T(8,128)} async-done(((f32[1536,256]{1,0:T(8,128)}), f32[192,256]{1,0:T(8,128)}) %reduce-scatter.18.cloned.1.call-update) | async-done | bytes 196624 | tf_op jit(solution)/shard_map/reduce_scatter | solution.py:298
  1120.8 99.0 %reduce-scatter.16.cloned.1.call-done = f32[192,768]{1,0:T(8,128)} async-done(((f32[1536,768]{1,0:T(8,128)}), f32[192,768]{1,0:T(8,128)}) %reduce-scatter.16.cloned.1.call-update) | async-done | bytes 589840 | tf_op jit(solution)/shard_map/reduce_scatter | solution.py:296
  (316 shorter events, 181.3 us)
Async XLA Ops:
  7.2 248.8 %copy-start = (bf16[1536,768]{1,0:T(8,128)(2,1)S(1)}, bf16[1536,768]{1,0:T(8,128)(2,1)}, u32[]{:S(2)}) copy-start(bf16[1536,768]{1,0:T(8,128)(2,1)} %param.27) | copy-start | bytes 7077892
  7.2 222.8 %all-gather.8.cloned.1.call-start = ((), (), s32[]{:S(2)}) async-start(), calls=%async_computation.15 | async-start | bytes 14155776 | tf_op jit(solution)/shard_map/all_gather | solution.py:26
  19.7 12.5 %copy-start.74 = (f32[768]{0:T(1024)S(1)}, f32[768]{0:T(1024)}, u32[]{:S(2)}) copy-start(f32[768]{0:T(1024)} %param.32) | copy-start | bytes 9220
  19.7 12.5 %copy-start.78 = (f32[256]{0:T(256)S(1)}, f32[256]{0:T(256)}, u32[]{:S(2)}) copy-start(f32[256]{0:T(256)} %param.34) | copy-start | bytes 3076
  19.7 12.5 %collective-permute-start = (bf16[4,3,1024]{2,1,0:T(4,128)(2,1)S(1)}, bf16[4,3,1024]{2,1,0:T(4,128)(2,1)S(1)}, u32[]{:S(2)}, u32[]{:S(2)}) collective-permute-start(bf16[4,3,1024]{2,1,0:T(4,128)(2,1)S(1)} %pad_maximum_fusion.1), channel_id=1, source_target_pairs={{0,4},{4,8},{8,12},{12,16},{16,20},{20,24},{24,28},{1,5},{5,9},{9,... | collective-permute-start | bytes 73736 | tf_op jit(solution)/shard_map/ppermute | solution.py:19
  31.5 21.6 %copy-start.50 = (f32[4,256]{1,0:T(4,128)}, f32[4,256]{1,0:T(4,128)S(1)}, u32[]{:S(2)}) copy-start(f32[4,256]{1,0:T(4,128)S(1)} %get-tuple-element.219) | copy-start | bytes 12292
  32.2 14.8 %copy-start.27 = (f32[4,256,12]{1,2,0:T(8,128)}, f32[4,256,12]{1,2,0:T(8,128)S(1)}, u32[]{:S(2)}) copy-start(f32[4,256,12]{1,2,0:T(8,128)S(1)} %get-tuple-element.209) | copy-start | bytes 147460
  53.0 307.6 %reduce-scatter.10.cloned.1.call-start = ((), (), s32[]{:S(2)}) async-start(), calls=%async_computation.7 | async-start | bytes 7864320 | tf_op jit(solution)/shard_map/reduce_scatter | solution.py:157
  236.3 16.1 %copy-start.20 = (f32[4,256,12,64]{1,3,2,0:T(8,128)}, f32[4,256,12,64]{1,3,2,0:T(8,128)S(1)}, u32[]{:S(2)}) copy-start(f32[4,256,12,64]{1,3,2,0:T(8,128)S(1)} %fusion.60) | copy-start | bytes 9437188
  281.6 111.8 %all-gather.6.cloned.1.call-start = ((), (), s32[]{:S(2)}) async-start(), calls=%async_computation.8 | async-start | bytes 3932160 | tf_op jit(solution)/shard_map/all_gather | solution.py:163
  364.8 238.8 %all-gather.10.cloned.1.call-start = ((), (), s32[]{:S(2)}) async-start(), calls=%async_computation.16 | async-start | bytes 14155776 | tf_op jit(solution)/shard_map/all_gather | solution.py:26
  425.9 281.5 %all-reduce.10.cloned.1.call-start = ((), (), s32[]{:S(2)}) async-start(), calls=%async_computation.9 | async-start | bytes 2097152 | tf_op jit(solution)/shard_map/psum | solution.py:225
  604.9 23.2 %copy-start.3 = (f32[4,12,64,128]{3,2,1,0:T(8,128)S(1)}, f32[4,12,64,128]{3,2,1,0:T(8,128)}, u32[]{:S(2)}) copy-start(f32[4,12,64,128]{3,2,1,0:T(8,128)} %get-tuple-element.145) | copy-start | bytes 4718596
  674.0 118.7 %reduce-scatter.22.cloned.1.call-start = ((), (), s32[]{:S(2)}) async-start(), calls=%async_computation.17 | async-start | bytes 884736
  674.2 33.2 %copy-start.55 = (f32[4,256]{1,0:T(4,128)S(1)}, f32[4,256]{1,0:T(4,128)}, u32[]{:S(2)}) copy-start(f32[4,256]{1,0:T(4,128)} %copy-done.54) | copy-start | bytes 12292
  674.2 33.2 %copy-start.57 = (f32[4,256]{1,0:T(4,128)S(1)}, f32[4,256]{1,0:T(4,128)}, u32[]{:S(2)}) copy-start(f32[4,256]{1,0:T(4,128)} %copy-done.56) | copy-start | bytes 12292
  674.2 33.2 %copy-start.59 = (f32[4,256]{1,0:T(4,128)S(1)}, f32[4,256]{1,0:T(4,128)}, u32[]{:S(2)}) copy-start(f32[4,256]{1,0:T(4,128)} %copy-done.58) | copy-start | bytes 12292
  707.4 15.4 %copy-start.49 = (f32[1,1024]{1,0:T(1,128)S(1)}, f32[1,1024]{1,0:T(1,128)}, u32[]{:S(2)}) copy-start(f32[1,1024]{1,0:T(1,128)} %copy-done.48) | copy-start | bytes 12292
  707.4 16.5 %copy-start.47 = (f32[1,1024]{1,0:T(1,128)S(1)}, f32[1,1024]{1,0:T(1,128)}, u32[]{:S(2)}) copy-start(f32[1,1024]{1,0:T(1,128)} %copy-done.46) | copy-start | bytes 12292
  707.4 19.1 %copy-start.13 = (bf16[4,256,1536]{2,1,0:T(8,128)(2,1)S(1)}, bf16[4,256,1536]{2,1,0:T(8,128)(2,1)}, u32[]{:S(2)}) copy-start(bf16[4,256,1536]{2,1,0:T(8,128)(2,1)} %copy-done.12) | copy-start | bytes 9437188
  725.1 9.7 collective-permute-start.1
  728.5 124.3 %reduce-scatter.12.cloned.1.call-start = ((), (), s32[]{:S(2)}) async-start(), calls=%async_computation.10 | async-start | bytes 7864320 | tf_op jit(solution)/shard_map/reduce_scatter | solution.py:268
  739.2 27.8 %copy-start.21 = (bf16[4,256,1024]{2,1,0:T(8,128)(2,1)}, bf16[4,256,1024]{2,1,0:T(8,128)(2,1)S(1)}, u32[]{:S(2)}) copy-start(bf16[4,256,1024]{2,1,0:T(8,128)(2,1)S(1)} %add_convert_fusion) | copy-start | bytes 6291460
  746.7 206.3 %reduce-scatter.20.cloned.1.call-start = ((), (), s32[]{:S(2)}) async-start(), calls=%async_computation.14 | async-start | bytes 5308416 | tf_op jit(solution)/shard_map/reduce_scatter | solution.py:299
  755.2 297.1 %reduce-scatter.14.cloned.1.call-start = ((), (), s32[]{:S(2)}) async-start(), calls=%async_computation.11 | async-start | bytes 5308416 | tf_op jit(solution)/shard_map/reduce_scatter | solution.py:295
  762.5 358.2 %reduce-scatter.18.cloned.1.call-start = ((), (), s32[]{:S(2)}) async-start(), calls=%async_computation.13 | async-start | bytes 1769472 | tf_op jit(solution)/shard_map/reduce_scatter | solution.py:298
  766.7 453.1 %reduce-scatter.16.cloned.1.call-start = ((), (), s32[]{:S(2)}) async-start(), calls=%async_computation.12 | async-start | bytes 5308416 | tf_op jit(solution)/shard_map/reduce_scatter | solution.py:296
  777.8 75.0 %copy-start.37 = (f32[4,256]{1,0:T(4,128)S(1)}, f32[4,256]{1,0:T(4,128)}, u32[]{:S(2)}) copy-start(f32[4,256]{1,0:T(4,128)} %copy-done.36) | copy-start | bytes 12292
  780.3 82.8 %copy-start.72 = (f32[768]{0:T(1024)S(1)}, f32[768]{0:T(1024)}, u32[]{:S(2)}) copy-start(f32[768]{0:T(1024)} %get-tuple-element.151) | copy-start | bytes 9220
  780.3 126.0 %copy-start.53 = (f32[4,256]{1,0:T(4,128)S(1)}, f32[4,256]{1,0:T(4,128)}, u32[]{:S(2)}) copy-start(f32[4,256]{1,0:T(4,128)} %get-tuple-element.196) | copy-start | bytes 12292
  780.3 126.0 %copy-start.63 = (f32[4,256]{1,0:T(4,128)S(1)}, f32[4,256]{1,0:T(4,128)}, u32[]{:S(2)}) copy-start(f32[4,256]{1,0:T(4,128)} %get-tuple-element.215) | copy-start | bytes 12292
  906.2 313.6 %copy-start.1 = (bf16[1536,768]{1,0:T(8,128)(2,1)S(1)}, bf16[1536,768]{1,0:T(8,128)(2,1)}, u32[]{:S(2)}) copy-start(bf16[1536,768]{1,0:T(8,128)(2,1)} %param.27) | copy-start | bytes 7077892
  (68 other events, 292.9 us)
Sparse Core Ops, SparseCore 0:
  53.1 176.7 all-gather.7
  281.7 78.8 reduce-scatter.9
  364.9 28.4 all-gather.5
  426.0 177.4 all-gather.9
  674.1 33.2 all-reduce.9
  728.6 63.9 reduce-scatter.21
  795.4 57.3 reduce-scatter.11
  857.0 95.9 reduce-scatter.19
  957.2 95.0 reduce-scatter.13
  1056.1 64.5 reduce-scatter.17
  1125.5 94.2 reduce-scatter.15
where the time goes:
time: 1240 us; the launch traced here: 1230 us
  waiting for transfers between devices  795 us (64%)
  matrix products  171 us (14%)
  other arithmetic  107 us (9%)
  blocking collectives  87.4 us (7%)
  local copies, waits for them, and re-layouts  42.1 us (3%)
  between operations  17.8 us (1%)
    all_gather x2, waiting for transfers between devices, carried_in(): gathered = jax.tree.map(lambda a: lax.all_gather(a, axis), part)  281 us
    reduce_scatter x1, waiting for transfers between devices, body(): lax.psum_scatter(gate_weight_part, 'seq', scatter_dimension=0, tiled=True)  99.3 us
    reduce_scatter x1, waiting for transfers between devices, body(): lax.psum_scatter(value_weight_part, 'seq', scatter_dimension=0, tiled=True)  99 us
    reduce_scatter x1, waiting for transfers between devices, body(): lax.psum_scatter(branch_terms, 'head', scatter_dimension=2, tiled=True)  75.7 us
    reduce_scatter x1, waiting for transfers between devices, body(): lax.psum_scatter(keyquery_weight_part, 'seq', scatter_dimension=0, tiled=...  68.5 us
    reduce_scatter x1, waiting for transfers between devices, body(): lax.psum_scatter(input_terms, 'head', scatter_dimension=2, tiled=True)  58.5 us
    reduce_scatter x1, waiting for transfers between devices, body(): lax.psum_scatter(column_grad, 'seq', scatter_dimension=1, tiled=True)  42.1 us
    psum x1, blocking collectives, body(): lax.psum((conv_weight_grad, conv_offset_grad, step_bias_grad, rate_log_gr...  40.7 us
  transfers between devices with their start and end apart: 13, of which 11 were waited for; matrix products, arithmetic and copies ran while one was open for 10% of the time, Pallas kernels for 0%

commit v1 on v0

v1 whole, which is shorter than its diff:
```python
import functools

import jax
import jax.numpy as jnp
from jax import lax
from jax.experimental import pallas as pl
from jax.experimental.pallas import tpu as pltpu
from jax.sharding import PartitionSpec as P

D = 1536
NHEADS = 48
HEADDIM = 64
STATE = 128
LANES = 128
VMEM_LIMIT = 56 << 20

norm_eps = 1e-05
highest = lax.Precision.HIGHEST
MESH = pl.DeviceIdType.MESH
f32 = jnp.float32
bf16 = jnp.bfloat16
NT = (((1,), (1,)), ((), ()))
TN = (((0,), (0,)), ((), ()))

in_vmem = pl.BlockSpec(memory_space=pltpu.VMEM)
in_smem = pl.BlockSpec(memory_space=pltpu.SMEM)


def params(cid):
    return pltpu.CompilerParams(
        collective_id=cid, has_side_effects=True, vmem_limit_bytes=VMEM_LIMIT
    )


def remote(src, dst, send, recv, target):
    return pltpu.make_async_remote_copy(
        src_ref=src,
        dst_ref=dst,
        send_sem=send,
        recv_sem=recv,
        device_id=target,
        device_id_type=MESH,
    )


def loop(count, fn):
    lax.fori_loop(0, count, lambda i, c: (fn(i), c)[1], 0)


def dot_nt(a, b, precision=None):
    return lax.dot_general(a, b, NT, precision=precision, preferred_element_type=f32)


def dot_tn(a, b, precision=None):
    return lax.dot_general(a, b, TN, precision=precision, preferred_element_type=f32)


def chain_kernel(
    reverse, group, decay_ref, local_ref, out_ref, held, outgoing, send_sem, recv_sem
):
    n = lax.axis_size("seq")
    place = lax.axis_index("seq")
    head = lax.axis_index("head")
    ahead = n - 1 - place if reverse else place
    by = -1 if reverse else 1
    chunks, rows = held.shape[0], held.shape[1]
    barrier = pltpu.get_barrier_semaphore()

    @pl.when(ahead > 0)
    def _():
        pl.semaphore_signal(barrier, inc=1, device_id=(place - by, head), device_id_type=MESH)

    @pl.when(ahead < n - 1)
    def _():
        pl.semaphore_wait(barrier, 1)

    def copy(c):
        return remote(
            outgoing.at[c], held.at[c], send_sem.at[c], recv_sem.at[c], (place + by, head)
        )

    def step(c):
        @pl.when(ahead > 0)
        def _():
            copy(c).wait_recv()

        @pl.when(ahead == 0)
        def _():
            held[c] = jnp.zeros(held.shape[1:], bf16)

        for g in range(group):
            part = pl.ds(g * HEADDIM, HEADDIM)
            inner = pl.ds(pl.multiple_of(c * rows + g * HEADDIM, HEADDIM), HEADDIM)
            state = held[c, part].astype(f32)
            outgoing[c, part] = (decay_ref[c * group + g] * state + local_ref[inner]).astype(bf16)

        @pl.when(ahead < n - 1)
        def _():
            copy(c).start()

        out_ref[pl.ds(pl.multiple_of(c * rows, rows), rows)] = held[c]

    loop(chunks, step)

    @pl.when(ahead < n - 1)
    def _():
        loop(chunks, lambda c: copy(c).wait_send())


def chain(decay, local, reverse, cid):
    total = local.shape[0] * local.shape[1]
    group = next(g for g in (3, 2, 1) if decay.shape[1] % g == 0)
    rows = group * HEADDIM
    chunks = total // rows
    out = pl.pallas_call(
        functools.partial(chain_kernel, reverse, group),
        out_shape=jax.ShapeDtypeStruct((total, STATE), bf16),
        in_specs=[in_smem, in_vmem],
        out_specs=in_vmem,
        scratch_shapes=[
            pltpu.VMEM((chunks, rows, STATE), bf16),
            pltpu.VMEM((chunks, rows, STATE), bf16),
            pltpu.SemaphoreType.DMA((chunks,)),
            pltpu.SemaphoreType.DMA((chunks,)),
        ],
        compiler_params=params(cid),
        name="chain_back" if reverse else "chain_forward",
    )(decay.reshape(-1), local.reshape(total, STATE))
    return out.reshape(local.shape)


def ring_place(n, index):
    odd, half = lax.rem(index, 2), lax.div(index, 2)
    return half * (1 - odd) + (n - 1 - half) * odd


def ring_index(n, spot):
    late = lax.div(2 * spot, n)
    return 2 * spot * (1 - late) + (2 * (n - 1 - spot) + 1) * late


def ring_kernel(n, count, cuts, *refs):
    parts, outs = refs[:count], refs[count : 2 * count]
    held, sems = refs[2 * count : 4 * count], refs[4 * count :]
    place = lax.axis_index("seq")
    head = lax.axis_index("head")
    spot = ring_place(n, place)
    after = (ring_index(n, lax.rem(spot + 1, n)), head)
    before = (ring_index(n, lax.rem(spot + n - 1, n)), head)
    barrier = pltpu.get_barrier_semaphore()
    for target in (after, before):
        pl.semaphore_signal(barrier, inc=1, device_id=target, device_id_type=MESH)
    pl.semaphore_wait(barrier, 2)

    streams = []
    for i in range(count):
        width = parts[i].shape[1]
        for way in range(2):
            columns = pl.ds(0, cuts[i]) if way == 0 else pl.ds(cuts[i], width - cuts[i])
            streams.append((parts[i], outs[i], held[2 * i + way], columns, way))
    send_sem, recv_sem = sems

    def piece(i, step):
        part, _, _, columns, way = streams[i]
        shift = -1 - step if way == 0 else 1 + step
        rows = part.shape[0] // n
        index = ring_index(n, lax.rem(spot + shift + 2 * n, n))
        return part.at[pl.ds(pl.multiple_of(index * rows, rows), rows), columns]

    def copy(i, step, src):
        slots, way = streams[i][2], streams[i][4]
        return remote(
            src,
            slots.at[step],
            send_sem.at[i, step],
            recv_sem.at[i, step],
            after if way == 0 else before,
        )

    for i in range(len(streams)):
        copy(i, 0, piece(i, 0)).start()

    def one(step):
        for i in range(len(streams)):
            slots = streams[i][2]
            copy(i, step, slots.at[step]).wait_recv()
            slots[step] = (slots[step].astype(f32) + piece(i, step + 1)[...].astype(f32)).astype(
                slots.dtype
            )
            copy(i, step + 1, slots.at[step]).start()

    loop(n - 2, one)
    for i in range(len(streams)):
        _, out, slots, columns, _ = streams[i]
        copy(i, n - 2, slots.at[n - 2]).wait_recv()
        out[:, columns] = slots[n - 2].astype(f32) + piece(i, n - 1)[...].astype(f32)
    for i in range(len(streams)):
        copy(i, 0, piece(i, 0)).wait_send()
        loop(n - 2, lambda step, i=i: copy(i, step + 1, streams[i][2].at[step]).wait_send())


def ring_sums(parts, cid):
    n = lax.axis_size("seq")
    cuts = [p.shape[1] // LANES // 2 * LANES for p in parts]
    rows = [p.shape[0] // n for p in parts]
    held = []
    for p, cut, r in zip(parts, cuts, rows):
        held += [
            pltpu.VMEM((n - 1, r, cut), p.dtype),
            pltpu.VMEM((n - 1, r, p.shape[1] - cut), p.dtype),
        ]
    count = len(parts)
    return pl.pallas_call(
        functools.partial(ring_kernel, n, count, cuts),
        out_shape=[jax.ShapeDtypeStruct((r, p.shape[1]), f32) for p, r in zip(parts, rows)],
        in_specs=[in_vmem] * count,
        out_specs=[in_vmem] * count,
        scratch_shapes=held
        + [
            pltpu.SemaphoreType.DMA((2 * count, n - 1)),
            pltpu.SemaphoreType.DMA((2 * count, n - 1)),
        ],
        compiler_params=params(cid),
        name="ring_sums",
    )(*parts)


class Group:
    def __init__(self, n):
        self.n = n
        self.chips = n // 2
        self.seq = lax.axis_index("seq")
        self.me = lax.axis_index("head")
        self.chip = lax.div(self.me, 2)
        self.core = lax.rem(self.me, 2)
        self.mate = self.me + 1 - 2 * self.core

    def at(self, head):
        return (self.seq, head)

    def chip_after(self, k):
        return lax.rem(self.chip + k, self.chips)

    def chip_before(self, k):
        return lax.rem(self.chip + self.chips - k, self.chips)

    def peer(self, k):
        return 2 * self.chip_after(k) + self.core

    def other(self, k):
        return lax.rem(self.me + k, self.n)

    def greet(self):
        barrier = pltpu.get_barrier_semaphore()
        for k in range(1, self.n):
            pl.semaphore_signal(
                barrier, inc=1, device_id=self.at(self.other(k)), device_id_type=MESH
            )
        pl.semaphore_wait(barrier, self.n - 1)


def share(group, source, table, send_sem, recv_sem):
    for k in range(1, group.n):
        remote(
            source,
            table.at[group.me],
            send_sem.at[k - 1],
            recv_sem.at[group.me],
            group.at(group.other(k)),
        ).start()


def shared(group, source, table, send_sem, recv_sem):
    for k in range(1, group.n):
        sender = group.other(k)
        copy = remote(
            source, table.at[sender], send_sem.at[k - 1], recv_sem.at[sender], group.at(sender)
        )
        copy.wait_send()
        copy.wait_recv()


def row_tile(chunk):
    return pl.ds(pl.multiple_of(chunk * LANES, LANES), LANES)


def as_column(row, width):
    tile = jnp.broadcast_to(row, (LANES, LANES)).T
    return jnp.concatenate([tile] * (-(-width // LANES)), axis=1)[:, :width]


def as_row(values):
    ones = jnp.ones((8, values.shape[1]), f32)
    return dot_nt(ones, values, highest)[:1]


def scatter_phases(group, chunks, part, mate_in, chip_out, chip_in, sems):
    mate_send, mate_recv, chip_send, chip_recv = sems

    def mate_copy(c, x):
        return remote(
            part.at[2 * x + 1 - group.core, row_tile(c)],
            mate_in.at[x, row_tile(c)],
            mate_send.at[x, c],
            mate_recv.at[x, c],
            group.at(group.mate),
        )

    def chip_copy(c, k):
        return remote(
            chip_out.at[k - 1, row_tile(c)],
            chip_in.at[k - 1, row_tile(c)],
            chip_send.at[k - 1, c],
            chip_recv.at[k - 1, c],
            group.at(group.peer(k)),
        )

    def start_mate(c):
        for x in range(group.chips):
            mate_copy(c, x).start()

    def start_chip(c):
        for x in range(group.chips):
            mate_copy(c, x).wait_recv()
        for k in range(1, group.chips):
            x = group.chip_after(k)
            both = part[2 * x + group.core, row_tile(c)].astype(f32) + mate_in[
                x, row_tile(c)
            ].astype(f32)
            chip_out[k - 1, row_tile(c)] = both.astype(bf16)
            chip_copy(c, k).start()

    def total(c):
        value = part[group.me, row_tile(c)].astype(f32) + mate_in[
            group.chip, row_tile(c)
        ].astype(f32)
        for k in range(1, group.chips):
            chip_copy(c, k).wait_recv()
            value = value + chip_in[k - 1, row_tile(c)].astype(f32)
        return value

    def finish(c):
        for x in range(group.chips):
            mate_copy(c, x).wait_send()
        for k in range(1, group.chips):
            chip_copy(c, k).wait_send()

    return start_mate, start_chip, total, finish


def out_kernel(
    n,
    gated_ref,
    weight_ref,
    square_ref,
    tokens_ref,
    teacher_ref,
    mask_ref,
    output_ref,
    grad_ref,
    rowdot_ref,
    squared_ref,
    loss_ref,
    part,
    mate_in,
    chip_out,
    chip_in,
    gathered,
    squares,
    dots,
    dot_out,
    mate_send,
    mate_recv,
    chip_send,
    chip_recv,
    gm_send,
    gm_recv,
    gc_send,
    gc_recv,
    gf_send,
    gf_recv,
    sq_send,
    sq_recv,
    rd_send,
    rd_recv,
):
    group = Group(n)
    group.greet()
    chunks = gated_ref.shape[0] // LANES
    width = tokens_ref.shape[1]
    share(group, square_ref, squares, sq_send, sq_recv)
    start_mate, start_chip, total, finish = scatter_phases(
        group, chunks, part, mate_in, chip_out, chip_in, (mate_send, mate_recv, chip_send, chip_recv)
    )

    def product(c):
        rows = gated_ref[row_tile(c)]
        for j in range(n):
            block = (
                weight_ref[:, j * width : (j + 1) * width] if len(weight_ref.shape) == 2 else weight_ref[j]
            )
            part[j, row_tile(c)] = jnp.dot(rows, block, preferred_element_type=f32).astype(bf16)
        start_mate(c)

    loop(chunks, product)
    loop(chunks, start_chip)
    shared(group, square_ref, squares, sq_send, sq_recv)
    squares[group.me] = square_ref[...]
    loss_ref[...] = jnp.zeros_like(loss_ref)

    def to_mate(c):
        block = gathered.at[group.me, row_tile(c)]
        return remote(block, block, gm_send.at[c], gm_recv.at[c], group.at(group.mate))

    def to_chip(c, k):
        block = gathered.at[group.me, row_tile(c)]
        return remote(
            block, block, gc_send.at[k - 1, c], gc_recv.at[k - 1, c], group.at(group.peer(k))
        )

    def forward(c, k):
        block = gathered.at[2 * group.chip_before(k) + group.core, row_tile(c)]
        return remote(
            block, block, gf_send.at[k - 1, c], gf_recv.at[k - 1, c], group.at(group.mate)
        )

    def rest(c):
        squared = squares[0, pl.ds(c, 1)]
        for j in range(1, n):
            squared = squared + squares[j, pl.ds(c, 1)]
        squared_ref[pl.ds(c, 1)] = squared
        scale = lax.rsqrt(squared * (1.0 / (NHEADS * HEADDIM)) + norm_eps)
        branch = total(c) * as_column(scale, width)
        output = tokens_ref[row_tile(c)] + branch
        output_ref[row_tile(c)] = output
        difference = output - teacher_ref[row_tile(c)]
        weighted = difference * as_column(mask_ref[pl.ds(c, 1)], width)
        low = weighted.astype(bf16)
        gathered[group.me, row_tile(c)] = low
        to_mate(c).start()
        for k in range(1, group.chips):
            to_chip(c, k).start()
        loss_ref[...] += jnp.sum(weighted * difference, axis=0, keepdims=True)
        dot_out[pl.ds(c, 1)] = as_row(low.astype(f32) * branch)

    loop(chunks, rest)
    share(group, dot_out, dots, rd_send, rd_recv)

    def pass_on(c):
        for k in range(1, group.chips):
            to_chip(c, k).wait_recv()
            forward(c, k).start()

    loop(chunks, pass_on)

    def end(c):
        to_mate(c).wait()
        for k in range(1, group.chips):
            to_chip(c, k).wait_send()
            forward(c, k).wait()
        finish(c)
        for j in range(n):
            grad_ref[j, row_tile(c)] = gathered[j, row_tile(c)]

    loop(chunks, end)
    shared(group, dot_out, dots, rd_send, rd_recv)
    row_sum = dot_out[...]
    for k in range(1, n):
        row_sum = row_sum + dots[group.other(k)]
    rowdot_ref[...] = row_sum


def scatter_scratch(n, rows, width):
    chips, chunks = n // 2, rows // LANES
    dma = pltpu.SemaphoreType.DMA
    return [
        pltpu.VMEM((n, rows, width), bf16),
        pltpu.VMEM((chips, rows, width), bf16),
        pltpu.VMEM((chips - 1, rows, width), bf16),
        pltpu.VMEM((chips - 1, rows, width), bf16),
    ], [dma((chips, chunks)), dma((chips, chunks)), dma((chips - 1, chunks)), dma((chips - 1, chunks))]


def blocked(weight, n):
    width = weight.shape[1] // n
    if width % LANES == 0:
        return weight
    return jnp.moveaxis(weight.reshape(weight.shape[0], n, width), 1, 0)


def out_phase(gated, weight, square_rows, tokens, teacher, mask_rows, cid):
    n = lax.axis_size("head")
    rows, width = tokens.shape
    chips, chunks = n // 2, rows // LANES
    buffers, sems = scatter_scratch(n, rows, width)
    dma = pltpu.SemaphoreType.DMA
    return pl.pallas_call(
        functools.partial(out_kernel, n),
        out_shape=[
            jax.ShapeDtypeStruct((rows, width), f32),
            jax.ShapeDtypeStruct((n, rows, width), bf16),
            jax.ShapeDtypeStruct((chunks, LANES), f32),
            jax.ShapeDtypeStruct((chunks, LANES), f32),
            jax.ShapeDtypeStruct((1, width), f32),
        ],
        in_specs=[in_vmem] * 6,
        out_specs=[in_vmem] * 5,
        scratch_shapes=buffers
        + [
            pltpu.VMEM((n, rows, width), bf16),
            pltpu.VMEM((n, chunks, LANES), f32),
            pltpu.VMEM((n, chunks, LANES), f32),
            pltpu.VMEM((chunks, LANES), f32),
        ]
        + sems
        + [
            dma((chunks,)),
            dma((chunks,)),
            dma((chips - 1, chunks)),
            dma((chips - 1, chunks)),
            dma((chips - 1, chunks)),
            dma((chips - 1, chunks)),
            dma((n - 1,)),
            dma((n,)),
            dma((n - 1,)),
            dma((n,)),
        ],
        compiler_params=params(cid),
        name="out_phase",
    )(gated, blocked(weight, n), square_rows, tokens, teacher, mask_rows)


def in_kernel(
    n,
    count,
    *refs,
):
    grads, weights = refs[:count], refs[count : 2 * count]
    (
        normed_ref,
        tokens_ref,
        output_ref,
        teacher_ref,
        gain_ref,
        mask_ref,
        inverse_ref,
        out_ref,
        columns_ref,
        part,
        mate_in,
        chip_out,
        chip_in,
        dots,
        dot_out,
        mate_send,
        mate_recv,
        chip_send,
        chip_recv,
        rd_send,
        rd_recv,
    ) = refs[2 * count :]
    group = Group(n)
    group.greet()
    chunks = tokens_ref.shape[0] // LANES
    width = tokens_ref.shape[1]
    start_mate, start_chip, total, finish = scatter_phases(
        group, chunks, part, mate_in, chip_out, chip_in, (mate_send, mate_recv, chip_send, chip_recv)
    )
    columns_ref[...] = jnp.zeros_like(columns_ref)

    def product(c):
        row_sum = jnp.zeros((1, LANES), f32)
        for j in range(n):
            place = slice(j * width, (j + 1) * width)
            value = jnp.zeros((LANES, width), f32)
            for g, w in zip(grads, weights):
                value = value + dot_nt(g[row_tile(c)], w[place])
            part[j, row_tile(c)] = value.astype(bf16)
            product_n = value * normed_ref[row_tile(c), place].astype(f32)
            columns_ref[:, place] += jnp.sum(product_n, axis=0, keepdims=True)
            row_sum = row_sum + as_row(product_n)
        dot_out[pl.ds(c, 1)] = row_sum
        start_mate(c)

    loop(chunks, product)
    share(group, dot_out, dots, rd_send, rd_recv)
    loop(chunks, start_chip)
    shared(group, dot_out, dots, rd_send, rd_recv)
    dots[group.me] = dot_out[...]

    def rest(c):
        row_sum = dots[0, pl.ds(c, 1)]
        for j in range(1, n):
            row_sum = row_sum + dots[j, pl.ds(c, 1)]
        inverse = inverse_ref[pl.ds(c, 1)]
        tokens = tokens_ref[row_tile(c)]
        out_grad = (output_ref[row_tile(c)] - teacher_ref[row_tile(c)]) * as_column(
            mask_ref[pl.ds(c, 1)], width
        )
        out_ref[row_tile(c)] = (
            out_grad
            + as_column(inverse, width) * gain_ref[...] * total(c)
            - tokens * as_column(inverse * inverse * row_sum * (1.0 / D), width)
        )

    loop(chunks, rest)
    loop(chunks, finish)


def in_phase(grads, weights, normed, tokens, output, teacher, gain, mask_rows, inverse_rows, cid):
    n = lax.axis_size("head")
    rows, width = tokens.shape
    chunks = rows // LANES
    buffers, sems = scatter_scratch(n, rows, width)
    dma = pltpu.SemaphoreType.DMA
    return pl.pallas_call(
        functools.partial(in_kernel, n, len(grads)),
        out_shape=[
            jax.ShapeDtypeStruct((rows, width), f32),
            jax.ShapeDtypeStruct((1, D), f32),
        ],
        in_specs=[in_vmem] * (2 * len(grads) + 7),
        out_specs=[in_vmem] * 2,
        scratch_shapes=buffers
        + [pltpu.VMEM((n, chunks, LANES), f32), pltpu.VMEM((chunks, LANES), f32)]
        + sems
        + [dma((n - 1,)), dma((n,))],
        compiler_params=params(cid),
        name="in_phase",
    )(*grads, *weights, normed, tokens, output, teacher, gain, mask_rows, inverse_rows)


def small_kernel(axis, n, source_ref, out_ref, table, send_sem, recv_sem):
    place = lax.axis_index(axis)
    fixed = lax.axis_index("seq" if axis == "head" else "head")

    def at(index):
        return (fixed, index) if axis == "head" else (index, fixed)

    barrier = pltpu.get_barrier_semaphore()
    for k in range(1, n):
        pl.semaphore_signal(
            barrier, inc=1, device_id=at(lax.rem(place + k, n)), device_id_type=MESH
        )
    pl.semaphore_wait(barrier, n - 1)

    def copy(k, sender, target):
        return remote(
            source_ref, table.at[sender], send_sem.at[k], recv_sem.at[sender], at(target)
        )

    for k in range(1, n):
        copy(k - 1, place, lax.rem(place + k, n)).start()
    for k in range(1, n):
        sender = lax.rem(place + k, n)
        copy(k - 1, sender, sender).wait()
    table[place] = source_ref[...]
    value = table[0]
    for k in range(1, n):
        value = value + table[k]
    out_ref[...] = value


def small_sum(source, axis, cid):
    n = lax.axis_size(axis)
    return pl.pallas_call(
        functools.partial(small_kernel, axis, n),
        out_shape=jax.ShapeDtypeStruct(source.shape, f32),
        in_specs=[in_vmem],
        out_specs=in_vmem,
        scratch_shapes=[
            pltpu.VMEM((n,) + source.shape, f32),
            pltpu.SemaphoreType.DMA((n - 1,)),
            pltpu.SemaphoreType.DMA((n,)),
        ],
        compiler_params=params(cid),
        name="small_sum_" + axis,
    )(source)


def packed(arrays):
    flat = jnp.concatenate([a.reshape(-1) for a in arrays])
    size = -(-flat.shape[0] // 1024) * 1024
    return jnp.pad(flat, (0, size - flat.shape[0])).reshape(-1, LANES)


def unpacked(value, arrays):
    flat, at, found = value.reshape(-1), 0, []
    for a in arrays:
        found.append(flat[at : at + a.size].reshape(a.shape))
        at += a.size
    return found


def passed_along(x, axis, by):
    count = lax.axis_size(axis)
    pairs = [(i, i + by) for i in range(count) if 0 <= i + by < count]
    return lax.ppermute(x, axis, pairs)


def silu_slope(linear):
    sigmoid_value = jax.nn.sigmoid(linear)
    return sigmoid_value * (1.0 + linear * (1.0 - sigmoid_value))


def body(
    tokens,
    teacher,
    document_start,
    valid_mask,
    input_gain,
    gate_weight,
    value_weight,
    keyquery_weight,
    step_weight,
    value_conv_weight,
    value_conv_bias,
    keyquery_conv_weight,
    keyquery_conv_bias,
    step_bias,
    rate_log,
    skip_gain,
    norm_gain,
    out_weight,
):
    head_index = lax.axis_index("head")
    sequence_index = lax.axis_index("seq")
    sequence_count = tokens.shape[0]
    shard_length = tokens.shape[1]
    rows = sequence_count * shard_length
    local_heads = skip_gain.shape[0]
    local_inner = local_heads * HEADDIM
    inner_total = NHEADS * HEADDIM
    column_count = D // lax.axis_size("head")
    column_start = head_index * column_count
    shard_begin = sequence_index * shard_length
    positions = shard_begin + jnp.arange(shard_length, dtype=jnp.int32)
    valid_count = jnp.sum(valid_mask.astype(f32))
    local_mask = lax.dynamic_slice_in_dim(valid_mask, shard_begin, shard_length, 1).astype(f32)
    mask_rows = (local_mask * (2.0 / (D * valid_count))).reshape(-1, LANES)
    inverse_root = lax.rsqrt(jnp.mean(tokens * tokens, axis=-1, keepdims=True) + norm_eps)
    normed = (tokens * inverse_root * input_gain).astype(bf16)
    values_linear = jnp.dot(normed, value_weight, preferred_element_type=f32).astype(bf16)
    keyquery_linear = jnp.dot(normed, keyquery_weight, preferred_element_type=f32).astype(bf16)
    conv_input = jnp.concatenate([values_linear, keyquery_linear], axis=-1)
    conv_lags = value_conv_weight.shape[0]
    previous = passed_along(conv_input[:, shard_length - (conv_lags - 1) :], "seq", 1)
    gate_linear = jnp.dot(normed, gate_weight, preferred_element_type=f32)
    steps_linear = jnp.dot(normed, step_weight, preferred_element_type=f32)
    extended = jnp.concatenate([previous, conv_input], axis=1).astype(f32)
    conv_weight = jnp.concatenate([value_conv_weight, keyquery_conv_weight], axis=1)
    conv_offset = jnp.concatenate([value_conv_bias, keyquery_conv_bias], axis=0)
    usable = []
    windows = []
    conv_linear = conv_offset + jnp.zeros_like(extended[:, :shard_length])
    for lag_index in range(conv_lags):
        usable.append((positions[None, :] - lag_index >= document_start).astype(f32)[:, :, None])
        windows.append(
            extended[:, conv_lags - 1 - lag_index : conv_lags - 1 - lag_index + shard_length]
        )
        conv_linear = conv_linear + conv_weight[lag_index] * windows[lag_index] * usable[lag_index]
    conv_out = jax.nn.silu(conv_linear)
    keys_input = conv_out[..., local_inner : local_inner + STATE]
    queries = conv_out[..., local_inner + STATE :]
    heads_input = conv_out[..., :local_inner].reshape(
        sequence_count, shard_length, local_heads, HEADDIM
    )
    steps = jax.nn.softplus(steps_linear + step_bias)
    decay_rate = -jnp.exp(rate_log)
    rates = steps * decay_rate
    cumulative = jnp.transpose(jnp.cumsum(rates, axis=1), (0, 2, 1))
    steps_heads = jnp.transpose(steps, (0, 2, 1))
    linked = (positions[None, None, :] >= document_start[:, :, None]) & (
        positions[None, None, :] <= positions[None, :, None]
    )
    linked_heads = linked[:, None]
    decay_mat = jnp.where(
        linked_heads,
        jnp.exp(
            jnp.where(linked_heads, cumulative[:, :, :, None] - cumulative[:, :, None, :], 0.0)
        ),
        0.0,
    )
    scores = jnp.einsum("btn,bun->btu", queries, keys_input, precision=highest)
    mixing = decay_mat * scores[:, None] * steps_heads[:, :, None, :]
    local_out = jnp.einsum("bhtu,buhp->bthp", mixing, heads_input, precision=highest)
    kept_mask = (document_start < shard_begin).astype(f32)
    entering = jnp.exp(cumulative) * kept_mask[:, None, :]
    trailing = (positions[None, :] >= document_start[:, -1:]).astype(f32)
    end_decay = jnp.exp(cumulative[:, :, -1:] - cumulative) * trailing[:, None, :]
    weights_end = end_decay * steps_heads
    state_local = jnp.einsum(
        "bhu,buhp,bun->bhpn", weights_end, heads_input, keys_input, precision=highest
    )
    passed = jnp.exp(cumulative[:, :, -1]) * kept_mask[:, -1:]
    folded = (sequence_count, local_inner, STATE)
    unfolded = (sequence_count, local_heads, HEADDIM, STATE)
    state_in = chain(passed, state_local.reshape(folded), False, 1).reshape(unfolded).astype(f32)
    projected = jnp.einsum("btn,bhpn->bthp", queries, state_in, precision=highest)
    entering_rows = jnp.transpose(entering, (0, 2, 1))
    mixed_heads = (
        local_out + entering_rows[..., None] * projected + skip_gain[:, None] * heads_input
    )
    mixed_flat = mixed_heads.reshape(rows, local_inner)
    gate_flat = gate_linear.reshape(rows, local_inner)
    gate_act = jax.nn.silu(gate_flat)
    gated_out = mixed_flat * gate_act
    square_rows = jnp.sum(gated_out * gated_out, axis=-1).reshape(-1, LANES)
    gained = (gated_out * norm_gain).astype(bf16)
    token_cols = lax.dynamic_slice_in_dim(tokens, column_start, column_count, 2).reshape(rows, -1)
    teacher_rows = teacher.reshape(rows, column_count)
    output, piece_blocks, rowdot, square_total, loss_cols = out_phase(
        gained, out_weight, square_rows, token_cols, teacher_rows, mask_rows, 2
    )
    piece_cols = jnp.moveaxis(piece_blocks, 0, 1).reshape(rows, D)
    row_scale = lax.rsqrt(square_total / inner_total + norm_eps).reshape(rows, 1)
    row_dot = rowdot.reshape(rows, 1)
    normed_out = (gated_out * row_scale * norm_gain).astype(bf16)
    column_grad = dot_tn(piece_cols, normed_out).astype(bf16)
    grad_rows = dot_nt(piece_cols, out_weight)
    gain_out_grad = jnp.sum(grad_rows * gated_out * row_scale, axis=0)
    gated_grad = row_scale * norm_gain * grad_rows - gated_out * (
        row_scale**2 * row_dot / inner_total
    )
    mixed_grad = gated_grad * gate_act
    gate_grad = (gated_grad * mixed_flat * silu_slope(gate_flat)).astype(bf16)
    heads_grad = mixed_grad.reshape(sequence_count, shard_length, local_heads, HEADDIM)
    skip_gain_grad = jnp.einsum("bthp,bthp->h", heads_grad, heads_input, precision=highest)
    state_local_grad = jnp.einsum(
        "bht,bthp,btn->bhpn", entering, heads_grad, queries, precision=highest
    )
    end_grad = (
        chain(passed, state_local_grad.reshape(folded), True, 3).reshape(unfolded).astype(f32)
    )
    pairwise = jnp.einsum("bthp,buhp->bhtu", heads_grad, heads_input, precision=highest)
    heads_input_grad = skip_gain[:, None] * heads_grad
    heads_input_grad = heads_input_grad + jnp.einsum(
        "bhtu,bthp->buhp", mixing, heads_grad, precision=highest
    )
    heads_input_grad = heads_input_grad + jnp.einsum(
        "bhu,bhpn,bun->buhp", weights_end, end_grad, keys_input, precision=highest
    )
    weighted = pairwise * decay_mat
    scores_grad = jnp.einsum("bhtu,bhu->btu", weighted, steps_heads, precision=highest)
    steps_grad = jnp.einsum("bhtu,btu->bhu", weighted, scores, precision=highest)
    cum_terms = weighted * scores[:, None] * steps_heads[:, :, None, :]
    cum_grad = jnp.sum(cum_terms, axis=-1) - jnp.sum(cum_terms, axis=-2)
    queries_grad = jnp.einsum("btu,bun->btn", scores_grad, keys_input, precision=highest)
    queries_grad = queries_grad + jnp.einsum(
        "bht,bthp,bhpn->btn", entering, heads_grad, state_in, precision=highest
    )
    keys_grad = jnp.einsum("btu,btn->bun", scores_grad, queries, precision=highest)
    keys_grad = keys_grad + jnp.einsum(
        "bhu,bhpn,buhp->bun", weights_end, end_grad, heads_input, precision=highest
    )
    entering_grad = jnp.einsum("bthp,bthp->bht", heads_grad, projected, precision=highest)
    cum_grad = cum_grad + entering_grad * entering
    passed_grad = jnp.einsum("bhpn,bhpn->bh", end_grad, state_in, precision=highest)
    end_term = jnp.einsum(
        "bhpn,buhp,bun->bhu", end_grad, heads_input, keys_input, precision=highest
    )
    steps_grad = steps_grad + end_term * end_decay
    end_mix = end_term * weights_end
    cum_grad = cum_grad - end_mix
    last_term = passed_grad * passed + jnp.sum(end_mix, axis=-1)
    last_slot = (jnp.arange(shard_length, dtype=jnp.int32) == shard_length - 1).astype(f32)
    cum_grad = cum_grad + last_term[:, :, None] * last_slot
    rates_grad = jnp.flip(jnp.cumsum(jnp.flip(cum_grad, axis=-1), axis=-1), axis=-1)
    steps_grad = steps_grad + rates_grad * decay_rate[None, :, None]
    rate_log_grad = jnp.sum(rates_grad * steps_heads, axis=(0, 2)) * decay_rate
    steps_linear_grad = jnp.transpose(steps_grad, (0, 2, 1)) * jax.nn.sigmoid(
        steps_linear + step_bias
    )
    step_bias_grad = jnp.sum(steps_linear_grad, axis=(0, 1))
    conv_out_grad = jnp.concatenate(
        [
            heads_input_grad.reshape(sequence_count, shard_length, local_inner),
            keys_grad,
            queries_grad,
        ],
        axis=-1,
    )
    conv_linear_grad = conv_out_grad * silu_slope(conv_linear)
    conv_offset_grad = jnp.sum(conv_linear_grad, axis=(0, 1))
    conv_channels = conv_linear_grad.shape[2]
    weight_rows = []
    conv_input_grad = conv_weight[0] * conv_linear_grad * usable[0]
    edge_grad = jnp.zeros((sequence_count, conv_lags - 1, conv_channels), f32)
    for lag_index in range(conv_lags):
        masked = conv_linear_grad * usable[lag_index]
        weight_rows.append(jnp.sum(masked * windows[lag_index], axis=(0, 1)))
        if lag_index > 0:
            tail_zeros = jnp.zeros((sequence_count, lag_index, conv_channels), f32)
            conv_input_grad = conv_input_grad + conv_weight[lag_index] * jnp.concatenate(
                [masked[:, lag_index:], tail_zeros], axis=1
            )
            head_zeros = jnp.zeros((sequence_count, conv_lags - 1 - lag_index, conv_channels), f32)
            edge_grad = edge_grad + jnp.concatenate(
                [head_zeros, conv_weight[lag_index] * masked[:, :lag_index]], axis=1
            )
    conv_weight_grad = jnp.stack(weight_rows, axis=0)
    incoming = passed_along(edge_grad, "seq", -1)
    lead_zeros = jnp.zeros((sequence_count, shard_length - (conv_lags - 1), conv_channels), f32)
    conv_input_grad = conv_input_grad + jnp.concatenate([lead_zeros, incoming], axis=1)
    step_pad = ((0, 0), (0, LANES - local_heads))
    values_grad = conv_input_grad[..., :local_inner].astype(bf16).reshape(rows, local_inner)
    narrow_grad = jnp.concatenate(
        [
            conv_input_grad[..., local_inner:].reshape(rows, 2 * STATE),
            jnp.pad(steps_linear_grad.reshape(rows, local_heads), step_pad),
        ],
        axis=-1,
    ).astype(bf16)
    narrow_weight = jnp.concatenate([keyquery_weight, jnp.pad(step_weight, step_pad)], axis=-1)
    normed = normed.reshape(rows, D)
    gain_cols = lax.dynamic_slice_in_dim(input_gain, column_start, column_count, 0)
    tokens_grad, gain_columns = in_phase(
        (gate_grad, values_grad, narrow_grad),
        (gate_weight, value_weight, narrow_weight),
        normed,
        token_cols,
        output,
        teacher_rows,
        gain_cols[None],
        mask_rows,
        inverse_root.reshape(-1, LANES),
        4,
    )
    gate_part = dot_tn(normed, gate_grad).astype(bf16)
    value_part = dot_tn(normed, values_grad).astype(bf16)
    narrow_part = dot_tn(normed, narrow_grad)
    out_total, gate_total, value_total, narrow_total = ring_sums(
        (column_grad, gate_part, value_part, narrow_part), 5
    )
    group_parts = [
        narrow_total[:, : 2 * STATE],
        conv_weight_grad[:, local_inner:],
        conv_offset_grad[local_inner:],
        gain_columns,
        jnp.sum(loss_cols)[None],
    ]
    (
        keyquery_total,
        keyquery_conv_part,
        keyquery_offset_part,
        gain_columns,
        loss_part,
    ) = unpacked(small_sum(packed(group_parts), "head", 6), group_parts)
    line_parts = [
        conv_weight_grad[:, :local_inner],
        conv_offset_grad[:local_inner],
        keyquery_conv_part,
        keyquery_offset_part,
        step_bias_grad,
        rate_log_grad,
        skip_gain_grad,
        gain_out_grad,
        lax.dynamic_slice_in_dim(gain_columns.reshape(-1), column_start, column_count, 0),
        loss_part,
    ]
    (
        value_conv_total,
        value_offset_total,
        keyquery_conv_total,
        keyquery_offset_total,
        step_bias_total,
        rate_log_total,
        skip_gain_total,
        norm_gain_total,
        input_gain_total,
        loss_total,
    ) = unpacked(small_sum(packed(line_parts), "seq", 7), line_parts)
    return (
        output.reshape(sequence_count, shard_length, column_count),
        loss_total[0] * 0.5,
        tokens_grad.reshape(sequence_count, shard_length, column_count),
        input_gain_total / gain_cols,
        gate_total,
        value_total,
        keyquery_total,
        narrow_total[:, 2 * STATE : 2 * STATE + local_heads],
        value_conv_total,
        value_offset_total,
        keyquery_conv_total,
        keyquery_offset_total,
        step_bias_total,
        rate_log_total,
        skip_gain_total,
        norm_gain_total,
        out_total.T,
    )


def solution(mesh):
    placed = (
        P(None, "seq", None),
        P(None, "seq", "head"),
        P(None, "seq"),
        P(),
        P(),
        P(None, "head"),
        P(None, "head"),
        P(),
        P(None, "head"),
        P(None, "head"),
        P("head"),
        P(),
        P(),
        P("head"),
        P("head"),
        P("head"),
        P("head"),
        P("head", None),
    )
    return jax.shard_map(
        body,
        mesh=mesh,
        in_specs=placed,
        out_specs=(
            P(None, "seq", "head"),
            P(),
            P(None, "seq", "head"),
            P("head"),
            P("seq", "head"),
            P("seq", "head"),
            P("seq", None),
            P("seq", "head"),
            P(None, "head"),
            P("head"),
            P(),
            P(),
            P("head"),
            P("head"),
            P("head"),
            P("head"),
            P("head", "seq"),
        ),
        check_vma=False,
    )
```

time: 1240 us -> 600 us (0.48)
  waiting for transfers between devices: 795 us -> 0.01 us
  Pallas kernels: 0 us -> 309 us
  blocking collectives: 87.4 us -> 0 us
  matrix products: 171 us -> 120 us
  local copies, waits for them, and re-layouts: 42.1 us -> 86.8 us
  other arithmetic: 107 us -> 66.2 us
  between operations: 17.8 us -> 4.48 us
    reduce_scatter x6 -> x0, waiting for transfers between devices: 443 us -> none  [the longest x1 99.3 us: body(): lax.psum_scatter(gate_weight_part, 'seq', scatter_dimension=0, tiled=True)]
    all_gather x3 -> x0, waiting for transfers between devices: 310 us -> none  [the longest x2 281 us: carried_in(): gathered = jax.tree.map(lambda a: lax.all_gather(a, axis), part)]
    pallas_call x0 -> x7, Pallas kernels: none -> 309 us  [the longest x1 101 us: ring_sums(): pl.pallas_call(functools.partial(ring_kernel, n, count, cuts), out_shape=...]
    psum x4 -> x0, blocking collectives: 60.6 us -> none  [the longest x1 40.7 us: body(): lax.psum((conv_weight_grad, conv_offset_grad, step_bias_grad, rate_log_gr...]
    dot_general x15 -> x9, matrix products: 80.1 us -> 36.6 us  [the longest x4 15.2 us: dot_tn(): lax.dot_general(a, b, TN, precision=precision, preferred_element_type=f32)]
    psum x1 -> x0, waiting for transfers between devices: 29.5 us -> none  [body(): lax.psum(jnp.concatenate([keys_grad, queries_grad], axis=-1), 'head')]
    all_gather x1 -> x0, blocking collectives: 26.8 us -> none  [carried_in(): gathered = jax.tree.map(lambda a: lax.all_gather(a, axis), part)]
    add x7 -> x0, other arithmetic: 22.7 us -> none  [combine_states(): later[0][:, :, None, None] * earlier[1] + later[1]]
  transfers between devices with their start and end apart: 13 -> 2, of which waited for: 11 -> 0; matrix products, arithmetic and copies ran while one was open for 10% -> 7% of each run, Pallas kernels for 0% -> 0%
where the time goes in v1:
time: 600 us; the launch traced here: 594 us
  Pallas kernels  309 us (52%)
  matrix products  120 us (20%)
  local copies, waits for them, and re-layouts  86.8 us (14%)
  other arithmetic  66.2 us (11%)
  starting transfers between devices  7.08 us (1%)
    pallas_call x1, Pallas kernels, ring_sums(): pl.pallas_call(functools.partial(ring_kernel, n, count, cuts), out_shape=...  101 us
    pallas_call x2, Pallas kernels, chain(): pl.pallas_call(functools.partial(chain_kernel, reverse, group), out_shape...  83.7 us
    pallas_call x1, Pallas kernels, in_phase(): pl.pallas_call(functools.partial(in_kernel, n, len(grads)), out_shape=[ja...  53.6 us
    pallas_call x1, Pallas kernels, out_phase(): pl.pallas_call(functools.partial(out_kernel, n), out_shape=[jax.ShapeDtyp...  48.7 us
    pallas_call x2, Pallas kernels, small_sum(): pl.pallas_call(functools.partial(small_kernel, axis, n), out_shape=jax.Sh...  22.2 us
    dot_general x1, matrix products, body(): jnp.einsum('bthp,buhp->bhtu', heads_grad, heads_input, precision=highest)  19.2 us
    unnamed x174, local copies, waits for them, and re-layouts  17.3 us
    dot_general x1, matrix products, body(): jnp.einsum('bhtu,buhp->bthp', mixing, heads_input, precision=highest)  16.5 us
  transfers between devices with their start and end apart: 2, of which 0 were waited for; matrix products, arithmetic and copies ran while one was open for 7% of the time, Pallas kernels for 0%

profile of v1, /device:TPU:0, one launch (start us, length us, event | category | flops | bytes accessed | tf_op | source)
XLA Modules:
  0.0 593.7 jit_solution(4397896995311786263)
XLA Ops:
  13.6 5.6 collective-permute-start
  33.6 5.9 %fusion.39 = f32[4,256,768]{2,1,0:T(8,128)} fusion(bf16[4,256,1536]{2,1,0:T(8,128)(2,1)S(1)} %multiply_convert_fusion, bf16[1536,768]{1,0:T(8,128)(2,1)} %refs_3_.1), kind=kOutput, calls=%fused_computation.72 | convolution fusion | flops 2415919104 | bytes 8650752 | tf_op jit(solution)/shard_map/dot_general | solution.py:748
  45.7 3.7 copy.123
  51.5 5.1 fusion.17
  63.3 5.5 fusion.33
  68.8 20.4 %chain_forward.1 = bf16[3072,128]{1,0:T(8,128)(2,1)} custom-call(f32[48]{0:T(128)} %mul.497.decay_ref, f32[3072,128]{1,0:T(8,128)} %bitcast.277), custom_call_target="tpu_custom_call" | custom-call | tf_op jit(solution)/shard_map/chain_forward/pallas_call | solution.py:115
  92.1 16.5 %multiply_reduce_fusion.11 = (f32[4,256]{1,0:T(4,128)S(1)}, f32[4,256,12,64]{1,3,2,0:T(8,128)}, f32[4,256,12,64]{1,3,2,0:T(8,128)}) fusion(f32[4,256,12,64]{1,3,2,0:T(8,128)S(1)} %bitcast.281, f32[4,256,12,64]{1,3,2,0:T(8,128)S(1)} %bitcast.253, f32[12]{0:T(128)S(1)} %copy-done.72, f32[4,256,12,64]{1,3,2,0:T(8,128)S(1)} %fusion.67, ...), kind=kOutput, calls=%fused_computation.56 | convolution fusion | flops 2440297472 | bytes 17190960 | tf_op jit(solution)/shard_map/bhtu,buhp->bthp/dot_general | solution.py:786
  109.1 3.9 copy.121
  115.5 3.7 copy.122
  119.2 4.0 multiply_convert_fusion.2.gated_ref
  123.2 48.7 %out_phase.1 = (f32[1024,384]{1,0:T(8,128)}, bf16[4,1024,384]{2,1,0:T(8,128)(2,1)}, f32[8,128]{1,0:T(8,128)}, f32[8,128]{1,0:T(8,128)}, f32[1,384]{1,0:T(1,128)}) custom-call(bf16[1024,768]{1,0:T(8,128)(2,1)} %multiply_convert_fusion.2.gated_ref, bf16[768,1536]{1,0:T(8,128)(2,1)} %weight_ref.1, f32[8,128]{1,0:T(8,128)} %reshape.340.square_ref, ...), custom_call_target="tpu_custom_call" | custom-call | tf_op jit(solution)/shard_map/out_phase/pallas_call | solution.py:497
  171.9 5.0 copy.124
  179.0 10.9 %fusion.25 = (bf16[1024,768]{1,0:T(8,128)(2,1)}, f32[1024,768]{1,0:T(8,128)}, f32[768]{0:T(1024)}) fusion(f32[4,256,768]{2,1,0:T(8,128)S(1)} %copy-done.11, f32[1024,768]{1,0:T(8,128)} %copy.122, f32[1024]{0:T(1024)S(1)} %fusion.92, f32[1024]{0:T(1024)S(1)} %get-tuple-element.125, f32[768]{0:T(1024)S(1)} %copy-done.60, bf16[1024,1536]{0,1:T(8,128)(2,1)} %bitcast.279, ...), kind=kOutput, calls=%fused_computation.47 | convolution fusion | flops 2431646976 | bytes 16529408 | tf_op jit(solution)/shard_map/dot_general | solution.py:51
  189.9 3.5 copy.125
  196.8 4.6 fusion.59
  201.5 5.5 fusion.29
  207.0 19.2 %fusion.3 = (f32[4,12,256]{2,1,0:T(8,128)}, f32[4,12,256]{2,1,0:T(8,128)}, f32[4,12,256,256]{3,2,1,0:T(8,128)}) fusion(f32[4,12,256]{2,1,0:T(8,128)S(1)} %get-tuple-element.112, f32[4,256,256]{2,1,0:T(8,128)S(1)} %copy-done.20, f32[4,12,256]{2,1,0:T(8,128)S(1)} %get-tuple-element.116, pred[4,256,256]{2,1,0:T(8,128)(4,1)S(1)} %copy-done.34, ...), kind=kOutput, calls=%fused_computation.8 | convolution fusion | flops 2441060352 | bytes 20381696 | tf_op jit(solution)/shard_map/bthp,buhp->bhtu/dot_general | solution.py:835
  230.4 3.9 convolution_convert_fusion.1.refs_0_
  235.3 63.3 %chain_back.1 = bf16[3072,128]{1,0:T(8,128)(2,1)} custom-call(f32[48]{0:T(128)} %mul.497.decay_ref, f32[3072,128]{1,0:T(8,128)} %bitcast.276), custom_call_target="tpu_custom_call" | custom-call | tf_op jit(solution)/shard_map/chain_back/pallas_call | solution.py:115
  298.6 4.7 fusion.56
  306.1 13.3 %fusion.18 = f32[4,256,12,64]{1,3,2,0:T(8,128)} fusion(f32[4,256,12,64]{1,3,2,0:T(8,128)S(1)} %get-tuple-element.136, f32[4,256,12,64]{1,0,3,2:T(4,128)S(1)} %reshape.347, f32[4,12,256]{2,1,0:T(8,128)S(1)} %copy-done.38, f32[4,256,256]{2,1,0:T(8,128)S(1)} %copy-done.21, f32[4,12,256]{2,1,0:T(8,128)S(1)} %copy-done.40, ...), kind=kOutput, calls=%fused_computation.37 | convolution fusion | flops 2434793472 | bytes 10895408 | tf_op jit(solution)/shard_map/bhtu,bthp->buhp/dot_general | solution.py:837
  319.4 3.6 copy.136
  329.1 6.4 %multiply_reduce_fusion = f32[4,256,12]{1,2,0:T(8,128)S(1)} fusion(f32[4,12,256,256]{3,2,1,0:T(8,128)} %get-tuple-element.134, f32[4,256,256]{1,2,0:T(8,128)} %bitcast.278), kind=kLoop, calls=%fused_computation | loop fusion | flops 6279168 | bytes 13680640 | tf_op jit(solution)/shard_map/bhtu,btu->bhu/dot_general | solution.py:845
  335.7 7.2 %multiply_reduce_fusion.1 = f32[4,256,256]{1,2,0:T(8,128)} fusion(f32[4,12,256,256]{3,2,1,0:T(8,128)} %get-tuple-element.134, f32[4,256,12]{1,2,0:T(8,128)S(1)} %get-tuple-element.111), kind=kLoop, calls=%fused_computation.1 | loop fusion | flops 6029312 | bytes 13680640 | tf_op jit(solution)/shard_map/bhtu,bhu->btu/dot_general | solution.py:844
  349.2 5.8 multiply_reduce_fusion.6
  359.0 4.0 convolution_convert_fusion.refs_1_
  371.5 6.9 %add_convert_fusion = bf16[4,256,1024]{2,1,0:T(8,128)(2,1)S(1)} fusion(f32[4,3,1024]{2,1,0:T(4,128)S(1)} %collective-permute-done.1, f32[4,253,1024]{2,1,0:T(8,128)} %slice.243, f32[4,254,1024]{2,1,0:T(8,128)} %slice.242, f32[4,255,1024]{2,1,0:T(8,128)} %slice.241, f32[4,256,1024]{2,1,0:T(8,128)} %get-tuple-element.102, f32[1024]{0:T(1024)S(1)} %bitcast.303, ...), kind=kLoop, calls=%fused_computation.26 | loop fusion | flops 10485760 | bytes 18845696 | tf_op jit(solution)/shard_map/convert.7
  384.1 4.0 bitcast_convert_fusion.refs_2_
  388.1 101.3 %ring_sums.1 = (f32[192,768]{1,0:T(8,128)}, f32[192,768]{1,0:T(8,128)}, f32[192,768]{1,0:T(8,128)}, f32[192,384]{1,0:T(8,128)}) custom-call(bf16[1536,768]{1,0:T(8,128)(2,1)} %convolution_convert_fusion.1.refs_0_, bf16[1536,768]{1,0:T(8,128)(2,1)} %convolution_convert_fusion.refs_1_, bf16[1536,768]{1,0:T(8,128)(2,1)} %bitcast_convert_fusion.refs_2_, ...), custom_call_target="tpu_custom_call" | custom-call | tf_op jit(solution)/shard_map/ring_sums/pallas_call | solution.py:213
  491.4 53.6 %in_phase.1 = (f32[1024,384]{1,0:T(8,128)}, f32[1,1536]{1,0:T(1,128)}) custom-call(bf16[1024,768]{1,0:T(8,128)(2,1)} %get-tuple-element.107.refs_0_, bf16[1024,768]{1,0:T(8,128)(2,1)} %bitcast.274, bf16[1024,384]{1,0:T(8,128)(2,1)} %fusion.63.refs_2_, bf16[1536,768]{1,0:T(8,128)(2,1)} %refs_3_.1, bf16[1536,768]{1,0:T(8,128)(2,1)} %refs_4_.1, ...), custom_call_target="tpu_custom_call" | custom-call | tf_op jit(solution)/shard_map/in_phase/pallas_call | solution.py:616
  547.3 12.7 %small_sum_head.1 = f32[408,128]{1,0:T(8,128)} custom-call(f32[408,128]{1,0:T(8,128)} %pad_bitcast_fusion.source_ref), custom_call_target="tpu_custom_call" | custom-call | tf_op jit(solution)/shard_map/small_sum_head/pallas_call | solution.py:666
  565.6 9.5 %small_sum_seq.1 = f32[56,128]{1,0:T(8,128)} custom-call(f32[56,128]{1,0:T(8,128)} %pad_bitcast_fusion.1.source_ref), custom_call_target="tpu_custom_call" | custom-call | tf_op jit(solution)/shard_map/small_sum_seq/pallas_call | solution.py:666
  (300 shorter events, 117.3 us)
Async XLA Ops:
  6.4 27.1 %copy-start.7 = (bf16[4,256,1536]{2,1,0:T(8,128)(2,1)}, bf16[4,256,1536]{2,1,0:T(8,128)(2,1)S(1)}, u32[]{:S(2)}) copy-start(bf16[4,256,1536]{2,1,0:T(8,128)(2,1)S(1)} %multiply_convert_fusion) | copy-start | bytes 9437188
  9.2 10.1 %copy-start.45 = (s32[4,2048]{1,0:T(4,128)S(1)}, s32[4,2048]{1,0:T(4,128)}, u32[]{:S(2)}) copy-start(s32[4,2048]{1,0:T(4,128)} %param.21) | copy-start | bytes 98308
  9.2 10.7 %copy-start.74 = (f32[12]{0:T(128)S(1)}, f32[12]{0:T(128)}, u32[]{:S(2)}) copy-start(f32[12]{0:T(128)} %param.32) | copy-start | bytes 148
  9.2 11.2 %copy-start.57 = (s32[4,256]{1,0:T(4,128)S(1)}, s32[4,256]{1,0:T(4,128)}, u32[]{:S(2)}) copy-start(s32[4,256]{1,0:T(4,128)} %param.20) | copy-start | bytes 12292
  9.2 11.4 %copy-start.62 = (f32[4,768]{1,0:T(4,128)S(1)}, f32[4,768]{1,0:T(4,128)}, u32[]{:S(2)}) copy-start(f32[4,768]{1,0:T(4,128)} %param.27) | copy-start | bytes 36868
  9.2 11.4 %copy-start.65 = (f32[4,256]{1,0:T(4,128)S(1)}, f32[4,256]{1,0:T(4,128)}, u32[]{:S(2)}) copy-start(f32[4,256]{1,0:T(4,128)} %param.29) | copy-start | bytes 12292
  13.6 36.3 %collective-permute-start = (bf16[4,3,1024]{2,1,0:T(4,128)(2,1)}, bf16[4,3,1024]{2,1,0:T(4,128)(2,1)}, u32[]{:S(2)}, u32[]{:S(2)}) collective-permute-start(bf16[4,3,1024]{2,1,0:T(4,128)(2,1)} %pad_maximum_fusion), channel_id=1, source_target_pairs={{0,4},{4,8},{8,12},{12,16},{16,20},{20,24},{24,28},{1,5},{5,9},{9,... | collective-permute-start | bytes 73736 | tf_op jit(solution)/shard_map/ppermute | solution.py:698
  30.6 176.4 %copy-start.37 = (f32[4,12,256]{2,1,0:T(8,128)}, f32[4,12,256]{2,1,0:T(8,128)S(1)}, u32[]{:S(2)}) copy-start(f32[4,12,256]{2,1,0:T(8,128)S(1)} %get-tuple-element.112) | copy-start | bytes 147460
  33.5 7.4 %copy-start.66 = (f32[768]{0:T(1024)S(1)}, f32[768]{0:T(1024)}, u32[]{:S(2)}) copy-start(f32[768]{0:T(1024)} %param.28) | copy-start | bytes 9220
  33.5 7.4 %copy-start.70 = (f32[256]{0:T(256)S(1)}, f32[256]{0:T(256)}, u32[]{:S(2)}) copy-start(f32[256]{0:T(256)} %param.30) | copy-start | bytes 3076
  33.5 7.4 %copy-start.44 = (f32[4,256]{1,0:T(4,128)S(1)}, f32[4,256]{1,0:T(4,128)}, u32[]{:S(2)}) copy-start(f32[4,256]{1,0:T(4,128)} %copy-done.43) | copy-start | bytes 12292
  33.6 8.8 %copy-start.47 = (f32[4,256]{1,0:T(4,128)S(1)}, f32[4,256]{1,0:T(4,128)}, u32[]{:S(2)}) copy-start(f32[4,256]{1,0:T(4,128)} %copy-done.46) | copy-start | bytes 12292
  33.6 10.6 %copy-start.59 = (f32[768]{0:T(1024)S(1)}, f32[768]{0:T(1024)}, u32[]{:S(2)}) copy-start(f32[768]{0:T(1024)} %param.34) | copy-start | bytes 9220
  41.0 165.9 %copy-start.39 = (f32[4,12,256]{2,1,0:T(8,128)}, f32[4,12,256]{2,1,0:T(8,128)S(1)}, u32[]{:S(2)}) copy-start(f32[4,12,256]{2,1,0:T(8,128)S(1)} %get-tuple-element.116) | copy-start | bytes 147460
  63.3 28.7 %copy-start.1 = (f32[4,256,768]{1,2,0:T(8,128)}, f32[4,256,768]{1,2,0:T(8,128)S(1)}, u32[]{:S(2)}) copy-start(f32[4,256,768]{1,2,0:T(8,128)S(1)} %copy.110) | copy-start | bytes 9437188
  68.8 23.2 %copy-start.19 = (f32[4,256,256]{2,1,0:T(8,128)S(1)}, f32[4,256,256]{2,1,0:T(8,128)}, u32[]{:S(2)}) copy-start(f32[4,256,256]{2,1,0:T(8,128)} %fusion.75) | copy-start | bytes 3145732
  68.8 23.2 %copy-start.23 = (f32[4,256,768]{1,2,0:T(8,128)S(1)}, f32[4,256,768]{1,2,0:T(8,128)}, u32[]{:S(2)}) copy-start(f32[4,256,768]{1,2,0:T(8,128)} %copy.123) | copy-start | bytes 9437188
  68.8 23.2 %copy-start.33 = (pred[4,256,256]{2,1,0:T(8,128)(4,1)S(1)}, pred[4,256,256]{2,1,0:T(8,128)(4,1)}, u32[]{:S(2)}) copy-start(pred[4,256,256]{2,1,0:T(8,128)(4,1)} %compare_and_fusion) | copy-start | bytes 786436
  68.8 23.2 %copy-start.72 = (f32[12]{0:T(128)S(1)}, f32[12]{0:T(128)}, u32[]{:S(2)}) copy-start(f32[12]{0:T(128)} %param.33) | copy-start | bytes 148
  92.0 16.5 %copy-start.13 = (f32[4,256,12,64]{1,3,2,0:T(8,128)}, f32[4,256,12,64]{1,3,2,0:T(8,128)S(1)}, u32[]{:S(2)}) copy-start(f32[4,256,12,64]{1,3,2,0:T(8,128)S(1)} %fusion.67) | copy-start | bytes 9437188
  207.0 19.2 %copy-start.61 = (f32[8,128]{1,0:T(8,128)S(1)}, f32[8,128]{1,0:T(8,128)}, u32[]{:S(2)}) copy-start(f32[8,128]{1,0:T(8,128)} %get-tuple-element.124) | copy-start | bytes 12292
  207.0 19.2 %copy-start.56 = (f32[12,64]{1,0:T(8,128)S(1)}, f32[12,64]{1,0:T(8,128)}, u32[]{:S(2)}) copy-start(f32[12,64]{1,0:T(8,128)} %mul.540) | copy-start | bytes 9220
  234.3 64.2 %copy-start.3 = (f32[4,256,768]{1,2,0:T(8,128)S(1)}, f32[4,256,768]{1,2,0:T(8,128)}, u32[]{:S(2)}) copy-start(f32[4,256,768]{1,2,0:T(8,128)} %copy-done.1) | copy-start | bytes 9437188
  335.7 13.5 %slice-start = ((s8[4325376]{0:T(1024)(128)(4,1)}), s8[4194304]{0:T(1024)(128)(4,1)S(1)}, s32[]{:S(2)}) async-start(s8[4325376]{0:T(1024)(128)(4,1)} %bitcast.248), calls=%async_computation | async-start | bytes 8388608
  335.7 13.4 %slice-start.1 = ((s8[4325376]{0:T(1024)(128)(4,1)}), s8[131072]{0:T(1024)(128)(4,1)S(1)}, s32[]{:S(2)}) async-start(s8[4325376]{0:T(1024)(128)(4,1)} %bitcast.248), calls=%async_computation.1 | async-start | bytes 262144
  335.7 13.4 %copy-start.12 = (f32[4,256,768]{2,1,0:T(8,128)S(1)}, f32[4,256,768]{2,1,0:T(8,128)}, u32[]{:S(2)}) copy-start(f32[4,256,768]{2,1,0:T(8,128)} %copy.136) | copy-start | bytes 9437188
  349.2 7.3 %copy-start.4 = (f32[4,256,768]{1,2,0:T(8,128)S(1)}, f32[4,256,768]{1,2,0:T(8,128)}, u32[]{:S(2)}) copy-start(f32[4,256,768]{1,2,0:T(8,128)} %copy-done.1) | copy-start | bytes 9437188
  355.1 16.4 %collective-permute-start.1 = (f32[4,3,1024]{2,1,0:T(4,128)S(1)}, f32[4,3,1024]{2,1,0:T(4,128)S(1)}, u32[]{:S(2)}, u32[]{:S(2)}) collective-permute-start(f32[4,3,1024]{2,1,0:T(4,128)S(1)} %fusion.81), channel_id=1, source_target_pairs={{4,0},{8,4},{12,8},{16,12},{20,16},{24,20},{28,24},{5,1},{9,5},{13... | collective-permute-start | bytes 147464 | tf_op jit(solution)/shard_map/ppermute | solution.py:698
  371.5 7.9 %copy-start.9 = (bf16[4,256,1536]{2,1,0:T(8,128)(2,1)S(1)}, bf16[4,256,1536]{2,1,0:T(8,128)(2,1)}, u32[]{:S(2)}) copy-start(bf16[4,256,1536]{2,1,0:T(8,128)(2,1)} %copy-done.7) | copy-start | bytes 9437188
  491.4 72.9 %copy-start.64 = (f32[768]{0:T(1024)S(1)}, f32[768]{0:T(1024)}, u32[]{:S(2)}) copy-start(f32[768]{0:T(1024)} %get-tuple-element.109) | copy-start | bytes 9220
  545.0 42.6 %copy-start.16 = (f32[1024,384]{1,0:T(8,128)S(1)}, f32[1024,384]{1,0:T(8,128)}, u32[]{:S(2)}) copy-start(f32[1024,384]{1,0:T(8,128)} %get-tuple-element.28.refs_8_) | copy-start | bytes 4718596
  545.0 43.8 %copy-start.28 = (f32[1024,384]{1,0:T(8,128)S(1)}, f32[1024,384]{1,0:T(8,128)}, u32[]{:S(2)}) copy-start(f32[1024,384]{1,0:T(8,128)} %get-tuple-element.35) | copy-start | bytes 4718596
  (48 other events, 166.4 us)

commit v2 on v1

--- a/solution.py
+++ b/solution.py
@@ -53,80 +53,6 @@
 
 def dot_tn(a, b, precision=None):
     return lax.dot_general(a, b, TN, precision=precision, preferred_element_type=f32)
-
-
-def chain_kernel(
-    reverse, group, decay_ref, local_ref, out_ref, held, outgoing, send_sem, recv_sem
-):
-    n = lax.axis_size("seq")
-    place = lax.axis_index("seq")
-    head = lax.axis_index("head")
-    ahead = n - 1 - place if reverse else place
-    by = -1 if reverse else 1
-    chunks, rows = held.shape[0], held.shape[1]
-    barrier = pltpu.get_barrier_semaphore()
-
-    @pl.when(ahead > 0)
-    def _():
-        pl.semaphore_signal(barrier, inc=1, device_id=(place - by, head), device_id_type=MESH)
-
-    @pl.when(ahead < n - 1)
-    def _():
-        pl.semaphore_wait(barrier, 1)
-
-    def copy(c):
-        return remote(
-            outgoing.at[c], held.at[c], send_sem.at[c], recv_sem.at[c], (place + by, head)
-        )
-
-    def step(c):
-        @pl.when(ahead > 0)
-        def _():
-            copy(c).wait_recv()
-
-        @pl.when(ahead == 0)
-        def _():
-            held[c] = jnp.zeros(held.shape[1:], bf16)
-
-        for g in range(group):
-            part = pl.ds(g * HEADDIM, HEADDIM)
-            inner = pl.ds(pl.multiple_of(c * rows + g * HEADDIM, HEADDIM), HEADDIM)
-            state = held[c, part].astype(f32)
-            outgoing[c, part] = (decay_ref[c * group + g] * state + local_ref[inner]).astype(bf16)
-
-        @pl.when(ahead < n - 1)
-        def _():
-            copy(c).start()
-
-        out_ref[pl.ds(pl.multiple_of(c * rows, rows), rows)] = held[c]
-
-    loop(chunks, step)
-
-    @pl.when(ahead < n - 1)
-    def _():
-        loop(chunks, lambda c: copy(c).wait_send())
-
-
-def chain(decay, local, reverse, cid):
-    total = local.shape[0] * local.shape[1]
-    group = next(g for g in (3, 2, 1) if decay.shape[1] % g == 0)
-    rows = group * HEADDIM
-    chunks = total // rows
-    out = pl.pallas_call(
-        functools.partial(chain_kernel, reverse, group),
-        out_shape=jax.ShapeDtypeStruct((total, STATE), bf16),
-        in_specs=[in_smem, in_vmem],
-        out_specs=in_vmem,
-        scratch_shapes=[
-            pltpu.VMEM((chunks, rows, STATE), bf16),
-            pltpu.VMEM((chunks, rows, STATE), bf16),
-            pltpu.SemaphoreType.DMA((chunks,)),
-            pltpu.SemaphoreType.DMA((chunks,)),
-        ],
-        compiler_params=params(cid),
-        name="chain_back" if reverse else "chain_forward",
-    )(decay.reshape(-1), local.reshape(total, STATE))
-    return out.reshape(local.shape)
 
 
 def ring_place(n, index):
@@ -290,8 +216,7 @@
 
 
 def as_row(values):
-    ones = jnp.ones((8, values.shape[1]), f32)
-    return dot_nt(ones, values, highest)[:1]
+    return rows_of(values)
 
 
 def scatter_phases(group, chunks, part, mate_in, chip_out, chip_in, sems):
@@ -692,15 +617,920 @@
     return found
 
 
-def passed_along(x, axis, by):
-    count = lax.axis_size(axis)
-    pairs = [(i, i + by) for i in range(count) if 0 <= i + by < count]
-    return lax.ppermute(x, axis, pairs)
-
-
-def silu_slope(linear):
-    sigmoid_value = jax.nn.sigmoid(linear)
-    return sigmoid_value * (1.0 + linear * (1.0 - sigmoid_value))
+def blocks(width, size=256):
+    return [(at, min(size, width - at)) for at in range(0, width, size)]
+
+
+def fold_lanes(values):
+    rows, width = values.shape
+    if width % LANES:
+        fill = jnp.zeros((rows, LANES - width % LANES), values.dtype)
+        values = jnp.concatenate([values, fill], axis=1)
+    total = values[:, :LANES]
+    for at in range(LANES, width, LANES):
+        total = total + values[:, at : at + LANES]
+    return total
+
+
+def rows_of(values):
+    return jnp.sum(fold_lanes(values).T, axis=0, keepdims=True)
+
+
+def head_spread(channels):
+    row = lax.broadcasted_iota(jnp.int32, (LANES, channels), 0)
+    head = lax.broadcasted_iota(jnp.int32, (LANES, channels), 1) // HEADDIM
+    return ((row % 16 == head) & (row < 48)).astype(f32).astype(bf16)
+
+
+def head_gather(channels):
+    head = lax.broadcasted_iota(jnp.int32, (channels, LANES), 0) // HEADDIM
+    return (lax.broadcasted_iota(jnp.int32, (channels, LANES), 1) == head).astype(f32).astype(bf16)
+
+
+def spread(values, marks):
+    lane = lax.broadcasted_iota(jnp.int32, values.shape, 1)
+    values = jnp.where(lane < 16, values, 0.0)
+    high = values.astype(bf16).astype(f32)
+    left = values - high
+    middle = left.astype(bf16).astype(f32)
+    low = (left - middle).astype(bf16).astype(f32)
+    three = high + pltpu.roll(middle, 16, 1) + pltpu.roll(low, 32, 1)
+    return jnp.dot(three.astype(bf16), marks, preferred_element_type=f32)
+
+
+def gather_heads(values, marks):
+    high = values.astype(bf16)
+    low = (values - high.astype(f32)).astype(bf16)
+    return jnp.dot(high, marks, preferred_element_type=f32) + jnp.dot(
+        low, marks, preferred_element_type=f32
+    )
+
+
+def softplus(x):
+    y = jnp.exp(-jnp.abs(x))
+    small = y * (1.0 - y * (1.0 / 2 - y * (1.0 / 3 - y * (1.0 / 4 - y * (1.0 / 5)))))
+    return jnp.maximum(x, 0.0) + jnp.where(y < 0.03, small, jnp.log(1.0 + y))
+
+
+def position_masks(docs_row, begin):
+    length = docs_row.shape[1]
+    column = jnp.broadcast_to(docs_row, (LANES, length)).T
+    place = begin + lax.broadcasted_iota(jnp.int32, (length, LANES), 0).astype(f32)
+    return column, place
+
+
+def front_kernel(
+    heads,
+    tokens_hbm,
+    gain_ref,
+    value_hbm,
+    keyquery_hbm,
+    step_ref,
+    gate_hbm,
+    docs_ref,
+    vectors_ref,
+    value_conv_ref,
+    value_offset_ref,
+    keyquery_conv_ref,
+    keyquery_offset_ref,
+    norm_gain_ref,
+    normed_out,
+    linear_out,
+    conv_out,
+    gate_out,
+    mixed_out,
+    gained_out,
+    halo_out,
+    state_out,
+    steps_out,
+    cumulative_out,
+    linear_steps_out,
+    square_out,
+    inverse_out,
+    tokens,
+    value_weight,
+    keyquery_weight,
+    gate_weight,
+    normed,
+    linear,
+    conv,
+    gate,
+    mixed,
+    gained,
+    tail,
+    halo,
+    extended,
+    heads_in,
+    keys,
+    queries,
+    scores,
+    mask_bias,
+    locals_,
+    held,
+    outgoing,
+    passed,
+    entering,
+    load_sem,
+    token_sem,
+    store_sem,
+    halo_sem,
+    chain_send,
+    chain_recv,
+):
+    n = lax.axis_size("seq")
+    place = lax.axis_index("seq")
+    head = lax.axis_index("head")
+    count, length, _ = tokens.shape
+    channels = value_weight.shape[1]
+    both = channels + 2 * STATE
+    lags = value_conv_ref.shape[0]
+    begin = (place * length).astype(f32)
+    chunk_rows = STATE // 4
+    chunks = count * 4
+
+    loads = [
+        pltpu.make_async_copy(value_hbm, value_weight, load_sem.at[0]),
+        pltpu.make_async_copy(keyquery_hbm, keyquery_weight, load_sem.at[1]),
+        pltpu.make_async_copy(gate_hbm, gate_weight, load_sem.at[2]),
+    ]
+
+    def token_load(b):
+        return pltpu.make_async_copy(tokens_hbm.at[b], tokens.at[b], token_sem.at[b])
+
+    for b in range(count):
+        token_load(b).start()
+        if b == 0:
+            loads[0].start()
+            loads[1].start()
+    loads[2].start()
+
+    stores = [
+        (normed, normed_out),
+        (linear, linear_out),
+        (conv, conv_out),
+        (gate, gate_out),
+        (mixed, mixed_out),
+        (gained, gained_out),
+    ]
+
+    def store(i, b):
+        source, target = stores[i]
+        return pltpu.make_async_copy(source.at[b], target.at[b], store_sem.at[i, b])
+
+    barrier = pltpu.get_barrier_semaphore()
+
+    @pl.when(place > 0)
+    def _():
+        pl.semaphore_signal(barrier, inc=1, device_id=(place - 1, head), device_id_type=MESH)
+
+    @pl.when(place < n - 1)
+    def _():
+        pl.semaphore_signal(barrier, inc=1, device_id=(place + 1, head), device_id_type=MESH)
+
+    def norm(b):
+        token_load(b).wait()
+        x = tokens[b]
+        inverse = lax.rsqrt(jnp.mean(x * x, axis=-1, keepdims=True) + norm_eps)
+        normed[b] = (x * inverse * gain_ref[...]).astype(bf16)
+        inverse_out[pl.ds(b, 1)] = jnp.broadcast_to(inverse, (length, LANES)).T[:1]
+        store(0, b).start()
+
+    loop(count, norm)
+    loads[0].wait()
+    loads[1].wait()
+
+    last = jnp.concatenate([normed[b, length - 16 :] for b in range(count)], axis=0)
+    for at, width in blocks(channels):
+        tail[:, at : at + width] = jnp.dot(
+            last, value_weight[:, at : at + width], preferred_element_type=f32
+        ).astype(bf16)
+    tail[:, channels:] = jnp.dot(last, keyquery_weight[...], preferred_element_type=f32).astype(bf16)
+    pl.semaphore_wait(barrier, (place > 0).astype(jnp.int32) + (place < n - 1).astype(jnp.int32))
+    halo_copy = remote(tail, halo, halo_sem.at[0], halo_sem.at[1], (place + 1, head))
+
+    @pl.when(place < n - 1)
+    def _():
+        halo_copy.start()
+
+    def project(b):
+        rows = normed[b]
+        for at, width in blocks(channels):
+            linear[b, :, at : at + width] = jnp.dot(
+                rows, value_weight[:, at : at + width], preferred_element_type=f32
+            ).astype(bf16)
+        linear[b, :, channels:] = jnp.dot(
+            rows, keyquery_weight[...], preferred_element_type=f32
+        ).astype(bf16)
+        linear_steps_out[b] = jnp.dot(rows, step_ref[...], preferred_element_type=f32)
+        store(1, b).start()
+
+    loop(count, project)
+
+    @pl.when(place > 0)
+    def _():
+        halo_copy.wait_recv()
+
+    @pl.when(place == 0)
+    def _():
+        halo[...] = jnp.zeros_like(halo)
+
+    halo_out[...] = halo[...]
+    marks = head_spread(channels)
+    step_bias = vectors_ref[0:1]
+    decay_rate = -jnp.exp(vectors_ref[1:2])
+    skip = spread(vectors_ref[...], marks)[2:3]
+    triangle = (
+        lax.broadcasted_iota(jnp.int32, (length, length), 0)
+        >= lax.broadcasted_iota(jnp.int32, (length, length), 1)
+    ).astype(f32)
+
+    def states(b):
+        column, spot = position_masks(docs_ref[pl.ds(b, 1)].astype(f32), begin)
+        extended[0:16] = halo[pl.ds(pl.multiple_of(b * 16, 16), 16)].astype(f32)
+        extended[16:] = linear[b].astype(f32)
+        usable = [None] + [(spot - lag >= column).astype(f32) for lag in range(1, lags)]
+        for at in range(0, both, LANES):
+            if at < channels:
+                weight, offset, place_at = value_conv_ref, value_offset_ref, at
+            else:
+                weight, offset, place_at = keyquery_conv_ref, keyquery_offset_ref, at - channels
+            lanes = slice(place_at, place_at + LANES)
+            value = offset[:, lanes] + weight[0:1, lanes] * extended[16:, at : at + LANES]
+            for lag in range(1, lags):
+                value = value + weight[lag : lag + 1, lanes] * (
+                    extended[16 - lag : 16 - lag + length, at : at + LANES] * usable[lag]
+                )
+            conv[b, :, at : at + LANES] = value
+            active = value * jax.nn.sigmoid(value)
+            if at < channels:
+                heads_in[b, :, at : at + LANES] = active
+            elif at < channels + STATE:
+                keys[b] = active.astype(bf16)
+            else:
+                queries[b] = active.astype(bf16)
+        store(2, b).start()
+        steps = softplus(linear_steps_out[b] + step_bias)
+        cumulative = jnp.dot(
+            triangle, steps * decay_rate, precision=highest, preferred_element_type=f32
+        )
+        steps_out[b] = steps
+        cumulative_out[b] = cumulative
+        kept = (column < begin).astype(f32)
+        trailing = (spot >= column[length - 1 :]).astype(f32)
+        entering[b] = jnp.exp(cumulative) * kept
+        end_weight = jnp.exp(cumulative[length - 1 :] - cumulative) * trailing * steps
+        weighted = (heads_in[b] * spread(end_weight, marks)).astype(bf16)
+        locals_[b] = dot_tn(keys[b], weighted)
+        last_entering = entering[b, length - 8 :]
+        passed[b] = spread(last_entering, marks)
+
+    loop(count, states)
+
+    def chain_copy(c):
+        part = (lax.div(c, 4), pl.ds(pl.multiple_of(lax.rem(c, 4) * chunk_rows, chunk_rows), chunk_rows))
+        return remote(
+            outgoing.at[part], held.at[part], chain_send.at[c], chain_recv.at[c], (place + 1, head)
+        )
+
+    def chain_step(c):
+        b = lax.div(c, 4)
+        rows = pl.ds(pl.multiple_of(lax.rem(c, 4) * chunk_rows, chunk_rows), chunk_rows)
+
+        @pl.when(place > 0)
+        def _():
+            chain_copy(c).wait_recv()
+
+        @pl.when(place == 0)
+        def _():
+            held[b, rows] = jnp.zeros((chunk_rows, channels), bf16)
+
+        outgoing[b, rows] = (
+            passed[b, 7:8] * held[b, rows].astype(f32) + locals_[b, rows]
+        ).astype(bf16)
+
+        @pl.when(place < n - 1)
+        def _():
+            chain_copy(c).start()
+
+    pairs = channels // LANES
+    lag_slots = 5
+    slots = chunks + lag_slots * (n - 1)
+
+    def chain_slot(i):
+        c = i - lag_slots * place
+
+        @pl.when((c >= 0) & (c < chunks))
+        def _():
+            chain_step(c)
+
+    first_half = lax.broadcasted_iota(jnp.int32, (length, LANES), 1) < HEADDIM
+    loads[2].wait()
+
+    def inside(b):
+        column, spot = position_masks(docs_ref[pl.ds(b, 1)].astype(f32), begin)
+        wide = jnp.concatenate([column] * (length // LANES), axis=1)
+        t = begin + lax.broadcasted_iota(jnp.int32, (length, length), 0).astype(f32)
+        u = begin + lax.broadcasted_iota(jnp.int32, (length, length), 1).astype(f32)
+        mask_bias[...] = jnp.where((u >= wide) & (u <= t), 0.0, -1e30)
+        scores[...] = dot_nt(queries[b], keys[b])
+        cumulative = cumulative_out[b]
+        across = cumulative.T
+        spread_steps = spread(steps_out[b], marks)
+        for pair in range(pairs):
+            lanes = slice(pair * LANES, (pair + 1) * LANES)
+            scaled = heads_in[b, :, lanes] * spread_steps[:, lanes]
+            value = jnp.zeros((length, LANES), f32)
+            for half in range(2):
+                h = 2 * pair + half
+                decay = jnp.exp(cumulative[:, h : h + 1] - across[h : h + 1] + mask_bias[...])
+                mixing = (decay * scores[...]).astype(bf16)
+                mine = jnp.where(first_half if half == 0 else ~first_half, scaled, 0.0).astype(bf16)
+                value = value + jnp.dot(mixing, mine, preferred_element_type=f32)
+            mixed[b, :, lanes] = value
+            chain_slot(b * (pairs + 1) + pair)
+        rows = normed[b]
+        for at, width in blocks(channels):
+            gate[b, :, at : at + width] = jnp.dot(
+                rows, gate_weight[:, at : at + width], preferred_element_type=f32
+            )
+        store(3, b).start()
+        chain_slot(b * (pairs + 1) + pairs)
+
+    loop(count, inside)
+    done = count * (pairs + 1)
+    if slots > done:
+        loop(slots - done, lambda i: chain_slot(i + done))
+
+    def close(b):
+        state_out[b] = held[b]
+        projected = jnp.dot(queries[b], held[b], preferred_element_type=f32)
+        value = mixed[b] + spread(entering[b], marks) * projected + skip * heads_in[b]
+        mixed[b] = value
+        store(4, b).start()
+        linear_gate = gate[b]
+        gated = value * (linear_gate * jax.nn.sigmoid(linear_gate))
+        gained[b] = (gated * norm_gain_ref[...]).astype(bf16)
+        store(5, b).start()
+        square_out[pl.ds(b, 1)] = rows_of(gated * gated)
+
+    loop(count, close)
+
+    @pl.when(place < n - 1)
+    def _():
+        halo_copy.wait_send()
+        loop(chunks, lambda c: chain_copy(c).wait_send())
+
+    for i in range(len(stores)):
+        loop(count, lambda b, i=i: store(i, b).wait())
+
+
+def front(tokens, gain, value_weight, keyquery_weight, step_weight, gate_weight, docs, vectors, conv, norm_gain, cid):
+    count, length, _ = tokens.shape
+    channels = value_weight.shape[1]
+    heads = channels // HEADDIM
+    both = channels + 2 * STATE
+    chunks = count * 4
+    dma = pltpu.SemaphoreType.DMA
+    hbm = pl.BlockSpec(memory_space=pl.ANY)
+    shape = jax.ShapeDtypeStruct
+    big = [
+        ((count, length, D), bf16),
+        ((count, length, both), bf16),
+        ((count, length, both), f32),
+        ((count, length, channels), f32),
+        ((count, length, channels), f32),
+        ((count, length, channels), bf16),
+    ]
+    small = [
+        ((count * 16, both), bf16),
+        ((count, STATE, channels), bf16),
+        ((count, length, LANES), f32),
+        ((count, length, LANES), f32),
+        ((count, length, LANES), f32),
+        ((count, length), f32),
+        ((count, length), f32),
+    ]
+    return pl.pallas_call(
+        functools.partial(front_kernel, heads),
+        out_shape=[shape(*s) for s in big + small],
+        in_specs=[hbm, in_vmem, hbm, hbm, in_vmem, hbm] + [in_vmem] * 7,
+        out_specs=[hbm] * len(big) + [in_vmem] * len(small),
+        scratch_shapes=[
+            pltpu.VMEM((count, length, D), f32),
+            pltpu.VMEM((D, channels), bf16),
+            pltpu.VMEM((D, 2 * STATE), bf16),
+            pltpu.VMEM((D, channels), bf16),
+        ]
+        + [pltpu.VMEM(*s) for s in big]
+        + [
+            pltpu.VMEM((count * 16, both), bf16),
+            pltpu.VMEM((count * 16, both), bf16),
+            pltpu.VMEM((length + 16, both), f32),
+            pltpu.VMEM((count, length, channels), f32),
+            pltpu.VMEM((count, length, STATE), bf16),
+            pltpu.VMEM((count, length, STATE), bf16),
+            pltpu.VMEM((length, length), f32),
+            pltpu.VMEM((length, length), f32),
+            pltpu.VMEM((count, STATE, channels), f32),
+            pltpu.VMEM((count, STATE, channels), bf16),
+            pltpu.VMEM((count, STATE, channels), bf16),
+            pltpu.VMEM((count, 8, channels), f32),
+            pltpu.VMEM((count, length, LANES), f32),
+            dma((3,)),
+            dma((count,)),
+            dma((len(big), count)),
+            dma((2,)),
+            dma((chunks,)),
+            dma((chunks,)),
+        ],
+        compiler_params=params(cid),
+        name="front",
+    )(tokens, gain, value_weight, keyquery_weight, step_weight, gate_weight, docs, vectors, *conv, norm_gain)
+
+
+def back_kernel(
+    pieces_hbm,
+    weight_hbm,
+    gate_hbm,
+    mixed_hbm,
+    conv_hbm,
+    linear_hbm,
+    halo_ref,
+    state_ref,
+    steps_ref,
+    cumulative_ref,
+    linear_steps_ref,
+    square_ref,
+    rowdot_ref,
+    docs_ref,
+    vectors_ref,
+    value_conv_ref,
+    keyquery_conv_ref,
+    norm_gain_ref,
+    normed_out_out,
+    gate_grad_out,
+    values_grad_out,
+    narrow_out,
+    conv_grad_out,
+    vector_grad_out,
+    gain_grad_out,
+    pieces,
+    weight,
+    gate,
+    mixed,
+    conv,
+    linear,
+    normed_out,
+    gate_grad,
+    values_grad,
+    narrow,
+    heads_in,
+    heads_grad,
+    keys,
+    queries,
+    scores,
+    scores_grad,
+    mask_bias,
+    inner,
+    narrow_grad,
+    locals_,
+    held,
+    outgoing,
+    passed,
+    extended,
+    spread_grad,
+    usable_rows,
+    edge,
+    edge_in,
+    tails,
+    load_sem,
+    row_sem,
+    store_sem,
+    edge_send,
+    edge_recv,
+    chain_send,
+    chain_recv,
+):
+    n = lax.axis_size("seq")
+    place = lax.axis_index("seq")
+    head = lax.axis_index("head")
+    ahead = n - 1 - place
+    count, length, channels = gate.shape
+    both = channels + 2 * STATE
+    lags = value_conv_ref.shape[0]
+    begin = (place * length).astype(f32)
+    chunk_rows = STATE // 4
+    chunks = count * 4
+    groups, width = pieces.shape[0], pieces.shape[2]
+    inner_total = NHEADS * HEADDIM
+
+    loads = [
+        pltpu.make_async_copy(weight_hbm, weight, load_sem.at[0]),
+        pltpu.make_async_copy(pieces_hbm, pieces, load_sem.at[1]),
+    ]
+    for copy in loads:
+        copy.start()
+    row_arrays = [(gate_hbm, gate), (mixed_hbm, mixed), (conv_hbm, conv), (linear_hbm, linear)]
+
+    def row_load(i, b):
+        source, target = row_arrays[i]
+        return pltpu.make_async_copy(source.at[b], target.at[b], row_sem.at[i, b])
+
+    for b in range(count):
+        for i in range(3):
+            row_load(i, b).start()
+    for b in range(count):
+        row_load(3, b).start()
+
+    stores = [
+        (normed_out, normed_out_out),
+        (gate_grad, gate_grad_out),
+        (values_grad, values_grad_out),
+        (narrow, narrow_out),
+    ]
+
+    def store(i, b):
+        source, target = stores[i]
+        return pltpu.make_async_copy(source.at[b], target.at[b], store_sem.at[i, b])
+
+    barrier = pltpu.get_barrier_semaphore()
+
+    @pl.when(place > 0)
+    def _():
+        pl.semaphore_signal(barrier, inc=1, device_id=(place - 1, head), device_id_type=MESH)
+
+    @pl.when(place < n - 1)
+    def _():
+        pl.semaphore_signal(barrier, inc=1, device_id=(place + 1, head), device_id_type=MESH)
+
+    marks = head_spread(channels)
+    collect = head_gather(channels)
+    step_bias = vectors_ref[0:1]
+    decay_rate = -jnp.exp(vectors_ref[1:2])
+    skip = spread(vectors_ref[...], marks)[2:3]
+    gain_grad_out[...] = jnp.zeros_like(gain_grad_out)
+    vector_grad_out[...] = jnp.zeros_like(vector_grad_out)
+    conv_grad_out[...] = jnp.zeros_like(conv_grad_out)
+    for copy in loads:
+        copy.wait()
+
+    def row_column(ref, b):
+        per = length // LANES
+        row = jnp.concatenate([ref[pl.ds(b * per + i, 1)] for i in range(per)], axis=1)
+        return jnp.broadcast_to(row, (LANES, length)).T
+
+    def widened(column, size):
+        return jnp.concatenate([column] * (size // LANES), axis=1)
+
+    def gated_norm(b):
+        for i in range(3):
+            row_load(i, b).wait()
+        scale = lax.rsqrt(row_column(square_ref, b) * (1.0 / inner_total) + norm_eps)
+        pull = scale * scale * row_column(rowdot_ref, b) * (1.0 / inner_total)
+        column, _ = position_masks(docs_ref[pl.ds(b, 1)].astype(f32), begin)
+        entering = spread(
+            jnp.exp(cumulative_ref[b]) * (column < begin).astype(f32), marks
+        )
+        passed[b] = entering[length - 8 :]
+        for at, size in blocks(channels):
+            lanes = slice(at, at + size)
+            grad_rows = jnp.zeros((length, size), f32)
+            for j in range(groups):
+                block = (
+                    weight[lanes, j * width : (j + 1) * width]
+                    if len(weight.shape) == 2
+                    else weight[j, lanes]
+                )
+                grad_rows = grad_rows + dot_nt(pieces[j, pl.ds(pl.multiple_of(b * length, length), length)], block)
+            linear_gate = gate[b, :, lanes]
+            sigmoid_value = jax.nn.sigmoid(linear_gate)
+            active = linear_gate * sigmoid_value
+            value = mixed[b, :, lanes]
+            gated = value * active
+            norm_gain = norm_gain_ref[:, lanes]
+            scaled = gated * widened(scale, size)
+            normed_out[b, :, lanes] = (scaled * norm_gain).astype(bf16)
+            gain_grad_out[:, lanes] += jnp.sum(grad_rows * scaled, axis=0, keepdims=True)
+            gated_grad = widened(scale, size) * norm_gain * grad_rows - gated * widened(pull, size)
+            heads_grad[b, :, lanes] = gated_grad * active
+            slope = sigmoid_value * (1.0 + linear_gate * (1.0 - sigmoid_value))
+            gate_grad[b, :, lanes] = (gated_grad * value * slope).astype(bf16)
+            values = conv[b, :, lanes]
+            heads_in[b, :, lanes] = values * jax.nn.sigmoid(values)
+        store(0, b).start()
+        store(1, b).start()
+        values = conv[b, :, channels : channels + STATE]
+        keys[b] = (values * jax.nn.sigmoid(values)).astype(bf16)
+        values = conv[b, :, channels + STATE :]
+        queries[b] = (values * jax.nn.sigmoid(values)).astype(bf16)
+        locals_[b] = dot_tn(queries[b], (heads_grad[b] * entering).astype(bf16))
+
+    loop(count, gated_norm)
+    pl.semaphore_wait(barrier, (place > 0).astype(jnp.int32) + (place < n - 1).astype(jnp.int32))
+
+    def chain_copy(c):
+        part = (lax.div(c, 4), pl.ds(pl.multiple_of(lax.rem(c, 4) * chunk_rows, chunk_rows), chunk_rows))
+        return remote(
+            outgoing.at[part], held.at[part], chain_send.at[c], chain_recv.at[c], (place - 1, head)
+        )
+
+    def chain_step(c):
+        b = lax.div(c, 4)
+        rows = pl.ds(pl.multiple_of(lax.rem(c, 4) * chunk_rows, chunk_rows), chunk_rows)
+
+        @pl.when(ahead > 0)
+        def _():
+            chain_copy(c).wait_recv()
+
+        @pl.when(ahead == 0)
+        def _():
+            held[b, rows] = jnp.zeros((chunk_rows, channels), bf16)
+
+        outgoing[b, rows] = (
+            passed[b, 7:8] * held[b, rows].astype(f32) + locals_[b, rows]
+        ).astype(bf16)
+
+        @pl.when(place > 0)
+        def _():
+            chain_copy(c).start()
+
+    pairs = channels // LANES
+    lag_slots = 4
+
+    def chain_slot(i):
+        c = i - lag_slots * ahead
+
+        @pl.when((c >= 0) & (c < chunks))
+        def _():
+            chain_step(c)
+
+    first_half = lax.broadcasted_iota(jnp.int32, (length, LANES), 1) < HEADDIM
+
+    def inside(b):
+        docs_row = docs_ref[pl.ds(b, 1)].astype(f32)
+        u = begin + lax.broadcasted_iota(jnp.int32, (length, length), 0).astype(f32)
+        t = begin + lax.broadcasted_iota(jnp.int32, (length, length), 1).astype(f32)
+        mask_bias[...] = jnp.where((u >= docs_row) & (u <= t), 0.0, -1e30)
+        scores[...] = dot_nt(keys[b], queries[b])
+        scores_grad[...] = jnp.zeros_like(scores_grad)
+        cumulative = cumulative_ref[b]
+        across = cumulative.T
+        spread_steps = spread(steps_ref[b], marks)
+        for pair in range(pairs):
+            lanes = slice(pair * LANES, (pair + 1) * LANES)
+            scaled = heads_in[b, :, lanes] * spread_steps[:, lanes]
+            grads = heads_grad[b, :, lanes]
+            low_grads = grads.astype(bf16)
+            value = jnp.zeros((length, LANES), f32)
+            for half in range(2):
+                h = 2 * pair + half
+                mine = first_half if half == 0 else ~first_half
+                decay = jnp.exp(across[h : h + 1] - cumulative[:, h : h + 1] + mask_bias[...])
+                mixing = (decay * scores[...]).astype(bf16)
+                value = value + jnp.dot(
+                    mixing, jnp.where(mine, grads, 0.0).astype(bf16), preferred_element_type=f32
+                )
+                pairwise = dot_nt(jnp.where(mine, scaled, 0.0).astype(bf16), low_grads)
+                scores_grad[...] += decay * pairwise
+            inner[b, :, lanes] = value
+            chain_slot(b * (pairs + 1) + pair)
+        low = scores_grad[...].astype(bf16)
+        narrow_grad[b, :, :STATE] = jnp.dot(low, queries[b], preferred_element_type=f32)
+        narrow_grad[b, :, STATE:] = dot_tn(low, keys[b])
+        chain_slot(b * (pairs + 1) + pairs)
+
+    loop(count, inside)
+    done = count * (pairs + 1)
+    extended[0:16] = jnp.zeros((16, both), f32)
+    spread_grad[0:16] = jnp.zeros((16, both), f32)
+    spread_grad[16 + length :] = jnp.zeros((16, both), f32)
+    usable_rows[...] = jnp.zeros_like(usable_rows)
+    upper = (
+        lax.broadcasted_iota(jnp.int32, (length, length), 0)
+        <= lax.broadcasted_iota(jnp.int32, (length, length), 1)
+    ).astype(f32)
+    last_row = lax.broadcasted_iota(jnp.int32, (length, LANES), 0) == length - 1
+
+    def edge_copy(b):
+        return remote(edge.at[b], edge_in.at[b], edge_send.at[b], edge_recv.at[b], (place - 1, head))
+
+    def close(b):
+        need = lag_slots * ahead + 4 * (b + 1)
+        start = jnp.maximum(done, lag_slots * ahead + 4 * b)
+        lax.fori_loop(start, jnp.maximum(start, need), lambda i, x: (chain_slot(i), x)[1], 0)
+        column, spot = position_masks(docs_ref[pl.ds(b, 1)].astype(f32), begin)
+        cumulative = cumulative_ref[b]
+        steps = steps_ref[b]
+        kept = (column < begin).astype(f32)
+        trailing = (spot >= column[length - 1 :]).astype(f32)
+        entering = jnp.exp(cumulative) * kept
+        end_decay = jnp.exp(cumulative[length - 1 :] - cumulative) * trailing
+        end_weight = end_decay * steps
+        end_grad = held[b]
+        x = heads_in[b]
+        dy = heads_grad[b]
+        grown = jnp.dot(keys[b], end_grad, preferred_element_type=f32)
+        spread_end = spread(end_weight, marks)
+        narrow_grad[b, :, :STATE] += dot_nt((x * spread_end).astype(bf16), end_grad)
+        narrow_grad[b, :, STATE:] += dot_nt(
+            (dy * spread(entering, marks)).astype(bf16), state_ref[b]
+        )
+        grad = skip * dy + spread(steps, marks) * inner[b] + spread_end * grown
+        dot_out = gather_heads(dy * (mixed[b] - skip * x), collect)
+        dot_inner = gather_heads(x * inner[b], collect)
+        dot_end = gather_heads(x * grown, collect)
+        dot_skip = gather_heads(dy * x, collect)
+        through = jnp.sum(
+            end_grad.astype(f32) * state_ref[b].astype(f32), axis=0, keepdims=True
+        )
+        passed_grad = gather_heads(jnp.broadcast_to(through, (8, channels)), collect)[:1]
+        end_mix = dot_end * end_weight
+        last_term = passed_grad * entering[length - 1 :] + jnp.sum(end_mix, axis=0, keepdims=True)
+        cum_grad = dot_out - steps * dot_inner - end_mix + jnp.where(last_row, last_term, 0.0)
+        rates_grad = jnp.dot(upper, cum_grad, precision=highest, preferred_element_type=f32)
+        steps_grad = dot_inner + end_decay * dot_end + rates_grad * decay_rate
+        linear_grad = steps_grad * jax.nn.sigmoid(linear_steps_ref[b] + step_bias)
+        narrow[b, :, 2 * STATE :] = linear_grad.astype(bf16)
+        vector_grad_out[0:1] += jnp.sum(linear_grad, axis=0, keepdims=True)
+        vector_grad_out[1:2] += jnp.sum(rates_grad * steps, axis=0, keepdims=True) * decay_rate
+        vector_grad_out[2:3] += jnp.sum(dot_skip, axis=0, keepdims=True)
+
+        row_load(3, b).wait()
+        extended[0:16] = halo_ref[pl.ds(pl.multiple_of(b * 16, 16), 16)].astype(f32)
+        extended[16:] = linear[b].astype(f32)
+        middle = slice(16, 16 + length)
+        for lag in range(1, lags):
+            usable_rows[lag - 1, middle] = (spot - lag >= column).astype(f32)
+        for at in range(0, both, LANES):
+            lanes = slice(at, at + LANES)
+            values = conv[b, :, lanes]
+            sigmoid_value = jax.nn.sigmoid(values)
+            slope = sigmoid_value * (1.0 + values * (1.0 - sigmoid_value))
+            if at < channels:
+                out_grad = grad[:, lanes]
+                taps, tap = value_conv_ref, lanes
+            else:
+                place_at = at - channels
+                out_grad = narrow_grad[b, :, place_at : place_at + LANES]
+                taps, tap = keyquery_conv_ref, slice(place_at, place_at + LANES)
+            local = out_grad * slope
+            spread_grad[middle, lanes] = local
+            input_grad = taps[0:1, tap] * local
+            edges = jnp.zeros((8, LANES), f32)
+            conv_grad_out[0:1, lanes] += jnp.sum(local * extended[middle, lanes], axis=0, keepdims=True)
+            conv_grad_out[lags : lags + 1, lanes] += jnp.sum(local, axis=0, keepdims=True)
+            for lag in range(1, lags):
+                mask = usable_rows[lag - 1, middle]
+                conv_grad_out[lag : lag + 1, lanes] += jnp.sum(
+                    local * mask * extended[16 - lag : 16 - lag + length, lanes],
+                    axis=0,
+                    keepdims=True,
+                )
+                later = slice(16 + lag, 16 + lag + length)
+                input_grad = input_grad + taps[lag : lag + 1, tap] * (
+                    spread_grad[later, lanes] * usable_rows[lag - 1, later]
+                )
+                first = slice(8 + lag, 16 + lag)
+                edges = edges + taps[lag : lag + 1, tap] * (
+                    spread_grad[first, lanes] * usable_rows[lag - 1, first]
+                )
+            edge[b, :, lanes] = edges
+            tails[b, :, lanes] = input_grad[length - 16 :]
+            if at < channels:
+                values_grad[b, :, lanes] = input_grad.astype(bf16)
+            else:
+                narrow[b, :, tap] = input_grad.astype(bf16)
+
+        @pl.when(place > 0)
+        def _():
+            edge_copy(b).start()
+
+    loop(count, close)
+
+    def finish(b):
+        @pl.when(place < n - 1)
+        def _():
+            edge_copy(b).wait_recv()
+            last = slice(length - 16, length)
+            tails[b, 8:] = tails[b, 8:] + edge_in[b]
+            values_grad[b, last] = tails[b, :, :channels].astype(bf16)
+            narrow[b, last, : 2 * STATE] = tails[b, :, channels:].astype(bf16)
+
+        store(2, b).start()
+        store(3, b).start()
+
+    loop(count, finish)
+
+    @pl.when(place > 0)
+    def _():
+        loop(count, lambda b: edge_copy(b).wait_send())
+        loop(chunks, lambda c: chain_copy(c).wait_send())
+
+    for i in range(len(stores)):
+        loop(count, lambda b, i=i: store(i, b).wait())
+
+
+def back(
+    pieces,
+    weight,
+    gate,
+    mixed,
+    conv,
+    linear,
+    halo,
+    state_in,
+    steps,
+    cumulative,
+    linear_steps,
+    square_rows,
+    rowdot,
+    docs,
+    vectors,
+    value_conv_weight,
+    keyquery_conv_weight,
+    norm_gain,
+    cid,
+):
+    count, length, channels = gate.shape
+    both = channels + 2 * STATE
+    lags = value_conv_weight.shape[0]
+    weight = blocked(weight, pieces.shape[0])
+    chunks = count * 4
+    dma = pltpu.SemaphoreType.DMA
+    hbm = pl.BlockSpec(memory_space=pl.ANY)
+    shape = jax.ShapeDtypeStruct
+    vmem = pltpu.VMEM
+    big = [
+        ((count, length, channels), bf16),
+        ((count, length, channels), bf16),
+        ((count, length, channels), bf16),
+        ((count, length, 2 * STATE + LANES), bf16),
+    ]
+    small = [((8, both), f32), ((8, LANES), f32), ((1, channels), f32)]
+    return pl.pallas_call(
+        back_kernel,
+        out_shape=[shape(*s) for s in big + small],
+        in_specs=[hbm] * 6 + [in_vmem] * 12,
+        out_specs=[hbm] * len(big) + [in_vmem] * len(small),
+        scratch_shapes=[
+            vmem(pieces.shape, bf16),
+            vmem(weight.shape, bf16),
+            vmem(gate.shape, f32),
+            vmem(mixed.shape, f32),
+            vmem(conv.shape, f32),
+            vmem(linear.shape, bf16),
+        ]
+        + [vmem(*s) for s in big]
+        + [
+            vmem((count, length, channels), f32),
+            vmem((count, length, channels), f32),
+            vmem((count, length, STATE), bf16),
+            vmem((count, length, STATE), bf16),
+            vmem((length, length), f32),
+            vmem((length, length), f32),
+            vmem((length, length), f32),
+            vmem((count, length, channels), f32),
+            vmem((count, length, 2 * STATE), f32),
+            vmem((count, STATE, channels), f32),
+            vmem((count, STATE, channels), bf16),
+            vmem((count, STATE, channels), bf16),
+            vmem((count, 8, channels), f32),
+            vmem((length + 16, both), f32),
+            vmem((length + 32, both), f32),
+            vmem((lags - 1, length + 32, LANES), f32),
+            vmem((count, 8, both), f32),
+            vmem((count, 8, both), f32),
+            vmem((count, 16, both), f32),
+            dma((2,)),
+            dma((4, count)),
+            dma((len(big), count)),
+            dma((count,)),
+            dma((count,)),
+            dma((chunks,)),
+            dma((chunks,)),
+        ],
+        compiler_params=params(cid),
+        name="back",
+    )(
+        pieces,
+        weight,
+        gate,
+        mixed,
+        conv,
+        linear,
+        halo,
+        state_in,
+        steps,
+        cumulative,
+        linear_steps,
+        square_rows,
+        rowdot,
+        docs,
+        vectors,
+        value_conv_weight,
+        keyquery_conv_weight,
+        norm_gain,
+    )
 
 
 def body(
@@ -730,187 +1560,90 @@
     rows = sequence_count * shard_length
     local_heads = skip_gain.shape[0]
     local_inner = local_heads * HEADDIM
-    inner_total = NHEADS * HEADDIM
     column_count = D // lax.axis_size("head")
     column_start = head_index * column_count
     shard_begin = sequence_index * shard_length
-    positions = shard_begin + jnp.arange(shard_length, dtype=jnp.int32)
     valid_count = jnp.sum(valid_mask.astype(f32))
     local_mask = lax.dynamic_slice_in_dim(valid_mask, shard_begin, shard_length, 1).astype(f32)
     mask_rows = (local_mask * (2.0 / (D * valid_count))).reshape(-1, LANES)
-    inverse_root = lax.rsqrt(jnp.mean(tokens * tokens, axis=-1, keepdims=True) + norm_eps)
-    normed = (tokens * inverse_root * input_gain).astype(bf16)
-    values_linear = jnp.dot(normed, value_weight, preferred_element_type=f32).astype(bf16)
-    keyquery_linear = jnp.dot(normed, keyquery_weight, preferred_element_type=f32).astype(bf16)
-    conv_input = jnp.concatenate([values_linear, keyquery_linear], axis=-1)
+    step_pad = ((0, 0), (0, LANES - local_heads))
+    vectors = jnp.pad(
+        jnp.stack([step_bias, rate_log, skip_gain]), ((0, 5), (0, LANES - local_heads))
+    )
+    (
+        normed,
+        linear,
+        conv_linear,
+        gate_linear,
+        mixed,
+        gained,
+        halo,
+        state_in,
+        steps,
+        cumulative,
+        steps_linear,
+        square_rows,
+        inverse_rows,
+    ) = front(
+        tokens,
+        input_gain[None],
+        value_weight,
+        keyquery_weight,
+        jnp.pad(step_weight, step_pad),
+        gate_weight,
+        document_start,
+        vectors,
+        (
+            value_conv_weight,
+            value_conv_bias[None],
+            keyquery_conv_weight,
+            keyquery_conv_bias[None],
+        ),
+        norm_gain[None],
+        1,
+    )
     conv_lags = value_conv_weight.shape[0]
-    previous = passed_along(conv_input[:, shard_length - (conv_lags - 1) :], "seq", 1)
-    gate_linear = jnp.dot(normed, gate_weight, preferred_element_type=f32)
-    steps_linear = jnp.dot(normed, step_weight, preferred_element_type=f32)
-    extended = jnp.concatenate([previous, conv_input], axis=1).astype(f32)
-    conv_weight = jnp.concatenate([value_conv_weight, keyquery_conv_weight], axis=1)
-    conv_offset = jnp.concatenate([value_conv_bias, keyquery_conv_bias], axis=0)
-    usable = []
-    windows = []
-    conv_linear = conv_offset + jnp.zeros_like(extended[:, :shard_length])
-    for lag_index in range(conv_lags):
-        usable.append((positions[None, :] - lag_index >= document_start).astype(f32)[:, :, None])
-        windows.append(
-            extended[:, conv_lags - 1 - lag_index : conv_lags - 1 - lag_index + shard_length]
-        )
-        conv_linear = conv_linear + conv_weight[lag_index] * windows[lag_index] * usable[lag_index]
-    conv_out = jax.nn.silu(conv_linear)
-    keys_input = conv_out[..., local_inner : local_inner + STATE]
-    queries = conv_out[..., local_inner + STATE :]
-    heads_input = conv_out[..., :local_inner].reshape(
-        sequence_count, shard_length, local_heads, HEADDIM
-    )
-    steps = jax.nn.softplus(steps_linear + step_bias)
-    decay_rate = -jnp.exp(rate_log)
-    rates = steps * decay_rate
-    cumulative = jnp.transpose(jnp.cumsum(rates, axis=1), (0, 2, 1))
-    steps_heads = jnp.transpose(steps, (0, 2, 1))
-    linked = (positions[None, None, :] >= document_start[:, :, None]) & (
-        positions[None, None, :] <= positions[None, :, None]
-    )
-    linked_heads = linked[:, None]
-    decay_mat = jnp.where(
-        linked_heads,
-        jnp.exp(
-            jnp.where(linked_heads, cumulative[:, :, :, None] - cumulative[:, :, None, :], 0.0)
-        ),
-        0.0,
-    )
-    scores = jnp.einsum("btn,bun->btu", queries, keys_input, precision=highest)
-    mixing = decay_mat * scores[:, None] * steps_heads[:, :, None, :]
-    local_out = jnp.einsum("bhtu,buhp->bthp", mixing, heads_input, precision=highest)
-    kept_mask = (document_start < shard_begin).astype(f32)
-    entering = jnp.exp(cumulative) * kept_mask[:, None, :]
-    trailing = (positions[None, :] >= document_start[:, -1:]).astype(f32)
-    end_decay = jnp.exp(cumulative[:, :, -1:] - cumulative) * trailing[:, None, :]
-    weights_end = end_decay * steps_heads
-    state_local = jnp.einsum(
-        "bhu,buhp,bun->bhpn", weights_end, heads_input, keys_input, precision=highest
-    )
-    passed = jnp.exp(cumulative[:, :, -1]) * kept_mask[:, -1:]
-    folded = (sequence_count, local_inner, STATE)
-    unfolded = (sequence_count, local_heads, HEADDIM, STATE)
-    state_in = chain(passed, state_local.reshape(folded), False, 1).reshape(unfolded).astype(f32)
-    projected = jnp.einsum("btn,bhpn->bthp", queries, state_in, precision=highest)
-    entering_rows = jnp.transpose(entering, (0, 2, 1))
-    mixed_heads = (
-        local_out + entering_rows[..., None] * projected + skip_gain[:, None] * heads_input
-    )
-    mixed_flat = mixed_heads.reshape(rows, local_inner)
-    gate_flat = gate_linear.reshape(rows, local_inner)
-    gate_act = jax.nn.silu(gate_flat)
-    gated_out = mixed_flat * gate_act
-    square_rows = jnp.sum(gated_out * gated_out, axis=-1).reshape(-1, LANES)
-    gained = (gated_out * norm_gain).astype(bf16)
+    square_rows = square_rows.reshape(-1, LANES)
+    gained = gained.reshape(rows, local_inner)
     token_cols = lax.dynamic_slice_in_dim(tokens, column_start, column_count, 2).reshape(rows, -1)
     teacher_rows = teacher.reshape(rows, column_count)
     output, piece_blocks, rowdot, square_total, loss_cols = out_phase(
         gained, out_weight, square_rows, token_cols, teacher_rows, mask_rows, 2
     )
+    (
+        normed_out,
+        gate_grad,
+        values_grad,
+        narrow_grad,
+        conv_grad,
+        vector_grad,
+        gain_out_grad,
+    ) = back(
+        piece_blocks,
+        out_weight,
+        gate_linear,
+        mixed,
+        conv_linear,
+        linear,
+        halo,
+        state_in,
+        steps,
+        cumulative,
+        steps_linear,
+        square_total,
+        rowdot,
+        document_start,
+        vectors,
+        value_conv_weight,
+        keyquery_conv_weight,
+        norm_gain[None],
+        3,
+    )
+    gate_grad = gate_grad.reshape(rows, local_inner)
+    values_grad = values_grad.reshape(rows, local_inner)
+    narrow_grad = narrow_grad.reshape(rows, -1)
     piece_cols = jnp.moveaxis(piece_blocks, 0, 1).reshape(rows, D)
-    row_scale = lax.rsqrt(square_total / inner_total + norm_eps).reshape(rows, 1)
-    row_dot = rowdot.reshape(rows, 1)
-    normed_out = (gated_out * row_scale * norm_gain).astype(bf16)
-    column_grad = dot_tn(piece_cols, normed_out).astype(bf16)
-    grad_rows = dot_nt(piece_cols, out_weight)
-    gain_out_grad = jnp.sum(grad_rows * gated_out * row_scale, axis=0)
-    gated_grad = row_scale * norm_gain * grad_rows - gated_out * (
-        row_scale**2 * row_dot / inner_total
-    )
-    mixed_grad = gated_grad * gate_act
-    gate_grad = (gated_grad * mixed_flat * silu_slope(gate_flat)).astype(bf16)
-    heads_grad = mixed_grad.reshape(sequence_count, shard_length, local_heads, HEADDIM)
-    skip_gain_grad = jnp.einsum("bthp,bthp->h", heads_grad, heads_input, precision=highest)
-    state_local_grad = jnp.einsum(
-        "bht,bthp,btn->bhpn", entering, heads_grad, queries, precision=highest
-    )
-    end_grad = (
-        chain(passed, state_local_grad.reshape(folded), True, 3).reshape(unfolded).astype(f32)
-    )
-    pairwise = jnp.einsum("bthp,buhp->bhtu", heads_grad, heads_input, precision=highest)
-    heads_input_grad = skip_gain[:, None] * heads_grad
-    heads_input_grad = heads_input_grad + jnp.einsum(
-        "bhtu,bthp->buhp", mixing, heads_grad, precision=highest
-    )
-    heads_input_grad = heads_input_grad + jnp.einsum(
-        "bhu,bhpn,bun->buhp", weights_end, end_grad, keys_input, precision=highest
-    )
-    weighted = pairwise * decay_mat
-    scores_grad = jnp.einsum("bhtu,bhu->btu", weighted, steps_heads, precision=highest)
-    steps_grad = jnp.einsum("bhtu,btu->bhu", weighted, scores, precision=highest)
-    cum_terms = weighted * scores[:, None] * steps_heads[:, :, None, :]
-    cum_grad = jnp.sum(cum_terms, axis=-1) - jnp.sum(cum_terms, axis=-2)
-    queries_grad = jnp.einsum("btu,bun->btn", scores_grad, keys_input, precision=highest)
-    queries_grad = queries_grad + jnp.einsum(
-        "bht,bthp,bhpn->btn", entering, heads_grad, state_in, precision=highest
-    )
-    keys_grad = jnp.einsum("btu,btn->bun", scores_grad, queries, precision=highest)
-    keys_grad = keys_grad + jnp.einsum(
-        "bhu,bhpn,buhp->bun", weights_end, end_grad, heads_input, precision=highest
-    )
-    entering_grad = jnp.einsum("bthp,bthp->bht", heads_grad, projected, precision=highest)
-    cum_grad = cum_grad + entering_grad * entering
-    passed_grad = jnp.einsum("bhpn,bhpn->bh", end_grad, state_in, precision=highest)
-    end_term = jnp.einsum(
-        "bhpn,buhp,bun->bhu", end_grad, heads_input, keys_input, precision=highest
-    )
-    steps_grad = steps_grad + end_term * end_decay
-    end_mix = end_term * weights_end
-    cum_grad = cum_grad - end_mix
-    last_term = passed_grad * passed + jnp.sum(end_mix, axis=-1)
-    last_slot = (jnp.arange(shard_length, dtype=jnp.int32) == shard_length - 1).astype(f32)
-    cum_grad = cum_grad + last_term[:, :, None] * last_slot
-    rates_grad = jnp.flip(jnp.cumsum(jnp.flip(cum_grad, axis=-1), axis=-1), axis=-1)
-    steps_grad = steps_grad + rates_grad * decay_rate[None, :, None]
-    rate_log_grad = jnp.sum(rates_grad * steps_heads, axis=(0, 2)) * decay_rate
-    steps_linear_grad = jnp.transpose(steps_grad, (0, 2, 1)) * jax.nn.sigmoid(
-        steps_linear + step_bias
-    )
-    step_bias_grad = jnp.sum(steps_linear_grad, axis=(0, 1))
-    conv_out_grad = jnp.concatenate(
-        [
-            heads_input_grad.reshape(sequence_count, shard_length, local_inner),
-            keys_grad,
-            queries_grad,
-        ],
-        axis=-1,
-    )
-    conv_linear_grad = conv_out_grad * silu_slope(conv_linear)
-    conv_offset_grad = jnp.sum(conv_linear_grad, axis=(0, 1))
-    conv_channels = conv_linear_grad.shape[2]
-    weight_rows = []
-    conv_input_grad = conv_weight[0] * conv_linear_grad * usable[0]
-    edge_grad = jnp.zeros((sequence_count, conv_lags - 1, conv_channels), f32)
-    for lag_index in range(conv_lags):
-        masked = conv_linear_grad * usable[lag_index]
-        weight_rows.append(jnp.sum(masked * windows[lag_index], axis=(0, 1)))
-        if lag_index > 0:
-            tail_zeros = jnp.zeros((sequence_count, lag_index, conv_channels), f32)
-            conv_input_grad = conv_input_grad + conv_weight[lag_index] * jnp.concatenate(
-                [masked[:, lag_index:], tail_zeros], axis=1
-            )
-            head_zeros = jnp.zeros((sequence_count, conv_lags - 1 - lag_index, conv_channels), f32)
-            edge_grad = edge_grad + jnp.concatenate(
-                [head_zeros, conv_weight[lag_index] * masked[:, :lag_index]], axis=1
-            )
-    conv_weight_grad = jnp.stack(weight_rows, axis=0)
-    incoming = passed_along(edge_grad, "seq", -1)
-    lead_zeros = jnp.zeros((sequence_count, shard_length - (conv_lags - 1), conv_channels), f32)
-    conv_input_grad = conv_input_grad + jnp.concatenate([lead_zeros, incoming], axis=1)
-    step_pad = ((0, 0), (0, LANES - local_heads))
-    values_grad = conv_input_grad[..., :local_inner].astype(bf16).reshape(rows, local_inner)
-    narrow_grad = jnp.concatenate(
-        [
-            conv_input_grad[..., local_inner:].reshape(rows, 2 * STATE),
-            jnp.pad(steps_linear_grad.reshape(rows, local_heads), step_pad),
-        ],
-        axis=-1,
-    ).astype(bf16)
+    column_grad = dot_tn(piece_cols, normed_out.reshape(rows, local_inner)).astype(bf16)
     narrow_weight = jnp.concatenate([keyquery_weight, jnp.pad(step_weight, step_pad)], axis=-1)
     normed = normed.reshape(rows, D)
     gain_cols = lax.dynamic_slice_in_dim(input_gain, column_start, column_count, 0)
@@ -923,7 +1656,7 @@
         teacher_rows,
         gain_cols[None],
         mask_rows,
-        inverse_root.reshape(-1, LANES),
+        inverse_rows.reshape(-1, LANES),
         4,
     )
     gate_part = dot_tn(normed, gate_grad).astype(bf16)
@@ -934,8 +1667,8 @@
     )
     group_parts = [
         narrow_total[:, : 2 * STATE],
-        conv_weight_grad[:, local_inner:],
-        conv_offset_grad[local_inner:],
+        conv_grad[:conv_lags, local_inner:],
+        conv_grad[conv_lags, local_inner:],
         gain_columns,
         jnp.sum(loss_cols)[None],
     ]
@@ -947,14 +1680,14 @@
         loss_part,
     ) = unpacked(small_sum(packed(group_parts), "head", 6), group_parts)
     line_parts = [
-        conv_weight_grad[:, :local_inner],
-        conv_offset_grad[:local_inner],
+        conv_grad[:conv_lags, :local_inner],
+        conv_grad[conv_lags, :local_inner],
         keyquery_conv_part,
         keyquery_offset_part,
-        step_bias_grad,
-        rate_log_grad,
-        skip_gain_grad,
-        gain_out_grad,
+        vector_grad[0, :local_heads],
+        vector_grad[1, :local_heads],
+        vector_grad[2, :local_heads],
+        gain_out_grad[0],
         lax.dynamic_slice_in_dim(gain_columns.reshape(-1), column_start, column_count, 0),
         loss_part,
     ]

time: 600 us -> 431 us (0.72)
  matrix products: 120 us -> 18.9 us
  other arithmetic: 66.2 us -> 5.74 us
  Pallas kernels: 309 us -> 361 us
  local copies, waits for them, and re-layouts: 86.8 us -> 40 us
  starting transfers between devices: 7.08 us -> 0 us
    dot_general x17 -> x0, matrix products: 105 us -> none  [the longest x1 19.2 us: body(): jnp.einsum('bthp,buhp->bhtu', heads_grad, heads_input, precision=highest)]
    pallas_call x2, Pallas kernels: 83.7 us -> 142 us  [the longest x1 103 us: back(): pl.pallas_call(back_kernel, out_shape=[shape(*s) for s in big + small], i...]
    dot_general x5 -> x0, other arithmetic: 17 us -> none  [the longest x1 7.23 us: body(): jnp.einsum('bhtu,bhu->btu', weighted, steps_heads, precision=highest)]
    slice x14 -> x3, local copies, waits for them, and re-layouts: 15.3 us -> 0.02 us  [the longest x1 0.02 us: body(): conv_grad[conv_lags, :local_inner]]
    another operation x8 -> x1, other arithmetic: 11.7 us -> 1.29 us  [body(): jnp.stack([step_bias, rate_log, skip_gain])]
    pallas_call x1, Pallas kernels: 53.6 us -> 43.7 us  [in_phase(): pl.pallas_call(functools.partial(in_kernel, n, len(grads)), out_shape=[ja...]
    reduce_sum x5 -> x0, other arithmetic: 9.73 us -> none  [the longest x1 5.78 us: body(): weight_rows.append(jnp.sum(masked * windows[lag_index], axis=(0, 1)))]
    convert_element_type x6 -> x0, other arithmetic: 9.46 us -> none  [the longest x1 3.98 us: body(): gained = (gated_out * norm_gain).astype(bf16)]
  transfers between devices with their start and end apart: 2 -> 0, of which waited for: 0 -> 0; matrix products, arithmetic and copies ran while one was open for 7% -> 0% of each run, Pallas kernels for 0% -> 0%
where the time goes in v2:
time: 431 us; the launch traced here: 429 us
  Pallas kernels  361 us (84%)
  local copies, waits for them, and re-layouts  40 us (9%)
  matrix products  18.9 us (4%)
  other arithmetic  5.74 us (1%)
    pallas_call x1, Pallas kernels, ring_sums(): pl.pallas_call(functools.partial(ring_kernel, n, count, cuts), out_shape=...  105 us
    pallas_call x1, Pallas kernels, back(): pl.pallas_call(back_kernel, out_shape=[shape(*s) for s in big + small], i...  103 us
    pallas_call x1, Pallas kernels, out_phase(): pl.pallas_call(functools.partial(out_kernel, n), out_shape=[jax.ShapeDtyp...  49.4 us
    pallas_call x1, Pallas kernels, in_phase(): pl.pallas_call(functools.partial(in_kernel, n, len(grads)), out_shape=[ja...  43.7 us
    pallas_call x1, Pallas kernels, front(): pl.pallas_call(functools.partial(front_kernel, heads), out_shape=[shape(*...  39.3 us
    pallas_call x2, Pallas kernels, small_sum(): pl.pallas_call(functools.partial(small_kernel, axis, n), out_shape=jax.Sh...  21.4 us
    dot_general x4, matrix products, dot_tn(): lax.dot_general(a, b, TN, precision=precision, preferred_element_type=f32)  18.9 us
    slice x12, local copies, waits for them, and re-layouts, unpacked(): found.append(flat[at:at + a.size].reshape(a.shape))  12.2 us

profile of v2, /device:TPU:0, one launch (start us, length us, event | category | flops | bytes accessed | tf_op | source)
XLA Modules:
  0.0 429.5 jit_solution(1692437168332412938)
XLA Ops:
  0.7 1.0 copy.40
  2.5 1.3 select_maximum_fusion.vectors_ref
  3.8 1.3 broadcast_in_dim.22.norm_gain_ref
  5.1 1.3 broadcast_in_dim.19.gain_ref
  6.4 1.3 broadcast_in_dim.20.value_offset_ref
  7.7 39.3 %front.1 = (bf16[4,256,1536]{2,1,0:T(8,128)(2,1)}, bf16[4,256,1024]{2,1,0:T(8,128)(2,1)}, f32[4,256,1024]{2,1,0:T(8,128)}, f32[4,256,768]{2,1,0:T(8,128)}, f32[4...) custom-call(f32[4,256,1536]{2,1,0:T(8,128)} %tokens_hbm.1, ...), custom_call_target="tpu_custom_call" | custom-call | tf_op jit(solution)/shard_map/front/pallas_call | solution.py:1013
  47.0 1.3 reshape.123.square_ref
  48.2 2.7 constant_dynamic-slice_fusion
  52.8 49.4 %out_phase.1 = (f32[1024,384]{1,0:T(8,128)}, bf16[4,1024,384]{2,1,0:T(8,128)(2,1)}, f32[8,128]{1,0:T(8,128)}, f32[8,128]{1,0:T(8,128)}, f32[1,384]{1,0:T(1,128)}) custom-call(bf16[1024,768]{1,0:T(8,128)(2,1)} %bitcast.73, bf16[768,1536]{1,0:T(8,128)(2,1)} %weight_hbm.1, f32[8,128]{1,0:T(8,128)} %reshape.123.square_ref, f32[1024,384]{1,0:T(8,128)} %bitcast.62, ...), custom_call_target="tpu_custom_call" | custom-call | tf_op jit(solution)/shard_map/out_phase/pallas_call | solution.py:422
  102.2 103.2 %back.1 = (bf16[4,256,768]{2,1,0:T(8,128)(2,1)}, bf16[4,256,768]{2,1,0:T(8,128)(2,1)}, bf16[4,256,768]{2,1,0:T(8,128)(2,1)}, bf16[4,256,384]{2,1,0:T(8,128)(2,1)...) custom-call(bf16[4,1024,384]{2,1,0:T(8,128)(2,1)} %get-tuple-element.51.pieces_hbm, ...), custom_call_target="tpu_custom_call" | custom-call | tf_op jit(solution)/shard_map/back/pallas_call | solution.py:1470
  206.7 1.1 pad_maximum_fusion.refs_5_
  207.8 43.7 %in_phase.1 = (f32[1024,384]{1,0:T(8,128)}, f32[1,1536]{1,0:T(1,128)}) custom-call(bf16[1024,768]{1,0:T(8,128)(2,1)} %bitcast.70, bf16[1024,768]{1,0:T(8,128)(2,1)} %bitcast.71, bf16[1024,384]{1,0:T(8,128)(2,1)} %bitcast.75, bf16[1536,768]{1,0:T(8,128)(2,1)} %refs_3_.1, bf16[1536,768]{1,0:T(8,128)(2,1)} %refs_4_.1, ...), custom_call_target="tpu_custom_call" | custom-call | tf_op jit(solution)/shard_map/in_phase/pallas_call | solution.py:541
  252.2 4.5 %convolution_bitcast_fusion.refs_3_ = f32[1536,384]{1,0:T(8,128)} fusion(bf16[4,256,1536]{2,1,0:T(8,128)(2,1)S(1)} %copy-done.3, bf16[4,256,384]{2,1,0:T(8,128)(2,1)} %get-tuple-element.68), kind=kOutput, calls=%fused_computation.3 | convolution fusion | flops 1207959552 | bytes 6291456 | tf_op jit(solution)/shard_map/dot_general | solution.py:55
  256.8 4.0 bitcast_convert_fusion.refs_2_
  260.7 4.0 bitcast_convert_fusion.1.refs_1_
  264.7 2.9 copy.41
  267.6 6.4 %convolution_convert_fusion.refs_0_ = bf16[1536,768]{1,0:T(8,128)(2,1)} fusion(bf16[1024,1536]{0,1:T(8,128)(2,1)} %bitcast.69, bf16[1024,768]{1,0:T(8,128)(2,1)} %bitcast.88), kind=kOutput, calls=%fused_computation.2 | convolution fusion | flops 2417098752 | bytes 7077888 | tf_op jit(solution)/shard_map/dot_general | solution.py:55
  274.0 104.5 %ring_sums.1 = (f32[192,768]{1,0:T(8,128)}, f32[192,768]{1,0:T(8,128)}, f32[192,768]{1,0:T(8,128)}, f32[192,384]{1,0:T(8,128)}) custom-call(bf16[1536,768]{1,0:T(8,128)(2,1)} %convolution_convert_fusion.refs_0_, bf16[1536,768]{1,0:T(8,128)(2,1)} %bitcast_convert_fusion.1.refs_1_, bf16[1536,768]{1,0:T(8,128)(2,1)} %bitcast_convert_fusion.refs_2_, ...), custom_call_target="tpu_custom_call" | custom-call | tf_op jit(solution)/shard_map/ring_sums/pallas_call | solution.py:139
  378.6 1.1 slice_bitcast_fusion
  381.8 12.9 %small_sum_head.1 = f32[408,128]{1,0:T(8,128)} custom-call(f32[408,128]{1,0:T(8,128)} %pad_bitcast_fusion.source_ref), custom_call_target="tpu_custom_call" | custom-call | tf_op jit(solution)/shard_map/small_sum_head/pallas_call | solution.py:591
  394.7 1.1 slice.107
  398.7 1.2 slice.119
  402.0 8.5 %small_sum_seq.1 = f32[56,128]{1,0:T(8,128)} custom-call(f32[56,128]{1,0:T(8,128)} %pad_bitcast_fusion.1.source_ref), custom_call_target="tpu_custom_call" | custom-call | tf_op jit(solution)/shard_map/small_sum_seq/pallas_call | solution.py:591
  411.9 1.4 slice_divide_fusion
  414.6 1.3 slice.125
  415.9 1.3 slice_bitcast_fusion.2
  417.2 1.4 fusion
  418.6 1.3 slice.120
  420.5 1.2 slice_bitcast_fusion.5
  421.7 0.9 slice.108
  423.3 1.1 copy.60
  424.5 1.1 copy.61
  (75 shorter events, 17.3 us)
Async XLA Ops:
  46.9 3.9 copy-start.12
  102.2 103.2 %copy-start.15 = (f32[4,256]{1,0:T(4,128)S(1)}, f32[4,256]{1,0:T(4,128)}, u32[]{:S(2)}) copy-start(f32[4,256]{1,0:T(4,128)} %get-tuple-element.70) | copy-start | bytes 12292
  102.2 103.8 %copy-start.13 = (f32[1536]{0:T(1024)S(1)}, f32[1536]{0:T(1024)}, u32[]{:S(2)}) copy-start(f32[1536]{0:T(1024)} %param.22) | copy-start | bytes 18436
  102.2 104.5 %copy-start.2 = (bf16[1536,128]{1,0:T(8,128)(2,1)S(1)}, bf16[1536,128]{1,0:T(8,128)(2,1)}, u32[]{:S(2)}) copy-start(bf16[1536,128]{1,0:T(8,128)(2,1)} %pad.17.step_ref) | copy-start | bytes 1179652
  102.2 104.5 %copy-start.5 = (bf16[1536,256]{1,0:T(8,128)(2,1)S(1)}, bf16[1536,256]{1,0:T(8,128)(2,1)}, u32[]{:S(2)}) copy-start(bf16[1536,256]{1,0:T(8,128)(2,1)} %keyquery_hbm.1) | copy-start | bytes 2359300
  207.8 44.4 %copy-start.3 = (bf16[4,256,1536]{2,1,0:T(8,128)(2,1)S(1)}, bf16[4,256,1536]{2,1,0:T(8,128)(2,1)}, u32[]{:S(2)}) copy-start(bf16[4,256,1536]{2,1,0:T(8,128)(2,1)} %get-tuple-element.65) | copy-start | bytes 9437188
  252.2 4.5 %copy-start.7 = (bf16[4,256,768]{2,1,0:T(8,128)(2,1)S(1)}, bf16[4,256,768]{2,1,0:T(8,128)(2,1)}, u32[]{:S(2)}) copy-start(bf16[4,256,768]{2,1,0:T(8,128)(2,1)} %get-tuple-element.67) | copy-start | bytes 4718596
  256.8 4.0 copy-start.4
  256.8 4.0 copy-start.6
  260.7 4.0 copy-start
  274.0 105.8 %copy-start.14 = (f32[8,1024]{1,0:T(8,128)S(1)}, f32[8,1024]{1,0:T(8,128)}, u32[]{:S(2)}) copy-start(f32[8,1024]{1,0:T(8,128)} %get-tuple-element.63) | copy-start | bytes 98308
  274.0 105.8 %copy-start.17 = (f32[1,384]{1,0:T(1,128)S(1)}, f32[1,384]{1,0:T(1,128)}, u32[]{:S(2)}) copy-start(f32[1,384]{1,0:T(1,128)} %get-tuple-element.72) | copy-start | bytes 4612
  378.6 21.3 %copy-start.16 = (f32[1,768]{1,0:T(1,128)S(1)}, f32[1,768]{1,0:T(1,128)}, u32[]{:S(2)}) copy-start(f32[1,768]{1,0:T(1,128)} %get-tuple-element.74) | copy-start | bytes 9220
  378.6 44.7 %copy-start.1 = (f32[1024,384]{1,0:T(8,128)S(1)}, f32[1024,384]{1,0:T(8,128)}, u32[]{:S(2)}) copy-start(f32[1024,384]{1,0:T(8,128)} %get-tuple-element.50.refs_8_) | copy-start | bytes 4718596
  394.7 29.8 %copy-start.8 = (f32[1024,384]{1,0:T(8,128)S(1)}, f32[1024,384]{1,0:T(8,128)}, u32[]{:S(2)}) copy-start(f32[1024,384]{1,0:T(8,128)} %get-tuple-element.75) | copy-start | bytes 4718596
  424.5 1.4 copy-start.11
  424.5 2.3 copy-start.10
  424.5 3.1 copy-start.9

commit v3 on v2

--- a/solution.py
+++ b/solution.py
@@ -65,92 +65,6 @@
     return 2 * spot * (1 - late) + (2 * (n - 1 - spot) + 1) * late
 
 
-def ring_kernel(n, count, cuts, *refs):
-    parts, outs = refs[:count], refs[count : 2 * count]
-    held, sems = refs[2 * count : 4 * count], refs[4 * count :]
-    place = lax.axis_index("seq")
-    head = lax.axis_index("head")
-    spot = ring_place(n, place)
-    after = (ring_index(n, lax.rem(spot + 1, n)), head)
-    before = (ring_index(n, lax.rem(spot + n - 1, n)), head)
-    barrier = pltpu.get_barrier_semaphore()
-    for target in (after, before):
-        pl.semaphore_signal(barrier, inc=1, device_id=target, device_id_type=MESH)
-    pl.semaphore_wait(barrier, 2)
-
-    streams = []
-    for i in range(count):
-        width = parts[i].shape[1]
-        for way in range(2):
-            columns = pl.ds(0, cuts[i]) if way == 0 else pl.ds(cuts[i], width - cuts[i])
-            streams.append((parts[i], outs[i], held[2 * i + way], columns, way))
-    send_sem, recv_sem = sems
-
-    def piece(i, step):
-        part, _, _, columns, way = streams[i]
-        shift = -1 - step if way == 0 else 1 + step
-        rows = part.shape[0] // n
-        index = ring_index(n, lax.rem(spot + shift + 2 * n, n))
-        return part.at[pl.ds(pl.multiple_of(index * rows, rows), rows), columns]
-
-    def copy(i, step, src):
-        slots, way = streams[i][2], streams[i][4]
-        return remote(
-            src,
-            slots.at[step],
-            send_sem.at[i, step],
-            recv_sem.at[i, step],
-            after if way == 0 else before,
-        )
-
-    for i in range(len(streams)):
-        copy(i, 0, piece(i, 0)).start()
-
-    def one(step):
-        for i in range(len(streams)):
-            slots = streams[i][2]
-            copy(i, step, slots.at[step]).wait_recv()
-            slots[step] = (slots[step].astype(f32) + piece(i, step + 1)[...].astype(f32)).astype(
-                slots.dtype
-            )
-            copy(i, step + 1, slots.at[step]).start()
-
-    loop(n - 2, one)
-    for i in range(len(streams)):
-        _, out, slots, columns, _ = streams[i]
-        copy(i, n - 2, slots.at[n - 2]).wait_recv()
-        out[:, columns] = slots[n - 2].astype(f32) + piece(i, n - 1)[...].astype(f32)
-    for i in range(len(streams)):
-        copy(i, 0, piece(i, 0)).wait_send()
-        loop(n - 2, lambda step, i=i: copy(i, step + 1, streams[i][2].at[step]).wait_send())
-
-
-def ring_sums(parts, cid):
-    n = lax.axis_size("seq")
-    cuts = [p.shape[1] // LANES // 2 * LANES for p in parts]
-    rows = [p.shape[0] // n for p in parts]
-    held = []
-    for p, cut, r in zip(parts, cuts, rows):
-        held += [
-            pltpu.VMEM((n - 1, r, cut), p.dtype),
-            pltpu.VMEM((n - 1, r, p.shape[1] - cut), p.dtype),
-        ]
-    count = len(parts)
-    return pl.pallas_call(
-        functools.partial(ring_kernel, n, count, cuts),
-        out_shape=[jax.ShapeDtypeStruct((r, p.shape[1]), f32) for p, r in zip(parts, rows)],
-        in_specs=[in_vmem] * count,
-        out_specs=[in_vmem] * count,
-        scratch_shapes=held
-        + [
-            pltpu.SemaphoreType.DMA((2 * count, n - 1)),
-            pltpu.SemaphoreType.DMA((2 * count, n - 1)),
-        ],
-        compiler_params=params(cid),
-        name="ring_sums",
-    )(*parts)
-
-
 class Group:
     def __init__(self, n):
         self.n = n
@@ -211,21 +125,17 @@
 
 
 def as_column(row, width):
-    tile = jnp.broadcast_to(row, (LANES, LANES)).T
+    tile = jnp.broadcast_to(row, (LANES, row.shape[1])).T
     return jnp.concatenate([tile] * (-(-width // LANES)), axis=1)[:, :width]
 
 
-def as_row(values):
-    return rows_of(values)
-
-
-def scatter_phases(group, chunks, part, mate_in, chip_out, chip_in, sems):
+def scatter_phases(group, row_block, part, mate_in, chip_out, chip_in, sems):
     mate_send, mate_recv, chip_send, chip_recv = sems
 
     def mate_copy(c, x):
         return remote(
-            part.at[2 * x + 1 - group.core, row_tile(c)],
-            mate_in.at[x, row_tile(c)],
+            part.at[2 * x + 1 - group.core, row_block(c)],
+            mate_in.at[x, row_block(c)],
             mate_send.at[x, c],
             mate_recv.at[x, c],
             group.at(group.mate),
@@ -233,8 +143,8 @@
 
     def chip_copy(c, k):
         return remote(
-            chip_out.at[k - 1, row_tile(c)],
-            chip_in.at[k - 1, row_tile(c)],
+            chip_out.at[k - 1, row_block(c)],
+            chip_in.at[k - 1, row_block(c)],
             chip_send.at[k - 1, c],
             chip_recv.at[k - 1, c],
             group.at(group.peer(k)),
@@ -249,19 +159,19 @@
             mate_copy(c, x).wait_recv()
         for k in range(1, group.chips):
             x = group.chip_after(k)
-            both = part[2 * x + group.core, row_tile(c)].astype(f32) + mate_in[
-                x, row_tile(c)
+            both = part[2 * x + group.core, row_block(c)].astype(f32) + mate_in[
+                x, row_block(c)
             ].astype(f32)
-            chip_out[k - 1, row_tile(c)] = both.astype(bf16)
+            chip_out[k - 1, row_block(c)] = both.astype(bf16)
             chip_copy(c, k).start()
 
     def total(c):
-        value = part[group.me, row_tile(c)].astype(f32) + mate_in[
-            group.chip, row_tile(c)
+        value = part[group.me, row_block(c)].astype(f32) + mate_in[
+            group.chip, row_block(c)
         ].astype(f32)
         for k in range(1, group.chips):
             chip_copy(c, k).wait_recv()
-            value = value + chip_in[k - 1, row_tile(c)].astype(f32)
+            value = value + chip_in[k - 1, row_block(c)].astype(f32)
         return value
 
     def finish(c):
@@ -278,14 +188,17 @@
     gated_ref,
     weight_ref,
     square_ref,
-    tokens_ref,
-    teacher_ref,
+    tokens_hbm,
+    teacher_hbm,
     mask_ref,
     output_ref,
     grad_ref,
     rowdot_ref,
     squared_ref,
     loss_ref,
+    tokens_out,
+    tokens_ref,
+    teacher_ref,
     part,
     mate_in,
     chip_out,
@@ -308,14 +221,29 @@
     sq_recv,
     rd_send,
     rd_recv,
+    load_sem,
 ):
     group = Group(n)
+    count, length, width = tokens_ref.shape
+    if tokens_hbm.shape[2] == width:
+        token_columns = tokens_hbm
+    else:
+        start = pl.multiple_of(group.me * width, LANES)
+        token_columns = tokens_hbm.at[:, :, pl.ds(start, width)]
+    token_load = pltpu.make_async_copy(token_columns, tokens_ref, load_sem.at[0])
+    token_load.start()
+    teacher_load = pltpu.make_async_copy(teacher_hbm, teacher_ref, load_sem.at[1])
+    teacher_load.start()
     group.greet()
     chunks = gated_ref.shape[0] // LANES
-    width = tokens_ref.shape[1]
+    per = length // LANES
+
+    def rows_in(c):
+        return lax.div(c, per), pl.ds(pl.multiple_of(lax.rem(c, per) * LANES, LANES), LANES)
+
     share(group, square_ref, squares, sq_send, sq_recv)
     start_mate, start_chip, total, finish = scatter_phases(
-        group, chunks, part, mate_in, chip_out, chip_in, (mate_send, mate_recv, chip_send, chip_recv)
+        group, row_tile, part, mate_in, chip_out, chip_in, (mate_send, mate_recv, chip_send, chip_recv)
     )
 
     def product(c):
@@ -349,6 +277,11 @@
             block, block, gf_send.at[k - 1, c], gf_recv.at[k - 1, c], group.at(group.mate)
         )
 
+    token_load.wait()
+    teacher_load.wait()
+    token_store = pltpu.make_async_copy(tokens_ref, tokens_out, load_sem.at[0])
+    token_store.start()
+
     def rest(c):
         squared = squares[0, pl.ds(c, 1)]
         for j in range(1, n):
@@ -356,9 +289,9 @@
         squared_ref[pl.ds(c, 1)] = squared
         scale = lax.rsqrt(squared * (1.0 / (NHEADS * HEADDIM)) + norm_eps)
         branch = total(c) * as_column(scale, width)
-        output = tokens_ref[row_tile(c)] + branch
+        output = tokens_ref[rows_in(c)] + branch
         output_ref[row_tile(c)] = output
-        difference = output - teacher_ref[row_tile(c)]
+        difference = output - teacher_ref[rows_in(c)]
         weighted = difference * as_column(mask_ref[pl.ds(c, 1)], width)
         low = weighted.astype(bf16)
         gathered[group.me, row_tile(c)] = low
@@ -366,7 +299,7 @@
         for k in range(1, group.chips):
             to_chip(c, k).start()
         loss_ref[...] += jnp.sum(weighted * difference, axis=0, keepdims=True)
-        dot_out[pl.ds(c, 1)] = as_row(low.astype(f32) * branch)
+        dot_out[pl.ds(c, 1)] = rows_of(low.astype(f32) * branch)
 
     loop(chunks, rest)
     share(group, dot_out, dots, rd_send, rd_recv)
@@ -393,10 +326,11 @@
     for k in range(1, n):
         row_sum = row_sum + dots[group.other(k)]
     rowdot_ref[...] = row_sum
-
-
-def scatter_scratch(n, rows, width):
-    chips, chunks = n // 2, rows // LANES
+    token_store.wait()
+
+
+def scatter_scratch(n, rows, width, chunks):
+    chips = n // 2
     dma = pltpu.SemaphoreType.DMA
     return [
         pltpu.VMEM((n, rows, width), bf16),
@@ -415,10 +349,14 @@
 
 def out_phase(gated, weight, square_rows, tokens, teacher, mask_rows, cid):
     n = lax.axis_size("head")
-    rows, width = tokens.shape
+    count, length, width = teacher.shape
+    rows = count * length
     chips, chunks = n // 2, rows // LANES
-    buffers, sems = scatter_scratch(n, rows, width)
+    if width % LANES:
+        tokens = lax.dynamic_slice_in_dim(tokens, lax.axis_index("head") * width, width, 2)
+    buffers, sems = scatter_scratch(n, rows, width, chunks)
     dma = pltpu.SemaphoreType.DMA
+    hbm = pl.BlockSpec(memory_space=pl.ANY)
     return pl.pallas_call(
         functools.partial(out_kernel, n),
         out_shape=[
@@ -427,10 +365,12 @@
             jax.ShapeDtypeStruct((chunks, LANES), f32),
             jax.ShapeDtypeStruct((chunks, LANES), f32),
             jax.ShapeDtypeStruct((1, width), f32),
+            jax.ShapeDtypeStruct((count, length, width), f32),
         ],
-        in_specs=[in_vmem] * 6,
-        out_specs=[in_vmem] * 5,
-        scratch_shapes=buffers
+        in_specs=[in_vmem] * 3 + [hbm] * 2 + [in_vmem],
+        out_specs=[in_vmem] * 5 + [hbm],
+        scratch_shapes=[pltpu.VMEM((count, length, width), f32)] * 2
+        + buffers
         + [
             pltpu.VMEM((n, rows, width), bf16),
             pltpu.VMEM((n, chunks, LANES), f32),
@@ -449,172 +389,11 @@
             dma((n,)),
             dma((n - 1,)),
             dma((n,)),
+            dma((2,)),
         ],
         compiler_params=params(cid),
         name="out_phase",
     )(gated, blocked(weight, n), square_rows, tokens, teacher, mask_rows)
-
-
-def in_kernel(
-    n,
-    count,
-    *refs,
-):
-    grads, weights = refs[:count], refs[count : 2 * count]
-    (
-        normed_ref,
-        tokens_ref,
-        output_ref,
-        teacher_ref,
-        gain_ref,
-        mask_ref,
-        inverse_ref,
-        out_ref,
-        columns_ref,
-        part,
-        mate_in,
-        chip_out,
-        chip_in,
-        dots,
-        dot_out,
-        mate_send,
-        mate_recv,
-        chip_send,
-        chip_recv,
-        rd_send,
-        rd_recv,
-    ) = refs[2 * count :]
-    group = Group(n)
-    group.greet()
-    chunks = tokens_ref.shape[0] // LANES
-    width = tokens_ref.shape[1]
-    start_mate, start_chip, total, finish = scatter_phases(
-        group, chunks, part, mate_in, chip_out, chip_in, (mate_send, mate_recv, chip_send, chip_recv)
-    )
-    columns_ref[...] = jnp.zeros_like(columns_ref)
-
-    def product(c):
-        row_sum = jnp.zeros((1, LANES), f32)
-        for j in range(n):
-            place = slice(j * width, (j + 1) * width)
-            value = jnp.zeros((LANES, width), f32)
-            for g, w in zip(grads, weights):
-                value = value + dot_nt(g[row_tile(c)], w[place])
-            part[j, row_tile(c)] = value.astype(bf16)
-            product_n = value * normed_ref[row_tile(c), place].astype(f32)
-            columns_ref[:, place] += jnp.sum(product_n, axis=0, keepdims=True)
-            row_sum = row_sum + as_row(product_n)
-        dot_out[pl.ds(c, 1)] = row_sum
-        start_mate(c)
-
-    loop(chunks, product)
-    share(group, dot_out, dots, rd_send, rd_recv)
-    loop(chunks, start_chip)
-    shared(group, dot_out, dots, rd_send, rd_recv)
-    dots[group.me] = dot_out[...]
-
-    def rest(c):
-        row_sum = dots[0, pl.ds(c, 1)]
-        for j in range(1, n):
-            row_sum = row_sum + dots[j, pl.ds(c, 1)]
-        inverse = inverse_ref[pl.ds(c, 1)]
-        tokens = tokens_ref[row_tile(c)]
-        out_grad = (output_ref[row_tile(c)] - teacher_ref[row_tile(c)]) * as_column(
-            mask_ref[pl.ds(c, 1)], width
-        )
-        out_ref[row_tile(c)] = (
-            out_grad
-            + as_column(inverse, width) * gain_ref[...] * total(c)
-            - tokens * as_column(inverse * inverse * row_sum * (1.0 / D), width)
-        )
-
-    loop(chunks, rest)
-    loop(chunks, finish)
-
-
-def in_phase(grads, weights, normed, tokens, output, teacher, gain, mask_rows, inverse_rows, cid):
-    n = lax.axis_size("head")
-    rows, width = tokens.shape
-    chunks = rows // LANES
-    buffers, sems = scatter_scratch(n, rows, width)
-    dma = pltpu.SemaphoreType.DMA
-    return pl.pallas_call(
-        functools.partial(in_kernel, n, len(grads)),
-        out_shape=[
-            jax.ShapeDtypeStruct((rows, width), f32),
-            jax.ShapeDtypeStruct((1, D), f32),
-        ],
-        in_specs=[in_vmem] * (2 * len(grads) + 7),
-        out_specs=[in_vmem] * 2,
-        scratch_shapes=buffers
-        + [pltpu.VMEM((n, chunks, LANES), f32), pltpu.VMEM((chunks, LANES), f32)]
-        + sems
-        + [dma((n - 1,)), dma((n,))],
-        compiler_params=params(cid),
-        name="in_phase",
-    )(*grads, *weights, normed, tokens, output, teacher, gain, mask_rows, inverse_rows)
-
-
-def small_kernel(axis, n, source_ref, out_ref, table, send_sem, recv_sem):
-    place = lax.axis_index(axis)
-    fixed = lax.axis_index("seq" if axis == "head" else "head")
-
-    def at(index):
-        return (fixed, index) if axis == "head" else (index, fixed)
-
-    barrier = pltpu.get_barrier_semaphore()
-    for k in range(1, n):
-        pl.semaphore_signal(
-            barrier, inc=1, device_id=at(lax.rem(place + k, n)), device_id_type=MESH
-        )
-    pl.semaphore_wait(barrier, n - 1)
-
-    def copy(k, sender, target):
-        return remote(
-            source_ref, table.at[sender], send_sem.at[k], recv_sem.at[sender], at(target)
-        )
-
-    for k in range(1, n):
-        copy(k - 1, place, lax.rem(place + k, n)).start()
-    for k in range(1, n):
-        sender = lax.rem(place + k, n)
-        copy(k - 1, sender, sender).wait()
-    table[place] = source_ref[...]
-    value = table[0]
-    for k in range(1, n):
-        value = value + table[k]
-    out_ref[...] = value
-
-
-def small_sum(source, axis, cid):
-    n = lax.axis_size(axis)
-    return pl.pallas_call(
-        functools.partial(small_kernel, axis, n),
-        out_shape=jax.ShapeDtypeStruct(source.shape, f32),
-        in_specs=[in_vmem],
-        out_specs=in_vmem,
-        scratch_shapes=[
-            pltpu.VMEM((n,) + source.shape, f32),
-            pltpu.SemaphoreType.DMA((n - 1,)),
-            pltpu.SemaphoreType.DMA((n,)),
-        ],
-        compiler_params=params(cid),
-        name="small_sum_" + axis,
-    )(source)
-
-
-def packed(arrays):
-    flat = jnp.concatenate([a.reshape(-1) for a in arrays])
-    size = -(-flat.shape[0] // 1024) * 1024
-    return jnp.pad(flat, (0, size - flat.shape[0])).reshape(-1, LANES)
-
-
-def unpacked(value, arrays):
-    flat, at, found = value.reshape(-1), 0, []
-    for a in arrays:
-        found.append(flat[at : at + a.size].reshape(a.shape))
-        at += a.size
-    return found
 
 
 def blocks(width, size=256):
@@ -672,6 +451,20 @@
     return jnp.maximum(x, 0.0) + jnp.where(y < 0.03, small, jnp.log(1.0 + y))
 
 
+def lane_row(ref):
+    row = ref[...][None, :]
+    return jnp.concatenate([row, jnp.zeros((1, LANES - row.shape[1]), f32)], axis=1)
+
+
+def long_row(ref, b, length):
+    per = length // LANES
+    return jnp.concatenate([ref[pl.ds(b * per + i, 1)] for i in range(per)], axis=1)
+
+
+def spread_row(row, marks):
+    return spread(jnp.broadcast_to(row, (8, LANES)), marks)[:1]
+
+
 def position_masks(docs_row, begin):
     length = docs_row.shape[1]
     column = jnp.broadcast_to(docs_row, (LANES, length)).T
@@ -688,7 +481,9 @@
     step_ref,
     gate_hbm,
     docs_ref,
-    vectors_ref,
+    step_bias_ref,
+    rate_log_ref,
+    skip_ref,
     value_conv_ref,
     value_offset_ref,
     keyquery_conv_ref,
@@ -791,7 +586,7 @@
         token_load(b).wait()
         x = tokens[b]
         inverse = lax.rsqrt(jnp.mean(x * x, axis=-1, keepdims=True) + norm_eps)
-        normed[b] = (x * inverse * gain_ref[...]).astype(bf16)
+        normed[b] = (x * inverse * gain_ref[...][None, :]).astype(bf16)
         inverse_out[pl.ds(b, 1)] = jnp.broadcast_to(inverse, (length, LANES)).T[:1]
         store(0, b).start()
 
@@ -821,7 +616,10 @@
         linear[b, :, channels:] = jnp.dot(
             rows, keyquery_weight[...], preferred_element_type=f32
         ).astype(bf16)
-        linear_steps_out[b] = jnp.dot(rows, step_ref[...], preferred_element_type=f32)
+        narrow_steps = dot_nt(rows, step_ref[...])
+        linear_steps_out[b] = jnp.concatenate(
+            [narrow_steps, jnp.zeros((length, LANES - heads), f32)], axis=1
+        )
         store(1, b).start()
 
     loop(count, project)
@@ -836,9 +634,9 @@
 
     halo_out[...] = halo[...]
     marks = head_spread(channels)
-    step_bias = vectors_ref[0:1]
-    decay_rate = -jnp.exp(vectors_ref[1:2])
-    skip = spread(vectors_ref[...], marks)[2:3]
+    step_bias = lane_row(step_bias_ref)
+    decay_rate = -jnp.exp(lane_row(rate_log_ref))
+    skip = spread_row(lane_row(skip_ref), marks)
     triangle = (
         lax.broadcasted_iota(jnp.int32, (length, length), 0)
         >= lax.broadcasted_iota(jnp.int32, (length, length), 1)
@@ -855,7 +653,7 @@
             else:
                 weight, offset, place_at = keyquery_conv_ref, keyquery_offset_ref, at - channels
             lanes = slice(place_at, place_at + LANES)
-            value = offset[:, lanes] + weight[0:1, lanes] * extended[16:, at : at + LANES]
+            value = offset[lanes][None, :] + weight[0:1, lanes] * extended[16:, at : at + LANES]
             for lag in range(1, lags):
                 value = value + weight[lag : lag + 1, lanes] * (
                     extended[16 - lag : 16 - lag + length, at : at + LANES] * usable[lag]
@@ -969,9 +767,13 @@
         store(4, b).start()
         linear_gate = gate[b]
         gated = value * (linear_gate * jax.nn.sigmoid(linear_gate))
-        gained[b] = (gated * norm_gain_ref[...]).astype(bf16)
+        gained[b] = (gated * norm_gain_ref[...][None, :]).astype(bf16)
         store(5, b).start()
-        square_out[pl.ds(b, 1)] = rows_of(gated * gated)
+        squared = rows_of(gated * gated)
+        for i in range(length // LANES):
+            square_out[pl.ds(b * (length // LANES) + i, 1)] = squared[
+                :, i * LANES : (i + 1) * LANES
+            ]
 
     loop(count, close)
 
@@ -1007,13 +809,13 @@
         ((count, length, LANES), f32),
         ((count, length, LANES), f32),
         ((count, length, LANES), f32),
-        ((count, length), f32),
+        ((count * length // LANES, LANES), f32),
         ((count, length), f32),
     ]
     return pl.pallas_call(
         functools.partial(front_kernel, heads),
         out_shape=[shape(*s) for s in big + small],
-        in_specs=[hbm, in_vmem, hbm, hbm, in_vmem, hbm] + [in_vmem] * 7,
+        in_specs=[hbm, in_vmem, hbm, hbm, in_vmem, hbm] + [in_vmem] * 9,
         out_specs=[hbm] * len(big) + [in_vmem] * len(small),
         scratch_shapes=[
             pltpu.VMEM((count, length, D), f32),
@@ -1045,7 +847,7 @@
         ],
         compiler_params=params(cid),
         name="front",
-    )(tokens, gain, value_weight, keyquery_weight, step_weight, gate_weight, docs, vectors, *conv, norm_gain)
+    )(tokens, gain, value_weight, keyquery_weight, step_weight, gate_weight, docs, *vectors, *conv, norm_gain)
 
 
 def back_kernel(
@@ -1063,7 +865,9 @@
     square_ref,
     rowdot_ref,
     docs_ref,
-    vectors_ref,
+    step_bias_ref,
+    rate_log_ref,
+    skip_ref,
     value_conv_ref,
     keyquery_conv_ref,
     norm_gain_ref,
@@ -1165,9 +969,9 @@
 
     marks = head_spread(channels)
     collect = head_gather(channels)
-    step_bias = vectors_ref[0:1]
-    decay_rate = -jnp.exp(vectors_ref[1:2])
-    skip = spread(vectors_ref[...], marks)[2:3]
+    step_bias = lane_row(step_bias_ref)
+    decay_rate = -jnp.exp(lane_row(rate_log_ref))
+    skip = spread_row(lane_row(skip_ref), marks)
     gain_grad_out[...] = jnp.zeros_like(gain_grad_out)
     vector_grad_out[...] = jnp.zeros_like(vector_grad_out)
     conv_grad_out[...] = jnp.zeros_like(conv_grad_out)
@@ -1175,9 +979,7 @@
         copy.wait()
 
     def row_column(ref, b):
-        per = length // LANES
-        row = jnp.concatenate([ref[pl.ds(b * per + i, 1)] for i in range(per)], axis=1)
-        return jnp.broadcast_to(row, (LANES, length)).T
+        return jnp.broadcast_to(long_row(ref, b, length), (LANES, length)).T
 
     def widened(column, size):
         return jnp.concatenate([column] * (size // LANES), axis=1)
@@ -1207,7 +1009,7 @@
             active = linear_gate * sigmoid_value
             value = mixed[b, :, lanes]
             gated = value * active
-            norm_gain = norm_gain_ref[:, lanes]
+            norm_gain = norm_gain_ref[lanes][None, :]
             scaled = gated * widened(scale, size)
             normed_out[b, :, lanes] = (scaled * norm_gain).astype(bf16)
             gain_grad_out[:, lanes] += jnp.sum(grad_rows * scaled, axis=0, keepdims=True)
@@ -1470,7 +1272,7 @@
     return pl.pallas_call(
         back_kernel,
         out_shape=[shape(*s) for s in big + small],
-        in_specs=[hbm] * 6 + [in_vmem] * 12,
+        in_specs=[hbm] * 6 + [in_vmem] * 14,
         out_specs=[hbm] * len(big) + [in_vmem] * len(small),
         scratch_shapes=[
             vmem(pieces.shape, bf16),
@@ -1526,11 +1328,626 @@
         square_rows,
         rowdot,
         docs,
-        vectors,
+        *vectors,
         value_conv_weight,
         keyquery_conv_weight,
         norm_gain,
     )
+
+
+class Ring:
+    def __init__(self, streams, send_sem, recv_sem):
+        self.n = lax.axis_size("seq")
+        self.streams, self.send_sem, self.recv_sem = streams, send_sem, recv_sem
+        head = lax.axis_index("head")
+        self.spot = ring_place(self.n, lax.axis_index("seq"))
+        self.after = (ring_index(self.n, lax.rem(self.spot + 1, self.n)), head)
+        self.before = (ring_index(self.n, lax.rem(self.spot + self.n - 1, self.n)), head)
+
+    def piece(self, i, step):
+        part, _, columns, way = self.streams[i]
+        shift = -1 - step if way == 0 else 1 + step
+        rows = part.shape[0] // self.n
+        index = ring_index(self.n, lax.rem(self.spot + shift + 2 * self.n, self.n))
+        return part.at[pl.ds(pl.multiple_of(index * rows, rows), rows), columns]
+
+    def copy(self, i, step, source):
+        slots, way = self.streams[i][1], self.streams[i][3]
+        return remote(
+            source,
+            slots.at[step],
+            self.send_sem.at[i, step],
+            self.recv_sem.at[i, step],
+            self.after if way == 0 else self.before,
+        )
+
+    def start(self, i):
+        self.copy(i, 0, self.piece(i, 0)).start()
+
+    def pass_on(self, i, step):
+        slots = self.streams[i][1]
+        self.copy(i, step, slots.at[step]).wait_recv()
+        total = slots[step].astype(f32) + self.piece(i, step + 1)[...].astype(f32)
+        slots[step] = total.astype(slots.dtype)
+        self.copy(i, step + 1, slots.at[step]).start()
+
+    def last(self, i):
+        slots, step = self.streams[i][1], self.n - 2
+        self.copy(i, step, slots.at[step]).wait_recv()
+        return slots[step].astype(f32) + self.piece(i, step + 1)[...].astype(f32)
+
+    def finish(self, i):
+        slots = self.streams[i][1]
+        self.copy(i, 0, self.piece(i, 0)).wait_send()
+        loop(self.n - 2, lambda step: self.copy(i, step + 1, slots.at[step]).wait_send())
+
+
+def ring_streams(part, slots):
+    cut, width = slots[0].shape[2], part.shape[1]
+    return [(part, slots[0], pl.ds(0, cut), 0), (part, slots[1], pl.ds(cut, width - cut), 1)]
+
+
+def ring_slots(n, rows, width, kind):
+    cut = width // LANES // 2 * LANES
+    return [pltpu.VMEM((n - 1, rows, cut), kind), pltpu.VMEM((n - 1, rows, width - cut), kind)]
+
+
+class Doubling:
+    def __init__(self, axis, current, table, send_sem, recv_sem):
+        self.axis, self.current, self.table = axis, current, table
+        self.send_sem, self.recv_sem = send_sem, recv_sem
+        self.stages = table.shape[0]
+
+    def copy(self, stage):
+        bit = 1 << stage
+        mine = lax.axis_index(self.axis)
+        other = mine + bit - 2 * bit * lax.rem(lax.div(mine, bit), 2)
+        if self.axis == "head":
+            target = (lax.axis_index("seq"), other)
+        else:
+            target = (other, lax.axis_index("head"))
+        return remote(
+            self.current,
+            self.table.at[stage],
+            self.send_sem.at[stage],
+            self.recv_sem.at[stage],
+            target,
+        )
+
+    def start(self, stage):
+        self.copy(stage).start()
+
+    def finish(self, stage):
+        self.copy(stage).wait()
+        self.current[...] = self.current[...] + self.table[stage]
+
+
+def stages_of(n):
+    return n.bit_length() - 1
+
+
+def tile_place(index, width):
+    per = width // LANES
+    return index // per, slice(index % per * LANES, index % per * LANES + LANES)
+
+
+class Tiles:
+    def __init__(self, ref):
+        self.ref, self.index = ref, 0
+
+    def put(self, row):
+        for at in range(0, row.shape[1], LANES):
+            r, lanes = tile_place(self.index, self.ref.shape[1])
+            self.ref[r : r + 1, lanes] = row[:, at : at + LANES]
+            self.index += 1
+
+    def take(self, width):
+        found = []
+        for _ in range(width // LANES):
+            r, lanes = tile_place(self.index, self.ref.shape[1])
+            found.append(self.ref[r : r + 1, lanes])
+            self.index += 1
+        return jnp.concatenate(found, axis=1)
+
+
+def tail_kernel(
+    heads,
+    normed_hbm,
+    values_grad_hbm,
+    narrow_hbm,
+    gate_grad_hbm,
+    pieces_hbm,
+    normed_out_hbm,
+    value_weight_hbm,
+    gate_weight_hbm,
+    keyquery_weight_hbm,
+    step_weight_ref,
+    tokens_ref,
+    output_ref,
+    teacher_ref,
+    gain_ref,
+    mask_ref,
+    inverse_ref,
+    conv_grad_ref,
+    vector_grad_ref,
+    gain_grad_ref,
+    loss_cols_ref,
+    tokens_grad_out,
+    value_out,
+    gate_out,
+    out_out,
+    keyquery_out,
+    step_out,
+    value_conv_out,
+    value_offset_out,
+    keyquery_conv_out,
+    keyquery_offset_out,
+    step_bias_out,
+    rate_log_out,
+    skip_out,
+    norm_gain_out,
+    input_gain_out,
+    loss_out,
+    normed,
+    values_grad,
+    narrow,
+    gate_grad,
+    pieces,
+    normed_out,
+    value_weight,
+    gate_weight,
+    keyquery_weight,
+    value_part,
+    gate_part,
+    out_part,
+    keyquery_part,
+    vs0,
+    vs1,
+    gs0,
+    gs1,
+    os0,
+    os1,
+    ks0,
+    ks1,
+    step_whole,
+    step_part,
+    step_table,
+    keyquery_sum,
+    keyquery_table,
+    group_sum,
+    group_table,
+    line_sum,
+    line_table,
+    columns,
+    part,
+    mate_in,
+    chip_out,
+    chip_in,
+    dots,
+    dot_out,
+    load_sem,
+    ring_send,
+    ring_recv,
+    step_send,
+    step_recv,
+    kq_send,
+    kq_recv,
+    group_send,
+    group_recv,
+    line_send,
+    line_recv,
+    mate_send,
+    mate_recv,
+    chip_send,
+    chip_recv,
+    rd_send,
+    rd_recv,
+):
+    heads_n = lax.axis_size("head")
+    n = lax.axis_size("seq")
+    place = lax.axis_index("seq")
+    count, length, width = tokens_ref.shape
+    rows = count * length
+    channels = value_part.shape[1]
+    both = channels + 2 * STATE
+    lags = value_conv_out.shape[0]
+    group = Group(heads_n)
+    loads = [
+        pltpu.make_async_copy(source, target, load_sem.at[i])
+        for i, (source, target) in enumerate(
+            [
+                (normed_hbm, normed),
+                (values_grad_hbm, values_grad),
+                (narrow_hbm, narrow),
+                (value_weight_hbm, value_weight),
+                (gate_grad_hbm, gate_grad),
+                (gate_weight_hbm, gate_weight),
+                (keyquery_weight_hbm, keyquery_weight),
+                (pieces_hbm, pieces),
+                (normed_out_hbm, normed_out),
+            ]
+        )
+    ]
+    for copy in loads:
+        copy.start()
+    barrier = pltpu.get_barrier_semaphore()
+    for k in range(1, heads_n):
+        pl.semaphore_signal(
+            barrier, inc=1, device_id=group.at(group.other(k)), device_id_type=MESH
+        )
+    for k in range(1, n):
+        pl.semaphore_signal(
+            barrier, inc=1, device_id=(lax.rem(place + k, n), group.me), device_id_type=MESH
+        )
+    pl.semaphore_wait(barrier, heads_n + n - 2)
+
+    ring = Ring(
+        ring_streams(value_part, (vs0, vs1))
+        + ring_streams(keyquery_part, (ks0, ks1))
+        + ring_streams(gate_part, (gs0, gs1))
+        + ring_streams(out_part, (os0, os1)),
+        ring_send,
+        ring_recv,
+    )
+    streams = range(len(ring.streams))
+    group_total = Doubling("head", group_sum, group_table, group_send, group_recv)
+    line_total = Doubling("seq", line_sum, line_table, line_send, line_recv)
+    keyquery_total = Doubling("head", keyquery_sum, keyquery_table, kq_send, kq_recv)
+
+    for i in (0, 1, 2):
+        loads[i].wait()
+
+    def weight_block(target, grads):
+        def one(i):
+            block = pl.ds(pl.multiple_of(i * 256, 256), 256)
+            target[block] = dot_tn(normed[:, block], grads[...]).astype(target.dtype)
+
+        loop(D // 256, one)
+
+    weight_block(value_part, values_grad)
+    ring.start(0)
+    ring.start(1)
+    weight_block(keyquery_part, narrow.at[:, : 2 * STATE])
+    ring.start(2)
+    ring.start(3)
+    loads[4].wait()
+    weight_block(gate_part, gate_grad)
+    ring.start(4)
+    ring.start(5)
+    loads[7].wait()
+    loads[8].wait()
+    for j in range(heads_n):
+        out_part[j * width : (j + 1) * width] = dot_tn(pieces[j], normed_out[...]).astype(bf16)
+    ring.start(6)
+    ring.start(7)
+
+    step_rows = D // n
+    for at, size in blocks(D):
+        step_whole[:, at : at + size] = dot_tn(narrow[:, 2 * STATE :], normed[:, at : at + size])
+    step_part[...] = jnp.zeros_like(step_part)
+    for s in range(n):
+        step_part[s, :, :step_rows] = step_whole[:16, s * step_rows : (s + 1) * step_rows]
+
+    def step_copy(k, index, sender):
+        return remote(
+            step_part.at[index],
+            step_table.at[sender],
+            step_send.at[k - 1],
+            step_recv.at[sender],
+            (index, group.me),
+        )
+
+    for k in range(1, n):
+        step_copy(k, lax.rem(place + k, n), place).start()
+
+    for i in (3, 5, 6):
+        loads[i].wait()
+    columns[...] = jnp.zeros_like(columns)
+
+    def own_columns(row):
+        mine = jnp.zeros((1, width), f32)
+        for j in range(heads_n):
+            mine = mine + jnp.where(group.me == j, row[:, j * width : (j + 1) * width], 0.0)
+        return mine
+
+    gain = own_columns(gain_ref[...][None, :])
+
+    def row_block(c):
+        return pl.ds(pl.multiple_of(c * length, length), length)
+
+    start_mate, start_chip, total, finish = scatter_phases(
+        group, row_block, part, mate_in, chip_out, chip_in, (mate_send, mate_recv, chip_send, chip_recv)
+    )
+
+    def product(c):
+        row_sum = jnp.zeros((length, LANES), f32)
+        for j in range(heads_n):
+            lanes = slice(j * width, (j + 1) * width)
+            value = dot_nt(gate_grad[row_block(c)], gate_weight[lanes])
+            value = value + dot_nt(values_grad[row_block(c)], value_weight[lanes])
+            value = value + dot_nt(narrow[row_block(c), : 2 * STATE], keyquery_weight[lanes])
+            value = value + jnp.dot(
+                narrow[row_block(c), 2 * STATE : 2 * STATE + heads],
+                step_weight_ref[:, lanes],
+                preferred_element_type=f32,
+            )
+            part[j, row_block(c)] = value.astype(bf16)
+            scaled = value * normed[row_block(c), lanes].astype(f32)
+            columns[:, lanes] += jnp.sum(scaled, axis=0, keepdims=True)
+            row_sum = row_sum + fold_lanes(scaled)
+        dot_out[pl.ds(c, 1)] = jnp.sum(row_sum.T, axis=0, keepdims=True)
+        start_mate(c)
+
+        @pl.when(c > 0)
+        def _():
+            start_chip(c - 1)
+
+        @pl.when(c < n - 2)
+        def _():
+            for i in streams:
+                ring.pass_on(i, c)
+
+    loop(count, product)
+    start_chip(count - 1)
+    share(group, dot_out, dots, rd_send, rd_recv)
+
+    tiles = Tiles(group_sum)
+    group_sum[...] = jnp.zeros_like(group_sum)
+    for lag in range(lags + 1):
+        tiles.put(conv_grad_ref[lag : lag + 1, channels:])
+    tiles.put(columns[...])
+    tiles.put(fold_lanes(loss_cols_ref[...]))
+    for stage in range(group_total.stages):
+        group_total.start(stage)
+        group_total.finish(stage)
+
+    tiles, summed = Tiles(line_sum), Tiles(group_sum)
+    line_sum[...] = jnp.zeros_like(line_sum)
+    for lag in range(lags + 1):
+        tiles.put(conv_grad_ref[lag : lag + 1, :channels])
+        tiles.put(summed.take(2 * STATE))
+    tiles.put(gain_grad_ref[...])
+    for i in range(3):
+        tiles.put(vector_grad_ref[i : i + 1])
+    tiles.put(summed.take(D))
+    tiles.put(summed.take(LANES))
+    shared(group, dot_out, dots, rd_send, rd_recv)
+    dots[group.me] = dot_out[...]
+
+    def rest(c):
+        row_sum = dots[0, pl.ds(c, 1)]
+        for j in range(1, heads_n):
+            row_sum = row_sum + dots[j, pl.ds(c, 1)]
+        inverse = inverse_ref[pl.ds(c, 1)]
+        tokens = tokens_ref[c]
+        out_grad = (output_ref[row_block(c)] - teacher_ref[c]) * as_column(
+            long_row(mask_ref, c, length), width
+        )
+        tokens_grad_out[row_block(c)] = (
+            out_grad
+            + as_column(inverse, width) * gain * total(c)
+            - tokens * as_column(inverse * inverse * row_sum * (1.0 / D), width)
+        )
+
+        @pl.when(count + c < n - 2)
+        def _():
+            for i in streams:
+                ring.pass_on(i, count + c)
+
+    loop(count, rest)
+    more = n - 2 - 2 * count
+    if more > 0:
+
+        def further(s):
+            for i in streams:
+                ring.pass_on(i, 2 * count + s)
+
+        loop(more, further)
+    for stage in range(line_total.stages):
+        line_total.start(stage)
+        line_total.finish(stage)
+    loop(count, finish)
+
+    cut = ks0.shape[2]
+    keyquery_sum[:, :cut] = ring.last(2)
+    keyquery_sum[:, cut:] = ring.last(3)
+    for stage in range(keyquery_total.stages):
+        keyquery_total.start(stage)
+        keyquery_total.finish(stage)
+    keyquery_out[...] = keyquery_sum[...]
+
+    cut = vs0.shape[2]
+    value_out[:, :cut] = ring.last(0)
+    value_out[:, cut:] = ring.last(1)
+    gate_out[:, :cut] = ring.last(4)
+    gate_out[:, cut:] = ring.last(5)
+    out_out[:, :cut] = ring.last(6)
+    out_out[:, cut:] = ring.last(7)
+
+    for k in range(1, n):
+        sender = lax.rem(place + k, n)
+        copy = step_copy(k, sender, sender)
+        copy.wait_send()
+        copy.wait_recv()
+    step_table[place] = step_part[place]
+    step_sum = step_table[0]
+    for s in range(1, n):
+        step_sum = step_sum + step_table[s]
+    step_out[...] = step_sum[:heads, :step_rows]
+
+    tiles = Tiles(line_sum)
+    for lag in range(lags + 1):
+        own_row, shared_row = tiles.take(channels), tiles.take(2 * STATE)
+        if lag < lags:
+            value_conv_out[lag : lag + 1] = own_row
+            keyquery_conv_out[lag : lag + 1] = shared_row
+        else:
+            value_offset_out[...] = own_row[0]
+            keyquery_offset_out[...] = shared_row[0]
+    norm_gain_out[...] = tiles.take(channels)[0]
+    for target in (step_bias_out, rate_log_out, skip_out):
+        target[...] = tiles.take(LANES)[0, :heads]
+    input_gain_out[...] = (own_columns(tiles.take(D)) / gain)[0]
+    loss_out[...] = 0.5 * jnp.sum(tiles.take(LANES), axis=1, keepdims=True)[0]
+    for i in streams:
+        ring.finish(i)
+
+
+def tail(
+    normed,
+    values_grad,
+    narrow,
+    gate_grad,
+    pieces,
+    normed_out,
+    value_weight,
+    gate_weight,
+    keyquery_weight,
+    step_weight,
+    tokens,
+    output,
+    teacher,
+    gain,
+    mask_rows,
+    inverse_rows,
+    conv_grad,
+    vector_grad,
+    gain_grad,
+    loss_cols,
+    lags,
+    cid,
+):
+    heads_n, n = lax.axis_size("head"), lax.axis_size("seq")
+    count, length, width = tokens.shape
+    rows = count * length
+    channels = value_weight.shape[1]
+    heads = channels // HEADDIM
+    both = channels + 2 * STATE
+    own = D // n
+    step_lanes = -(-own // LANES) * LANES
+    buffers, sems = scatter_scratch(heads_n, rows, width, count)
+    shape, vmem, dma = jax.ShapeDtypeStruct, pltpu.VMEM, pltpu.SemaphoreType.DMA
+    hbm = pl.BlockSpec(memory_space=pl.ANY)
+    group_tiles = (lags + 1) * 2 * STATE // LANES + D // LANES + 1
+    line_tiles = (lags + 1) * both // LANES + channels // LANES + 3 + D // LANES + 1
+    group_shape = (-(-group_tiles * LANES // (8 * 512)) * 8, 512)
+    line_shape = (-(-line_tiles * LANES // (8 * both)) * 8, both)
+    head_stages, line_stages = stages_of(heads_n), stages_of(n)
+    outs = [
+        (rows, width),
+        (own, channels),
+        (own, channels),
+        (own, channels),
+        (own, 2 * STATE),
+        (heads, own),
+        (lags, channels),
+        (channels,),
+        (lags, 2 * STATE),
+        (2 * STATE,),
+        (heads,),
+        (heads,),
+        (heads,),
+        (channels,),
+        (width,),
+        (1,),
+    ]
+    slots = ring_slots(n, own, channels, bf16)
+    return pl.pallas_call(
+        functools.partial(tail_kernel, heads),
+        out_shape=[shape(s, f32) for s in outs],
+        in_specs=[hbm] * 9 + [in_vmem] * 11,
+        out_specs=[in_vmem] * len(outs),
+        scratch_shapes=[
+            vmem(a.shape, a.dtype)
+            for a in (
+                normed,
+                values_grad,
+                narrow,
+                gate_grad,
+                pieces,
+                normed_out,
+                value_weight,
+                gate_weight,
+                keyquery_weight,
+            )
+        ]
+        + [
+            vmem((D, channels), bf16),
+            vmem((D, channels), bf16),
+            vmem((D, channels), bf16),
+            vmem((D, 2 * STATE), f32),
+        ]
+        + slots * 3
+        + ring_slots(n, own, 2 * STATE, f32)
+        + [
+            vmem((LANES, D), f32),
+            vmem((n, 16, step_lanes), f32),
+            vmem((n, 16, step_lanes), f32),
+            vmem((own, 2 * STATE), f32),
+            vmem((head_stages, own, 2 * STATE), f32),
+            vmem(group_shape, f32),
+            vmem((head_stages,) + group_shape, f32),
+            vmem(line_shape, f32),
+            vmem((line_stages,) + line_shape, f32),
+            vmem((1, D), f32),
+        ]
+        + buffers
+        + [vmem((heads_n, count, length), f32), vmem((count, length), f32)]
+        + [
+            dma((9,)),
+            dma((8, n - 1)),
+            dma((8, n - 1)),
+            dma((n - 1,)),
+            dma((n,)),
+            dma((head_stages,)),
+            dma((head_stages,)),
+            dma((head_stages,)),
+            dma((head_stages,)),
+            dma((line_stages,)),
+            dma((line_stages,)),
+        ]
+        + sems
+        + [dma((heads_n - 1,)), dma((heads_n,))],
+        compiler_params=params(cid),
+        name="tail",
+    )(
+        normed,
+        values_grad,
+        narrow,
+        gate_grad,
+        pieces,
+        normed_out,
+        value_weight,
+        gate_weight,
+        keyquery_weight,
+        step_weight,
+        tokens,
+        output,
+        teacher,
+        gain,
+        mask_rows,
+        inverse_rows,
+        conv_grad,
+        vector_grad,
+        gain_grad,
+        loss_cols,
+    )
+
+
+def deliver_kernel(count, *refs):
+    for source, target in zip(refs[:count], refs[count:]):
+        target[...] = source[...]
+
+
+def deliver(arrays):
+    return pl.pallas_call(
+        functools.partial(deliver_kernel, len(arrays)),
+        out_shape=[jax.ShapeDtypeStruct(a.shape, a.dtype) for a in arrays],
+        in_specs=[in_vmem] * len(arrays),
+        out_specs=[in_vmem] * len(arrays),
+        compiler_params=pltpu.CompilerParams(vmem_limit_bytes=VMEM_LIMIT),
+        name="deliver",
+    )(*arrays)
 
 
 def body(
@@ -1553,23 +1970,16 @@
     norm_gain,
     out_weight,
 ):
-    head_index = lax.axis_index("head")
     sequence_index = lax.axis_index("seq")
-    sequence_count = tokens.shape[0]
-    shard_length = tokens.shape[1]
-    rows = sequence_count * shard_length
-    local_heads = skip_gain.shape[0]
-    local_inner = local_heads * HEADDIM
-    column_count = D // lax.axis_size("head")
-    column_start = head_index * column_count
-    shard_begin = sequence_index * shard_length
+    count, length, _ = tokens.shape
+    channels = gate_weight.shape[1]
+    width = teacher.shape[2]
+    rows = count * length
+    lags = value_conv_weight.shape[0]
     valid_count = jnp.sum(valid_mask.astype(f32))
-    local_mask = lax.dynamic_slice_in_dim(valid_mask, shard_begin, shard_length, 1).astype(f32)
-    mask_rows = (local_mask * (2.0 / (D * valid_count))).reshape(-1, LANES)
-    step_pad = ((0, 0), (0, LANES - local_heads))
-    vectors = jnp.pad(
-        jnp.stack([step_bias, rate_log, skip_gain]), ((0, 5), (0, LANES - local_heads))
-    )
+    local_mask = lax.dynamic_slice_in_dim(valid_mask, sequence_index * length, length, 1)
+    mask_rows = (local_mask.astype(f32) * (2.0 / (D * valid_count))).reshape(-1, LANES)
+    vectors = (step_bias, rate_log, skip_gain)
     (
         normed,
         linear,
@@ -1586,29 +1996,19 @@
         inverse_rows,
     ) = front(
         tokens,
-        input_gain[None],
+        input_gain,
         value_weight,
         keyquery_weight,
-        jnp.pad(step_weight, step_pad),
+        step_weight.T,
         gate_weight,
         document_start,
         vectors,
-        (
-            value_conv_weight,
-            value_conv_bias[None],
-            keyquery_conv_weight,
-            keyquery_conv_bias[None],
-        ),
-        norm_gain[None],
+        (value_conv_weight, value_conv_bias, keyquery_conv_weight, keyquery_conv_bias),
+        norm_gain,
         1,
     )
-    conv_lags = value_conv_weight.shape[0]
-    square_rows = square_rows.reshape(-1, LANES)
-    gained = gained.reshape(rows, local_inner)
-    token_cols = lax.dynamic_slice_in_dim(tokens, column_start, column_count, 2).reshape(rows, -1)
-    teacher_rows = teacher.reshape(rows, column_count)
-    output, piece_blocks, rowdot, square_total, loss_cols = out_phase(
-        gained, out_weight, square_rows, token_cols, teacher_rows, mask_rows, 2
+    output, pieces, rowdot, square_total, loss_cols, token_cols = out_phase(
+        gained.reshape(rows, channels), out_weight, square_rows, tokens, teacher, mask_rows, 2
     )
     (
         normed_out,
@@ -1617,9 +2017,9 @@
         narrow_grad,
         conv_grad,
         vector_grad,
-        gain_out_grad,
+        gain_grad,
     ) = back(
-        piece_blocks,
+        pieces,
         out_weight,
         gate_linear,
         mixed,
@@ -1636,91 +2036,78 @@
         vectors,
         value_conv_weight,
         keyquery_conv_weight,
-        norm_gain[None],
+        norm_gain,
         3,
     )
-    gate_grad = gate_grad.reshape(rows, local_inner)
-    values_grad = values_grad.reshape(rows, local_inner)
-    narrow_grad = narrow_grad.reshape(rows, -1)
-    piece_cols = jnp.moveaxis(piece_blocks, 0, 1).reshape(rows, D)
-    column_grad = dot_tn(piece_cols, normed_out.reshape(rows, local_inner)).astype(bf16)
-    narrow_weight = jnp.concatenate([keyquery_weight, jnp.pad(step_weight, step_pad)], axis=-1)
-    normed = normed.reshape(rows, D)
-    gain_cols = lax.dynamic_slice_in_dim(input_gain, column_start, column_count, 0)
-    tokens_grad, gain_columns = in_phase(
-        (gate_grad, values_grad, narrow_grad),
-        (gate_weight, value_weight, narrow_weight),
-        normed,
-        token_cols,
-        output,
-        teacher_rows,
-        gain_cols[None],
-        mask_rows,
-        inverse_rows.reshape(-1, LANES),
-        4,
-    )
-    gate_part = dot_tn(normed, gate_grad).astype(bf16)
-    value_part = dot_tn(normed, values_grad).astype(bf16)
-    narrow_part = dot_tn(normed, narrow_grad)
-    out_total, gate_total, value_total, narrow_total = ring_sums(
-        (column_grad, gate_part, value_part, narrow_part), 5
-    )
-    group_parts = [
-        narrow_total[:, : 2 * STATE],
-        conv_grad[:conv_lags, local_inner:],
-        conv_grad[conv_lags, local_inner:],
-        gain_columns,
-        jnp.sum(loss_cols)[None],
-    ]
     (
+        tokens_grad,
+        value_total,
+        gate_total,
+        out_total,
         keyquery_total,
-        keyquery_conv_part,
-        keyquery_offset_part,
-        gain_columns,
-        loss_part,
-    ) = unpacked(small_sum(packed(group_parts), "head", 6), group_parts)
-    line_parts = [
-        conv_grad[:conv_lags, :local_inner],
-        conv_grad[conv_lags, :local_inner],
-        keyquery_conv_part,
-        keyquery_offset_part,
-        vector_grad[0, :local_heads],
-        vector_grad[1, :local_heads],
-        vector_grad[2, :local_heads],
-        gain_out_grad[0],
-        lax.dynamic_slice_in_dim(gain_columns.reshape(-1), column_start, column_count, 0),
-        loss_part,
-    ]
-    (
+        step_total,
         value_conv_total,
         value_offset_total,
         keyquery_conv_total,
         keyquery_offset_total,
         step_bias_total,
         rate_log_total,
-        skip_gain_total,
+        skip_total,
         norm_gain_total,
         input_gain_total,
         loss_total,
-    ) = unpacked(small_sum(packed(line_parts), "seq", 7), line_parts)
+    ) = tail(
+        normed.reshape(rows, D),
+        values_grad.reshape(rows, channels),
+        narrow_grad.reshape(rows, -1),
+        gate_grad.reshape(rows, channels),
+        pieces,
+        normed_out.reshape(rows, channels),
+        value_weight,
+        gate_weight,
+        keyquery_weight,
+        step_weight.T,
+        token_cols,
+        output,
+        teacher,
+        input_gain,
+        mask_rows,
+        inverse_rows,
+        conv_grad,
+        vector_grad,
+        gain_grad,
+        loss_cols,
+        lags,
+        4,
+    )
+    results = deliver(
+        (
+            output.reshape(count, length, width),
+            loss_total,
+            tokens_grad.reshape(count, length, width),
+            input_gain_total,
+            gate_total,
+            value_total,
+            keyquery_total,
+            step_total,
+            value_conv_total,
+            value_offset_total,
+            keyquery_conv_total,
+            keyquery_offset_total,
+            step_bias_total,
+            rate_log_total,
+            skip_total,
+            norm_gain_total,
+            out_total,
+        )
+    )
     return (
-        output.reshape(sequence_count, shard_length, column_count),
-        loss_total[0] * 0.5,
-        tokens_grad.reshape(sequence_count, shard_length, column_count),
-        input_gain_total / gain_cols,
-        gate_total,
-        value_total,
-        keyquery_total,
-        narrow_total[:, 2 * STATE : 2 * STATE + local_heads],
-        value_conv_total,
-        value_offset_total,
-        keyquery_conv_total,
-        keyquery_offset_total,
-        step_bias_total,
-        rate_log_total,
-        skip_gain_total,
-        norm_gain_total,
-        out_total.T,
+        results[0],
+        results[1].reshape(()),
+        *results[2:7],
+        results[7].T,
+        *results[8:16],
+        results[16].T,
     )
 
 

time: 431 us -> 310 us (0.72)
  Pallas kernels: 361 us -> 306 us
  local copies, waits for them, and re-layouts: 40 us -> 0.6 us
  matrix products: 18.9 us -> 0 us
    pallas_call x4 -> x2, Pallas kernels: 170 us -> 115 us  [the longest x1 110 us: tail(): pl.pallas_call(functools.partial(tail_kernel, heads), out_shape=[shape(s,...]
    dot_general x4 -> x0, matrix products: 18.9 us -> none  [dot_tn(): lax.dot_general(a, b, TN, precision=precision, preferred_element_type=f32)]
    slice x16 -> x0, local copies, waits for them, and re-layouts: 13.1 us -> none  [the longest x12 12.2 us: unpacked(): found.append(flat[at:at + a.size].reshape(a.shape))]
    unnamed x51 -> x0, local copies, waits for them, and re-layouts: 8.03 us -> none
    reshape x9 -> x1, local copies, waits for them, and re-layouts: 5.75 us -> 0.6 us  [body(): (local_mask.astype(f32) * (2.0 / (D * valid_count))).reshape(-1, LANES)]
    broadcast_in_dim x4 -> x0, local copies, waits for them, and re-layouts: 4.39 us -> none  [the longest x1 1.29 us: body(): input_gain[None]]
where the time goes in v3:
time: 310 us
  Pallas kernels  306 us (99%)
    pallas_call x1, Pallas kernels, tail(): pl.pallas_call(functools.partial(tail_kernel, heads), out_shape=[shape(s,...  110 us
    pallas_call x1, Pallas kernels, back(): pl.pallas_call(back_kernel, out_shape=[shape(*s) for s in big + small], i...  103 us
    pallas_call x1, Pallas kernels, out_phase(): pl.pallas_call(functools.partial(out_kernel, n), out_shape=[jax.ShapeDtyp...  48.4 us
    pallas_call x1, Pallas kernels, front(): pl.pallas_call(functools.partial(front_kernel, heads), out_shape=[shape(*...  39.1 us

profile of v3, /device:TPU:0, one launch (start us, length us, event | category | flops | bytes accessed | tf_op | source)
XLA Modules:
  0.0 310.0 jit_solution(1068355079628779097)
XLA Ops:
  0.7 1.4 convert_reduce_fusion
  2.7 0.7 convert_multiply_fusion
  3.4 0.6 reshape.65.mask_ref
  4.0 39.1 %front.1 = (bf16[4,256,1536]{2,1,0:T(8,128)(2,1)}, bf16[4,256,1024]{2,1,0:T(8,128)(2,1)}, f32[4,256,1024]{2,1,0:T(8,128)}, f32[4,256,768]{2,1,0:T(8,128)}, f32[4...) custom-call(f32[4,256,1536]{2,1,0:T(8,128)} %tokens_hbm.3, ...), custom_call_target="tpu_custom_call" | custom-call | tf_op jit(solution)/shard_map/front/pallas_call | solution.py:815
  43.2 48.4 %out_phase.1 = (f32[1024,384]{1,0:T(8,128)}, bf16[4,1024,384]{2,1,0:T(8,128)(2,1)}, f32[8,128]{1,0:T(8,128)}, f32[8,128]{1,0:T(8,128)}, f32[1,384]{1,0:T(1,128)}, /*index=5*/f32[4,256,384]{2,1,0:T(8,128)}) custom-call(bf16[1024,768]{1,0:T(8,128)(2,1)} %bitcast.17, bf16[768,1536]{1,0:T(8,128)(2,1)} %weight_hbm.1, f32[8,128]{1,0:T(8,128)} %get-tuple-element.77.square_ref, ...), custom_call_target="tpu_custom_call" | custom-call | tf_op jit(solution)/shard_map/out_phase/pallas_call | solution.py:360
  91.6 103.0 %back.1 = (bf16[4,256,768]{2,1,0:T(8,128)(2,1)}, bf16[4,256,768]{2,1,0:T(8,128)(2,1)}, bf16[4,256,768]{2,1,0:T(8,128)(2,1)}, bf16[4,256,384]{2,1,0:T(8,128)(2,1)...) custom-call(bf16[4,1024,384]{2,1,0:T(8,128)(2,1)} %get-tuple-element.80.pieces_hbm, ...), custom_call_target="tpu_custom_call" | custom-call | tf_op jit(solution)/shard_map/back/pallas_call | solution.py:1272
  194.6 109.7 %tail.1 = (f32[1024,384]{1,0:T(8,128)}, f32[192,768]{1,0:T(8,128)}, f32[192,768]{1,0:T(8,128)}, f32[192,768]{1,0:T(8,128)}, f32[192,256]{1,0:T(8,128)}, /*index=...) custom-call(bf16[1024,1536]{1,0:T(8,128)(2,1)} %bitcast.13, ...), custom_call_target="tpu_custom_call" | custom-call | tf_op jit(solution)/shard_map/tail/pallas_call | solution.py:1855
  304.3 5.5 %deliver.1 = (f32[4,256,384]{2,1,0:T(8,128)}, f32[1]{0:T(128)}, f32[4,256,384]{2,1,0:T(8,128)}, f32[384]{0:T(512)}, f32[192,768]{1,0:T(8,128)}, /*index=5*/f32[1...) custom-call(f32[4,256,384]{2,1,0:T(8,128)} %bitcast.12, ...), custom_call_target="tpu_custom_call" | custom-call | tf_op jit(solution)/shard_map/deliver/pallas_call | solution.py:1943

commit v4 on v3

--- a/solution.py
+++ b/solution.py
@@ -12,7 +12,7 @@
 HEADDIM = 64
 STATE = 128
 LANES = 128
-VMEM_LIMIT = 56 << 20
+VMEM_LIMIT = 60 << 20
 
 norm_eps = 1e-05
 highest = lax.Precision.HIGHEST
@@ -63,6 +63,248 @@
 def ring_index(n, spot):
     late = lax.div(2 * spot, n)
     return 2 * spot * (1 - late) + (2 * (n - 1 - spot) + 1) * late
+
+
+class Ring:
+    def __init__(self, streams, send_sem, recv_sem):
+        self.n = lax.axis_size("seq")
+        self.streams, self.send_sem, self.recv_sem = streams, send_sem, recv_sem
+        head = lax.axis_index("head")
+        self.spot = ring_place(self.n, lax.axis_index("seq"))
+        self.after = (ring_index(self.n, lax.rem(self.spot + 1, self.n)), head)
+        self.before = (ring_index(self.n, lax.rem(self.spot + self.n - 1, self.n)), head)
+
+    def piece(self, i, step):
+        part, _, columns, way = self.streams[i]
+        shift = -1 - step if way == 0 else 1 + step
+        rows = part.shape[0] // self.n
+        index = ring_index(self.n, lax.rem(self.spot + shift + 2 * self.n, self.n))
+        return part.at[pl.ds(pl.multiple_of(index * rows, rows), rows), columns]
+
+    def copy(self, i, step, source):
+        slots, way = self.streams[i][1], self.streams[i][3]
+        return remote(
+            source,
+            slots.at[step],
+            self.send_sem.at[i, step],
+            self.recv_sem.at[i, step],
+            self.after if way == 0 else self.before,
+        )
+
+    def start(self, i):
+        self.copy(i, 0, self.piece(i, 0)).start()
+
+    def pass_on(self, i, step):
+        slots = self.streams[i][1]
+        self.copy(i, step, slots.at[step]).wait_recv()
+        total = slots[step].astype(f32) + self.piece(i, step + 1)[...].astype(f32)
+        slots[step] = total.astype(slots.dtype)
+        self.copy(i, step + 1, slots.at[step]).start()
+
+    def last(self, i):
+        slots, step = self.streams[i][1], self.n - 2
+        self.copy(i, step, slots.at[step]).wait_recv()
+        return slots[step].astype(f32) + self.piece(i, step + 1)[...].astype(f32)
+
+    def finish(self, i):
+        slots = self.streams[i][1]
+        self.copy(i, 0, self.piece(i, 0)).wait_send()
+        loop(self.n - 2, lambda step: self.copy(i, step + 1, slots.at[step]).wait_send())
+
+
+def ring_streams(part, slots):
+    cut, width = slots[0].shape[2], part.shape[1]
+    return [(part, slots[0], pl.ds(0, cut), 0), (part, slots[1], pl.ds(cut, width - cut), 1)]
+
+
+def ring_slots(n, rows, width, kind):
+    cut = width // LANES // 2 * LANES
+    return [pltpu.VMEM((n - 1, rows, cut), kind), pltpu.VMEM((n - 1, rows, width - cut), kind)]
+
+
+class PairChain:
+    def __init__(self, ahead, by, local, passed, buffers, send_sem, recv_sem):
+        self.n = lax.axis_size("seq")
+        self.place, self.head = lax.axis_index("seq"), lax.axis_index("head")
+        self.by, self.pair, self.second = by, lax.div(ahead, 2), lax.rem(ahead, 2)
+        self.local, self.passed = local, passed
+        (
+            self.state,
+            self.offer_a,
+            self.offer_b,
+            self.offered_a,
+            self.offered_b,
+            self.inflow,
+            self.through,
+            self.next_a,
+            self.next_b,
+        ) = buffers
+        self.send_sem, self.recv_sem = send_sem, recv_sem
+        self.cut = self.inflow.shape[2]
+        self.count, _, channels = self.state.shape
+        self.low, self.high = pl.ds(0, self.cut), pl.ds(self.cut, channels - self.cut)
+        self.all_rows = pl.ds(0, STATE)
+
+    def copy(self, kind, b, source, target, ahead):
+        return remote(
+            source,
+            target,
+            self.send_sem.at[kind, b],
+            self.recv_sem.at[kind, b],
+            (self.place + self.by * ahead, self.head),
+        )
+
+    def greet(self, barrier):
+        mate = self.place + self.by * (1 - 2 * self.second)
+        before, after = self.pair > 0, self.pair < self.n // 2 - 1
+        pl.semaphore_signal(barrier, inc=1, device_id=(mate, self.head), device_id_type=MESH)
+        for there, step in ((before, -2), (after, 2)):
+
+            @pl.when(there)
+            def _():
+                pl.semaphore_signal(
+                    barrier,
+                    inc=1,
+                    device_id=(self.place + self.by * step, self.head),
+                    device_id_type=MESH,
+                )
+
+        return 1 + before.astype(jnp.int32) + after.astype(jnp.int32)
+
+    def offering(self, b, second):
+        if second:
+            return self.copy(0, b, self.offer_b.at[b], self.offered_b.at[b], -1)
+        return self.copy(0, b, self.offer_a.at[b], self.offered_a.at[b], 1)
+
+    def handing(self, b, second):
+        if second:
+            return self.copy(
+                1, b, self.inflow.at[b], self.state.at[b, self.all_rows, self.low], -1
+            )
+        return self.copy(1, b, self.through.at[b], self.state.at[b, self.all_rows, self.high], 1)
+
+    def passing(self, b, second):
+        if second:
+            return self.copy(2, b, self.next_a.at[b], self.inflow.at[b], 2)
+        return self.copy(2, b, self.next_b.at[b], self.state.at[b, self.all_rows, self.high], 2)
+
+    def offer(self, b):
+        for second in (False, True):
+
+            @pl.when(self.second == int(second))
+            def _():
+                lanes = self.high if second else self.low
+                buffer = self.offer_b if second else self.offer_a
+                buffer[b, :STATE] = self.local[b, :, lanes].astype(bf16)
+                decay = self.passed[b, 7:8, lanes]
+                high = decay.astype(bf16).astype(f32)
+                row = lax.broadcasted_iota(jnp.int32, (16, decay.shape[1]), 0)
+                rows = jnp.where(row == 0, high, jnp.where(row == 1, decay - high, 0.0))
+                buffer[b, STATE:] = rows.astype(bf16)
+                self.offering(b, second).start()
+
+    def pass_on(self, b):
+        more = self.pair < self.n // 2 - 1
+
+        @pl.when(self.second == 0)
+        def _():
+            self.offering(b, True).wait_recv()
+
+            @pl.when(self.pair > 0)
+            def _():
+                self.passing(b, False).wait_recv()
+
+            @pl.when(self.pair == 0)
+            def _():
+                self.state[b, :, self.high] = jnp.zeros(self.next_b.shape[1:], bf16)
+
+            state = self.state[b, :, self.high].astype(f32)
+            value = self.passed[b, 7:8, self.high] * state + self.local[b, :, self.high]
+            self.through[b] = value.astype(bf16)
+            self.handing(b, False).start()
+
+            @pl.when(more)
+            def _():
+                decay = self.offered_b[b, STATE:].astype(f32)
+                decay = decay[0:1] + decay[1:2]
+                self.next_b[b] = (
+                    decay * value + self.offered_b[b, :STATE].astype(f32)
+                ).astype(bf16)
+                self.passing(b, False).start()
+
+        @pl.when(self.second == 1)
+        def _():
+            self.offering(b, False).wait_recv()
+
+            @pl.when(self.pair > 0)
+            def _():
+                self.passing(b, True).wait_recv()
+
+            @pl.when(self.pair == 0)
+            def _():
+                self.inflow[b] = jnp.zeros(self.inflow.shape[1:], bf16)
+
+            self.handing(b, True).start()
+            decay = self.offered_a[b, STATE:].astype(f32)
+            decay = decay[0:1] + decay[1:2]
+            value = decay * self.inflow[b].astype(f32) + self.offered_a[b, :STATE].astype(f32)
+            self.state[b, :, self.low] = value.astype(bf16)
+
+            @pl.when(more)
+            def _():
+                self.next_a[b] = (
+                    self.passed[b, 7:8, self.low] * value + self.local[b, :, self.low]
+                ).astype(bf16)
+                self.passing(b, True).start()
+
+    def ready(self, b):
+        for second in (False, True):
+
+            @pl.when(self.second == int(second))
+            def _():
+                self.handing(b, not second).wait_recv()
+
+    def slot(self, i, first, lag):
+        turn = i - first - lag * self.pair
+
+        @pl.when((turn >= 0) & (turn < 4 * self.count) & (lax.rem(turn + 4 * self.n, 4) == 0))
+        def _():
+            self.pass_on(lax.div(turn, 4))
+
+    def slots(self, first, lag):
+        return first + 4 * (self.count - 1) + 1 + lag * (self.n // 2 - 1)
+
+    def finish(self):
+        for second in (False, True):
+
+            @pl.when(self.second == int(second))
+            def _():
+                def one(b):
+                    self.offering(b, second).wait_send()
+                    self.handing(b, second).wait_send()
+
+                    @pl.when(self.pair < self.n // 2 - 1)
+                    def _():
+                        self.passing(b, second).wait_send()
+
+                loop(self.count, one)
+
+
+def chain_buffers(count, channels):
+    cut = channels // LANES // 2 * LANES
+    rest = channels - cut
+    shapes = [
+        (STATE, channels),
+        (STATE + 16, cut),
+        (STATE + 16, rest),
+        (STATE + 16, cut),
+        (STATE + 16, rest),
+        (STATE, cut),
+        (STATE, rest),
+        (STATE, cut),
+        (STATE, rest),
+    ]
+    return [pltpu.VMEM((count,) + s, bf16) for s in shapes]
 
 
 class Group:
@@ -503,6 +745,7 @@
     square_out,
     inverse_out,
     tokens,
+    last_tokens,
     value_weight,
     keyquery_weight,
     gate_weight,
@@ -521,11 +764,19 @@
     scores,
     mask_bias,
     locals_,
-    held,
-    outgoing,
+    state,
+    offer_a,
+    offer_b,
+    offered_a,
+    offered_b,
+    inflow,
+    through,
+    next_a,
+    next_b,
     passed,
     entering,
     load_sem,
+    last_sem,
     token_sem,
     store_sem,
     halo_sem,
@@ -540,8 +791,6 @@
     both = channels + 2 * STATE
     lags = value_conv_ref.shape[0]
     begin = (place * length).astype(f32)
-    chunk_rows = STATE // 4
-    chunks = count * 4
 
     loads = [
         pltpu.make_async_copy(value_hbm, value_weight, load_sem.at[0]),
@@ -552,11 +801,17 @@
     def token_load(b):
         return pltpu.make_async_copy(tokens_hbm.at[b], tokens.at[b], token_sem.at[b])
 
+    def last_load(b):
+        return pltpu.make_async_copy(
+            tokens_hbm.at[b, length - 16 :], last_tokens.at[b], last_sem.at[b]
+        )
+
+    for b in range(count):
+        last_load(b).start()
+    loads[0].start()
+    loads[1].start()
     for b in range(count):
         token_load(b).start()
-        if b == 0:
-            loads[0].start()
-            loads[1].start()
     loads[2].start()
 
     stores = [
@@ -574,6 +829,27 @@
 
     barrier = pltpu.get_barrier_semaphore()
 
+    chain = PairChain(
+        place,
+        1,
+        locals_,
+        passed,
+        (
+            state,
+            offer_a,
+            offer_b,
+            offered_a,
+            offered_b,
+            inflow,
+            through,
+            next_a,
+            next_b,
+        ),
+        chain_send,
+        chain_recv,
+    )
+    expected = chain.greet(barrier)
+
     @pl.when(place > 0)
     def _():
         pl.semaphore_signal(barrier, inc=1, device_id=(place - 1, head), device_id_type=MESH)
@@ -582,37 +858,54 @@
     def _():
         pl.semaphore_signal(barrier, inc=1, device_id=(place + 1, head), device_id_type=MESH)
 
-    def norm(b):
-        token_load(b).wait()
-        x = tokens[b]
+    expected = expected + (place > 0).astype(jnp.int32) + (place < n - 1).astype(jnp.int32)
+
+    def normalized(x):
         inverse = lax.rsqrt(jnp.mean(x * x, axis=-1, keepdims=True) + norm_eps)
-        normed[b] = (x * inverse * gain_ref[...][None, :]).astype(bf16)
-        inverse_out[pl.ds(b, 1)] = jnp.broadcast_to(inverse, (length, LANES)).T[:1]
-        store(0, b).start()
-
-    loop(count, norm)
+        return inverse, (x * inverse * gain_ref[...][None, :]).astype(bf16)
+
+    for b in range(count):
+        last_load(b).wait()
+    last = jnp.concatenate([normalized(last_tokens[b])[1] for b in range(count)], axis=0)
     loads[0].wait()
     loads[1].wait()
-
-    last = jnp.concatenate([normed[b, length - 16 :] for b in range(count)], axis=0)
     for at, width in blocks(channels):
         tail[:, at : at + width] = jnp.dot(
             last, value_weight[:, at : at + width], preferred_element_type=f32
         ).astype(bf16)
     tail[:, channels:] = jnp.dot(last, keyquery_weight[...], preferred_element_type=f32).astype(bf16)
-    pl.semaphore_wait(barrier, (place > 0).astype(jnp.int32) + (place < n - 1).astype(jnp.int32))
+    pl.semaphore_wait(barrier, expected)
     halo_copy = remote(tail, halo, halo_sem.at[0], halo_sem.at[1], (place + 1, head))
 
     @pl.when(place < n - 1)
     def _():
         halo_copy.start()
 
-    def project(b):
+    marks = head_spread(channels)
+    step_bias = lane_row(step_bias_ref)
+    decay_rate = -jnp.exp(lane_row(rate_log_ref))
+    skip = spread_row(lane_row(skip_ref), marks)
+    triangle = (
+        lax.broadcasted_iota(jnp.int32, (length, length), 0)
+        >= lax.broadcasted_iota(jnp.int32, (length, length), 1)
+    ).astype(f32)
+
+    def norm(b):
+        token_load(b).wait()
+        inverse, rows = normalized(tokens[b])
+        normed[b] = rows
+        inverse_out[pl.ds(b, 1)] = jnp.broadcast_to(inverse, (length, LANES)).T[:1]
+        store(0, b).start()
+
+    def project_values(b):
         rows = normed[b]
         for at, width in blocks(channels):
             linear[b, :, at : at + width] = jnp.dot(
                 rows, value_weight[:, at : at + width], preferred_element_type=f32
             ).astype(bf16)
+
+    def project_rest(b):
+        rows = normed[b]
         linear[b, :, channels:] = jnp.dot(
             rows, keyquery_weight[...], preferred_element_type=f32
         ).astype(bf16)
@@ -622,27 +915,15 @@
         )
         store(1, b).start()
 
-    loop(count, project)
-
-    @pl.when(place > 0)
-    def _():
-        halo_copy.wait_recv()
-
-    @pl.when(place == 0)
-    def _():
-        halo[...] = jnp.zeros_like(halo)
-
-    halo_out[...] = halo[...]
-    marks = head_spread(channels)
-    step_bias = lane_row(step_bias_ref)
-    decay_rate = -jnp.exp(lane_row(rate_log_ref))
-    skip = spread_row(lane_row(skip_ref), marks)
-    triangle = (
-        lax.broadcasted_iota(jnp.int32, (length, length), 0)
-        >= lax.broadcasted_iota(jnp.int32, (length, length), 1)
-    ).astype(f32)
-
     def states(b):
+        @pl.when((b == 0) & (place > 0))
+        def _():
+            halo_copy.wait_recv()
+
+        @pl.when((b == 0) & (place == 0))
+        def _():
+            halo[...] = jnp.zeros_like(halo)
+
         column, spot = position_masks(docs_ref[pl.ds(b, 1)].astype(f32), begin)
         extended[0:16] = halo[pl.ds(pl.multiple_of(b * 16, 16), 16)].astype(f32)
         extended[16:] = linear[b].astype(f32)
@@ -682,45 +963,21 @@
         last_entering = entering[b, length - 8 :]
         passed[b] = spread(last_entering, marks)
 
-    loop(count, states)
-
-    def chain_copy(c):
-        part = (lax.div(c, 4), pl.ds(pl.multiple_of(lax.rem(c, 4) * chunk_rows, chunk_rows), chunk_rows))
-        return remote(
-            outgoing.at[part], held.at[part], chain_send.at[c], chain_recv.at[c], (place + 1, head)
-        )
-
-    def chain_step(c):
-        b = lax.div(c, 4)
-        rows = pl.ds(pl.multiple_of(lax.rem(c, 4) * chunk_rows, chunk_rows), chunk_rows)
-
-        @pl.when(place > 0)
-        def _():
-            chain_copy(c).wait_recv()
-
-        @pl.when(place == 0)
-        def _():
-            held[b, rows] = jnp.zeros((chunk_rows, channels), bf16)
-
-        outgoing[b, rows] = (
-            passed[b, 7:8] * held[b, rows].astype(f32) + locals_[b, rows]
-        ).astype(bf16)
-
-        @pl.when(place < n - 1)
-        def _():
-            chain_copy(c).start()
-
     pairs = channels // LANES
-    lag_slots = 5
-    slots = chunks + lag_slots * (n - 1)
+    first_slot, lag_slots = 7, 6
 
     def chain_slot(i):
-        c = i - lag_slots * place
-
-        @pl.when((c >= 0) & (c < chunks))
-        def _():
-            chain_step(c)
-
+        chain.slot(i, first_slot, lag_slots)
+
+    def begin_sequence(b):
+        for k, unit in enumerate((norm, project_values, project_rest, states)):
+            unit(b)
+            if unit is states:
+                chain.offer(b)
+            chain_slot(4 * b + k)
+
+    loop(count, begin_sequence)
+    halo_out[...] = halo[...]
     first_half = lax.broadcasted_iota(jnp.int32, (length, LANES), 1) < HEADDIM
     loads[2].wait()
 
@@ -745,23 +1002,25 @@
                 mine = jnp.where(first_half if half == 0 else ~first_half, scaled, 0.0).astype(bf16)
                 value = value + jnp.dot(mixing, mine, preferred_element_type=f32)
             mixed[b, :, lanes] = value
-            chain_slot(b * (pairs + 1) + pair)
+            chain_slot(4 * count + b * (pairs + 1) + pair)
         rows = normed[b]
         for at, width in blocks(channels):
             gate[b, :, at : at + width] = jnp.dot(
                 rows, gate_weight[:, at : at + width], preferred_element_type=f32
             )
         store(3, b).start()
-        chain_slot(b * (pairs + 1) + pairs)
+        chain_slot(4 * count + b * (pairs + 1) + pairs)
 
     loop(count, inside)
-    done = count * (pairs + 1)
+    done = count * (pairs + 5)
+    slots = chain.slots(first_slot, lag_slots)
     if slots > done:
         loop(slots - done, lambda i: chain_slot(i + done))
 
     def close(b):
-        state_out[b] = held[b]
-        projected = jnp.dot(queries[b], held[b], preferred_element_type=f32)
+        chain.ready(b)
+        state_out[b] = state[b]
+        projected = jnp.dot(queries[b], state[b], preferred_element_type=f32)
         value = mixed[b] + spread(entering[b], marks) * projected + skip * heads_in[b]
         mixed[b] = value
         store(4, b).start()
@@ -780,7 +1039,8 @@
     @pl.when(place < n - 1)
     def _():
         halo_copy.wait_send()
-        loop(chunks, lambda c: chain_copy(c).wait_send())
+
+    chain.finish()
 
     for i in range(len(stores)):
         loop(count, lambda b, i=i: store(i, b).wait())
@@ -791,7 +1051,6 @@
     channels = value_weight.shape[1]
     heads = channels // HEADDIM
     both = channels + 2 * STATE
-    chunks = count * 4
     dma = pltpu.SemaphoreType.DMA
     hbm = pl.BlockSpec(memory_space=pl.ANY)
     shape = jax.ShapeDtypeStruct
@@ -819,6 +1078,7 @@
         out_specs=[hbm] * len(big) + [in_vmem] * len(small),
         scratch_shapes=[
             pltpu.VMEM((count, length, D), f32),
+            pltpu.VMEM((count, 16, D), f32),
             pltpu.VMEM((D, channels), bf16),
             pltpu.VMEM((D, 2 * STATE), bf16),
             pltpu.VMEM((D, channels), bf16),
@@ -834,16 +1094,18 @@
             pltpu.VMEM((length, length), f32),
             pltpu.VMEM((length, length), f32),
             pltpu.VMEM((count, STATE, channels), f32),
-            pltpu.VMEM((count, STATE, channels), bf16),
-            pltpu.VMEM((count, STATE, channels), bf16),
+        ]
+        + chain_buffers(count, channels)
+        + [
             pltpu.VMEM((count, 8, channels), f32),
             pltpu.VMEM((count, length, LANES), f32),
             dma((3,)),
             dma((count,)),
+            dma((count,)),
             dma((len(big), count)),
             dma((2,)),
-            dma((chunks,)),
-            dma((chunks,)),
+            dma((3, count)),
+            dma((3, count)),
         ],
         compiler_params=params(cid),
         name="front",
@@ -857,6 +1119,7 @@
     mixed_hbm,
     conv_hbm,
     linear_hbm,
+    normed_hbm,
     halo_ref,
     state_ref,
     steps_ref,
@@ -871,23 +1134,31 @@
     value_conv_ref,
     keyquery_conv_ref,
     norm_gain_ref,
-    normed_out_out,
     gate_grad_out,
     values_grad_out,
     narrow_out,
     conv_grad_out,
     vector_grad_out,
     gain_grad_out,
+    out_total,
+    gate_total,
     pieces,
     weight,
     gate,
     mixed,
     conv,
     linear,
+    normed,
     normed_out,
     gate_grad,
     values_grad,
     narrow,
+    out_part,
+    gate_part,
+    os0,
+    os1,
+    gs0,
+    gs1,
     heads_in,
     heads_grad,
     keys,
@@ -895,11 +1166,17 @@
     scores,
     scores_grad,
     mask_bias,
-    inner,
     narrow_grad,
     locals_,
-    held,
-    outgoing,
+    state,
+    offer_a,
+    offer_b,
+    offered_a,
+    offered_b,
+    inflow,
+    through,
+    next_a,
+    next_b,
     passed,
     extended,
     spread_grad,
@@ -914,6 +1191,8 @@
     edge_recv,
     chain_send,
     chain_recv,
+    ring_send,
+    ring_recv,
 ):
     n = lax.axis_size("seq")
     place = lax.axis_index("seq")
@@ -923,17 +1202,16 @@
     both = channels + 2 * STATE
     lags = value_conv_ref.shape[0]
     begin = (place * length).astype(f32)
-    chunk_rows = STATE // 4
-    chunks = count * 4
     groups, width = pieces.shape[0], pieces.shape[2]
     inner_total = NHEADS * HEADDIM
 
     loads = [
         pltpu.make_async_copy(weight_hbm, weight, load_sem.at[0]),
         pltpu.make_async_copy(pieces_hbm, pieces, load_sem.at[1]),
+        pltpu.make_async_copy(normed_hbm, normed, load_sem.at[2]),
     ]
-    for copy in loads:
-        copy.start()
+    loads[0].start()
+    loads[1].start()
     row_arrays = [(gate_hbm, gate), (mixed_hbm, mixed), (conv_hbm, conv), (linear_hbm, linear)]
 
     def row_load(i, b):
@@ -943,11 +1221,12 @@
     for b in range(count):
         for i in range(3):
             row_load(i, b).start()
+    loads[2].start()
     for b in range(count):
         row_load(3, b).start()
+    inner = gate
 
     stores = [
-        (normed_out, normed_out_out),
         (gate_grad, gate_grad_out),
         (values_grad, values_grad_out),
         (narrow, narrow_out),
@@ -966,6 +1245,31 @@
     @pl.when(place < n - 1)
     def _():
         pl.semaphore_signal(barrier, inc=1, device_id=(place + 1, head), device_id_type=MESH)
+
+    chain = PairChain(
+        ahead,
+        -1,
+        locals_,
+        passed,
+        (
+            state,
+            offer_a,
+            offer_b,
+            offered_a,
+            offered_b,
+            inflow,
+            through,
+            next_a,
+            next_b,
+        ),
+        chain_send,
+        chain_recv,
+    )
+    expected = chain.greet(barrier)
+    spot_here = ring_place(n, place)
+    for step in (1, n - 1):
+        neighbour = ring_index(n, lax.rem(spot_here + step, n))
+        pl.semaphore_signal(barrier, inc=1, device_id=(neighbour, head), device_id_type=MESH)
 
     marks = head_spread(channels)
     collect = head_gather(channels)
@@ -975,14 +1279,37 @@
     gain_grad_out[...] = jnp.zeros_like(gain_grad_out)
     vector_grad_out[...] = jnp.zeros_like(vector_grad_out)
     conv_grad_out[...] = jnp.zeros_like(conv_grad_out)
-    for copy in loads:
-        copy.wait()
+    loads[0].wait()
+    loads[1].wait()
+    ring = Ring(
+        ring_streams(out_part, (os0, os1)) + ring_streams(gate_part, (gs0, gs1)),
+        ring_send,
+        ring_recv,
+    )
+    ring_steps = n - 2
+
+    def pass_on(first, step):
+        @pl.when((step >= 0) & (step < ring_steps))
+        def _():
+            ring.pass_on(first, step)
+            ring.pass_on(first + 1, step)
 
     def row_column(ref, b):
         return jnp.broadcast_to(long_row(ref, b, length), (LANES, length)).T
 
     def widened(column, size):
         return jnp.concatenate([column] * (size // LANES), axis=1)
+
+    pl.semaphore_wait(
+        barrier,
+        expected + 2 + (place > 0).astype(jnp.int32) + (place < n - 1).astype(jnp.int32),
+    )
+
+    pairs = channels // LANES
+    first_slot, lag_slots = 7, 6
+
+    def chain_slot(i):
+        chain.slot(i, first_slot, lag_slots)
 
     def gated_norm(b):
         for i in range(3):
@@ -994,7 +1321,8 @@
             jnp.exp(cumulative_ref[b]) * (column < begin).astype(f32), marks
         )
         passed[b] = entering[length - 8 :]
-        for at, size in blocks(channels):
+        column_blocks = blocks(channels)
+        for k, (at, size) in enumerate(column_blocks):
             lanes = slice(at, at + size)
             grad_rows = jnp.zeros((length, size), f32)
             for j in range(groups):
@@ -1019,52 +1347,41 @@
             gate_grad[b, :, lanes] = (gated_grad * value * slope).astype(bf16)
             values = conv[b, :, lanes]
             heads_in[b, :, lanes] = values * jax.nn.sigmoid(values)
+            chain_slot(4 * b + k)
         store(0, b).start()
-        store(1, b).start()
         values = conv[b, :, channels : channels + STATE]
         keys[b] = (values * jax.nn.sigmoid(values)).astype(bf16)
         values = conv[b, :, channels + STATE :]
         queries[b] = (values * jax.nn.sigmoid(values)).astype(bf16)
         locals_[b] = dot_tn(queries[b], (heads_grad[b] * entering).astype(bf16))
+        chain.offer(b)
+        for k in range(len(column_blocks), 4):
+            chain_slot(4 * b + k)
 
     loop(count, gated_norm)
-    pl.semaphore_wait(barrier, (place > 0).astype(jnp.int32) + (place < n - 1).astype(jnp.int32))
-
-    def chain_copy(c):
-        part = (lax.div(c, 4), pl.ds(pl.multiple_of(lax.rem(c, 4) * chunk_rows, chunk_rows), chunk_rows))
-        return remote(
-            outgoing.at[part], held.at[part], chain_send.at[c], chain_recv.at[c], (place - 1, head)
-        )
-
-    def chain_step(c):
-        b = lax.div(c, 4)
-        rows = pl.ds(pl.multiple_of(lax.rem(c, 4) * chunk_rows, chunk_rows), chunk_rows)
-
-        @pl.when(ahead > 0)
-        def _():
-            chain_copy(c).wait_recv()
-
-        @pl.when(ahead == 0)
-        def _():
-            held[b, rows] = jnp.zeros((chunk_rows, channels), bf16)
-
-        outgoing[b, rows] = (
-            passed[b, 7:8] * held[b, rows].astype(f32) + locals_[b, rows]
-        ).astype(bf16)
-
-        @pl.when(place > 0)
-        def _():
-            chain_copy(c).start()
-
-    pairs = channels // LANES
-    lag_slots = 4
-
-    def chain_slot(i):
-        c = i - lag_slots * ahead
-
-        @pl.when((c >= 0) & (c < chunks))
-        def _():
-            chain_step(c)
+
+    slot = 4 * count
+    for j in range(groups):
+        grads = jnp.concatenate([normed_out[b] for b in range(count)], axis=0)
+        out_part[j * width : (j + 1) * width] = dot_tn(pieces[j], grads).astype(bf16)
+        chain_slot(slot + j)
+    slot += groups
+    ring.start(0)
+    ring.start(1)
+    loads[2].wait()
+    gate_blocks = D // 256
+
+    def gate_block(i):
+        block = pl.ds(pl.multiple_of(i * 256, 256), 256)
+        rows = jnp.concatenate([normed[b, :, block] for b in range(count)], axis=0)
+        grads = jnp.concatenate([gate_grad[b] for b in range(count)], axis=0)
+        gate_part[block] = dot_tn(rows, grads).astype(bf16)
+        chain_slot(slot + i)
+
+    loop(gate_blocks, gate_block)
+    slot += gate_blocks
+    ring.start(2)
+    ring.start(3)
 
     first_half = lax.broadcasted_iota(jnp.int32, (length, LANES), 1) < HEADDIM
 
@@ -1095,14 +1412,21 @@
                 pairwise = dot_nt(jnp.where(mine, scaled, 0.0).astype(bf16), low_grads)
                 scores_grad[...] += decay * pairwise
             inner[b, :, lanes] = value
-            chain_slot(b * (pairs + 1) + pair)
+            chain_slot(slot + b * (pairs + 1) + pair)
+            if pair == 1:
+                pass_on(0, b)
+            if pair == pairs - 2:
+                pass_on(2, b)
         low = scores_grad[...].astype(bf16)
         narrow_grad[b, :, :STATE] = jnp.dot(low, queries[b], preferred_element_type=f32)
         narrow_grad[b, :, STATE:] = dot_tn(low, keys[b])
-        chain_slot(b * (pairs + 1) + pairs)
+        chain_slot(slot + b * (pairs + 1) + pairs)
 
     loop(count, inside)
-    done = count * (pairs + 1)
+    done = slot + count * (pairs + 1)
+    slots = chain.slots(first_slot, lag_slots)
+    if slots > done:
+        loop(slots - done, lambda i: chain_slot(i + done))
     extended[0:16] = jnp.zeros((16, both), f32)
     spread_grad[0:16] = jnp.zeros((16, both), f32)
     spread_grad[16 + length :] = jnp.zeros((16, both), f32)
@@ -1117,9 +1441,7 @@
         return remote(edge.at[b], edge_in.at[b], edge_send.at[b], edge_recv.at[b], (place - 1, head))
 
     def close(b):
-        need = lag_slots * ahead + 4 * (b + 1)
-        start = jnp.maximum(done, lag_slots * ahead + 4 * b)
-        lax.fori_loop(start, jnp.maximum(start, need), lambda i, x: (chain_slot(i), x)[1], 0)
+        pass_on(0, count + b)
         column, spot = position_masks(docs_ref[pl.ds(b, 1)].astype(f32), begin)
         cumulative = cumulative_ref[b]
         steps = steps_ref[b]
@@ -1128,7 +1450,8 @@
         entering = jnp.exp(cumulative) * kept
         end_decay = jnp.exp(cumulative[length - 1 :] - cumulative) * trailing
         end_weight = end_decay * steps
-        end_grad = held[b]
+        chain.ready(b)
+        end_grad = state[b]
         x = heads_in[b]
         dy = heads_grad[b]
         grown = jnp.dot(keys[b], end_grad, preferred_element_type=f32)
@@ -1157,6 +1480,7 @@
         vector_grad_out[1:2] += jnp.sum(rates_grad * steps, axis=0, keepdims=True) * decay_rate
         vector_grad_out[2:3] += jnp.sum(dot_skip, axis=0, keepdims=True)
 
+        pass_on(2, count + b)
         row_load(3, b).wait()
         extended[0:16] = halo_ref[pl.ds(pl.multiple_of(b * 16, 16), 16)].astype(f32)
         extended[16:] = linear[b].astype(f32)
@@ -1218,15 +1542,31 @@
             values_grad[b, last] = tails[b, :, :channels].astype(bf16)
             narrow[b, last, : 2 * STATE] = tails[b, :, channels:].astype(bf16)
 
+        store(1, b).start()
         store(2, b).start()
-        store(3, b).start()
 
     loop(count, finish)
+
+    if ring_steps > 2 * count:
+
+        def further(s):
+            pass_on(0, 2 * count + s)
+            pass_on(2, 2 * count + s)
+
+        loop(ring_steps - 2 * count, further)
+    cut = os0.shape[2]
+    out_total[:, :cut] = ring.last(0)
+    out_total[:, cut:] = ring.last(1)
+    gate_total[:, :cut] = ring.last(2)
+    gate_total[:, cut:] = ring.last(3)
+    for i in range(4):
+        ring.finish(i)
 
     @pl.when(place > 0)
     def _():
         loop(count, lambda b: edge_copy(b).wait_send())
-        loop(chunks, lambda c: chain_copy(c).wait_send())
+
+    chain.finish()
 
     for i in range(len(stores)):
         loop(count, lambda b, i=i: store(i, b).wait())
@@ -1239,6 +1579,7 @@
     mixed,
     conv,
     linear,
+    normed,
     halo,
     state_in,
     steps,
@@ -1257,22 +1598,28 @@
     both = channels + 2 * STATE
     lags = value_conv_weight.shape[0]
     weight = blocked(weight, pieces.shape[0])
-    chunks = count * 4
     dma = pltpu.SemaphoreType.DMA
     hbm = pl.BlockSpec(memory_space=pl.ANY)
     shape = jax.ShapeDtypeStruct
     vmem = pltpu.VMEM
+    n = lax.axis_size("seq")
+    own = D // n
     big = [
-        ((count, length, channels), bf16),
         ((count, length, channels), bf16),
         ((count, length, channels), bf16),
         ((count, length, 2 * STATE + LANES), bf16),
     ]
-    small = [((8, both), f32), ((8, LANES), f32), ((1, channels), f32)]
+    small = [
+        ((8, both), f32),
+        ((8, LANES), f32),
+        ((1, channels), f32),
+        ((own, channels), f32),
+        ((own, channels), f32),
+    ]
     return pl.pallas_call(
         back_kernel,
         out_shape=[shape(*s) for s in big + small],
-        in_specs=[hbm] * 6 + [in_vmem] * 14,
+        in_specs=[hbm] * 7 + [in_vmem] * 14,
         out_specs=[hbm] * len(big) + [in_vmem] * len(small),
         scratch_shapes=[
             vmem(pieces.shape, bf16),
@@ -1281,8 +1628,12 @@
             vmem(mixed.shape, f32),
             vmem(conv.shape, f32),
             vmem(linear.shape, bf16),
+            vmem(normed.shape, bf16),
+            vmem((count, length, channels), bf16),
         ]
         + [vmem(*s) for s in big]
+        + [vmem((D, channels), bf16), vmem((D, channels), bf16)]
+        + ring_slots(n, own, channels, bf16) * 2
         + [
             vmem((count, length, channels), f32),
             vmem((count, length, channels), f32),
@@ -1291,11 +1642,11 @@
             vmem((length, length), f32),
             vmem((length, length), f32),
             vmem((length, length), f32),
-            vmem((count, length, channels), f32),
             vmem((count, length, 2 * STATE), f32),
             vmem((count, STATE, channels), f32),
-            vmem((count, STATE, channels), bf16),
-            vmem((count, STATE, channels), bf16),
+        ]
+        + chain_buffers(count, channels)
+        + [
             vmem((count, 8, channels), f32),
             vmem((length + 16, both), f32),
             vmem((length + 32, both), f32),
@@ -1303,13 +1654,15 @@
             vmem((count, 8, both), f32),
             vmem((count, 8, both), f32),
             vmem((count, 16, both), f32),
-            dma((2,)),
+            dma((3,)),
             dma((4, count)),
             dma((len(big), count)),
             dma((count,)),
             dma((count,)),
-            dma((chunks,)),
-            dma((chunks,)),
+            dma((3, count)),
+            dma((3, count)),
+            dma((4, n - 1)),
+            dma((4, n - 1)),
         ],
         compiler_params=params(cid),
         name="back",
@@ -1320,6 +1673,7 @@
         mixed,
         conv,
         linear,
+        normed,
         halo,
         state_in,
         steps,
@@ -1333,63 +1687,6 @@
         keyquery_conv_weight,
         norm_gain,
     )
-
-
-class Ring:
-    def __init__(self, streams, send_sem, recv_sem):
-        self.n = lax.axis_size("seq")
-        self.streams, self.send_sem, self.recv_sem = streams, send_sem, recv_sem
-        head = lax.axis_index("head")
-        self.spot = ring_place(self.n, lax.axis_index("seq"))
-        self.after = (ring_index(self.n, lax.rem(self.spot + 1, self.n)), head)
-        self.before = (ring_index(self.n, lax.rem(self.spot + self.n - 1, self.n)), head)
-
-    def piece(self, i, step):
-        part, _, columns, way = self.streams[i]
-        shift = -1 - step if way == 0 else 1 + step
-        rows = part.shape[0] // self.n
-        index = ring_index(self.n, lax.rem(self.spot + shift + 2 * self.n, self.n))
-        return part.at[pl.ds(pl.multiple_of(index * rows, rows), rows), columns]
-
-    def copy(self, i, step, source):
-        slots, way = self.streams[i][1], self.streams[i][3]
-        return remote(
-            source,
-            slots.at[step],
-            self.send_sem.at[i, step],
-            self.recv_sem.at[i, step],
-            self.after if way == 0 else self.before,
-        )
-
-    def start(self, i):
-        self.copy(i, 0, self.piece(i, 0)).start()
-
-    def pass_on(self, i, step):
-        slots = self.streams[i][1]
-        self.copy(i, step, slots.at[step]).wait_recv()
-        total = slots[step].astype(f32) + self.piece(i, step + 1)[...].astype(f32)
-        slots[step] = total.astype(slots.dtype)
-        self.copy(i, step + 1, slots.at[step]).start()
-
-    def last(self, i):
-        slots, step = self.streams[i][1], self.n - 2
-        self.copy(i, step, slots.at[step]).wait_recv()
-        return slots[step].astype(f32) + self.piece(i, step + 1)[...].astype(f32)
-
-    def finish(self, i):
-        slots = self.streams[i][1]
-        self.copy(i, 0, self.piece(i, 0)).wait_send()
-        loop(self.n - 2, lambda step: self.copy(i, step + 1, slots.at[step]).wait_send())
-
-
-def ring_streams(part, slots):
-    cut, width = slots[0].shape[2], part.shape[1]
-    return [(part, slots[0], pl.ds(0, cut), 0), (part, slots[1], pl.ds(cut, width - cut), 1)]
-
-
-def ring_slots(n, rows, width, kind):
-    cut = width // LANES // 2 * LANES
-    return [pltpu.VMEM((n - 1, rows, cut), kind), pltpu.VMEM((n - 1, rows, width - cut), kind)]
 
 
 class Doubling:
@@ -1456,8 +1753,6 @@
     values_grad_hbm,
     narrow_hbm,
     gate_grad_hbm,
-    pieces_hbm,
-    normed_out_hbm,
     value_weight_hbm,
     gate_weight_hbm,
     keyquery_weight_hbm,
@@ -1474,8 +1769,6 @@
     loss_cols_ref,
     tokens_grad_out,
     value_out,
-    gate_out,
-    out_out,
     keyquery_out,
     step_out,
     value_conv_out,
@@ -1492,21 +1785,13 @@
     values_grad,
     narrow,
     gate_grad,
-    pieces,
-    normed_out,
     value_weight,
     gate_weight,
     keyquery_weight,
     value_part,
-    gate_part,
-    out_part,
     keyquery_part,
     vs0,
     vs1,
-    gs0,
-    gs1,
-    os0,
-    os1,
     ks0,
     ks1,
     step_whole,
@@ -1563,8 +1848,6 @@
                 (gate_grad_hbm, gate_grad),
                 (gate_weight_hbm, gate_weight),
                 (keyquery_weight_hbm, keyquery_weight),
-                (pieces_hbm, pieces),
-                (normed_out_hbm, normed_out),
             ]
         )
     ]
@@ -1583,9 +1866,7 @@
 
     ring = Ring(
         ring_streams(value_part, (vs0, vs1))
-        + ring_streams(keyquery_part, (ks0, ks1))
-        + ring_streams(gate_part, (gs0, gs1))
-        + ring_streams(out_part, (os0, os1)),
+        + ring_streams(keyquery_part, (ks0, ks1)),
         ring_send,
         ring_recv,
     )
@@ -1610,17 +1891,6 @@
     weight_block(keyquery_part, narrow.at[:, : 2 * STATE])
     ring.start(2)
     ring.start(3)
-    loads[4].wait()
-    weight_block(gate_part, gate_grad)
-    ring.start(4)
-    ring.start(5)
-    loads[7].wait()
-    loads[8].wait()
-    for j in range(heads_n):
-        out_part[j * width : (j + 1) * width] = dot_tn(pieces[j], normed_out[...]).astype(bf16)
-    ring.start(6)
-    ring.start(7)
-
     step_rows = D // n
     for at, size in blocks(D):
         step_whole[:, at : at + size] = dot_tn(narrow[:, 2 * STATE :], normed[:, at : at + size])
@@ -1640,7 +1910,7 @@
     for k in range(1, n):
         step_copy(k, lax.rem(place + k, n), place).start()
 
-    for i in (3, 5, 6):
+    for i in (3, 4, 5, 6):
         loads[i].wait()
     columns[...] = jnp.zeros_like(columns)
 
@@ -1759,10 +2029,6 @@
     cut = vs0.shape[2]
     value_out[:, :cut] = ring.last(0)
     value_out[:, cut:] = ring.last(1)
-    gate_out[:, :cut] = ring.last(4)
-    gate_out[:, cut:] = ring.last(5)
-    out_out[:, :cut] = ring.last(6)
-    out_out[:, cut:] = ring.last(7)
 
     for k in range(1, n):
         sender = lax.rem(place + k, n)
@@ -1798,8 +2064,6 @@
     values_grad,
     narrow,
     gate_grad,
-    pieces,
-    normed_out,
     value_weight,
     gate_weight,
     keyquery_weight,
@@ -1836,8 +2100,6 @@
     outs = [
         (rows, width),
         (own, channels),
-        (own, channels),
-        (own, channels),
         (own, 2 * STATE),
         (heads, own),
         (lags, channels),
@@ -1855,7 +2117,7 @@
     return pl.pallas_call(
         functools.partial(tail_kernel, heads),
         out_shape=[shape(s, f32) for s in outs],
-        in_specs=[hbm] * 9 + [in_vmem] * 11,
+        in_specs=[hbm] * 7 + [in_vmem] * 11,
         out_specs=[in_vmem] * len(outs),
         scratch_shapes=[
             vmem(a.shape, a.dtype)
@@ -1864,8 +2126,6 @@
                 values_grad,
                 narrow,
                 gate_grad,
-                pieces,
-                normed_out,
                 value_weight,
                 gate_weight,
                 keyquery_weight,
@@ -1873,11 +2133,9 @@
         ]
         + [
             vmem((D, channels), bf16),
-            vmem((D, channels), bf16),
-            vmem((D, channels), bf16),
             vmem((D, 2 * STATE), f32),
         ]
-        + slots * 3
+        + slots
         + ring_slots(n, own, 2 * STATE, f32)
         + [
             vmem((LANES, D), f32),
@@ -1894,9 +2152,9 @@
         + buffers
         + [vmem((heads_n, count, length), f32), vmem((count, length), f32)]
         + [
-            dma((9,)),
-            dma((8, n - 1)),
-            dma((8, n - 1)),
+            dma((7,)),
+            dma((4, n - 1)),
+            dma((4, n - 1)),
             dma((n - 1,)),
             dma((n,)),
             dma((head_stages,)),
@@ -1915,8 +2173,6 @@
         values_grad,
         narrow,
         gate_grad,
-        pieces,
-        normed_out,
         value_weight,
         gate_weight,
         keyquery_weight,
@@ -2011,13 +2267,14 @@
         gained.reshape(rows, channels), out_weight, square_rows, tokens, teacher, mask_rows, 2
     )
     (
-        normed_out,
         gate_grad,
         values_grad,
         narrow_grad,
         conv_grad,
         vector_grad,
         gain_grad,
+        out_total,
+        gate_total,
     ) = back(
         pieces,
         out_weight,
@@ -2025,6 +2282,7 @@
         mixed,
         conv_linear,
         linear,
+        normed,
         halo,
         state_in,
         steps,
@@ -2042,8 +2300,6 @@
     (
         tokens_grad,
         value_total,
-        gate_total,
-        out_total,
         keyquery_total,
         step_total,
         value_conv_total,
@@ -2061,8 +2317,6 @@
         values_grad.reshape(rows, channels),
         narrow_grad.reshape(rows, -1),
         gate_grad.reshape(rows, channels),
-        pieces,
-        normed_out.reshape(rows, channels),
         value_weight,
         gate_weight,
         keyquery_weight,

time: 310 us -> 269 us (0.87)
  Pallas kernels: 306 us -> 265 us
    pallas_call x1, Pallas kernels: 110 us -> 69.8 us  [tail(): pl.pallas_call(functools.partial(tail_kernel, heads), out_shape=[shape(s,...]
    pallas_call x1, Pallas kernels: 103 us -> 95.9 us  [back(): pl.pallas_call(back_kernel, out_shape=[shape(*s) for s in big + small], i...]
    pallas_call x1, Pallas kernels: 39.1 us -> 45.6 us  [front(): pl.pallas_call(functools.partial(front_kernel, heads), out_shape=[shape(*...]
where the time goes in v4:
time: 269 us
  Pallas kernels  265 us (99%)
    pallas_call x1, Pallas kernels, back(): pl.pallas_call(back_kernel, out_shape=[shape(*s) for s in big + small], i...  95.9 us
    pallas_call x1, Pallas kernels, tail(): pl.pallas_call(functools.partial(tail_kernel, heads), out_shape=[shape(s,...  69.8 us
    pallas_call x1, Pallas kernels, out_phase(): pl.pallas_call(functools.partial(out_kernel, n), out_shape=[jax.ShapeDtyp...  47.9 us
    pallas_call x1, Pallas kernels, front(): pl.pallas_call(functools.partial(front_kernel, heads), out_shape=[shape(*...  45.6 us
    pallas_call x1, Pallas kernels, deliver(): pl.pallas_call(functools.partial(deliver_kernel, len(arrays)), out_shape=...  5.52 us

profile of v4, /device:TPU:0, one launch (start us, length us, event | category | flops | bytes accessed | tf_op | source)
XLA Modules:
  0.0 269.1 jit_solution(10985522937398507117)
XLA Ops:
  0.7 1.4 convert_reduce_fusion
  2.7 0.7 convert_multiply_fusion
  3.4 0.6 reshape.62.mask_ref
  4.0 45.6 %front.1 = (bf16[4,256,1536]{2,1,0:T(8,128)(2,1)}, bf16[4,256,1024]{2,1,0:T(8,128)(2,1)}, f32[4,256,1024]{2,1,0:T(8,128)}, f32[4,256,768]{2,1,0:T(8,128)}, f32[4...) custom-call(f32[4,256,1536]{2,1,0:T(8,128)} %tokens_hbm.3, ...), custom_call_target="tpu_custom_call" | custom-call | tf_op jit(solution)/shard_map/front/pallas_call | solution.py:1074
  49.6 47.9 %out_phase.1 = (f32[1024,384]{1,0:T(8,128)}, bf16[4,1024,384]{2,1,0:T(8,128)(2,1)}, f32[8,128]{1,0:T(8,128)}, f32[8,128]{1,0:T(8,128)}, f32[1,384]{1,0:T(1,128)}, /*index=5*/f32[4,256,384]{2,1,0:T(8,128)}) custom-call(bf16[1024,768]{1,0:T(8,128)(2,1)} %bitcast.15, bf16[768,1536]{1,0:T(8,128)(2,1)} %weight_hbm.1, f32[8,128]{1,0:T(8,128)} %get-tuple-element.76.square_ref, ...), custom_call_target="tpu_custom_call" | custom-call | tf_op jit(solution)/shard_map/out_phase/pallas_call | solution.py:602
  97.6 95.9 %back.1 = (bf16[4,256,768]{2,1,0:T(8,128)(2,1)}, bf16[4,256,768]{2,1,0:T(8,128)(2,1)}, bf16[4,256,384]{2,1,0:T(8,128)(2,1)}, f32[8,1024]{1,0:T(8,128)}, f32[8,12...) custom-call(bf16[4,1024,384]{2,1,0:T(8,128)(2,1)} %get-tuple-element.79.pieces_hbm, ...), custom_call_target="tpu_custom_call" | custom-call | tf_op jit(solution)/shard_map/back/pallas_call | solution.py:1619
  193.5 69.8 %tail.1 = (f32[1024,384]{1,0:T(8,128)}, f32[192,768]{1,0:T(8,128)}, f32[192,256]{1,0:T(8,128)}, f32[12,192]{1,0:T(8,128)}, f32[4,768]{1,0:T(4,128)}, /*index=5*/...) custom-call(bf16[1024,1536]{1,0:T(8,128)(2,1)} %bitcast.11, ...), custom_call_target="tpu_custom_call" | custom-call | tf_op jit(solution)/shard_map/tail/pallas_call | solution.py:2117
  263.3 5.5 %deliver.1 = (f32[4,256,384]{2,1,0:T(8,128)}, f32[1]{0:T(128)}, f32[4,256,384]{2,1,0:T(8,128)}, f32[384]{0:T(512)}, f32[192,768]{1,0:T(8,128)}, /*index=5*/f32[1...) custom-call(f32[4,256,384]{2,1,0:T(8,128)} %bitcast.12, ...), custom_call_target="tpu_custom_call" | custom-call | tf_op jit(solution)/shard_map/deliver/pallas_call | solution.py:2199

commit v5 on v1

v5 whole, which is shorter than its diff:
```python
import functools
import types

import jax
import jax.numpy as jnp
from jax import lax
from jax.experimental import pallas as pl
from jax.experimental.pallas import tpu as pltpu
from jax.sharding import PartitionSpec as P

D = 1536
NHEADS = 48
HEADDIM = 64
STATE = 128
LANES = 128
VMEM_LIMIT = 62 << 20

norm_eps = 1e-05
highest = lax.Precision.HIGHEST
MESH = pl.DeviceIdType.MESH
f32 = jnp.float32
bf16 = jnp.bfloat16
NT = (((1,), (1,)), ((), ()))
TN = (((0,), (0,)), ((), ()))

in_vmem = pl.BlockSpec(memory_space=pltpu.VMEM)
in_smem = pl.BlockSpec(memory_space=pltpu.SMEM)


def params(cid):
    return pltpu.CompilerParams(
        collective_id=cid, has_side_effects=True, vmem_limit_bytes=VMEM_LIMIT
    )


def remote(src, dst, send, recv, target):
    return pltpu.make_async_remote_copy(
        src_ref=src,
        dst_ref=dst,
        send_sem=send,
        recv_sem=recv,
        device_id=target,
        device_id_type=MESH,
    )


def loop(count, fn):
    lax.fori_loop(0, count, lambda i, c: (fn(i), c)[1], 0)


def dot_nt(a, b, precision=None):
    return lax.dot_general(a, b, NT, precision=precision, preferred_element_type=f32)


def dot_tn(a, b, precision=None):
    return lax.dot_general(a, b, TN, precision=precision, preferred_element_type=f32)


def ring_place(n, index):
    odd, half = lax.rem(index, 2), lax.div(index, 2)
    return half * (1 - odd) + (n - 1 - half) * odd


def ring_index(n, spot):
    late = lax.div(2 * spot, n)
    return 2 * spot * (1 - late) + (2 * (n - 1 - spot) + 1) * late


class Ring:
    def __init__(self, send_sem, recv_sem):
        self.n = lax.axis_size("seq")
        self.streams, self.send_sem, self.recv_sem = [], send_sem, recv_sem
        head = lax.axis_index("head")
        self.spot = ring_place(self.n, lax.axis_index("seq"))
        self.after = (ring_index(self.n, lax.rem(self.spot + 1, self.n)), head)
        self.before = (ring_index(self.n, lax.rem(self.spot + self.n - 1, self.n)), head)

    def add(self, part, slots, by_rows=False, first=0):
        rows, width = part.shape[0] // self.n, part.shape[1]
        cut = slots[0].shape[1] if by_rows else slots[0].shape[2]
        if by_rows:
            halves = tuple(((first + way * cut, cut), (0, width)) for way in range(2))
        else:
            halves = (((0, rows), (0, cut)), ((0, rows), (cut, width - cut)))
        for way in range(2):
            lines, columns = halves[way]
            self.streams.append((part, slots[way], lines, pl.ds(*columns), way))

    def piece(self, i, step):
        part, _, (first, count), columns, way = self.streams[i]
        shift = -1 - step if way == 0 else 1 + step
        rows = part.shape[0] // self.n
        index = ring_index(self.n, lax.rem(self.spot + shift + 2 * self.n, self.n))
        return part.at[pl.ds(pl.multiple_of(index * rows + first, 8), count), columns]

    def copy(self, i, step, source):
        slots, way = self.streams[i][1], self.streams[i][4]
        return remote(
            source,
            slots.at[step],
            self.send_sem.at[i, step],
            self.recv_sem.at[i, step],
            self.after if way == 0 else self.before,
        )

    def start(self, i):
        self.copy(i, 0, self.piece(i, 0)).start()

    def pass_on(self, i, step):
        slots = self.streams[i][1]
        self.copy(i, step, slots.at[step]).wait_recv()
        total = slots[step].astype(f32) + self.piece(i, step + 1)[...].astype(f32)
        slots[step] = total.astype(slots.dtype)
        self.copy(i, step + 1, slots.at[step]).start()

    def last(self, i):
        slots, step = self.streams[i][1], self.n - 2
        self.copy(i, step, slots.at[step]).wait_recv()
        return slots[step].astype(f32) + self.piece(i, step + 1)[...].astype(f32)

    def finish(self, i):
        slots = self.streams[i][1]
        self.copy(i, 0, self.piece(i, 0)).wait_send()
        loop(self.n - 2, lambda step: self.copy(i, step + 1, slots.at[step]).wait_send())


def ring_slots(n, rows, width, kind):
    cut = width // LANES // 2 * LANES
    return [pltpu.VMEM((n - 1, rows, cut), kind), pltpu.VMEM((n - 1, rows, width - cut), kind)]


def step_at(table, here):
    found, here = jnp.int32(-1), jnp.asarray(here, jnp.int32)
    for place, step in table:
        found = found + (step + 1) * (here == place).astype(jnp.int32)
    return found


def sequence_at(table, here, pair):
    found, here = jnp.int32(-1), jnp.asarray(here, jnp.int32)
    for place, owner, b in table:
        found = found + (b + 1) * ((here == place) & (pair == owner)).astype(jnp.int32)
    return found


class PairChain:
    def __init__(self, ahead, by, local, passed, buffers, send_sem, recv_sem):
        self.n = lax.axis_size("seq")
        self.place, self.head = lax.axis_index("seq"), lax.axis_index("head")
        self.by, self.pair, self.second = by, lax.div(ahead, 2), lax.rem(ahead, 2)
        self.local, self.passed = local, passed
        self.state, self.offers, self.offered, self.hand, self.following = buffers
        self.send_sem, self.recv_sem = send_sem, recv_sem
        self.count, _, channels = self.state.shape
        cut = channels // LANES // 2 * LANES
        self.sizes = (channels - cut, cut)
        self.lanes = (pl.ds(cut, channels - cut), pl.ds(0, cut))

    def copy(self, kind, b, source, target, ahead):
        return remote(
            source,
            target,
            self.send_sem.at[kind, b],
            self.recv_sem.at[kind, b],
            (self.place + self.by * ahead, self.head),
        )

    def within(self, buffer, b, second):
        return buffer.at[b, pl.ds(0, buffer.shape[1]), pl.ds(0, self.sizes[second])]

    def offering(self, b, second):
        other = 1 - second
        return self.copy(
            0,
            b,
            self.within(self.offers, b, other),
            self.within(self.offered, b, other),
            1 - 2 * second,
        )

    def handing(self, b, second):
        target = self.state.at[b, pl.ds(0, STATE), self.lanes[second]]
        return self.copy(1, b, self.within(self.hand, b, second), target, 1 - 2 * second)

    def passing(self, b, second):
        if second:
            target = self.within(self.hand, b, second)
        else:
            target = self.state.at[b, pl.ds(0, STATE), self.lanes[second]]
        return self.copy(2, b, self.within(self.following, b, second), target, 2)

    def offer(self, b):
        for second in range(2):

            @pl.when(self.second == second)
            def _():
                other = 1 - second
                lanes, size = self.lanes[other], self.sizes[other]
                self.offers[b, :STATE, :size] = self.local[b, :, lanes].astype(bf16)
                decay = self.passed[b, 7:8, lanes]
                high = decay.astype(bf16).astype(f32)
                row = lax.broadcasted_iota(jnp.int32, (16, size), 0)
                rows = jnp.where(row == 0, high, jnp.where(row == 1, decay - high, 0.0))
                self.offers[b, STATE:, :size] = rows.astype(bf16)
                self.offering(b, second).start()

    def pass_on(self, b):
        more = self.pair < self.n // 2 - 1
        for second in range(2):

            @pl.when(self.second == second)
            def _():
                lanes, size = self.lanes[second], self.sizes[second]
                self.offering(b, 1 - second).wait_recv()

                @pl.when(self.pair > 0)
                def _():
                    self.passing(b, second).wait_recv()

                @pl.when(self.pair == 0)
                def _():
                    zeros = jnp.zeros((STATE, size), bf16)
                    if second:
                        self.hand[b, :, :size] = zeros
                    else:
                        self.state[b, :, lanes] = zeros

                own_decay, own = self.passed[b, 7:8, lanes], self.local[b, :, lanes]
                decay = self.offered[b, STATE:, :size].astype(f32)
                decay = decay[0:1] + decay[1:2]
                offered = self.offered[b, :STATE, :size].astype(f32)
                if second:
                    self.handing(b, second).start()
                    value = decay * self.hand[b, :, :size].astype(f32) + offered
                    self.state[b, :, lanes] = value.astype(bf16)
                    following = own_decay * value + own
                else:
                    value = own_decay * self.state[b, :, lanes].astype(f32) + own
                    self.hand[b, :, :size] = value.astype(bf16)
                    self.handing(b, second).start()
                    following = decay * value + offered

                @pl.when(more)
                def _():
                    self.following[b, :, :size] = following.astype(bf16)
                    self.passing(b, second).start()

    def ready(self, b):
        for second in range(2):

            @pl.when(self.second == second)
            def _():
                self.handing(b, 1 - second).wait_recv()

    def turn(self, here, table):
        b = sequence_at(table, here, self.pair)

        @pl.when(b >= 0)
        def _():
            self.pass_on(b)

    def rest(self, table):
        held = {(pair, b) for _, pair, b in table}
        for pair in range(self.n // 2):
            for b in range(self.count):
                if (pair, b) not in held:

                    @pl.when(self.pair == pair)
                    def _():
                        self.pass_on(b)

    def finish(self):
        for second in range(2):

            @pl.when(self.second == second)
            def _():
                def one(b):
                    self.offering(b, second).wait_send()
                    self.handing(b, second).wait_send()

                    @pl.when(self.pair < self.n // 2 - 1)
                    def _():
                        self.passing(b, second).wait_send()

                loop(self.count, one)


def chain_buffers(count, channels):
    wide = channels - channels // LANES // 2 * LANES
    shapes = [(STATE, channels), (STATE + 16, wide), (STATE + 16, wide), (STATE, wide), (STATE, wide)]
    return [pltpu.VMEM((count,) + s, bf16) for s in shapes]


class Group:
    def __init__(self, n):
        self.n = n
        self.chips = n // 2
        self.seq = lax.axis_index("seq")
        self.me = lax.axis_index("head")
        self.chip = lax.div(self.me, 2)
        self.core = lax.rem(self.me, 2)
        self.mate = self.me + 1 - 2 * self.core

    def at(self, head):
        return (self.seq, head)

    def chip_after(self, k):
        return lax.rem(self.chip + k, self.chips)

    def chip_before(self, k):
        return lax.rem(self.chip + self.chips - k, self.chips)

    def peer(self, k):
        return 2 * self.chip_after(k) + self.core

    def other(self, k):
        return lax.rem(self.me + k, self.n)

    def greet(self):
        barrier = pltpu.get_barrier_semaphore()
        for k in range(1, self.n):
            pl.semaphore_signal(
                barrier, inc=1, device_id=self.at(self.other(k)), device_id_type=MESH
            )
        pl.semaphore_wait(barrier, self.n - 1)


def share(group, source, table, send_sem, recv_sem):
    for k in range(1, group.n):
        remote(
            source,
            table.at[group.me],
            send_sem.at[k - 1],
            recv_sem.at[group.me],
            group.at(group.other(k)),
        ).start()


def shared(group, source, table, send_sem, recv_sem):
    for k in range(1, group.n):
        sender = group.other(k)
        copy = remote(
            source, table.at[sender], send_sem.at[k - 1], recv_sem.at[sender], group.at(sender)
        )
        copy.wait_send()
        copy.wait_recv()


def row_tile(chunk):
    return pl.ds(pl.multiple_of(chunk * LANES, LANES), LANES)


def as_column(row, width):
    tile = jnp.broadcast_to(row, (LANES, row.shape[1])).T
    return jnp.concatenate([tile] * (-(-width // LANES)), axis=1)[:, :width]


def scatter_phases(group, row_block, part, mate_in, chip_out, chip_in, sems):
    mate_send, mate_recv, chip_send, chip_recv = sems

    def mate_copy(c, x):
        return remote(
            part.at[2 * x + 1 - group.core, row_block(c)],
            mate_in.at[x, row_block(c)],
            mate_send.at[x, c],
            mate_recv.at[x, c],
            group.at(group.mate),
        )

    def chip_copy(c, k):
        return remote(
            chip_out.at[k - 1, row_block(c)],
            chip_in.at[k - 1, row_block(c)],
            chip_send.at[k - 1, c],
            chip_recv.at[k - 1, c],
            group.at(group.peer(k)),
        )

    def start_mate(c):
        for x in range(group.chips):
            mate_copy(c, x).start()

    def start_chip(c):
        for x in range(group.chips):
            mate_copy(c, x).wait_recv()
        for k in range(1, group.chips):
            x = group.chip_after(k)
            both = part[2 * x + group.core, row_block(c)].astype(f32) + mate_in[
                x, row_block(c)
            ].astype(f32)
            chip_out[k - 1, row_block(c)] = both.astype(bf16)
            chip_copy(c, k).start()

    def total(c):
        value = part[group.me, row_block(c)].astype(f32) + mate_in[
            group.chip, row_block(c)
        ].astype(f32)
        for k in range(1, group.chips):
            chip_copy(c, k).wait_recv()
            value = value + chip_in[k - 1, row_block(c)].astype(f32)
        return value

    def finish(c):
        for x in range(group.chips):
            mate_copy(c, x).wait_send()
        for k in range(1, group.chips):
            chip_copy(c, k).wait_send()

    return start_mate, start_chip, total, finish


def out_kernel(
    n,
    gated_ref,
    weight_ref,
    square_ref,
    tokens_hbm,
    teacher_hbm,
    mask_ref,
    output_ref,
    grad_ref,
    rowdot_ref,
    squared_ref,
    loss_ref,
    tokens_out,
    tokens_ref,
    teacher_ref,
    part,
    mate_in,
    chip_out,
    chip_in,
    gathered,
    squares,
    dots,
    dot_out,
    mate_send,
    mate_recv,
    chip_send,
    chip_recv,
    gm_send,
    gm_recv,
    gc_send,
    gc_recv,
    gf_send,
    gf_recv,
    sq_send,
    sq_recv,
    rd_send,
    rd_recv,
    load_sem,
):
    group = Group(n)
    count, length, width = tokens_ref.shape
    if tokens_hbm.shape[2] == width:
        token_columns = tokens_hbm
    else:
        start = pl.multiple_of(group.me * width, LANES)
        token_columns = tokens_hbm.at[:, :, pl.ds(start, width)]
    token_load = pltpu.make_async_copy(token_columns, tokens_ref, load_sem.at[0])
    token_load.start()
    teacher_load = pltpu.make_async_copy(teacher_hbm, teacher_ref, load_sem.at[1])
    teacher_load.start()
    group.greet()
    chunks = gated_ref.shape[0] // LANES
    per = length // LANES

    def rows_in(c):
        return lax.div(c, per), pl.ds(pl.multiple_of(lax.rem(c, per) * LANES, LANES), LANES)

    share(group, square_ref, squares, sq_send, sq_recv)
    start_mate, start_chip, total, finish = scatter_phases(
        group, row_tile, part, mate_in, chip_out, chip_in, (mate_send, mate_recv, chip_send, chip_recv)
    )

    def product(c):
        rows = gated_ref[row_tile(c)]
        for j in range(n):
            block = (
                weight_ref[:, j * width : (j + 1) * width] if len(weight_ref.shape) == 2 else weight_ref[j]
            )
            part[j, row_tile(c)] = jnp.dot(rows, block, preferred_element_type=f32).astype(bf16)
        start_mate(c)

    loop(chunks, product)
    loop(chunks, start_chip)
    shared(group, square_ref, squares, sq_send, sq_recv)
    squares[group.me] = square_ref[...]
    loss_ref[...] = jnp.zeros_like(loss_ref)

    def to_mate(c):
        block = gathered.at[group.me, row_tile(c)]
        return remote(block, block, gm_send.at[c], gm_recv.at[c], group.at(group.mate))

    def to_chip(c, k):
        block = gathered.at[group.me, row_tile(c)]
        return remote(
            block, block, gc_send.at[k - 1, c], gc_recv.at[k - 1, c], group.at(group.peer(k))
        )

    def forward(c, k):
        block = gathered.at[2 * group.chip_before(k) + group.core, row_tile(c)]
        return remote(
            block, block, gf_send.at[k - 1, c], gf_recv.at[k - 1, c], group.at(group.mate)
        )

    token_load.wait()
    teacher_load.wait()
    token_store = pltpu.make_async_copy(tokens_ref, tokens_out, load_sem.at[0])
    token_store.start()

    def rest(c):
        squared = squares[0, pl.ds(c, 1)]
        for j in range(1, n):
            squared = squared + squares[j, pl.ds(c, 1)]
        squared_ref[pl.ds(c, 1)] = squared
        scale = lax.rsqrt(squared * (1.0 / (NHEADS * HEADDIM)) + norm_eps)
        branch = total(c) * as_column(scale, width)
        output = tokens_ref[rows_in(c)] + branch
        output_ref[row_tile(c)] = output
        difference = output - teacher_ref[rows_in(c)]
        weighted = difference * as_column(mask_ref[pl.ds(c, 1)], width)
        low = weighted.astype(bf16)
        gathered[group.me, row_tile(c)] = low
        to_mate(c).start()
        for k in range(1, group.chips):
            to_chip(c, k).start()
        loss_ref[...] += jnp.sum(weighted * difference, axis=0, keepdims=True)
        dot_out[pl.ds(c, 1)] = rows_of(low.astype(f32) * branch)

    loop(chunks, rest)
    share(group, dot_out, dots, rd_send, rd_recv)

    def pass_on(c):
        for k in range(1, group.chips):
            to_chip(c, k).wait_recv()
            forward(c, k).start()

    loop(chunks, pass_on)

    def end(c):
        to_mate(c).wait()
        for k in range(1, group.chips):
            to_chip(c, k).wait_send()
            forward(c, k).wait()
        finish(c)
        for j in range(n):
            grad_ref[j, row_tile(c)] = gathered[j, row_tile(c)]

    loop(chunks, end)
    shared(group, dot_out, dots, rd_send, rd_recv)
    row_sum = dot_out[...]
    for k in range(1, n):
        row_sum = row_sum + dots[group.other(k)]
    rowdot_ref[...] = row_sum
    token_store.wait()


def scatter_scratch(n, rows, width, chunks):
    chips = n // 2
    dma = pltpu.SemaphoreType.DMA
    return [
        pltpu.VMEM((n, rows, width), bf16),
        pltpu.VMEM((chips, rows, width), bf16),
        pltpu.VMEM((chips - 1, rows, width), bf16),
        pltpu.VMEM((chips - 1, rows, width), bf16),
    ], [dma((chips, chunks)), dma((chips, chunks)), dma((chips - 1, chunks)), dma((chips - 1, chunks))]


def blocked(weight, n):
    width = weight.shape[1] // n
    if width % LANES == 0:
        return weight
    return jnp.moveaxis(weight.reshape(weight.shape[0], n, width), 1, 0)


def out_phase(gated, weight, square_rows, tokens, teacher, mask_rows, cid):
    n = lax.axis_size("head")
    count, length, width = teacher.shape
    rows = count * length
    chips, chunks = n // 2, rows // LANES
    if width % LANES:
        tokens = lax.dynamic_slice_in_dim(tokens, lax.axis_index("head") * width, width, 2)
    buffers, sems = scatter_scratch(n, rows, width, chunks)
    dma = pltpu.SemaphoreType.DMA
    hbm = pl.BlockSpec(memory_space=pl.ANY)
    return pl.pallas_call(
        functools.partial(out_kernel, n),
        out_shape=[
            jax.ShapeDtypeStruct((rows, width), f32),
            jax.ShapeDtypeStruct((n, rows, width), bf16),
            jax.ShapeDtypeStruct((chunks, LANES), f32),
            jax.ShapeDtypeStruct((chunks, LANES), f32),
            jax.ShapeDtypeStruct((1, width), f32),
            jax.ShapeDtypeStruct((count, length, width), f32),
        ],
        in_specs=[in_vmem] * 3 + [hbm] * 2 + [in_vmem],
        out_specs=[in_vmem] * 5 + [hbm],
        scratch_shapes=[pltpu.VMEM((count, length, width), f32)] * 2
        + buffers
        + [
            pltpu.VMEM((n, rows, width), bf16),
            pltpu.VMEM((n, chunks, LANES), f32),
            pltpu.VMEM((n, chunks, LANES), f32),
            pltpu.VMEM((chunks, LANES), f32),
        ]
        + sems
        + [
            dma((chunks,)),
            dma((chunks,)),
            dma((chips - 1, chunks)),
            dma((chips - 1, chunks)),
            dma((chips - 1, chunks)),
            dma((chips - 1, chunks)),
            dma((n - 1,)),
            dma((n,)),
            dma((n - 1,)),
            dma((n,)),
            dma((2,)),
        ],
        compiler_params=params(cid),
        name="out_phase",
    )(gated, blocked(weight, n), square_rows, tokens, teacher, mask_rows)


def blocks(width, size=256):
    return [(at, min(size, width - at)) for at in range(0, width, size)]


def fold_lanes(values):
    rows, width = values.shape
    if width % LANES:
        fill = jnp.zeros((rows, LANES - width % LANES), values.dtype)
        values = jnp.concatenate([values, fill], axis=1)
    total = values[:, :LANES]
    for at in range(LANES, width, LANES):
        total = total + values[:, at : at + LANES]
    return total


def rows_of(values):
    return jnp.sum(fold_lanes(values).T, axis=0, keepdims=True)


def head_spread(channels):
    row = lax.broadcasted_iota(jnp.int32, (LANES, channels), 0)
    head = lax.broadcasted_iota(jnp.int32, (LANES, channels), 1) // HEADDIM
    return ((row % 16 == head) & (row < 48)).astype(f32).astype(bf16)


def head_gather(channels):
    head = lax.broadcasted_iota(jnp.int32, (channels, LANES), 0) // HEADDIM
    return (lax.broadcasted_iota(jnp.int32, (channels, LANES), 1) == head).astype(f32).astype(bf16)


def spread(values, marks):
    lane = lax.broadcasted_iota(jnp.int32, values.shape, 1)
    values = jnp.where(lane < 16, values, 0.0)
    high = values.astype(bf16).astype(f32)
    left = values - high
    middle = left.astype(bf16).astype(f32)
    low = (left - middle).astype(bf16).astype(f32)
    three = high + pltpu.roll(middle, 16, 1) + pltpu.roll(low, 32, 1)
    return jnp.dot(three.astype(bf16), marks, preferred_element_type=f32)


def gather_heads(values, marks):
    high = values.astype(bf16)
    low = (values - high.astype(f32)).astype(bf16)
    return jnp.dot(high, marks, preferred_element_type=f32) + jnp.dot(
        low, marks, preferred_element_type=f32
    )


def softplus(x):
    y = jnp.exp(-jnp.abs(x))
    small = y * (1.0 - y * (1.0 / 2 - y * (1.0 / 3 - y * (1.0 / 4 - y * (1.0 / 5)))))
    return jnp.maximum(x, 0.0) + jnp.where(y < 0.03, small, jnp.log(1.0 + y))


def lane_row(ref):
    row = ref[...][None, :]
    return jnp.concatenate([row, jnp.zeros((1, LANES - row.shape[1]), f32)], axis=1)


def long_row(ref, b, length):
    per = length // LANES
    return jnp.concatenate([ref[pl.ds(b * per + i, 1)] for i in range(per)], axis=1)


def spread_row(row, marks):
    return spread(jnp.broadcast_to(row, (8, LANES)), marks)[:1]


def position_masks(docs_row, begin):
    length = docs_row.shape[1]
    column = jnp.broadcast_to(docs_row, (LANES, length)).T
    place = begin + lax.broadcasted_iota(jnp.int32, (length, LANES), 0).astype(f32)
    return column, place


def front_kernel(
    heads,
    tokens_hbm,
    gain_ref,
    value_hbm,
    keyquery_hbm,
    step_ref,
    gate_hbm,
    docs_ref,
    step_bias_ref,
    rate_log_ref,
    skip_ref,
    value_conv_ref,
    value_offset_ref,
    keyquery_conv_ref,
    keyquery_offset_ref,
    norm_gain_ref,
    valid_ref,
    normed_out,
    linear_out,
    conv_out,
    gate_out,
    mixed_out,
    gained_out,
    halo_out,
    state_out,
    steps_out,
    cumulative_out,
    linear_steps_out,
    square_out,
    inverse_out,
    mask_out,
    tokens,
    last_tokens,
    value_weight,
    keyquery_weight,
    gate_weight,
    normed,
    linear,
    conv,
    gate,
    mixed,
    gained,
    tail,
    halo,
    extended,
    heads_in,
    keys,
    queries,
    scores,
    mask_bias,
    locals_,
    state,
    offers,
    offered,
    hand,
    following,
    passed,
    entering,
    load_sem,
    last_sem,
    token_sem,
    store_sem,
    halo_sem,
    chain_send,
    chain_recv,
):
    n = lax.axis_size("seq")
    place = lax.axis_index("seq")
    head = lax.axis_index("head")
    count, length, _ = tokens.shape
    channels = value_weight.shape[1]
    both = channels + 2 * STATE
    lags = value_conv_ref.shape[0]
    begin = (place * length).astype(f32)

    loads = [
        pltpu.make_async_copy(value_hbm, value_weight, load_sem.at[0]),
        pltpu.make_async_copy(keyquery_hbm, keyquery_weight, load_sem.at[1]),
        pltpu.make_async_copy(gate_hbm, gate_weight, load_sem.at[2]),
    ]

    def token_load(b):
        return pltpu.make_async_copy(tokens_hbm.at[b], tokens.at[b], token_sem.at[b])

    def last_load(b):
        return pltpu.make_async_copy(
            tokens_hbm.at[b, length - 16 :], last_tokens.at[b], last_sem.at[b]
        )

    for b in range(count):
        last_load(b).start()
    loads[0].start()
    loads[1].start()
    for b in range(count):
        token_load(b).start()
    loads[2].start()

    stores = [
        (normed, normed_out),
        (linear, linear_out),
        (conv, conv_out),
        (gate, gate_out),
        (mixed, mixed_out),
        (gained, gained_out),
    ]

    def store(i, b):
        source, target = stores[i]
        return pltpu.make_async_copy(source.at[b], target.at[b], store_sem.at[i, b])

    barrier = pltpu.get_barrier_semaphore()

    chain = PairChain(
        place,
        1,
        locals_,
        passed,
        (state, offers, offered, hand, following),
        chain_send,
        chain_recv,
    )
    for k in range(1, n):
        pl.semaphore_signal(
            barrier, inc=1, device_id=(lax.rem(place + k, n), head), device_id_type=MESH
        )

    def normalized(x):
        inverse = lax.rsqrt(jnp.mean(x * x, axis=-1, keepdims=True) + norm_eps)
        return inverse, (x * inverse * gain_ref[...][None, :]).astype(bf16)

    for b in range(count):
        last_load(b).wait()
    last = jnp.concatenate([normalized(last_tokens[b])[1] for b in range(count)], axis=0)
    loads[0].wait()
    loads[1].wait()
    for at, width in blocks(channels):
        tail[:, at : at + width] = jnp.dot(
            last, value_weight[:, at : at + width], preferred_element_type=f32
        ).astype(bf16)
    tail[:, channels:] = jnp.dot(last, keyquery_weight[...], preferred_element_type=f32).astype(bf16)
    pl.semaphore_wait(barrier, n - 1)
    halo_copy = remote(tail, halo, halo_sem.at[0], halo_sem.at[1], (place + 1, head))

    @pl.when(place < n - 1)
    def _():
        halo_copy.start()

    marks = head_spread(channels)
    step_bias = lane_row(step_bias_ref)
    decay_rate = -jnp.exp(lane_row(rate_log_ref))
    skip = spread_row(lane_row(skip_ref), marks)
    triangle = (
        lax.broadcasted_iota(jnp.int32, (length, length), 0)
        >= lax.broadcasted_iota(jnp.int32, (length, length), 1)
    ).astype(f32)

    def norm(b):
        token_load(b).wait()
        inverse, rows = normalized(tokens[b])
        normed[b] = rows
        inverse_out[pl.ds(b, 1)] = jnp.broadcast_to(inverse, (length, LANES)).T[:1]
        store(0, b).start()

    def project_values(b):
        rows = normed[b]
        for at, width in blocks(channels):
            linear[b, :, at : at + width] = jnp.dot(
                rows, value_weight[:, at : at + width], preferred_element_type=f32
            ).astype(bf16)

    def project_rest(b):
        rows = normed[b]
        linear[b, :, channels:] = jnp.dot(
            rows, keyquery_weight[...], preferred_element_type=f32
        ).astype(bf16)
        narrow_steps = dot_nt(rows, step_ref[...])
        linear_steps_out[b] = jnp.concatenate(
            [narrow_steps, jnp.zeros((length, LANES - heads), f32)], axis=1
        )
        store(1, b).start()

    def states(b):
        @pl.when((b == 0) & (place > 0))
        def _():
            halo_copy.wait_recv()

        @pl.when((b == 0) & (place == 0))
        def _():
            halo[...] = jnp.zeros_like(halo)

        column, spot = position_masks(docs_ref[pl.ds(b, 1)].astype(f32), begin)
        extended[0:16] = halo[pl.ds(pl.multiple_of(b * 16, 16), 16)].astype(f32)
        extended[16:] = linear[b].astype(f32)
        usable = [None] + [(spot - lag >= column).astype(f32) for lag in range(1, lags)]
        for at in range(0, both, LANES):
            if at < channels:
                weight, offset, place_at = value_conv_ref, value_offset_ref, at
            else:
                weight, offset, place_at = keyquery_conv_ref, keyquery_offset_ref, at - channels
            lanes = slice(place_at, place_at + LANES)
            value = offset[lanes][None, :] + weight[0:1, lanes] * extended[16:, at : at + LANES]
            for lag in range(1, lags):
                value = value + weight[lag : lag + 1, lanes] * (
                    extended[16 - lag : 16 - lag + length, at : at + LANES] * usable[lag]
                )
            conv[b, :, at : at + LANES] = value
            active = value * jax.nn.sigmoid(value)
            if at < channels:
                heads_in[b, :, at : at + LANES] = active
            elif at < channels + STATE:
                keys[b] = active.astype(bf16)
            else:
                queries[b] = active.astype(bf16)
        store(2, b).start()
        steps = softplus(linear_steps_out[b] + step_bias)
        cumulative = jnp.dot(
            triangle, steps * decay_rate, precision=highest, preferred_element_type=f32
        )
        steps_out[b] = steps
        cumulative_out[b] = cumulative
        kept = (column < begin).astype(f32)
        trailing = (spot >= column[length - 1 :]).astype(f32)
        entering[b] = jnp.exp(cumulative) * kept
        end_weight = jnp.exp(cumulative[length - 1 :] - cumulative) * trailing * steps
        weighted = (heads_in[b] * spread(end_weight, marks)).astype(bf16)
        locals_[b] = dot_tn(keys[b], weighted)
        last_entering = entering[b, length - 8 :]
        passed[b] = spread(last_entering, marks)

    pairs = channels // LANES
    turns = (
        [(b + 1 + k, k, b) for b, k in ((0, 0), (1, 0), (2, 0), (0, 1), (1, 1), (0, 2))]
        + [(5, 0, 3), (5, 1, 2), (5, 2, 1), (5, 3, 0), (7, 1, 3), (7, 2, 2), (7, 3, 1)]
        if n == 8 and count == 4
        else []
    )

    def begin_sequence(b):
        norm(b)
        project_values(b)
        project_rest(b)
        states(b)
        chain.offer(b)
        chain.turn(b, turns)

    loop(count, begin_sequence)
    halo_out[...] = halo[...]
    per_row = 2.0 / (D * jnp.sum(valid_ref[...].astype(f32), keepdims=True))
    here = pl.ds(pl.multiple_of(place * length, length), length)
    for b in range(count):
        row = valid_ref[b : b + 1, here].astype(f32) * per_row
        for i in range(length // LANES):
            at = b * (length // LANES) + i
            mask_out[at : at + 1] = row[:, i * LANES : (i + 1) * LANES]
    first_half = lax.broadcasted_iota(jnp.int32, (length, LANES), 1) < HEADDIM
    loads[2].wait()

    def inside(b):
        column, spot = position_masks(docs_ref[pl.ds(b, 1)].astype(f32), begin)
        wide = jnp.concatenate([column] * (length // LANES), axis=1)
        t = begin + lax.broadcasted_iota(jnp.int32, (length, length), 0).astype(f32)
        u = begin + lax.broadcasted_iota(jnp.int32, (length, length), 1).astype(f32)
        mask_bias[...] = jnp.where((u >= wide) & (u <= t), 0.0, -1e30)
        scores[...] = dot_nt(queries[b], keys[b])
        cumulative = cumulative_out[b]
        across = cumulative.T
        spread_steps = spread(steps_out[b], marks)
        for pair in range(pairs):
            lanes = slice(pair * LANES, (pair + 1) * LANES)
            scaled = heads_in[b, :, lanes] * spread_steps[:, lanes]
            value = jnp.zeros((length, LANES), f32)
            for half in range(2):
                h = 2 * pair + half
                decay = jnp.exp(cumulative[:, h : h + 1] - across[h : h + 1] + mask_bias[...])
                mixing = (decay * scores[...]).astype(bf16)
                mine = jnp.where(first_half if half == 0 else ~first_half, scaled, 0.0).astype(bf16)
                value = value + jnp.dot(mixing, mine, preferred_element_type=f32)
            mixed[b, :, lanes] = value
        rows = normed[b]
        for at, width in blocks(channels):
            gate[b, :, at : at + width] = jnp.dot(
                rows, gate_weight[:, at : at + width], preferred_element_type=f32
            )
        store(3, b).start()
        chain.turn(count + b, turns)

    loop(count, inside)
    chain.rest(turns)

    def close(b):
        chain.ready(b)
        state_out[b] = state[b]
        projected = jnp.dot(queries[b], state[b], preferred_element_type=f32)
        value = mixed[b] + spread(entering[b], marks) * projected + skip * heads_in[b]
        mixed[b] = value
        store(4, b).start()
        linear_gate = gate[b]
        gated = value * (linear_gate * jax.nn.sigmoid(linear_gate))
        gained[b] = (gated * norm_gain_ref[...][None, :]).astype(bf16)
        store(5, b).start()
        squared = rows_of(gated * gated)
        for i in range(length // LANES):
            square_out[pl.ds(b * (length // LANES) + i, 1)] = squared[
                :, i * LANES : (i + 1) * LANES
            ]

    loop(count, close)

    @pl.when(place < n - 1)
    def _():
        halo_copy.wait_send()

    chain.finish()

    for i in range(len(stores)):
        loop(count, lambda b, i=i: store(i, b).wait())


def front(tokens, gain, value_weight, keyquery_weight, step_weight, gate_weight, docs, vectors, conv, norm_gain, valid, cid):
    count, length, _ = tokens.shape
    channels = value_weight.shape[1]
    heads = channels // HEADDIM
    both = channels + 2 * STATE
    dma = pltpu.SemaphoreType.DMA
    hbm = pl.BlockSpec(memory_space=pl.ANY)
    shape = jax.ShapeDtypeStruct
    big = [
        ((count, length, D), bf16),
        ((count, length, both), bf16),
        ((count, length, both), f32),
        ((count, length, channels), f32),
        ((count, length, channels), f32),
        ((count, length, channels), bf16),
    ]
    small = [
        ((count * 16, both), bf16),
        ((count, STATE, channels), bf16),
        ((count, length, LANES), f32),
        ((count, length, LANES), f32),
        ((count, length, LANES), f32),
        ((count * length // LANES, LANES), f32),
        ((count, length), f32),
        ((count * length // LANES, LANES), f32),
    ]
    return pl.pallas_call(
        functools.partial(front_kernel, heads),
        out_shape=[shape(*s) for s in big + small],
        in_specs=[hbm, in_vmem, hbm, hbm, in_vmem, hbm] + [in_vmem] * 10,
        out_specs=[hbm] * len(big) + [in_vmem] * len(small),
        scratch_shapes=[
            pltpu.VMEM((count, length, D), f32),
            pltpu.VMEM((count, 16, D), f32),
            pltpu.VMEM((D, channels), bf16),
            pltpu.VMEM((D, 2 * STATE), bf16),
            pltpu.VMEM((D, channels), bf16),
        ]
        + [pltpu.VMEM(*s) for s in big]
        + [
            pltpu.VMEM((count * 16, both), bf16),
            pltpu.VMEM((count * 16, both), bf16),
            pltpu.VMEM((length + 16, both), f32),
            pltpu.VMEM((count, length, channels), f32),
            pltpu.VMEM((count, length, STATE), bf16),
            pltpu.VMEM((count, length, STATE), bf16),
            pltpu.VMEM((length, length), f32),
            pltpu.VMEM((length, length), f32),
            pltpu.VMEM((count, STATE, channels), f32),
        ]
        + chain_buffers(count, channels)
        + [
            pltpu.VMEM((count, 8, channels), f32),
            pltpu.VMEM((count, length, LANES), f32),
            dma((3,)),
            dma((count,)),
            dma((count,)),
            dma((len(big), count)),
            dma((2,)),
            dma((3, count)),
            dma((3, count)),
        ],
        compiler_params=params(cid),
        name="front",
    )(tokens, gain, value_weight, keyquery_weight, step_weight, gate_weight, docs, *vectors, *conv, norm_gain, valid)


class Doubling:
    def __init__(self, axis, bits, current, table, send_sem, recv_sem):
        self.axis, self.bits, self.current, self.table = axis, list(bits), current, table
        self.send_sem, self.recv_sem = send_sem, recv_sem

    def copy(self, stage):
        bit = 1 << self.bits[stage]
        mine = lax.axis_index(self.axis)
        other = mine + bit - 2 * bit * lax.rem(lax.div(mine, bit), 2)
        if self.axis == "head":
            target = (lax.axis_index("seq"), other)
        else:
            target = (other, lax.axis_index("head"))
        return remote(
            self.current,
            self.table.at[stage],
            self.send_sem.at[stage],
            self.recv_sem.at[stage],
            target,
        )

    def start(self, stage):
        self.copy(stage).start()

    def run(self, first, last=None):
        for stage in range(first, len(self.bits) if last is None else min(last, len(self.bits))):
            self.copy(stage).wait()
            self.current[...] = self.current[...] + self.table[stage]
            if stage + 1 < len(self.bits):
                self.start(stage + 1)


def stages_of(n):
    return n.bit_length() - 1


def tile_place(index, width):
    per = width // LANES
    return index // per, slice(index % per * LANES, index % per * LANES + LANES)


class Tiles:
    def __init__(self, ref):
        self.ref, self.index = ref, 0

    def put(self, row):
        for at in range(0, row.shape[1], LANES):
            r, lanes = tile_place(self.index, self.ref.shape[1])
            self.ref[r : r + 1, lanes] = row[:, at : at + LANES]
            self.index += 1

    def take(self, width):
        found = []
        for _ in range(width // LANES):
            r, lanes = tile_place(self.index, self.ref.shape[1])
            found.append(self.ref[r : r + 1, lanes])
            self.index += 1
        return jnp.concatenate(found, axis=1)


def rear_kernel(names, scoped, heads, *refs):
    r = types.SimpleNamespace(**dict(zip(names, refs)))
    n, heads_n = lax.axis_size("seq"), lax.axis_size("head")
    place = lax.axis_index("seq")
    group = Group(heads_n)
    head = group.me
    ahead = n - 1 - place
    count, length, channels = r.gate_grad.shape
    rows = count * length
    both = channels + 2 * STATE
    lags = r.value_conv.shape[0]
    width = r.mate_in.shape[2]
    begin = (place * length).astype(f32)
    inner_total = NHEADS * HEADDIM
    ring_steps = n - 2
    own = D // n
    quarters = own % 64 == 0
    turns, out_steps, gate_steps = [], [], []
    if n == 8 and count == 4:
        turns = [(3, 0, 0), (4, 0, 1), (5, 0, 2), (7, 0, 3)]
        turns += [(6, 1, 0), (8, 1, 1), (9, 1, 2), (11, 1, 3)]
        turns += [(10, 2, 0), (12, 2, 1), (13, 2, 2), (14, 2, 3)]
        turns += [(13, 3, 0), (15, 3, 1), (16, 3, 2), (17, 3, 3)]
        out_steps = [(8, 0), (11, 1), (14, 2), (17, 3), (19, 4), (22, 5)]
        gate_steps = [(18, 0), (21, 1), (23, 2), (25, 3), (28, 4), (30, 5)]

    barrier = pltpu.get_barrier_semaphore()
    for k in range(1, heads_n):
        pl.semaphore_signal(
            barrier, inc=1, device_id=group.at(group.other(k)), device_id_type=MESH
        )
    for k in range(1, n):
        pl.semaphore_signal(
            barrier, inc=1, device_id=(lax.rem(place + k, n), head), device_id_type=MESH
        )

    normed_load = pltpu.make_async_copy(r.normed_hbm, r.normed, r.load_sem.at[0])
    marks = head_spread(channels)
    collect = head_gather(channels)
    step_bias = lane_row(r.step_bias)
    decay_rate = -jnp.exp(lane_row(r.rate_log))
    skip = spread_row(lane_row(r.skip), marks)
    r.gain_grad[...] = jnp.zeros_like(r.gain_grad)
    r.vector_grad[...] = jnp.zeros_like(r.vector_grad)
    r.conv_grad[...] = jnp.zeros_like(r.conv_grad)
    ring = Ring(r.ring_send, r.ring_recv)
    def matrix(part, slots):
        first = len(ring.streams)
        if quarters:
            ring.add(part, slots[:2], by_rows=True)
            ring.add(part, slots[2:], by_rows=True, first=own // 2)
            return first, first + 2
        ring.add(part, slots[:2])
        return (first,)

    out_halves = matrix(r.out_part, (r.os0, r.os1, r.os2, r.os3))
    gate_halves = matrix(r.gate_part, (r.gs0, r.gs1, r.gs2, r.gs3))

    def pass_on(first, step):
        @pl.when((step >= 0) & (step < ring_steps))
        def _():
            ring.pass_on(first, step)
            ring.pass_on(first + 1, step)

    def weights_turn(here, rounds=1):
        known = range(here, here + 2 * rounds, 2) if isinstance(here, int) else None
        for halves, table in ((out_halves, out_steps), (gate_halves, gate_steps)):
            if known is None or any(place in known for place, _ in table):
                step = step_at(table, here)
                for first in halves:
                    pass_on(first, step)

    def start(first):
        ring.start(first)
        ring.start(first + 1)

    def rest_of_ring(halves, done):
        if ring_steps > done:

            def further(s):
                for first in halves:
                    pass_on(first, done + s)

            loop(ring_steps - done, further)

    def total_of(i, halves, sums, targets):
        for k in [first + way for first in halves for way in range(2)]:
            _, _, (first, lines), columns, _ = ring.streams[k]
            sums[i, first : first + lines, columns] = ring.last(k)
        copy = pltpu.make_async_copy(sums.at[i], targets[i], r.total_sem.at[i])
        copy.start()
        return copy

    def as_wide(ref, b):
        return jnp.broadcast_to(long_row(ref, b, length), (LANES, length)).T

    def widened(column, size):
        return jnp.concatenate([column] * (size // LANES), axis=1)

    def weight_block(target, grads, block):
        sides = jnp.concatenate([r.normed[b, :, block] for b in range(count)], axis=0)
        whole = jnp.concatenate([grads(b) for b in range(count)], axis=0)
        target[block] = dot_tn(sides, whole).astype(target.dtype)

    def phase_one(*locals_one):
        q = types.SimpleNamespace(**dict(zip(scoped[0], locals_one)))
        loads = [
            pltpu.make_async_copy(r.out_weight_hbm, q.weight, r.load_sem.at[1]),
            pltpu.make_async_copy(r.pieces_hbm, q.pieces, r.load_sem.at[2]),
        ]
        for copy in loads:
            copy.start()
        row_arrays = [(r.gate_hbm, q.gate), (r.mixed_hbm, q.mixed), (r.conv_hbm, q.conv)]

        def row_load(i, b):
            source, target = row_arrays[i]
            return pltpu.make_async_copy(source.at[b], target.at[b], r.row_sem.at[i, b])

        def linear_load(b):
            slot = lax.rem(b, 2)
            return pltpu.make_async_copy(r.linear_hbm.at[b], q.linear.at[slot], r.line_load.at[slot])

        for b in range(count):
            for i in range(3):
                row_load(i, b).start()
        normed_load.start()
        linear_load(0).start()
        inner = q.gate
        normed_out = r.values_grad
        chain = PairChain(
            ahead,
            -1,
            q.local,
            q.passed,
            (r.state, q.offer, r.offered, r.hand, q.following),
            r.chain_send,
            r.chain_recv,
        )
        pairs = channels // LANES
        for copy in loads:
            copy.wait()
        pl.semaphore_wait(barrier, heads_n + n - 2)
        groups = q.pieces.shape[0]

        def gated_norm(b):
            for i in range(3):
                row_load(i, b).wait()
            scale = lax.rsqrt(as_wide(r.square, b) * (1.0 / inner_total) + norm_eps)
            pull = scale * scale * as_wide(r.rowdot, b) * (1.0 / inner_total)
            column, _ = position_masks(r.docs[pl.ds(b, 1)].astype(f32), begin)
            entering = spread(jnp.exp(r.cumulative[b]) * (column < begin).astype(f32), marks)
            q.passed[b] = entering[length - 8 :]
            here = pl.ds(pl.multiple_of(b * length, length), length)
            for at, size in blocks(channels):
                lanes = slice(at, at + size)
                grad_rows = jnp.zeros((length, size), f32)
                for j in range(groups):
                    block = (
                        q.weight[lanes, j * width : (j + 1) * width]
                        if len(q.weight.shape) == 2
                        else q.weight[j, lanes]
                    )
                    grad_rows = grad_rows + dot_nt(q.pieces[j, here], block)
                linear_gate = q.gate[b, :, lanes]
                sigmoid_value = jax.nn.sigmoid(linear_gate)
                active = linear_gate * sigmoid_value
                value = q.mixed[b, :, lanes]
                gated = value * active
                norm_gain = r.norm_gain[lanes][None, :]
                scaled = gated * widened(scale, size)
                normed_out[b, :, lanes] = (scaled * norm_gain).astype(bf16)
                r.gain_grad[:, lanes] += jnp.sum(grad_rows * scaled, axis=0, keepdims=True)
                gated_grad = widened(scale, size) * norm_gain * grad_rows - gated * widened(
                    pull, size
                )
                q.heads_grad[b, :, lanes] = gated_grad * active
                slope = sigmoid_value * (1.0 + linear_gate * (1.0 - sigmoid_value))
                r.gate_grad[b, :, lanes] = (gated_grad * value * slope).astype(bf16)
                values = q.conv[b, :, lanes]
                q.heads_in[b, :, lanes] = values * jax.nn.sigmoid(values)
            values = q.conv[b, :, channels : channels + STATE]
            q.keys[b] = (values * jax.nn.sigmoid(values)).astype(bf16)
            values = q.conv[b, :, channels + STATE :]
            q.queries[b] = (values * jax.nn.sigmoid(values)).astype(bf16)
            q.local[b] = dot_tn(q.queries[b], (q.heads_grad[b] * entering).astype(bf16))
            chain.offer(b)

        loop(count, gated_norm)
        chain.turn(3, turns)

        for j in range(groups):
            grads = jnp.concatenate([normed_out[b] for b in range(count)], axis=0)
            r.out_part[j * width : (j + 1) * width] = dot_tn(q.pieces[j], grads).astype(bf16)
            if j == groups // 2 - 1:
                chain.turn(4, turns)
        for first in out_halves:
            start(first)
        chain.turn(5, turns)
        normed_load.wait()

        first_half = lax.broadcasted_iota(jnp.int32, (length, LANES), 1) < HEADDIM

        def inside(b):
            docs_row = r.docs[pl.ds(b, 1)].astype(f32)
            u = begin + lax.broadcasted_iota(jnp.int32, (length, length), 0).astype(f32)
            t = begin + lax.broadcasted_iota(jnp.int32, (length, length), 1).astype(f32)
            q.mask_bias[...] = jnp.where((u >= docs_row) & (u <= t), 0.0, -1e30)
            q.scores[...] = dot_nt(q.keys[b], q.queries[b])
            q.scores_grad[...] = jnp.zeros_like(q.scores_grad)
            cumulative = r.cumulative[b]
            across = cumulative.T
            spread_steps = spread(r.steps[b], marks)
            for pair in range(pairs):
                lanes = slice(pair * LANES, (pair + 1) * LANES)
                scaled = q.heads_in[b, :, lanes] * spread_steps[:, lanes]
                grads = q.heads_grad[b, :, lanes]
                low_grads = grads.astype(bf16)
                value = jnp.zeros((length, LANES), f32)
                for half in range(2):
                    h = 2 * pair + half
                    mine = first_half if half == 0 else ~first_half
                    decay = jnp.exp(
                        across[h : h + 1] - cumulative[:, h : h + 1] + q.mask_bias[...]
                    )
                    mixing = (decay * q.scores[...]).astype(bf16)
                    value = value + jnp.dot(
                        mixing, jnp.where(mine, grads, 0.0).astype(bf16), preferred_element_type=f32
                    )
                    pairwise = dot_nt(jnp.where(mine, scaled, 0.0).astype(bf16), low_grads)
                    q.scores_grad[...] += decay * pairwise
                inner[b, :, lanes] = value
                if pair == (pairs - 1) // 2:
                    weights_turn(6 + 2 * b)
                    chain.turn(6 + 2 * b, turns)
            low = q.scores_grad[...].astype(bf16)
            q.narrow_grad[b, :, :STATE] = jnp.dot(low, q.queries[b], preferred_element_type=f32)
            column, _ = position_masks(docs_row, begin)
            entering = jnp.exp(cumulative) * (column < begin).astype(f32)
            x = q.heads_in[b]
            dy = q.heads_grad[b]
            q.narrow_grad[b, :, STATE:] = dot_tn(low, q.keys[b]) + dot_nt(
                (dy * spread(entering, marks)).astype(bf16), r.state_in[b]
            )
            dot_inner = gather_heads(x * inner[b], collect)
            dot_skip = gather_heads(dy * x, collect)
            q.dot_inner[b] = dot_inner
            q.cum_part[b] = (
                gather_heads(dy * (q.mixed[b] - skip * x), collect) - r.steps[b] * dot_inner
            )
            r.vector_grad[2:3] += jnp.sum(dot_skip, axis=0, keepdims=True)
            inner[b] = skip * dy + spread_steps * inner[b]
            weights_turn(7 + 2 * b)
            chain.turn(7 + 2 * b, turns)

        loop(count, inside)
        chain.rest(turns)

        def gate_block(i):
            block = pl.ds(pl.multiple_of(i * 256, 256), 256)
            weight_block(r.gate_part, lambda b: r.gate_grad[b], block)

        loop(D // 512, gate_block)
        weights_turn(14)
        chain.turn(14, turns)
        loop(D // 512, lambda i: gate_block(i + D // 512))
        for first in gate_halves:
            start(first)
        weights_turn(15)
        chain.turn(15, turns)
        q.around[...] = jnp.zeros_like(q.around)
        q.usable[...] = jnp.zeros_like(q.usable)
        upper = (
            lax.broadcasted_iota(jnp.int32, (length, length), 0)
            <= lax.broadcasted_iota(jnp.int32, (length, length), 1)
        ).astype(f32)
        last_row = lax.broadcasted_iota(jnp.int32, (length, LANES), 0) == length - 1

        def edge_copy(b):
            return remote(
                r.edge.at[b], r.edge_in.at[b], r.edge_send.at[b], r.edge_recv.at[b], (place - 1, head)
            )

        def close(b):
            @pl.when(b + 1 < count)
            def _():
                linear_load(b + 1).start()

            column, spot = position_masks(r.docs[pl.ds(b, 1)].astype(f32), begin)
            cumulative = r.cumulative[b]
            steps = r.steps[b]
            kept = (column < begin).astype(f32)
            trailing = (spot >= column[length - 1 :]).astype(f32)
            entering = jnp.exp(cumulative) * kept
            end_decay = jnp.exp(cumulative[length - 1 :] - cumulative) * trailing
            end_weight = end_decay * steps
            chain.ready(b)
            end_grad = r.state[b]
            x = q.heads_in[b]
            grown = jnp.dot(q.keys[b], end_grad, preferred_element_type=f32)
            spread_end = spread(end_weight, marks)
            q.narrow_grad[b, :, :STATE] += dot_nt((x * spread_end).astype(bf16), end_grad)
            grad = inner[b] + spread_end * grown
            dot_end = gather_heads(x * grown, collect)
            through = jnp.sum(
                end_grad.astype(f32) * r.state_in[b].astype(f32), axis=0, keepdims=True
            )
            passed_grad = gather_heads(jnp.broadcast_to(through, (8, channels)), collect)[:1]
            end_mix = dot_end * end_weight
            last_term = passed_grad * entering[length - 1 :] + jnp.sum(
                end_mix, axis=0, keepdims=True
            )
            cum_grad = q.cum_part[b] - end_mix + jnp.where(last_row, last_term, 0.0)
            rates_grad = jnp.dot(upper, cum_grad, precision=highest, preferred_element_type=f32)
            steps_grad = q.dot_inner[b] + end_decay * dot_end + rates_grad * decay_rate
            linear_grad = steps_grad * jax.nn.sigmoid(r.linear_steps[b] + step_bias)
            r.narrow[b, :, 2 * STATE :] = linear_grad.astype(bf16)
            r.vector_grad[0:1] += jnp.sum(linear_grad, axis=0, keepdims=True)
            r.vector_grad[1:2] += jnp.sum(rates_grad * steps, axis=0, keepdims=True) * decay_rate

            weights_turn(16 + 2 * b)
            chain.turn(16 + 2 * b, turns)
            linear_load(b).wait()
            halo_rows = pl.ds(pl.multiple_of(b * 16, 16), 16)
            line = lax.rem(b, 2)
            middle = slice(16, 16 + length)
            for lag in range(1, lags):
                q.usable[lag - 1, middle] = (spot - lag >= column).astype(f32)
            for at in range(0, both, LANES):
                lanes = slice(at, at + LANES)
                slot = at // LANES % 2
                q.extended[slot, 0:16] = r.halo[halo_rows, lanes].astype(f32)
                q.extended[slot, 16:] = q.linear[line, :, lanes].astype(f32)
                values = q.conv[b, :, lanes]
                sigmoid_value = jax.nn.sigmoid(values)
                slope = sigmoid_value * (1.0 + values * (1.0 - sigmoid_value))
                if at < channels:
                    out_grad = grad[:, lanes]
                    taps, tap = r.value_conv, lanes
                else:
                    place_at = at - channels
                    out_grad = q.narrow_grad[b, :, place_at : place_at + LANES]
                    taps, tap = r.keyquery_conv, slice(place_at, place_at + LANES)
                local = out_grad * slope
                q.around[slot, middle] = local
                input_grad = taps[0:1, tap] * local
                edges = jnp.zeros((8, LANES), f32)
                r.conv_grad[0:1, lanes] += jnp.sum(
                    local * q.extended[slot, middle], axis=0, keepdims=True
                )
                r.conv_grad[lags : lags + 1, lanes] += jnp.sum(local, axis=0, keepdims=True)
                for lag in range(1, lags):
                    mask = q.usable[lag - 1, middle]
                    r.conv_grad[lag : lag + 1, lanes] += jnp.sum(
                        local * mask * q.extended[slot, 16 - lag : 16 - lag + length],
                        axis=0,
                        keepdims=True,
                    )
                    later = slice(16 + lag, 16 + lag + length)
                    input_grad = input_grad + taps[lag : lag + 1, tap] * (
                        q.around[slot, later] * q.usable[lag - 1, later]
                    )
                    first = slice(8 + lag, 16 + lag)
                    edges = edges + taps[lag : lag + 1, tap] * (
                        q.around[slot, first] * q.usable[lag - 1, first]
                    )
                r.edge[b, :, lanes] = edges
                q.tails[b, :, lanes] = input_grad[length - 16 :]
                if at < channels:
                    r.values_grad[b, :, lanes] = input_grad.astype(bf16)
                else:
                    r.narrow[b, :, tap] = input_grad.astype(bf16)

            @pl.when(place > 0)
            def _():
                edge_copy(b).start()

            weights_turn(17 + 2 * b)
            chain.turn(17 + 2 * b, turns)

        loop(count, close)

        @pl.when(place < n - 1)
        def _():
            def join(b):
                edge_copy(b).wait_recv()
                last = slice(length - 16, length)
                q.tails[b, 8:] = q.tails[b, 8:] + r.edge_in[b]
                r.values_grad[b, last] = q.tails[b, :, :channels].astype(bf16)
                r.narrow[b, last, : 2 * STATE] = q.tails[b, :, channels:].astype(bf16)

            loop(count, join)

        @pl.when(place > 0)
        def _():
            loop(count, lambda b: edge_copy(b).wait_send())

        chain.finish()

    pl.run_scoped(phase_one, *scoped[1])

    def phase_two(*locals_two):
        q = types.SimpleNamespace(**dict(zip(scoped[2], locals_two)))
        loads = [
            pltpu.make_async_copy(source, target, r.load_two.at[i])
            for i, (source, target) in enumerate(
                [
                    (r.gate_weight_hbm, q.gate_weight),
                    (r.value_weight_hbm, q.value_weight),
                    (r.keyquery_weight_hbm, q.keyquery_weight),
                    (r.tokens_hbm, q.tokens),
                    (r.output_hbm, q.output),
                    (r.teacher_hbm, q.teacher),
                ]
            )
        ]
        for copy in loads:
            copy.start()
        value_halves = matrix(q.value_part, (r.vs0, r.vs1, r.vs2, r.vs3))
        keyquery_first = len(ring.streams)
        ring.add(q.keyquery_half, (r.ks0, r.ks1), by_rows=True)

        def value_block(i):
            block = pl.ds(pl.multiple_of(i * 256, 256), 256)
            weight_block(q.value_part, lambda b: r.values_grad[b], block)

        loop(D // 512, value_block)
        weights_turn(24)
        loop(D // 512, lambda i: value_block(i + D // 512))
        for first in value_halves:
            start(first)
        weights_turn(25)

        def narrow_block(i):
            block = pl.ds(pl.multiple_of(i * 256, 256), 256)
            for half in range(2):
                lanes = slice(half * STATE, (half + 1) * STATE)
                weight_block(q.keyquery_part.at[half], lambda b: r.narrow[b, :, lanes], block)

        loop(D // 256, narrow_block)
        keyquery_mate = remote(
            q.keyquery_part.at[1 - group.core],
            r.keyquery_in,
            r.small_send.at[0],
            r.small_recv.at[0],
            group.at(group.mate),
        )
        keyquery_mate.start()
        weights_turn(26)
        targets = (r.out_total, r.gate_total, r.value_total)

        def end_ring(i, halves, done):
            rest_of_ring(halves, done)
            return total_of(i, halves, q.sums, targets)

        for copy in loads[:3]:
            copy.wait()
        q.columns[...] = jnp.zeros_like(q.columns)

        def own_columns(row):
            mine = jnp.zeros((1, width), f32)
            for j in range(heads_n):
                mine = mine + jnp.where(head == j, row[:, j * width : (j + 1) * width], 0.0)
            return mine

        gain = own_columns(r.gain[...][None, :])

        def row_block(c):
            return pl.ds(pl.multiple_of(c * length, length), length)

        start_mate, start_chip, total, finish = scatter_phases(
            group,
            row_block,
            q.part,
            r.mate_in,
            q.chip_out,
            r.chip_in,
            (r.mate_send, r.mate_recv, r.chip_send, r.chip_recv),
        )

        def value_turn(s):
            if s < ring_steps:
                for first in value_halves:
                    pass_on(first, s)

        def keyquery_turn(s):
            if s < ring_steps:
                pass_on(keyquery_first, s)

        def product(c):
            row_sum = jnp.zeros((length, LANES), f32)
            for j in range(heads_n):
                lanes = slice(j * width, (j + 1) * width)
                value = dot_nt(r.gate_grad[c], q.gate_weight[lanes])
                value = value + dot_nt(r.values_grad[c], q.value_weight[lanes])
                value = value + dot_nt(r.narrow[c, :, : 2 * STATE], q.keyquery_weight[lanes])
                value = value + jnp.dot(
                    r.narrow[c, :, 2 * STATE : 2 * STATE + heads],
                    r.step_weight[:, lanes],
                    preferred_element_type=f32,
                )
                q.part[j, row_block(c)] = value.astype(bf16)
                scaled = value * r.normed[c, :, lanes].astype(f32)
                q.columns[:, lanes] += jnp.sum(scaled, axis=0, keepdims=True)
                row_sum = row_sum + fold_lanes(scaled)
            r.dot_out[pl.ds(c, 1)] = jnp.sum(row_sum.T, axis=0, keepdims=True)
            start_mate(c)

            @pl.when(c > 0)
            def _():
                start_chip(c - 1)

        product(0)
        keyquery_mate.wait_recv()
        q.keyquery_half[...] = q.keyquery_part[group.core] + r.keyquery_in[...]
        start(keyquery_first)
        total_copies = [end_ring(0, out_halves, len(out_steps))]
        product(1)
        weights_turn(28)
        product(2)
        value_turn(0)
        keyquery_turn(0)
        product(3)
        start_chip(count - 1)
        weights_turn(30)
        share(group, r.dot_out, r.dots, r.rd_send, r.rd_recv)

        group_total = Doubling(
            "head", range(stages_of(heads_n)), r.group_sum, r.group_table, r.group_send, r.group_recv
        )
        line_total = Doubling(
            "seq", range(stages_of(n)), r.line_sum, r.line_table, r.line_send, r.line_recv
        )
        chip_total = Doubling(
            "head",
            range(1, stages_of(heads_n)),
            r.keyquery_sum,
            r.keyquery_table,
            r.kq_send,
            r.kq_recv,
        )
        tiles = Tiles(r.group_sum)
        r.group_sum[...] = jnp.zeros_like(r.group_sum)
        for lag in range(lags + 1):
            tiles.put(r.conv_grad[lag : lag + 1, channels:])
        tiles.put(q.columns[...])
        tiles.put(fold_lanes(r.loss_cols[...]))
        group_total.start(0)
        value_turn(1)
        keyquery_turn(1)

        for at, size in blocks(D):
            whole = jnp.concatenate([r.normed[b, :, at : at + size] for b in range(count)], axis=0)
            grads = jnp.concatenate([r.narrow[b, :, 2 * STATE :] for b in range(count)], axis=0)
            q.step_whole[:, at : at + size] = dot_tn(grads, whole)
        q.step_part[...] = jnp.zeros_like(q.step_part)
        for s in range(n):
            q.step_part[s, :, :own] = q.step_whole[:16, s * own : (s + 1) * own]

        def step_copy(k, index, sender):
            return remote(
                q.step_part.at[index],
                r.step_table.at[sender],
                r.step_send.at[k - 1],
                r.step_recv.at[sender],
                (index, head),
            )

        for k in range(1, n):
            step_copy(k, lax.rem(place + k, n), place).start()
        total_copies.append(end_ring(1, gate_halves, len(gate_steps)))
        value_turn(2)
        keyquery_turn(2)
        group_total.run(0, 1)
        shared(group, r.dot_out, r.dots, r.rd_send, r.rd_recv)
        r.dots[head] = r.dot_out[...]
        for copy in loads[3:]:
            copy.wait()

        def fill_line():
            tiles, summed = Tiles(r.line_sum), Tiles(r.group_sum)
            r.line_sum[...] = jnp.zeros_like(r.line_sum)
            for lag in range(lags + 1):
                tiles.put(r.conv_grad[lag : lag + 1, :channels])
                tiles.put(summed.take(2 * STATE))
            tiles.put(r.gain_grad[...])
            for i in range(3):
                tiles.put(r.vector_grad[i : i + 1])
            tiles.put(summed.take(D))
            tiles.put(summed.take(LANES))

        def grad_store(c):
            return pltpu.make_async_copy(q.tokens_grad.at[c], r.tokens_grad.at[c], r.grad_sem.at[c])

        def rest(c):
            row_sum = r.dots[0, c : c + 1]
            for j in range(1, heads_n):
                row_sum = row_sum + r.dots[j, c : c + 1]
            inverse = r.inverse[c : c + 1]
            out_grad = (q.output[row_block(c)] - q.teacher[c]) * as_column(
                long_row(r.mask, c, length), width
            )
            q.tokens_grad[c] = (
                out_grad
                + as_column(inverse, width) * gain * total(c)
                - q.tokens[c] * as_column(inverse * inverse * row_sum * (1.0 / D), width)
            )
            grad_store(c).start()

        rest(0)
        rest(1)
        value_turn(3)
        keyquery_turn(3)
        group_total.run(1)
        fill_line()
        line_total.start(0)
        rest(2)
        value_turn(4)
        keyquery_turn(4)
        line_total.run(0, 1)
        for c in range(3, count):
            rest(c)
        value_turn(5)
        keyquery_turn(5)
        line_total.run(1, 2)
        if ring_steps > 6:

            def remaining(s):
                for first in value_halves + (keyquery_first,):
                    pass_on(first, s + 6)

            loop(ring_steps - 6, remaining)
        for k in (keyquery_first, keyquery_first + 1):
            _, _, (first, lines), _, _ = ring.streams[k]
            r.keyquery_sum[first : first + lines] = ring.last(k)
        chip_total.start(0)
        total_copies.append(total_of(2, value_halves, q.sums, targets))
        for k in range(1, n):
            sender = lax.rem(place + k, n)
            copy = step_copy(k, sender, sender)
            copy.wait_send()
            copy.wait_recv()
        r.step_table[place] = q.step_part[place]
        step_sum = r.step_table[0]
        for s in range(1, n):
            step_sum = step_sum + r.step_table[s]
        r.step_total[...] = step_sum[:heads, :own]
        line_total.run(2)
        chip_total.run(0)
        keyquery_swap = remote(
            r.keyquery_sum,
            r.keyquery_other,
            r.small_send.at[1],
            r.small_recv.at[1],
            group.at(group.mate),
        )
        keyquery_swap.start()

        tiles = Tiles(r.line_sum)
        for lag in range(lags + 1):
            own_row, shared_row = tiles.take(channels), tiles.take(2 * STATE)
            if lag < lags:
                r.value_conv_total[lag : lag + 1] = own_row
                r.keyquery_conv_total[lag : lag + 1] = shared_row
            else:
                r.value_offset_total[...] = own_row[0]
                r.keyquery_offset_total[...] = shared_row[0]
        r.norm_gain_total[...] = tiles.take(channels)[0]
        for target in (r.step_bias_total, r.rate_log_total, r.skip_total):
            target[...] = tiles.take(LANES)[0, :heads]
        r.input_gain_total[...] = (own_columns(tiles.take(D)) / gain)[0]
        r.loss_total[...] = 0.5 * jnp.sum(tiles.take(LANES), axis=1, keepdims=True)[0]

        loop(count, finish)
        for c in range(count):
            grad_store(c).wait()
        for copy in total_copies:
            copy.wait()
        keyquery_mate.wait_send()
        keyquery_swap.wait()
        mine, other = r.keyquery_sum[...], r.keyquery_other[...]
        r.keyquery_total[:, :STATE] = jnp.where(group.core == 0, mine, other)
        r.keyquery_total[:, STATE:] = jnp.where(group.core == 0, other, mine)
        for i in range(len(ring.streams)):
            ring.finish(i)

    pl.run_scoped(phase_two, *scoped[3])


def rear(inputs, lags, cid):
    heads_n, n = lax.axis_size("head"), lax.axis_size("seq")
    count, length, channels = inputs["gate_hbm"].shape
    pieces = inputs["pieces_hbm"]
    rows, width = pieces.shape[1:]
    heads = channels // HEADDIM
    both = channels + 2 * STATE
    own = D // n
    step_lanes = -(-own // LANES) * LANES
    chips = heads_n // 2
    vmem, dma = pltpu.VMEM, pltpu.SemaphoreType.DMA
    hbm = pl.BlockSpec(memory_space=pl.ANY)
    group_tiles = (lags + 1) * 2 * STATE // LANES + D // LANES + 1
    line_tiles = (lags + 1) * both // LANES + channels // LANES + 3 + D // LANES + 1
    group_shape = (-(-group_tiles * LANES // (8 * 512)) * 8, 512)
    line_shape = (-(-line_tiles * LANES // (8 * both)) * 8, both)
    head_stages, line_stages = stages_of(heads_n), stages_of(n)
    outs = {
        "tokens_grad": (count, length, width),
        "out_total": (own, channels),
        "gate_total": (own, channels),
        "value_total": (own, channels),
        "keyquery_total": (own, 2 * STATE),
        "step_total": (heads, own),
        "value_conv_total": (lags, channels),
        "value_offset_total": (channels,),
        "keyquery_conv_total": (lags, 2 * STATE),
        "keyquery_offset_total": (2 * STATE,),
        "step_bias_total": (heads,),
        "rate_log_total": (heads,),
        "skip_total": (heads,),
        "norm_gain_total": (channels,),
        "input_gain_total": (width,),
        "loss_total": (1,),
    }
    if own % 64 == 0:
        slots = [vmem((n - 1, own // 4, channels), bf16)] * 4
    else:
        slots = ring_slots(n, own, channels, bf16) + [vmem((16, LANES), bf16)] * 2
    chained = chain_buffers(count, channels)
    scratch = {
        "normed": vmem((count, length, D), bf16),
        "gate_grad": vmem((count, length, channels), bf16),
        "values_grad": vmem((count, length, channels), bf16),
        "narrow": vmem((count, length, 2 * STATE + LANES), bf16),
        "out_part": vmem((D, channels), bf16),
        "gate_part": vmem((D, channels), bf16),
        "os0": slots[0],
        "os1": slots[1],
        "os2": slots[2],
        "os3": slots[3],
        "gs0": slots[0],
        "gs1": slots[1],
        "gs2": slots[2],
        "gs3": slots[3],
        "vs0": slots[0],
        "vs1": slots[1],
        "vs2": slots[2],
        "vs3": slots[3],
        "ks0": vmem((n - 1, own // 2, STATE), f32),
        "ks1": vmem((n - 1, own // 2, STATE), f32),
        "state": chained[0],
        "offered": chained[2],
        "hand": chained[3],
        "edge": vmem((count, 8, both), f32),
        "edge_in": vmem((count, 8, both), f32),
        "gain_grad": vmem((1, channels), f32),
        "vector_grad": vmem((8, LANES), f32),
        "conv_grad": vmem((8, both), f32),
        "mate_in": vmem((chips, rows, width), bf16),
        "chip_in": vmem((chips - 1, rows, width), bf16),
        "dots": vmem((heads_n, count, length), f32),
        "dot_out": vmem((count, length), f32),
        "keyquery_in": vmem((D, STATE), f32),
        "keyquery_sum": vmem((own, STATE), f32),
        "keyquery_other": vmem((own, STATE), f32),
        "keyquery_table": vmem((head_stages - 1, own, STATE), f32),
        "step_table": vmem((n, 16, step_lanes), f32),
        "group_sum": vmem(group_shape, f32),
        "group_table": vmem((head_stages,) + group_shape, f32),
        "line_sum": vmem(line_shape, f32),
        "line_table": vmem((line_stages,) + line_shape, f32),
        "load_sem": dma((3,)),
        "row_sem": dma((3, count)),
        "line_load": dma((2,)),
        "load_two": dma((6,)),
        "grad_sem": dma((count,)),
        "total_sem": dma((3,)),
        "edge_send": dma((count,)),
        "edge_recv": dma((count,)),
        "chain_send": dma((3, count)),
        "chain_recv": dma((3, count)),
        "ring_send": dma((14, n - 1)),
        "ring_recv": dma((14, n - 1)),
        "mate_send": dma((chips, count)),
        "mate_recv": dma((chips, count)),
        "chip_send": dma((chips - 1, count)),
        "chip_recv": dma((chips - 1, count)),
        "rd_send": dma((heads_n - 1,)),
        "rd_recv": dma((heads_n,)),
        "small_send": dma((2,)),
        "small_recv": dma((2,)),
        "kq_send": dma((head_stages - 1,)),
        "kq_recv": dma((head_stages - 1,)),
        "group_send": dma((head_stages,)),
        "group_recv": dma((head_stages,)),
        "line_send": dma((line_stages,)),
        "line_recv": dma((line_stages,)),
        "step_send": dma((n - 1,)),
        "step_recv": dma((n,)),
    }
    first = {
        "weight": vmem(inputs["out_weight_hbm"].shape, bf16),
        "pieces": vmem(pieces.shape, bf16),
        "gate": vmem((count, length, channels), f32),
        "mixed": vmem((count, length, channels), f32),
        "conv": vmem((count, length, both), f32),
        "linear": vmem((2, length, both), bf16),
        "heads_in": vmem((count, length, channels), f32),
        "heads_grad": vmem((count, length, channels), f32),
        "keys": vmem((count, length, STATE), bf16),
        "queries": vmem((count, length, STATE), bf16),
        "scores": vmem((length, length), f32),
        "scores_grad": vmem((length, length), f32),
        "mask_bias": vmem((length, length), f32),
        "narrow_grad": vmem((count, length, 2 * STATE), f32),
        "local": vmem((count, STATE, channels), f32),
        "passed": vmem((count, 8, channels), f32),
        "offer": chained[1],
        "following": chained[4],
        "extended": vmem((2, length + 16, LANES), f32),
        "around": vmem((2, length + 32, LANES), f32),
        "usable": vmem((lags - 1, length + 32, LANES), f32),
        "tails": vmem((count, 16, both), f32),
        "dot_inner": vmem((count, length, LANES), f32),
        "cum_part": vmem((count, length, LANES), f32),
    }
    second = {
        "gate_weight": vmem((D, channels), bf16),
        "value_weight": vmem((D, channels), bf16),
        "keyquery_weight": vmem((D, 2 * STATE), bf16),
        "tokens": vmem((count, length, width), f32),
        "output": vmem((rows, width), f32),
        "teacher": vmem((count, length, width), f32),
        "tokens_grad": vmem((count, length, width), f32),
        "value_part": vmem((D, channels), bf16),
        "keyquery_part": vmem((2, D, STATE), f32),
        "keyquery_half": vmem((D, STATE), f32),
        "part": vmem((heads_n, rows, width), bf16),
        "chip_out": vmem((chips - 1, rows, width), bf16),
        "columns": vmem((1, D), f32),
        "step_whole": vmem((LANES, D), f32),
        "step_part": vmem((n, 16, step_lanes), f32),
        "sums": vmem((3, own, channels), f32),
    }
    names = list(inputs) + list(outs) + list(scratch)
    scoped = (list(first), list(first.values()), list(second), list(second.values()))
    in_hbm = [name.endswith("_hbm") for name in inputs]
    found = pl.pallas_call(
        functools.partial(rear_kernel, names, scoped, heads),
        out_shape=[jax.ShapeDtypeStruct(s, f32) for s in outs.values()],
        in_specs=[hbm if there else in_vmem for there in in_hbm],
        out_specs=[hbm] * 4 + [in_vmem] * (len(outs) - 4),
        scratch_shapes=list(scratch.values()),
        compiler_params=params(cid),
        name="rear",
    )(*inputs.values())
    return dict(zip(outs, found))


def deliver_kernel(count, *refs):
    for source, target in zip(refs[:count], refs[count:]):
        target[...] = source[...]


def deliver(arrays):
    return pl.pallas_call(
        functools.partial(deliver_kernel, len(arrays)),
        out_shape=[jax.ShapeDtypeStruct(a.shape, a.dtype) for a in arrays],
        in_specs=[in_vmem] * len(arrays),
        out_specs=[in_vmem] * len(arrays),
        compiler_params=pltpu.CompilerParams(vmem_limit_bytes=VMEM_LIMIT),
        name="deliver",
    )(*arrays)


def body(
    tokens,
    teacher,
    document_start,
    valid_mask,
    input_gain,
    gate_weight,
    value_weight,
    keyquery_weight,
    step_weight,
    value_conv_weight,
    value_conv_bias,
    keyquery_conv_weight,
    keyquery_conv_bias,
    step_bias,
    rate_log,
    skip_gain,
    norm_gain,
    out_weight,
):
    count, length, _ = tokens.shape
    channels = gate_weight.shape[1]
    width = teacher.shape[2]
    rows = count * length
    lags = value_conv_weight.shape[0]
    vectors = (step_bias, rate_log, skip_gain)
    (
        normed,
        linear,
        conv_linear,
        gate_linear,
        mixed,
        gained,
        halo,
        state_in,
        steps,
        cumulative,
        steps_linear,
        square_rows,
        inverse_rows,
        mask_rows,
    ) = front(
        tokens,
        input_gain,
        value_weight,
        keyquery_weight,
        step_weight.T,
        gate_weight,
        document_start,
        vectors,
        (value_conv_weight, value_conv_bias, keyquery_conv_weight, keyquery_conv_bias),
        norm_gain,
        valid_mask,
        1,
    )
    output, pieces, rowdot, square_total, loss_cols, token_cols = out_phase(
        gained.reshape(rows, channels), out_weight, square_rows, tokens, teacher, mask_rows, 2
    )
    totals = rear(
        {
            "pieces_hbm": pieces,
            "out_weight_hbm": blocked(out_weight, pieces.shape[0]),
            "gate_hbm": gate_linear,
            "mixed_hbm": mixed,
            "conv_hbm": conv_linear,
            "linear_hbm": linear,
            "normed_hbm": normed,
            "gate_weight_hbm": gate_weight,
            "value_weight_hbm": value_weight,
            "keyquery_weight_hbm": keyquery_weight,
            "tokens_hbm": token_cols,
            "output_hbm": output,
            "teacher_hbm": teacher,
            "step_weight": step_weight.T,
            "halo": halo,
            "state_in": state_in,
            "steps": steps,
            "cumulative": cumulative,
            "linear_steps": steps_linear,
            "square": square_total,
            "rowdot": rowdot,
            "docs": document_start,
            "step_bias": step_bias,
            "rate_log": rate_log,
            "skip": skip_gain,
            "value_conv": value_conv_weight,
            "keyquery_conv": keyquery_conv_weight,
            "norm_gain": norm_gain,
            "gain": input_gain,
            "mask": mask_rows,
            "inverse": inverse_rows,
            "loss_cols": loss_cols,
        },
        lags,
        3,
    )
    results = deliver(
        (
            output.reshape(count, length, width),
            totals["loss_total"],
            totals["tokens_grad"],
            totals["input_gain_total"],
            totals["gate_total"],
            totals["value_total"],
            totals["keyquery_total"],
            totals["step_total"],
            totals["value_conv_total"],
            totals["value_offset_total"],
            totals["keyquery_conv_total"],
            totals["keyquery_offset_total"],
            totals["step_bias_total"],
            totals["rate_log_total"],
            totals["skip_total"],
            totals["norm_gain_total"],
            totals["out_total"],
        )
    )
    return (
        results[0],
        results[1].reshape(()),
        *results[2:7],
        results[7].T,
        *results[8:16],
        results[16].T,
    )


def solution(mesh):
    placed = (
        P(None, "seq", None),
        P(None, "seq", "head"),
        P(None, "seq"),
        P(),
        P(),
        P(None, "head"),
        P(None, "head"),
        P(),
        P(None, "head"),
        P(None, "head"),
        P("head"),
        P(),
        P(),
        P("head"),
        P("head"),
        P("head"),
        P("head"),
        P("head", None),
    )
    return jax.shard_map(
        body,
        mesh=mesh,
        in_specs=placed,
        out_specs=(
            P(None, "seq", "head"),
            P(),
            P(None, "seq", "head"),
            P("head"),
            P("seq", "head"),
            P("seq", "head"),
            P("seq", None),
            P("seq", "head"),
            P(None, "head"),
            P("head"),
            P(),
            P(),
            P("head"),
            P("head"),
            P("head"),
            P("head"),
            P("head", "seq"),
        ),
        check_vma=False,
    )
```

time: 600 us -> 225 us (0.38); the launches traced: 594 us -> 225 us
  matrix products: 120 us -> 0 us
  local copies, waits for them, and re-layouts: 86.8 us -> 0 us
  Pallas kernels: 309 us -> 224 us
  other arithmetic: 66.2 us -> 0 us
  starting transfers between devices: 7.08 us -> 0 us
    dot_general x21 -> x0, matrix products: 120 us -> none  [the longest x1 19.2 us: body(): jnp.einsum('bthp,buhp->bhtu', heads_grad, heads_input, precision=highest)]
    pallas_call x6 -> x3, Pallas kernels: 261 us -> 176 us  [the longest x1 132 us: rear(): pl.pallas_call(functools.partial(rear_kernel, names, scoped, heads), out_...]
    slice x27 -> x0, local copies, waits for them, and re-layouts: 28.2 us -> none  [the longest x12 12.1 us: unpacked(): found.append(flat[at:at + a.size].reshape(a.shape))]
    unnamed x174 -> x0, local copies, waits for them, and re-layouts: 17.3 us -> none
    dot_general x5 -> x0, other arithmetic: 17 us -> none  [the longest x1 7.23 us: body(): jnp.einsum('bhtu,bhu->btu', weighted, steps_heads, precision=highest)]
    reshape x13 -> x0, local copies, waits for them, and re-layouts: 15.2 us -> none  [the longest x1 3.71 us: body(): mixed_flat = mixed_heads.reshape(rows, local_inner)]
    another operation x8 -> x0, other arithmetic: 11.7 us -> none
    reduce_sum x7 -> x0, other arithmetic: 11 us -> none  [the longest x1 5.78 us: body(): weight_rows.append(jnp.sum(masked * windows[lag_index], axis=(0, 1)))]
  transfers between devices with their start and end apart: 2 -> 0, of which waited for: 0 -> 0; matrix products, arithmetic and copies ran while one was open for 7% -> 0% of each run, Pallas kernels for 0% -> 0%
where the time goes in v5:
time: 225 us
  Pallas kernels  224 us (100%)
    pallas_call x1, Pallas kernels, rear(): pl.pallas_call(functools.partial(rear_kernel, names, scoped, heads), out_...  132 us
    pallas_call x1, Pallas kernels, out_phase(): pl.pallas_call(functools.partial(out_kernel, n), out_shape=[jax.ShapeDtyp...  47.7 us
    pallas_call x1, Pallas kernels, front(): pl.pallas_call(functools.partial(front_kernel, heads), out_shape=[shape(*...  38.7 us
    pallas_call x1, Pallas kernels, deliver(): pl.pallas_call(functools.partial(deliver_kernel, len(arrays)), out_shape=...  5.53 us

profile of v5, /device:TPU:0, one launch (start us, length us, event | category | flops | bytes accessed | tf_op | source)
XLA Modules:
  0.0 224.8 jit_solution(3221916030949369339)
XLA Ops:
  0.7 38.7 %front.1 = (bf16[4,256,1536]{2,1,0:T(8,128)(2,1)}, bf16[4,256,1024]{2,1,0:T(8,128)(2,1)}, f32[4,256,1024]{2,1,0:T(8,128)}, f32[4,256,768]{2,1,0:T(8,128)}, f32[4...) custom-call(f32[4,256,1536]{2,1,0:T(8,128)} %tokens_hbm.3, ...), custom_call_target="tpu_custom_call" | custom-call | tf_op jit(solution)/shard_map/front/pallas_call | solution.py:1046
  39.4 47.7 %out_phase.1 = (f32[1024,384]{1,0:T(8,128)}, bf16[4,1024,384]{2,1,0:T(8,128)(2,1)}, f32[8,128]{1,0:T(8,128)}, f32[8,128]{1,0:T(8,128)}, f32[1,384]{1,0:T(1,128)}, /*index=5*/f32[4,256,384]{2,1,0:T(8,128)}) custom-call(bf16[1024,768]{1,0:T(8,128)(2,1)} %bitcast.7, bf16[768,1536]{1,0:T(8,128)(2,1)} %refs_1_.1, f32[8,128]{1,0:T(8,128)} %get-tuple-element.71.square_ref, ...), custom_call_target="tpu_custom_call" | custom-call | tf_op jit(solution)/shard_map/out_phase/pallas_call | solution.py:586
  87.1 132.0 %rear.1 = (f32[4,256,384]{2,1,0:T(8,128)}, f32[192,768]{1,0:T(8,128)}, f32[192,768]{1,0:T(8,128)}, f32[192,768]{1,0:T(8,128)}, f32[192,256]{1,0:T(8,128)}, /*ind...) custom-call(bf16[4,1024,384]{2,1,0:T(8,128)(2,1)} %get-tuple-element, ...), custom_call_target="tpu_custom_call" | custom-call | tf_op jit(solution)/shard_map/rear/pallas_call | solution.py:1993
  219.1 5.5 %deliver.1 = (f32[4,256,384]{2,1,0:T(8,128)}, f32[1]{0:T(128)}, f32[4,256,384]{2,1,0:T(8,128)}, f32[384]{0:T(512)}, f32[192,768]{1,0:T(8,128)}, /*index=5*/f32[1...) custom-call(f32[4,256,384]{2,1,0:T(8,128)} %bitcast.6, ...), custom_call_target="tpu_custom_call" | custom-call | tf_op jit(solution)/shard_map/deliver/pallas_call | solution.py:2011

commit v6 on v5

--- a/solution.py
+++ b/solution.py
@@ -56,14 +56,22 @@
     return lax.dot_general(a, b, TN, precision=precision, preferred_element_type=f32)
 
 
+def is_true(condition):
+    return condition.astype(jnp.int32)
+
+
 def ring_place(n, index):
     odd, half = lax.rem(index, 2), lax.div(index, 2)
     return half * (1 - odd) + (n - 1 - half) * odd
 
 
 def ring_index(n, spot):
-    late = lax.div(2 * spot, n)
-    return 2 * spot * (1 - late) + (2 * (n - 1 - spot) + 1) * late
+    late = is_true(2 * spot >= n)
+    return 2 * spot + late * (2 * n - 1 - 4 * spot)
+
+
+def wrapped(n, spot):
+    return spot + n * is_true(spot < 0) - n * is_true(spot >= n)
 
 
 class Ring:
@@ -72,8 +80,8 @@
         self.streams, self.send_sem, self.recv_sem = [], send_sem, recv_sem
         head = lax.axis_index("head")
         self.spot = ring_place(self.n, lax.axis_index("seq"))
-        self.after = (ring_index(self.n, lax.rem(self.spot + 1, self.n)), head)
-        self.before = (ring_index(self.n, lax.rem(self.spot + self.n - 1, self.n)), head)
+        self.after = (ring_index(self.n, wrapped(self.n, self.spot + 1)), head)
+        self.before = (ring_index(self.n, wrapped(self.n, self.spot - 1)), head)
 
     def add(self, part, slots, by_rows=False, first=0):
         rows, width = part.shape[0] // self.n, part.shape[1]
@@ -90,15 +98,16 @@
         part, _, (first, count), columns, way = self.streams[i]
         shift = -1 - step if way == 0 else 1 + step
         rows = part.shape[0] // self.n
-        index = ring_index(self.n, lax.rem(self.spot + shift + 2 * self.n, self.n))
-        return part.at[pl.ds(pl.multiple_of(index * rows + first, 8), count), columns]
+        index = ring_index(self.n, wrapped(self.n, self.spot + shift))
+        tile = 16 if part.dtype == bf16 else 8
+        return part.at[pl.ds(pl.multiple_of(index * rows + first, tile), count), columns]
 
     def copy(self, i, step, source):
         slots, way = self.streams[i][1], self.streams[i][4]
         return remote(
             source,
             slots.at[step],
-            self.send_sem.at[i, step],
+            self.send_sem.at[i],
             self.recv_sem.at[i, step],
             self.after if way == 0 else self.before,
         )
@@ -119,9 +128,14 @@
         return slots[step].astype(f32) + self.piece(i, step + 1)[...].astype(f32)
 
     def finish(self, i):
-        slots = self.streams[i][1]
-        self.copy(i, 0, self.piece(i, 0)).wait_send()
-        loop(self.n - 2, lambda step: self.copy(i, step + 1, slots.at[step]).wait_send())
+        slots, way = self.streams[i][1], self.streams[i][4]
+        remote(
+            slots,
+            slots,
+            self.send_sem.at[i],
+            self.recv_sem.at[i, 0],
+            self.after if way == 0 else self.before,
+        ).wait_send()
 
 
 def ring_slots(n, rows, width, kind):
@@ -346,10 +360,6 @@
         copy.wait_recv()
 
 
-def row_tile(chunk):
-    return pl.ds(pl.multiple_of(chunk * LANES, LANES), LANES)
-
-
 def as_column(row, width):
     tile = jnp.broadcast_to(row, (LANES, row.shape[1])).T
     return jnp.concatenate([tile] * (-(-width // LANES)), axis=1)[:, :width]
@@ -409,152 +419,6 @@
     return start_mate, start_chip, total, finish
 
 
-def out_kernel(
-    n,
-    gated_ref,
-    weight_ref,
-    square_ref,
-    tokens_hbm,
-    teacher_hbm,
-    mask_ref,
-    output_ref,
-    grad_ref,
-    rowdot_ref,
-    squared_ref,
-    loss_ref,
-    tokens_out,
-    tokens_ref,
-    teacher_ref,
-    part,
-    mate_in,
-    chip_out,
-    chip_in,
-    gathered,
-    squares,
-    dots,
-    dot_out,
-    mate_send,
-    mate_recv,
-    chip_send,
-    chip_recv,
-    gm_send,
-    gm_recv,
-    gc_send,
-    gc_recv,
-    gf_send,
-    gf_recv,
-    sq_send,
-    sq_recv,
-    rd_send,
-    rd_recv,
-    load_sem,
-):
-    group = Group(n)
-    count, length, width = tokens_ref.shape
-    if tokens_hbm.shape[2] == width:
-        token_columns = tokens_hbm
-    else:
-        start = pl.multiple_of(group.me * width, LANES)
-        token_columns = tokens_hbm.at[:, :, pl.ds(start, width)]
-    token_load = pltpu.make_async_copy(token_columns, tokens_ref, load_sem.at[0])
-    token_load.start()
-    teacher_load = pltpu.make_async_copy(teacher_hbm, teacher_ref, load_sem.at[1])
-    teacher_load.start()
-    group.greet()
-    chunks = gated_ref.shape[0] // LANES
-    per = length // LANES
-
-    def rows_in(c):
-        return lax.div(c, per), pl.ds(pl.multiple_of(lax.rem(c, per) * LANES, LANES), LANES)
-
-    share(group, square_ref, squares, sq_send, sq_recv)
-    start_mate, start_chip, total, finish = scatter_phases(
-        group, row_tile, part, mate_in, chip_out, chip_in, (mate_send, mate_recv, chip_send, chip_recv)
-    )
-
-    def product(c):
-        rows = gated_ref[row_tile(c)]
-        for j in range(n):
-            block = (
-                weight_ref[:, j * width : (j + 1) * width] if len(weight_ref.shape) == 2 else weight_ref[j]
-            )
-            part[j, row_tile(c)] = jnp.dot(rows, block, preferred_element_type=f32).astype(bf16)
-        start_mate(c)
-
-    loop(chunks, product)
-    loop(chunks, start_chip)
-    shared(group, square_ref, squares, sq_send, sq_recv)
-    squares[group.me] = square_ref[...]
-    loss_ref[...] = jnp.zeros_like(loss_ref)
-
-    def to_mate(c):
-        block = gathered.at[group.me, row_tile(c)]
-        return remote(block, block, gm_send.at[c], gm_recv.at[c], group.at(group.mate))
-
-    def to_chip(c, k):
-        block = gathered.at[group.me, row_tile(c)]
-        return remote(
-            block, block, gc_send.at[k - 1, c], gc_recv.at[k - 1, c], group.at(group.peer(k))
-        )
-
-    def forward(c, k):
-        block = gathered.at[2 * group.chip_before(k) + group.core, row_tile(c)]
-        return remote(
-            block, block, gf_send.at[k - 1, c], gf_recv.at[k - 1, c], group.at(group.mate)
-        )
-
-    token_load.wait()
-    teacher_load.wait()
-    token_store = pltpu.make_async_copy(tokens_ref, tokens_out, load_sem.at[0])
-    token_store.start()
-
-    def rest(c):
-        squared = squares[0, pl.ds(c, 1)]
-        for j in range(1, n):
-            squared = squared + squares[j, pl.ds(c, 1)]
-        squared_ref[pl.ds(c, 1)] = squared
-        scale = lax.rsqrt(squared * (1.0 / (NHEADS * HEADDIM)) + norm_eps)
-        branch = total(c) * as_column(scale, width)
-        output = tokens_ref[rows_in(c)] + branch
-        output_ref[row_tile(c)] = output
-        difference = output - teacher_ref[rows_in(c)]
-        weighted = difference * as_column(mask_ref[pl.ds(c, 1)], width)
-        low = weighted.astype(bf16)
-        gathered[group.me, row_tile(c)] = low
-        to_mate(c).start()
-        for k in range(1, group.chips):
-            to_chip(c, k).start()
-        loss_ref[...] += jnp.sum(weighted * difference, axis=0, keepdims=True)
-        dot_out[pl.ds(c, 1)] = rows_of(low.astype(f32) * branch)
-
-    loop(chunks, rest)
-    share(group, dot_out, dots, rd_send, rd_recv)
-
-    def pass_on(c):
-        for k in range(1, group.chips):
-            to_chip(c, k).wait_recv()
-            forward(c, k).start()
-
-    loop(chunks, pass_on)
-
-    def end(c):
-        to_mate(c).wait()
-        for k in range(1, group.chips):
-            to_chip(c, k).wait_send()
-            forward(c, k).wait()
-        finish(c)
-        for j in range(n):
-            grad_ref[j, row_tile(c)] = gathered[j, row_tile(c)]
-
-    loop(chunks, end)
-    shared(group, dot_out, dots, rd_send, rd_recv)
-    row_sum = dot_out[...]
-    for k in range(1, n):
-        row_sum = row_sum + dots[group.other(k)]
-    rowdot_ref[...] = row_sum
-    token_store.wait()
-
-
 def scatter_scratch(n, rows, width, chunks):
     chips = n // 2
     dma = pltpu.SemaphoreType.DMA
@@ -573,55 +437,6 @@
     return jnp.moveaxis(weight.reshape(weight.shape[0], n, width), 1, 0)
 
 
-def out_phase(gated, weight, square_rows, tokens, teacher, mask_rows, cid):
-    n = lax.axis_size("head")
-    count, length, width = teacher.shape
-    rows = count * length
-    chips, chunks = n // 2, rows // LANES
-    if width % LANES:
-        tokens = lax.dynamic_slice_in_dim(tokens, lax.axis_index("head") * width, width, 2)
-    buffers, sems = scatter_scratch(n, rows, width, chunks)
-    dma = pltpu.SemaphoreType.DMA
-    hbm = pl.BlockSpec(memory_space=pl.ANY)
-    return pl.pallas_call(
-        functools.partial(out_kernel, n),
-        out_shape=[
-            jax.ShapeDtypeStruct((rows, width), f32),
-            jax.ShapeDtypeStruct((n, rows, width), bf16),
-            jax.ShapeDtypeStruct((chunks, LANES), f32),
-            jax.ShapeDtypeStruct((chunks, LANES), f32),
-            jax.ShapeDtypeStruct((1, width), f32),
-            jax.ShapeDtypeStruct((count, length, width), f32),
-        ],
-        in_specs=[in_vmem] * 3 + [hbm] * 2 + [in_vmem],
-        out_specs=[in_vmem] * 5 + [hbm],
-        scratch_shapes=[pltpu.VMEM((count, length, width), f32)] * 2
-        + buffers
-        + [
-            pltpu.VMEM((n, rows, width), bf16),
-            pltpu.VMEM((n, chunks, LANES), f32),
-            pltpu.VMEM((n, chunks, LANES), f32),
-            pltpu.VMEM((chunks, LANES), f32),
-        ]
-        + sems
-        + [
-            dma((chunks,)),
-            dma((chunks,)),
-            dma((chips - 1, chunks)),
-            dma((chips - 1, chunks)),
-            dma((chips - 1, chunks)),
-            dma((chips - 1, chunks)),
-            dma((n - 1,)),
-            dma((n,)),
-            dma((n - 1,)),
-            dma((n,)),
-            dma((2,)),
-        ],
-        compiler_params=params(cid),
-        name="out_phase",
-    )(gated, blocked(weight, n), square_rows, tokens, teacher, mask_rows)
-
-
 def blocks(width, size=256):
     return [(at, min(size, width - at)) for at in range(0, width, size)]
 
@@ -685,6 +500,12 @@
 def long_row(ref, b, length):
     per = length // LANES
     return jnp.concatenate([ref[pl.ds(b * per + i, 1)] for i in range(per)], axis=1)
+
+
+def put_row(ref, b, row):
+    per = row.shape[1] // LANES
+    for i in range(per):
+        ref[pl.ds(b * per + i, 1)] = row[:, i * LANES : (i + 1) * LANES]
 
 
 def spread_row(row, marks):
@@ -716,12 +537,15 @@
     keyquery_offset_ref,
     norm_gain_ref,
     valid_ref,
+    out_weight_hbm,
+    teacher_hbm,
     normed_out,
     linear_out,
     conv_out,
     gate_out,
     mixed_out,
-    gained_out,
+    output_out,
+    pieces_out,
     halo_out,
     state_out,
     steps_out,
@@ -730,6 +554,9 @@
     square_out,
     inverse_out,
     mask_out,
+    rowdot_ref,
+    squared_ref,
+    loss_ref,
     tokens,
     last_tokens,
     value_weight,
@@ -764,10 +591,41 @@
     halo_sem,
     chain_send,
     chain_recv,
+    out_weight,
+    teacher,
+    output_cols,
+    part,
+    mate_in,
+    chip_out,
+    chip_in,
+    gathered,
+    squares,
+    dots,
+    dot_out,
+    mate_send,
+    mate_recv,
+    chip_send,
+    chip_recv,
+    gm_send,
+    gm_recv,
+    gc_send,
+    gc_recv,
+    gf_send,
+    gf_recv,
+    sq_send,
+    sq_recv,
+    rd_send,
+    rd_recv,
+    output_sem,
+    pieces_sem,
 ):
     n = lax.axis_size("seq")
     place = lax.axis_index("seq")
-    head = lax.axis_index("head")
+    heads_n = lax.axis_size("head")
+    group = Group(heads_n)
+    head = group.me
+    width = teacher.shape[2]
+    chunks = tokens.shape[0]
     count, length, _ = tokens.shape
     channels = value_weight.shape[1]
     both = channels + 2 * STATE
@@ -778,6 +636,8 @@
         pltpu.make_async_copy(value_hbm, value_weight, load_sem.at[0]),
         pltpu.make_async_copy(keyquery_hbm, keyquery_weight, load_sem.at[1]),
         pltpu.make_async_copy(gate_hbm, gate_weight, load_sem.at[2]),
+        pltpu.make_async_copy(out_weight_hbm, out_weight, load_sem.at[3]),
+        pltpu.make_async_copy(teacher_hbm, teacher, load_sem.at[4]),
     ]
 
     def token_load(b):
@@ -794,7 +654,8 @@
     loads[1].start()
     for b in range(count):
         token_load(b).start()
-    loads[2].start()
+    for copy in loads[2:]:
+        copy.start()
 
     stores = [
         (normed, normed_out),
@@ -802,7 +663,6 @@
         (conv, conv_out),
         (gate, gate_out),
         (mixed, mixed_out),
-        (gained, gained_out),
     ]
 
     def store(i, b):
@@ -820,6 +680,10 @@
         chain_send,
         chain_recv,
     )
+    for k in range(1, heads_n):
+        pl.semaphore_signal(
+            barrier, inc=1, device_id=group.at(group.other(k)), device_id_type=MESH
+        )
     for k in range(1, n):
         pl.semaphore_signal(
             barrier, inc=1, device_id=(lax.rem(place + k, n), head), device_id_type=MESH
@@ -834,12 +698,12 @@
     last = jnp.concatenate([normalized(last_tokens[b])[1] for b in range(count)], axis=0)
     loads[0].wait()
     loads[1].wait()
-    for at, width in blocks(channels):
-        tail[:, at : at + width] = jnp.dot(
-            last, value_weight[:, at : at + width], preferred_element_type=f32
+    for at, size in blocks(channels):
+        tail[:, at : at + size] = jnp.dot(
+            last, value_weight[:, at : at + size], preferred_element_type=f32
         ).astype(bf16)
     tail[:, channels:] = jnp.dot(last, keyquery_weight[...], preferred_element_type=f32).astype(bf16)
-    pl.semaphore_wait(barrier, n - 1)
+    pl.semaphore_wait(barrier, n + heads_n - 2)
     halo_copy = remote(tail, halo, halo_sem.at[0], halo_sem.at[1], (place + 1, head))
 
     @pl.when(place < n - 1)
@@ -864,9 +728,9 @@
 
     def project_values(b):
         rows = normed[b]
-        for at, width in blocks(channels):
-            linear[b, :, at : at + width] = jnp.dot(
-                rows, value_weight[:, at : at + width], preferred_element_type=f32
+        for at, size in blocks(channels):
+            linear[b, :, at : at + size] = jnp.dot(
+                rows, value_weight[:, at : at + size], preferred_element_type=f32
             ).astype(bf16)
 
     def project_rest(b):
@@ -929,12 +793,12 @@
         passed[b] = spread(last_entering, marks)
 
     pairs = channels // LANES
-    turns = (
-        [(b + 1 + k, k, b) for b, k in ((0, 0), (1, 0), (2, 0), (0, 1), (1, 1), (0, 2))]
-        + [(5, 0, 3), (5, 1, 2), (5, 2, 1), (5, 3, 0), (7, 1, 3), (7, 2, 2), (7, 3, 1)]
-        if n == 8 and count == 4
-        else []
-    )
+    turns = []
+    if n == 8 and count == 4:
+        turns = [(1, 0, 0), (2, 0, 1), (3, 0, 2), (5, 0, 3)]
+        turns += [(2, 1, 0), (3, 1, 1), (5, 1, 2), (7, 1, 3)]
+        turns += [(3, 2, 0), (5, 2, 1), (7, 2, 2), (9, 2, 3)]
+        turns += [(5, 3, 0), (7, 3, 1), (9, 3, 2), (10, 3, 3)]
 
     def begin_sequence(b):
         norm(b)
@@ -978,9 +842,9 @@
                 value = value + jnp.dot(mixing, mine, preferred_element_type=f32)
             mixed[b, :, lanes] = value
         rows = normed[b]
-        for at, width in blocks(channels):
-            gate[b, :, at : at + width] = jnp.dot(
-                rows, gate_weight[:, at : at + width], preferred_element_type=f32
+        for at, size in blocks(channels):
+            gate[b, :, at : at + size] = jnp.dot(
+                rows, gate_weight[:, at : at + size], preferred_element_type=f32
             )
         store(3, b).start()
         chain.turn(count + b, turns)
@@ -998,14 +862,124 @@
         linear_gate = gate[b]
         gated = value * (linear_gate * jax.nn.sigmoid(linear_gate))
         gained[b] = (gated * norm_gain_ref[...][None, :]).astype(bf16)
-        store(5, b).start()
-        squared = rows_of(gated * gated)
-        for i in range(length // LANES):
-            square_out[pl.ds(b * (length // LANES) + i, 1)] = squared[
-                :, i * LANES : (i + 1) * LANES
-            ]
-
-    loop(count, close)
+        put_row(square_out, b, rows_of(gated * gated))
+
+    def row_block(c):
+        return pl.ds(pl.multiple_of(c * length, length), length)
+
+    start_mate, start_chip, total, finish = scatter_phases(
+        group, row_block, part, mate_in, chip_out, chip_in, (mate_send, mate_recv, chip_send, chip_recv)
+    )
+
+    def product(c):
+        rows = gained[c]
+        for j in range(heads_n):
+            block = (
+                out_weight[:, j * width : (j + 1) * width] if len(out_weight.shape) == 2 else out_weight[j]
+            )
+            part[j, row_block(c)] = jnp.dot(rows, block, preferred_element_type=f32).astype(bf16)
+        start_mate(c)
+
+    loads[3].wait()
+
+    def close_and_send(b):
+        close(b)
+        product(b)
+
+        @pl.when(b > 0)
+        def _():
+            start_chip(b - 1)
+
+        chain.turn(9 + b, turns)
+
+    loop(count, close_and_send)
+    start_chip(count - 1)
+    share(group, square_out, squares, sq_send, sq_recv)
+    shared(group, square_out, squares, sq_send, sq_recv)
+    squares[group.me] = square_out[...]
+    loss_ref[...] = jnp.zeros_like(loss_ref)
+
+    def to_mate(c):
+        block = gathered.at[group.me, row_block(c)]
+        return remote(block, block, gm_send.at[c], gm_recv.at[c], group.at(group.mate))
+
+    def to_chip(c, k):
+        block = gathered.at[group.me, row_block(c)]
+        return remote(
+            block, block, gc_send.at[k - 1, c], gc_recv.at[k - 1, c], group.at(group.peer(k))
+        )
+
+    def forward(c, k):
+        block = gathered.at[2 * group.chip_before(k) + group.core, row_block(c)]
+        return remote(
+            block, block, gf_send.at[k - 1, c], gf_recv.at[k - 1, c], group.at(group.mate)
+        )
+
+    loads[4].wait()
+
+    def own_tokens(c):
+        if width % LANES == 0:
+            return tokens[c, :, pl.ds(pl.multiple_of(head * width, LANES), width)]
+        found = jnp.zeros((length, width), f32)
+        for j in range(heads_n):
+            mine = tokens[c, :, j * width : (j + 1) * width]
+            found = found + jnp.where(head == j, mine, 0.0)
+        return found
+
+    def rest(c):
+        squared = long_row(squares.at[0], c, length)
+        for j in range(1, heads_n):
+            squared = squared + long_row(squares.at[j], c, length)
+        put_row(squared_ref, c, squared)
+        scale = lax.rsqrt(squared * (1.0 / (NHEADS * HEADDIM)) + norm_eps)
+        branch = total(c) * as_column(scale, width)
+        output = own_tokens(c) + branch
+        output_cols[row_block(c)] = output
+        difference = output - teacher[c]
+        weighted = difference * as_column(long_row(mask_out, c, length), width)
+        low = weighted.astype(bf16)
+        gathered[group.me, row_block(c)] = low
+        to_mate(c).start()
+        for k in range(1, group.chips):
+            to_chip(c, k).start()
+        loss_ref[...] += jnp.sum(weighted * difference, axis=0, keepdims=True)
+        put_row(dot_out, c, rows_of(low.astype(f32) * branch))
+
+    loop(chunks, rest)
+    output_store = pltpu.make_async_copy(output_cols, output_out, output_sem.at[0])
+    output_store.start()
+    share(group, dot_out, dots, rd_send, rd_recv)
+
+    def pass_on(c):
+        for k in range(1, group.chips):
+            to_chip(c, k).wait_recv()
+            forward(c, k).start()
+
+    loop(chunks, pass_on)
+
+    def pieces_store(c):
+        return pltpu.make_async_copy(
+            gathered.at[pl.ds(0, heads_n), row_block(c)],
+            pieces_out.at[pl.ds(0, heads_n), row_block(c)],
+            pieces_sem.at[c],
+        )
+
+    def end(c):
+        to_mate(c).wait()
+        for k in range(1, group.chips):
+            to_chip(c, k).wait_send()
+            forward(c, k).wait()
+        finish(c)
+        pieces_store(c).start()
+
+    loop(chunks, end)
+    shared(group, dot_out, dots, rd_send, rd_recv)
+    row_sum = dot_out[...]
+    for k in range(1, heads_n):
+        row_sum = row_sum + dots[group.other(k)]
+    rowdot_ref[...] = row_sum
+    output_store.wait()
+    loop(chunks, lambda c: pieces_store(c).wait())
 
     @pl.when(place < n - 1)
     def _():
@@ -1017,7 +991,7 @@
         loop(count, lambda b, i=i: store(i, b).wait())
 
 
-def front(tokens, gain, value_weight, keyquery_weight, step_weight, gate_weight, docs, vectors, conv, norm_gain, valid, cid):
+def front(tokens, gain, value_weight, keyquery_weight, step_weight, gate_weight, docs, vectors, conv, norm_gain, valid, out_weight, teacher, cid):
     count, length, _ = tokens.shape
     channels = value_weight.shape[1]
     heads = channels // HEADDIM
@@ -1025,14 +999,19 @@
     dma = pltpu.SemaphoreType.DMA
     hbm = pl.BlockSpec(memory_space=pl.ANY)
     shape = jax.ShapeDtypeStruct
+    heads_n, width = lax.axis_size("head"), teacher.shape[2]
+    rows, chips = count * length, heads_n // 2
+    chunks, lines = count, rows // LANES
+    out_weight = blocked(out_weight, heads_n)
+    buffers, sems = scatter_scratch(heads_n, rows, width, chunks)
     big = [
         ((count, length, D), bf16),
         ((count, length, both), bf16),
         ((count, length, both), f32),
         ((count, length, channels), f32),
         ((count, length, channels), f32),
-        ((count, length, channels), bf16),
     ]
+    results = [((rows, width), f32), ((heads_n, rows, width), bf16)]
     small = [
         ((count * 16, both), bf16),
         ((count, STATE, channels), bf16),
@@ -1042,12 +1021,15 @@
         ((count * length // LANES, LANES), f32),
         ((count, length), f32),
         ((count * length // LANES, LANES), f32),
+        ((lines, LANES), f32),
+        ((lines, LANES), f32),
+        ((1, width), f32),
     ]
     return pl.pallas_call(
         functools.partial(front_kernel, heads),
-        out_shape=[shape(*s) for s in big + small],
-        in_specs=[hbm, in_vmem, hbm, hbm, in_vmem, hbm] + [in_vmem] * 10,
-        out_specs=[hbm] * len(big) + [in_vmem] * len(small),
+        out_shape=[shape(*s) for s in big + results + small],
+        in_specs=[hbm, in_vmem, hbm, hbm, in_vmem, hbm] + [in_vmem] * 10 + [hbm] * 2,
+        out_specs=[hbm] * (len(big) + 2) + [in_vmem] * len(small),
         scratch_shapes=[
             pltpu.VMEM((count, length, D), f32),
             pltpu.VMEM((count, 16, D), f32),
@@ -1057,6 +1039,7 @@
         ]
         + [pltpu.VMEM(*s) for s in big]
         + [
+            pltpu.VMEM((count, length, channels), bf16),
             pltpu.VMEM((count * 16, both), bf16),
             pltpu.VMEM((count * 16, both), bf16),
             pltpu.VMEM((length + 16, both), f32),
@@ -1071,17 +1054,42 @@
         + [
             pltpu.VMEM((count, 8, channels), f32),
             pltpu.VMEM((count, length, LANES), f32),
-            dma((3,)),
+            dma((5,)),
             dma((count,)),
             dma((count,)),
             dma((len(big), count)),
             dma((2,)),
             dma((3, count)),
             dma((3, count)),
+            pltpu.VMEM(out_weight.shape, bf16),
+            pltpu.VMEM((count, length, width), f32),
+            pltpu.VMEM((rows, width), f32),
+        ]
+        + buffers
+        + [
+            pltpu.VMEM((heads_n, rows, width), bf16),
+            pltpu.VMEM((heads_n, lines, LANES), f32),
+            pltpu.VMEM((heads_n, lines, LANES), f32),
+            pltpu.VMEM((lines, LANES), f32),
+        ]
+        + sems
+        + [
+            dma((chunks,)),
+            dma((chunks,)),
+            dma((chips - 1, chunks)),
+            dma((chips - 1, chunks)),
+            dma((chips - 1, chunks)),
+            dma((chips - 1, chunks)),
+            dma((heads_n - 1,)),
+            dma((heads_n,)),
+            dma((heads_n - 1,)),
+            dma((heads_n,)),
+            dma((1,)),
+            dma((chunks,)),
         ],
         compiler_params=params(cid),
         name="front",
-    )(tokens, gain, value_weight, keyquery_weight, step_weight, gate_weight, docs, *vectors, *conv, norm_gain, valid)
+    )(tokens, gain, value_weight, keyquery_weight, step_weight, gate_weight, docs, *vectors, *conv, norm_gain, valid, out_weight, teacher)
 
 
 class Doubling:
@@ -1190,17 +1198,19 @@
     r.vector_grad[...] = jnp.zeros_like(r.vector_grad)
     r.conv_grad[...] = jnp.zeros_like(r.conv_grad)
     ring = Ring(r.ring_send, r.ring_recv)
-    def matrix(part, slots):
+    def matrix(part, slots, cut):
         first = len(ring.streams)
-        if quarters:
-            ring.add(part, slots[:2], by_rows=True)
-            ring.add(part, slots[2:], by_rows=True, first=own // 2)
-            return first, first + 2
-        ring.add(part, slots[:2])
-        return (first,)
-
-    out_halves = matrix(r.out_part, (r.os0, r.os1, r.os2, r.os3))
-    gate_halves = matrix(r.gate_part, (r.gs0, r.gs1, r.gs2, r.gs3))
+        if not quarters:
+            ring.add(part, slots[:2])
+            return (first,)
+        ring.add(part, slots[:2], by_rows=True)
+        if not cut:
+            return (first,)
+        ring.add(part, slots[2:], by_rows=True, first=own // 2)
+        return first, first + 2
+
+    out_halves = matrix(r.out_part, (r.os0, r.os1), False)
+    gate_halves = matrix(r.gate_part, (r.gs0, r.gs1), False)
 
     def pass_on(first, step):
         @pl.when((step >= 0) & (step < ring_steps))
@@ -1546,6 +1556,10 @@
 
     def phase_two(*locals_two):
         q = types.SimpleNamespace(**dict(zip(scoped[2], locals_two)))
+        token_columns = r.tokens_hbm
+        if token_columns.shape[2] != width:
+            first_column = pl.multiple_of(head * width, LANES)
+            token_columns = token_columns.at[:, :, pl.ds(first_column, width)]
         loads = [
             pltpu.make_async_copy(source, target, r.load_two.at[i])
             for i, (source, target) in enumerate(
@@ -1553,7 +1567,7 @@
                     (r.gate_weight_hbm, q.gate_weight),
                     (r.value_weight_hbm, q.value_weight),
                     (r.keyquery_weight_hbm, q.keyquery_weight),
-                    (r.tokens_hbm, q.tokens),
+                    (token_columns, q.tokens),
                     (r.output_hbm, q.output),
                     (r.teacher_hbm, q.teacher),
                 ]
@@ -1561,7 +1575,7 @@
         ]
         for copy in loads:
             copy.start()
-        value_halves = matrix(q.value_part, (r.vs0, r.vs1, r.vs2, r.vs3))
+        value_halves = matrix(q.value_part, (r.vs0, r.vs1, r.vs2, r.vs3), True)
         keyquery_first = len(ring.streams)
         ring.add(q.keyquery_half, (r.ks0, r.ks1), by_rows=True)
 
@@ -1868,9 +1882,11 @@
         "loss_total": (1,),
     }
     if own % 64 == 0:
+        wide_slots = [vmem((n - 1, own // 2, channels), bf16)] * 2
         slots = [vmem((n - 1, own // 4, channels), bf16)] * 4
     else:
-        slots = ring_slots(n, own, channels, bf16) + [vmem((16, LANES), bf16)] * 2
+        wide_slots = ring_slots(n, own, channels, bf16)
+        slots = wide_slots + [vmem((16, LANES), bf16)] * 2
     chained = chain_buffers(count, channels)
     scratch = {
         "normed": vmem((count, length, D), bf16),
@@ -1879,14 +1895,10 @@
         "narrow": vmem((count, length, 2 * STATE + LANES), bf16),
         "out_part": vmem((D, channels), bf16),
         "gate_part": vmem((D, channels), bf16),
-        "os0": slots[0],
-        "os1": slots[1],
-        "os2": slots[2],
-        "os3": slots[3],
-        "gs0": slots[0],
-        "gs1": slots[1],
-        "gs2": slots[2],
-        "gs3": slots[3],
+        "os0": wide_slots[0],
+        "os1": wide_slots[1],
+        "gs0": wide_slots[0],
+        "gs1": wide_slots[1],
         "vs0": slots[0],
         "vs1": slots[1],
         "vs2": slots[2],
@@ -1924,8 +1936,8 @@
         "edge_recv": dma((count,)),
         "chain_send": dma((3, count)),
         "chain_recv": dma((3, count)),
-        "ring_send": dma((14, n - 1)),
-        "ring_recv": dma((14, n - 1)),
+        "ring_send": dma((10,)),
+        "ring_recv": dma((10, n - 1)),
         "mate_send": dma((chips, count)),
         "mate_recv": dma((chips, count)),
         "chip_send": dma((chips - 1, count)),
@@ -2050,7 +2062,8 @@
         conv_linear,
         gate_linear,
         mixed,
-        gained,
+        output,
+        pieces,
         halo,
         state_in,
         steps,
@@ -2059,6 +2072,9 @@
         square_rows,
         inverse_rows,
         mask_rows,
+        rowdot,
+        square_total,
+        loss_cols,
     ) = front(
         tokens,
         input_gain,
@@ -2071,11 +2087,13 @@
         (value_conv_weight, value_conv_bias, keyquery_conv_weight, keyquery_conv_bias),
         norm_gain,
         valid_mask,
+        out_weight,
+        teacher,
         1,
     )
-    output, pieces, rowdot, square_total, loss_cols, token_cols = out_phase(
-        gained.reshape(rows, channels), out_weight, square_rows, tokens, teacher, mask_rows, 2
-    )
+    token_cols = tokens
+    if width % LANES:
+        token_cols = lax.dynamic_slice_in_dim(tokens, lax.axis_index("head") * width, width, 2)
     totals = rear(
         {
             "pieces_hbm": pieces,

time: 225 us -> 210 us (0.933)
  Pallas kernels: 224 us -> 209 us
    pallas_call x1 -> x0, Pallas kernels: 47.7 us -> none  [out_phase(): pl.pallas_call(functools.partial(out_kernel, n), out_shape=[jax.ShapeDtyp...]
    pallas_call x1, Pallas kernels: 38.7 us -> 80.3 us  [front(): pl.pallas_call(functools.partial(front_kernel, heads), out_shape=[shape(*...]
    pallas_call x1, Pallas kernels: 132 us -> 123 us  [rear(): pl.pallas_call(functools.partial(rear_kernel, names, scoped, heads), out_...]
where the time goes in v6:
time: 210 us
  Pallas kernels  209 us (100%)
    pallas_call x1, Pallas kernels, rear(): pl.pallas_call(functools.partial(rear_kernel, names, scoped, heads), out_...  123 us
    pallas_call x1, Pallas kernels, front(): pl.pallas_call(functools.partial(front_kernel, heads), out_shape=[shape(*...  80.3 us
    pallas_call x1, Pallas kernels, deliver(): pl.pallas_call(functools.partial(deliver_kernel, len(arrays)), out_shape=...  5.47 us

profile of v6, /device:TPU:0, one launch (start us, length us, event | category | flops | bytes accessed | tf_op | source)
XLA Modules:
  0.0 210.1 jit_solution(7393167966765219315)
XLA Ops:
  0.7 80.3 %front.1 = (bf16[4,256,1536]{2,1,0:T(8,128)(2,1)}, bf16[4,256,1024]{2,1,0:T(8,128)(2,1)}, f32[4,256,1024]{2,1,0:T(8,128)}, f32[4,256,768]{2,1,0:T(8,128)}, f32[4...) custom-call(f32[4,256,1536]{2,1,0:T(8,128)} %refs_10_.1, ...), custom_call_target="tpu_custom_call" | custom-call | tf_op jit(solution)/shard_map/front/pallas_call | solution.py:1028
  81.0 123.5 %rear.1 = (f32[4,256,384]{2,1,0:T(8,128)}, f32[192,768]{1,0:T(8,128)}, f32[192,768]{1,0:T(8,128)}, f32[192,768]{1,0:T(8,128)}, f32[192,256]{1,0:T(8,128)}, /*ind...) custom-call(bf16[4,1024,384]{2,1,0:T(8,128)(2,1)} %get-tuple-element, ...), custom_call_target="tpu_custom_call" | custom-call | tf_op jit(solution)/shard_map/rear/pallas_call | solution.py:2005
  204.5 5.5 %deliver.1 = (f32[4,256,384]{2,1,0:T(8,128)}, f32[1]{0:T(128)}, f32[4,256,384]{2,1,0:T(8,128)}, f32[384]{0:T(512)}, f32[192,768]{1,0:T(8,128)}, /*index=5*/f32[1...) custom-call(f32[4,256,384]{2,1,0:T(8,128)} %bitcast.5, ...), custom_call_target="tpu_custom_call" | custom-call | tf_op jit(solution)/shard_map/deliver/pallas_call | solution.py:2023

commit v7 on v6

--- a/solution.py
+++ b/solution.py
@@ -1676,11 +1676,13 @@
         total_copies = [end_ring(0, out_halves, len(out_steps))]
         product(1)
         weights_turn(28)
+        keyquery_turn(0)
         product(2)
         value_turn(0)
-        keyquery_turn(0)
+        keyquery_turn(1)
         product(3)
         start_chip(count - 1)
+        keyquery_turn(2)
         weights_turn(30)
         share(group, r.dot_out, r.dots, r.rd_send, r.rd_recv)
 
@@ -1706,7 +1708,7 @@
         tiles.put(fold_lanes(r.loss_cols[...]))
         group_total.start(0)
         value_turn(1)
-        keyquery_turn(1)
+        keyquery_turn(3)
 
         for at, size in blocks(D):
             whole = jnp.concatenate([r.normed[b, :, at : at + size] for b in range(count)], axis=0)
@@ -1729,7 +1731,7 @@
             step_copy(k, lax.rem(place + k, n), place).start()
         total_copies.append(end_ring(1, gate_halves, len(gate_steps)))
         value_turn(2)
-        keyquery_turn(2)
+        keyquery_turn(4)
         group_total.run(0, 1)
         shared(group, r.dot_out, r.dots, r.rd_send, r.rd_recv)
         r.dots[head] = r.dot_out[...]
@@ -1769,30 +1771,39 @@
         rest(0)
         rest(1)
         value_turn(3)
-        keyquery_turn(3)
+        keyquery_turn(5)
         group_total.run(1)
         fill_line()
         line_total.start(0)
         rest(2)
+        if ring_steps > 6:
+            loop(ring_steps - 6, lambda s: pass_on(keyquery_first, s + 6))
         value_turn(4)
-        keyquery_turn(4)
         line_total.run(0, 1)
         for c in range(3, count):
             rest(c)
-        value_turn(5)
-        keyquery_turn(5)
-        line_total.run(1, 2)
-        if ring_steps > 6:
-
-            def remaining(s):
-                for first in value_halves + (keyquery_first,):
-                    pass_on(first, s + 6)
-
-            loop(ring_steps - 6, remaining)
         for k in (keyquery_first, keyquery_first + 1):
             _, _, (first, lines), _, _ = ring.streams[k]
             r.keyquery_sum[first : first + lines] = ring.last(k)
         chip_total.start(0)
+        value_turn(5)
+        line_total.run(1, 2)
+        chip_total.run(0)
+        keyquery_swap = remote(
+            r.keyquery_sum,
+            r.keyquery_other,
+            r.small_send.at[1],
+            r.small_recv.at[1],
+            group.at(group.mate),
+        )
+        keyquery_swap.start()
+        if ring_steps > 6:
+
+            def remaining(s):
+                for first in value_halves:
+                    pass_on(first, s + 6)
+
+            loop(ring_steps - 6, remaining)
         total_copies.append(total_of(2, value_halves, q.sums, targets))
         for k in range(1, n):
             sender = lax.rem(place + k, n)
@@ -1805,15 +1816,6 @@
             step_sum = step_sum + r.step_table[s]
         r.step_total[...] = step_sum[:heads, :own]
         line_total.run(2)
-        chip_total.run(0)
-        keyquery_swap = remote(
-            r.keyquery_sum,
-            r.keyquery_other,
-            r.small_send.at[1],
-            r.small_recv.at[1],
-            group.at(group.mate),
-        )
-        keyquery_swap.start()
 
         tiles = Tiles(r.line_sum)
         for lag in range(lags + 1):
@@ -2015,16 +2017,29 @@
 
 
 def deliver_kernel(count, *refs):
-    for source, target in zip(refs[:count], refs[count:]):
-        target[...] = source[...]
+    sources, targets, held = refs[:count], refs[count : 2 * count], refs[2 * count : 3 * count]
+    sem = refs[3 * count]
+    loads = [pltpu.make_async_copy(a, b, sem.at[0, i]) for i, (a, b) in enumerate(zip(sources, held))]
+    stores = [pltpu.make_async_copy(a, b, sem.at[1, i]) for i, (a, b) in enumerate(zip(held, targets))]
+    for copy in loads:
+        copy.start()
+    for load, store in zip(loads, stores):
+        load.wait()
+        store.start()
+    for copy in stores:
+        copy.wait()
 
 
 def deliver(arrays):
+    hbm = pl.BlockSpec(memory_space=pl.ANY)
+    count = len(arrays)
     return pl.pallas_call(
-        functools.partial(deliver_kernel, len(arrays)),
+        functools.partial(deliver_kernel, count),
         out_shape=[jax.ShapeDtypeStruct(a.shape, a.dtype) for a in arrays],
-        in_specs=[in_vmem] * len(arrays),
-        out_specs=[in_vmem] * len(arrays),
+        in_specs=[hbm] * count,
+        out_specs=[hbm] * count,
+        scratch_shapes=[pltpu.VMEM(a.shape, a.dtype) for a in arrays]
+        + [pltpu.SemaphoreType.DMA((2, count))],
         compiler_params=pltpu.CompilerParams(vmem_limit_bytes=VMEM_LIMIT),
         name="deliver",
     )(*arrays)

time: 210 us -> 209 us (level)
  no operation moved by 1% of the time
where the time goes in v7:
time: 209 us; the launch traced here: 208 us
  Pallas kernels  208 us (100%)
    pallas_call x1, Pallas kernels, rear(): pl.pallas_call(functools.partial(rear_kernel, names, scoped, heads), out_...  123 us
    pallas_call x1, Pallas kernels, front(): pl.pallas_call(functools.partial(front_kernel, heads), out_shape=[shape(*...  80.3 us
    pallas_call x1, Pallas kernels, deliver(): pl.pallas_call(functools.partial(deliver_kernel, count), out_shape=[jax.S...  4.64 us

profile of v7, /device:TPU:0, one launch (start us, length us, event | category | flops | bytes accessed | tf_op | source)
XLA Modules:
  0.0 208.5 jit_solution(3600757073715490505)
XLA Ops:
  0.7 80.3 %front.1 = (bf16[4,256,1536]{2,1,0:T(8,128)(2,1)}, bf16[4,256,1024]{2,1,0:T(8,128)(2,1)}, f32[4,256,1024]{2,1,0:T(8,128)}, f32[4,256,768]{2,1,0:T(8,128)}, f32[4...) custom-call(f32[4,256,1536]{2,1,0:T(8,128)} %refs_10_.1, ...), custom_call_target="tpu_custom_call" | custom-call | tf_op jit(solution)/shard_map/front/pallas_call | solution.py:1028
  81.0 122.6 %rear.1 = (f32[4,256,384]{2,1,0:T(8,128)}, f32[192,768]{1,0:T(8,128)}, f32[192,768]{1,0:T(8,128)}, f32[192,768]{1,0:T(8,128)}, f32[192,256]{1,0:T(8,128)}, /*ind...) custom-call(bf16[4,1024,384]{2,1,0:T(8,128)(2,1)} %get-tuple-element, ...), custom_call_target="tpu_custom_call" | custom-call | tf_op jit(solution)/shard_map/rear/pallas_call | solution.py:2007
  203.6 4.6 %deliver.1 = (f32[4,256,384]{2,1,0:T(8,128)}, f32[1]{0:T(128)}, f32[4,256,384]{2,1,0:T(8,128)}, f32[384]{0:T(512)}, f32[192,768]{1,0:T(8,128)}, /*index=5*/f32[1...) custom-call(f32[4,256,384]{2,1,0:T(8,128)} %bitcast.5, ...), custom_call_target="tpu_custom_call" | custom-call | tf_op jit(solution)/shard_map/deliver/pallas_call | solution.py:2036

commit v8 on v7

--- a/solution.py
+++ b/solution.py
@@ -1276,11 +1276,8 @@
             slot = lax.rem(b, 2)
             return pltpu.make_async_copy(r.linear_hbm.at[b], q.linear.at[slot], r.line_load.at[slot])
 
-        for b in range(count):
-            for i in range(3):
-                row_load(i, b).start()
-        normed_load.start()
-        linear_load(0).start()
+        for i in range(3):
+            row_load(i, 0).start()
         inner = q.gate
         normed_out = r.values_grad
         chain = PairChain(
@@ -1295,6 +1292,11 @@
         pairs = channels // LANES
         for copy in loads:
             copy.wait()
+        for b in range(1, count):
+            for i in range(3):
+                row_load(i, b).start()
+        normed_load.start()
+        linear_load(0).start()
         pl.semaphore_wait(barrier, heads_n + n - 2)
         groups = q.pieces.shape[0]
 

time: 209 us -> 209 us (level)
  no operation moved by 1% of the time
where the time goes in v8:
time: 209 us; the launch traced here: 208 us
  Pallas kernels  208 us (100%)
    pallas_call x1, Pallas kernels, rear(): pl.pallas_call(functools.partial(rear_kernel, names, scoped, heads), out_...  123 us
    pallas_call x1, Pallas kernels, front(): pl.pallas_call(functools.partial(front_kernel, heads), out_shape=[shape(*...  80.3 us
    pallas_call x1, Pallas kernels, deliver(): pl.pallas_call(functools.partial(deliver_kernel, count), out_shape=[jax.S...  4.64 us

profile of v8, /device:TPU:0, one launch (start us, length us, event | category | flops | bytes accessed | tf_op | source)
XLA Modules:
  0.0 208.5 jit_solution(8989298386681155624)
XLA Ops:
  0.7 80.3 %front.1 = (bf16[4,256,1536]{2,1,0:T(8,128)(2,1)}, bf16[4,256,1024]{2,1,0:T(8,128)(2,1)}, f32[4,256,1024]{2,1,0:T(8,128)}, f32[4,256,768]{2,1,0:T(8,128)}, f32[4...) custom-call(f32[4,256,1536]{2,1,0:T(8,128)} %refs_10_.1, ...), custom_call_target="tpu_custom_call" | custom-call | tf_op jit(solution)/shard_map/front/pallas_call | solution.py:1028
  81.0 122.6 %rear.1 = (f32[4,256,384]{2,1,0:T(8,128)}, f32[192,768]{1,0:T(8,128)}, f32[192,768]{1,0:T(8,128)}, f32[192,768]{1,0:T(8,128)}, f32[192,256]{1,0:T(8,128)}, /*ind...) custom-call(bf16[4,1024,384]{2,1,0:T(8,128)(2,1)} %get-tuple-element, ...), custom_call_target="tpu_custom_call" | custom-call | tf_op jit(solution)/shard_map/rear/pallas_call | solution.py:2009
  203.6 4.6 %deliver.1 = (f32[4,256,384]{2,1,0:T(8,128)}, f32[1]{0:T(128)}, f32[4,256,384]{2,1,0:T(8,128)}, f32[384]{0:T(512)}, f32[192,768]{1,0:T(8,128)}, /*index=5*/f32[1...) custom-call(f32[4,256,384]{2,1,0:T(8,128)} %bitcast.5, ...), custom_call_target="tpu_custom_call" | custom-call | tf_op jit(solution)/shard_map/deliver/pallas_call | solution.py:2038
